TPU v7x, 256 devices: a whole 4x4x8 slice. The times are simulated.
256 devices in a mesh: group: 4 (over y), vocab: 32 (over z, x), rows: 2 (over core).
Axes of the slice: x: 4, y: 4, z: 8, core: 2. Of those that a mesh axis runs over, the one named last changes fastest.
Arguments:
- teacher_logits: bfloat16 [768, 98304], P(None, ('group', 'vocab', 'rows')), may hold values from -240 to 240
- student_hidden: bfloat16 [768, 4096], P('rows'), may hold values from -70 to 70
- head_weight: bfloat16 [4096, 98304], P(None, ('group', 'vocab')), may hold values from -0.25 to 0.25
- sampled_ids: int32 [768], P('rows'), may hold values from 0 to 98303
- assignment: int32 [768], replicated, may hold values from 0 to 767, each once
- row_scale: float32 [768], P('rows'), may hold values from 64 to 640
Outputs:
- loss: float32 [1], replicated
- hidden_grad: bfloat16 [768, 4096], P('rows', ('group', 'vocab'))
- head_grad: bfloat16 [4096, 98304], P('rows', ('group', 'vocab'))
Inputs may be any that keep to these rules, and one draw needn't show every extreme that they name: `assignment`: each of 0 to 767 appears once.
All inputs are finite; a program needn't handle non-finite values.
Results may differ from a plain program's by a relative error of at most 0.0015.
The roundings to bfloat16 on the way count: a program that leaves them out, or rounds other values in their place, can miss the bound.
Values may be sent and summed in bfloat16 or wider, within the bound.
No kernel may reach another device: no remote copies, remote signals or barrier semaphores. Data moves between devices by JAX's collectives and lax.ppermute only.
A program may use at most 128 MiB of HBM per device.

v0:
```python
import jax
import jax.numpy as jnp
from jax import lax
from jax.sharding import PartitionSpec as P

CE_WEIGHT = 0.5


def local_sums(logits, teacher, sampled_hot, top_student, top_teacher):
    exp_student = jnp.exp(logits - top_student[:, None])
    exp_teacher = jnp.exp(teacher - top_teacher[:, None])
    sum_student = jnp.sum(exp_student, axis=1)
    sum_teacher = jnp.sum(exp_teacher, axis=1)
    cross_term = jnp.sum(exp_teacher * (teacher - logits), axis=1)
    picked = jnp.sum(sampled_hot * logits, axis=1)
    return (sum_student, sum_teacher, cross_term, picked)


def body(teacher_logits, student_hidden, head_weight, sampled_ids, assignment, row_scale):
    ordered = jnp.take(teacher_logits, assignment, axis=0)
    teacher = lax.all_to_all(ordered, "rows", split_axis=0, concat_axis=1, tiled=True).astype(
        jnp.float32
    )
    logits = jnp.dot(student_hidden, head_weight, preferred_element_type=jnp.float32)
    vocab_cols = head_weight.shape[1]
    offset = lax.axis_index(("group", "vocab")) * vocab_cols
    columns = offset + lax.iota(jnp.int32, vocab_cols)
    sampled_hot = (columns[None, :] == sampled_ids[:, None]).astype(jnp.float32)
    top_student, top_teacher = lax.pmax(
        (jnp.max(logits, axis=1), jnp.max(teacher, axis=1)), ("group", "vocab")
    )
    sum_student, sum_teacher, cross_term, picked = lax.psum(
        local_sums(logits, teacher, sampled_hot, top_student, top_teacher), ("group", "vocab")
    )
    norm_student = top_student + jnp.log(sum_student)
    norm_teacher = top_teacher + jnp.log(sum_teacher)
    row_terms = (
        cross_term / sum_teacher - norm_teacher + norm_student + CE_WEIGHT * (norm_student - picked)
    )
    loss_sum = lax.psum(jnp.sum(row_terms), "rows")
    loss = (loss_sum / (logits.shape[0] * lax.axis_size("rows"))).reshape(1)
    prob_student = jnp.exp(logits - norm_student[:, None])
    prob_teacher = jnp.exp(teacher - norm_teacher[:, None])
    grad_logits = (
        row_scale[:, None]
        * ((1.0 + CE_WEIGHT) * prob_student - prob_teacher - CE_WEIGHT * sampled_hot)
    ).astype(jnp.bfloat16)
    partial_hidden = lax.dot_general(
        grad_logits, head_weight, (((1,), (1,)), ((), ())), preferred_element_type=jnp.float32
    )
    hidden_grad = lax.psum_scatter(
        partial_hidden, ("group", "vocab"), scatter_dimension=1, tiled=True
    ).astype(jnp.bfloat16)
    head_sum = lax.psum_scatter(
        lax.dot_general(
            student_hidden,
            grad_logits,
            (((0,), (0,)), ((), ())),
            preferred_element_type=jnp.float32,
        ),
        "rows",
        scatter_dimension=0,
        tiled=True,
    )
    return (loss, hidden_grad, head_sum.astype(jnp.bfloat16))


def solution(mesh):
    in_specs = (
        P(None, ("group", "vocab", "rows")),
        P("rows", None),
        P(None, ("group", "vocab")),
        P("rows"),
        P(),
        P("rows"),
    )
    out_specs = (P(), P("rows", ("group", "vocab")), P("rows", ("group", "vocab")))
    return jax.shard_map(body, mesh=mesh, in_specs=in_specs, out_specs=out_specs, check_vma=False)
```

profile of v0, /device:TPU:32, one launch (start us, length us, event | category | flops | bytes accessed | tf_op | source)
XLA Modules:
  0.0 1590.9 jit_solution(893303823522357418)
XLA Ops:
  7.2 0.0 copy-start
  7.2 0.8 compare_and_fusion
  8.0 0.8 compare_select_fusion.2
  8.8 4.2 gather_fusion
  13.1 2.1 broadcast_select_fusion
  15.1 4.2 all-to-all-start
  19.4 0.0 reduce-scatter.3.cloned.1.call-start
  19.4 1.8 all-to-all-done
  21.3 1.4 fusion.9
  22.7 1.1 copy.16
  23.8 0.0 copy-done
  23.8 0.0 copy-start.1
  23.8 6.5 fusion.10
  30.3 341.9 %all-reduce.1 = (f32[384]{0:T(512)S(1)}, f32[384]{0:T(512)S(1)}) all-reduce(f32[384]{0:T(512)S(1)} %get-tuple-element.26, bf16[384]{0:T(512)(128)(2,1)S(1)} %get-tuple-element.23), channel_id=1, replica_groups=mesh['group'=4,'vocab'=32,'rows'=2] {'group','vocab'}, use_global_device_ids=true, to_apply=%region_7.8 | all-reduce | flops 768 | bytes 5376 | tf_op jit(solution)/shard_map/pmax | solution.py:29
  372.2 0.0 copy-done.1
  372.2 0.0 copy-start.2
  372.2 2.4 multiply_reduce_fusion
  374.6 1.4 fusion.1
  376.0 346.4 %all-reduce = (f32[384]{0:T(512)S(1)}, f32[384]{0:T(512)S(1)}, f32[384]{0:T(512)S(1)}, f32[384]{0:T(512)S(1)}) all-reduce(f32[384]{0:T(512)S(1)} %get-tuple-element.14, f32[384]{0:T(512)S(1)} %get-tuple-element.13, f32[384]{0:T(512)S(1)} %get-tuple-element.12, ...), channel_id=1, replica_groups=mesh['group'=4,'vocab'=32,'rows'=2] {'group','vocab'}, use_global_device_ids=true, to_apply=%region_9.10 | all-reduce | flops 1536 | bytes 12288 | tf_op jit(solution)/shard_map/psum | solution.py:32
  722.4 0.6 add_reduce_fusion
  723.0 0.0 copy-done.2
  723.0 9.9 fusion.7
  732.9 0.0 reduce-scatter.3.cloned.1.call-update
  732.9 0.0 reduce-scatter.5.cloned.1.call-start
  733.0 8.6 convolution_bitcast_fusion
  741.6 0.0 reduce-scatter.5.cloned.1.call-update
  741.6 3.1 psum.39
  745.4 799.2 %reduce-scatter.3.cloned.1.call-done = f32[384,32]{0,1:T(8,128)} async-done(((f32[384,4096]{0,1:T(8,128)}), f32[384,32]{0,1:T(8,128)}) %reduce-scatter.3.cloned.1.call-update) | async-done | bytes 49168 | tf_op jit(solution)/shard_map/reduce_scatter | solution.py:51
  1544.6 1.4 convert_element_type.28
  1546.0 27.3 %reduce-scatter.5.cloned.1.call-done = f32[2048,768]{0,1:T(8,128)} async-done(((f32[4096,768]{0,1:T(8,128)}), f32[2048,768]{0,1:T(8,128)}) %reduce-scatter.5.cloned.1.call-update) | async-done | bytes 6291472 | tf_op jit(solution)/shard_map/reduce_scatter | solution.py:54
  1573.3 4.9 convert_element_type.29
  1578.3 4.6 copy.15
  (3 shorter events, 0.0 us)
Async XLA Ops:
  7.2 16.6 %copy-start = (bf16[384,4096]{1,0:T(8,128)(2,1)S(1)}, bf16[384,4096]{1,0:T(8,128)(2,1)}, u32[]{:S(2)}) copy-start(bf16[384,4096]{1,0:T(8,128)(2,1)} %param.7) | copy-start | bytes 9437188
  15.1 6.1 all-to-all-start
  19.4 1525.2 %reduce-scatter.3.cloned.1.call-start = ((), (), s32[]{:S(2)}) async-start(), calls=%async_computation.3 | async-start | bytes 6340608 | tf_op jit(solution)/shard_map/reduce_scatter | solution.py:51
  23.8 348.4 %copy-start.1 = (s32[384]{0:T(512)S(1)}, s32[384]{0:T(512)}, u32[]{:S(2)}) copy-start(s32[384]{0:T(512)} %param.9) | copy-start | bytes 4612
  372.2 350.8 %copy-start.2 = (f32[384]{0:T(512)S(1)}, f32[384]{0:T(512)}, u32[]{:S(2)}) copy-start(f32[384]{0:T(512)} %param.11) | copy-start | bytes 4612
  732.9 840.4 %reduce-scatter.5.cloned.1.call-start = ((), (), s32[]{:S(2)}) async-start(), calls=%async_computation.4 | async-start | bytes 18874368 | tf_op jit(solution)/shard_map/reduce_scatter | solution.py:54
Sparse Core Ops, SparseCore 0:
  733.1 811.4 reduce-scatter.2
  1547.3 25.9 reduce-scatter.4
where the time goes:
time: 1590 us
  waiting for transfers between devices  828 us (52%)
  blocking collectives  691 us (43%)
  matrix products  25 us (2%)
  other arithmetic  15.9 us (1%)
  between operations  15.9 us (1%)
    reduce_scatter x1, waiting for transfers between devices, body(): lax.psum_scatter(partial_hidden, ('group', 'vocab'), scatter_dimension=1,...  799 us
    psum x1, blocking collectives, body(): lax.psum(local_sums(logits, teacher, sampled_hot, top_student, top_teache...  346 us
    pmax x1, blocking collectives, body(): lax.pmax((jnp.max(logits, axis=1), jnp.max(teacher, axis=1)), ('group', '...  342 us
  transfers between devices with their start and end apart: 3, of which 3 were waited for; matrix products, arithmetic and copies ran while one was open for 1% of the time, Pallas kernels for 0%

commit v1 on v0

v1 whole, which is shorter than its diff:
```python
import functools

import jax
import jax.numpy as jnp
from jax import lax
from jax.experimental import pallas as pl
from jax.experimental.pallas import tpu as pltpu
from jax.sharding import Mesh, PartitionSpec as P

CE_WEIGHT = 0.5
SEND_SCALE = 64.0
VMEM = 48 * 1024 * 1024
F32 = jnp.float32
BF16 = jnp.bfloat16
F16 = jnp.float16


def params(*semantics):
    return pltpu.CompilerParams(vmem_limit_bytes=VMEM, dimension_semantics=semantics or None)


def shift(a, axis, by):
    n = lax.axis_size(axis)
    return lax.ppermute(a, axis, [(i, (i + by) % n) for i in range(n)])


def logits_kernel(h_ref, w_ref, out_ref):
    k = pl.program_id(0)
    part = jnp.dot(h_ref[...], w_ref[...], preferred_element_type=F32)

    @pl.when(k == 0)
    def _():
        out_ref[...] = part

    @pl.when(k > 0)
    def _():
        out_ref[...] += part


def student_logits(hidden, head, steps=8):
    rows, depth = hidden.shape
    cols = head.shape[1]
    kb = depth // steps
    return pl.pallas_call(
        logits_kernel,
        out_shape=jax.ShapeDtypeStruct((rows, cols), F32),
        grid=(steps,),
        in_specs=[
            pl.BlockSpec((rows, kb), lambda k: (0, k)),
            pl.BlockSpec((kb, cols), lambda k: (k, 0)),
        ],
        out_specs=pl.BlockSpec((rows, cols), lambda k: (0, 0)),
        compiler_params=params("arbitrary"),
        cost_estimate=pl.CostEstimate(
            flops=2 * rows * depth * cols,
            bytes_accessed=2 * (rows * depth + depth * cols) + 4 * rows * cols,
            transcendentals=0,
        ),
        name="student_logits",
    )(hidden, head)


def stats_kernel(pos_ref, l_ref, own_ref, oth_ref, assign_ref, ids_ref, stats_ref, t_ref):
    rows, cols = l_ref.shape
    half = cols // 2
    total = own_ref.shape[0]
    pick = (lax.broadcasted_iota(jnp.int32, (rows, total), 1) == assign_ref[...]).astype(BF16)
    own = jnp.dot(pick, own_ref[...], preferred_element_type=F32)
    oth = jnp.dot(pick, oth_ref[...], preferred_element_type=F32)
    first = pos_ref[0] == 0
    teacher = jnp.concatenate([jnp.where(first, own, oth), jnp.where(first, oth, own)], axis=1)
    t_ref[...] = teacher.astype(BF16)
    logits = l_ref[...]
    top_s = jnp.max(logits, axis=1, keepdims=True)
    sum_s = jnp.sum(jnp.exp(logits - top_s), axis=1, keepdims=True)
    top_t = jnp.max(teacher, axis=1, keepdims=True)
    exp_t = jnp.exp(teacher - top_t)
    sum_t = jnp.sum(exp_t, axis=1, keepdims=True)
    cross = jnp.sum(exp_t * (teacher - logits), axis=1, keepdims=True)
    columns = pos_ref[1] + lax.broadcasted_iota(jnp.int32, (rows, cols), 1)
    picked = jnp.sum(jnp.where(columns == ids_ref[...], logits, 0.0), axis=1, keepdims=True)
    lane = lax.broadcasted_iota(jnp.int32, (rows, 128), 1)
    packed = jnp.zeros((rows, 128), F32)
    for at, value in enumerate((top_s, sum_s, top_t, sum_t, cross, picked)):
        packed = jnp.where(lane == at, value, packed)
    stats_ref[...] = packed.T[:8, :]


def local_stats(pos, logits, own, oth, assign, ids):
    rows, cols = logits.shape
    whole = pl.BlockSpec(memory_space=pltpu.VMEM)
    return pl.pallas_call(
        stats_kernel,
        out_shape=(
            jax.ShapeDtypeStruct((8, rows), F32),
            jax.ShapeDtypeStruct((rows, cols), BF16),
        ),
        in_specs=[pl.BlockSpec(memory_space=pltpu.SMEM)] + [whole] * 5,
        out_specs=(whole, whole),
        compiler_params=params(),
        cost_estimate=pl.CostEstimate(
            flops=2 * rows * cols * own.shape[0],
            bytes_accessed=4 * rows * cols + 4 * own.size + 2 * rows * cols,
            transcendentals=2 * rows * cols,
        ),
        name="local_stats",
    )(pos, logits, own, oth, assign, ids)


def merge(parts):
    row = lambda at: [p[at : at + 1, :] for p in parts]
    tops_s, sums_s, tops_t, sums_t, crosses, pickeds = (row(at) for at in range(6))
    top_s = functools.reduce(jnp.maximum, tops_s)
    top_t = functools.reduce(jnp.maximum, tops_t)
    scale_s = [jnp.exp(t - top_s) for t in tops_s]
    scale_t = [jnp.exp(t - top_t) for t in tops_t]
    add = lambda xs: functools.reduce(jnp.add, xs)
    return (
        top_s,
        add([a * b for a, b in zip(sums_s, scale_s)]),
        top_t,
        add([a * b for a, b in zip(sums_t, scale_t)]),
        add([a * b for a, b in zip(crosses, scale_t)]),
        add(pickeds),
    )


def merge_kernel(*refs):
    out = refs[-1]
    merged = merge([r[...] for r in refs[:-1]])
    out[...] = jnp.zeros_like(out)
    for at, value in enumerate(merged):
        out[at : at + 1, :] = value


def merge_stats(parts):
    whole = pl.BlockSpec(memory_space=pltpu.VMEM)
    return pl.pallas_call(
        merge_kernel,
        out_shape=jax.ShapeDtypeStruct(parts[0].shape, F32),
        in_specs=[whole] * len(parts),
        out_specs=whole,
        compiler_params=params(),
        name="merge_stats",
    )(*parts)


def grad_kernel(n_parts, pos_ref, l_ref, t_ref, ids_ref, scale_ref, *refs):
    parts, (g_ref, loss_ref) = refs[:n_parts], refs[n_parts:]
    rows, cols = l_ref.shape
    top_s, sum_s, top_t, sum_t, cross, picked = merge([p[...] for p in parts])
    norm_s = top_s + jnp.log(sum_s)
    norm_t = top_t + jnp.log(sum_t)
    terms = cross / sum_t - norm_t + norm_s + CE_WEIGHT * (norm_s - picked)
    loss_ref[...] = jnp.broadcast_to(jnp.sum(terms, axis=1, keepdims=True), loss_ref.shape)
    sub = lax.broadcasted_iota(jnp.int32, (128, rows), 0)
    turned = jnp.where(sub == 0, norm_s, jnp.where(sub == 1, norm_t, 0.0)).T
    norm_s, norm_t = turned[:, 0:1], turned[:, 1:2]
    columns = pos_ref[1] + lax.broadcasted_iota(jnp.int32, (rows, cols), 1)
    hot = jnp.where(columns == ids_ref[...], CE_WEIGHT, 0.0)
    prob_s = jnp.exp(l_ref[...] - norm_s)
    prob_t = jnp.exp(t_ref[...].astype(F32) - norm_t)
    g_ref[...] = (scale_ref[...] * ((1.0 + CE_WEIGHT) * prob_s - prob_t - hot)).astype(BF16)


def grad_logits(pos, logits, teacher, ids, scale, parts):
    rows, cols = logits.shape
    whole = pl.BlockSpec(memory_space=pltpu.VMEM)
    return pl.pallas_call(
        functools.partial(grad_kernel, len(parts)),
        out_shape=(
            jax.ShapeDtypeStruct((rows, cols), BF16),
            jax.ShapeDtypeStruct((8, 128), F32),
        ),
        in_specs=[pl.BlockSpec(memory_space=pltpu.SMEM)] + [whole] * (4 + len(parts)),
        out_specs=(whole, whole),
        compiler_params=params(),
        cost_estimate=pl.CostEstimate(
            flops=8 * rows * cols,
            bytes_accessed=8 * rows * cols,
            transcendentals=2 * rows * cols,
        ),
        name="grad_logits",
    )(pos, logits, teacher, ids, scale, *parts)


def hidden_kernel(nz, pos_ref, w_ref, g_ref, o1, o2, o3, o0):
    step = pl.program_id(0)
    w = w_ref[...].reshape(nz * 16, w_ref.shape[-1])
    part = lax.dot_general(w, g_ref[...], (((1,), (1,)), ((), ())), preferred_element_type=F32)
    z = pos_ref[4]

    def put(ref, value):
        for at in range(nz):
            ref[0, lax.rem(at - z + nz, nz)] = value[at * 16 : (at + 1) * 16].astype(ref.dtype)

    for k, ref in enumerate((o1, o2, o3, o0)):

        @pl.when(step // 4 == k)
        def _(ref=ref, k=k):
            put(ref, part * SEND_SCALE if k < 3 else part)


def hidden_part(pos, head6, g, first_x, half):
    ny, nz, nx, _, sub, cols = head6.shape
    rows = g.shape[0]

    def w_map(s, pos):
        far, near = (s // 4 + 1) % 4, s % 4
        dx, dy = (far, near) if first_x else (near, far)
        return ((pos[2] + dy) % ny, 0, (pos[3] + dx) % nx, half, 0, 0)

    def out_spec(k):
        return pl.BlockSpec(
            (1, nz, sub, rows), lambda s, pos: (jnp.clip(s - 4 * k, 0, 3), 0, 0, 0)
        )

    shape = (4, nz, sub, rows)
    return pl.pallas_call(
        functools.partial(hidden_kernel, nz),
        out_shape=[jax.ShapeDtypeStruct(shape, F32)] * 4,
        grid_spec=pltpu.PrefetchScalarGridSpec(
            num_scalar_prefetch=1,
            grid=(16,),
            in_specs=[
                pl.BlockSpec((1, nz, 1, 1, sub, cols), w_map),
                pl.BlockSpec((rows, cols), lambda s, pos: (0, 0)),
            ],
            out_specs=[out_spec(k) for k in range(4)],
        ),
        compiler_params=params("arbitrary"),
        cost_estimate=pl.CostEstimate(
            flops=rows * cols * ny * nz * nx * 2 * sub,
            bytes_accessed=head6.size + 8 * rows * ny * nz * nx * sub,
            transcendentals=0,
        ),
        name="hidden_part",
    )(pos, head6, g)


def head_kernel(pos_ref, own_ref, oth_ref, g_own_ref, g_oth_ref, out_ref):
    dims = (((0,), (0,)), ((), ()))
    total = lax.dot_general(own_ref[...], g_own_ref[...], dims, preferred_element_type=F32)
    total += lax.dot_general(oth_ref[...], g_oth_ref[...], dims, preferred_element_type=F32)
    out_ref[...] = total.astype(BF16)


def head_grad(pos, hidden, hidden_oth, g, g_oth, block=256):
    rows, depth = hidden.shape
    cols = g.shape[1]
    width = hidden_oth.shape[1]
    steps = width // block
    return pl.pallas_call(
        head_kernel,
        out_shape=jax.ShapeDtypeStruct((width, cols), BF16),
        grid_spec=pltpu.PrefetchScalarGridSpec(
            num_scalar_prefetch=1,
            grid=(steps,),
            in_specs=[
                pl.BlockSpec((rows, block), lambda i, pos: (0, pos[0] * steps + i)),
                pl.BlockSpec((rows, block), lambda i, pos: (0, i)),
                pl.BlockSpec((rows, cols), lambda i, pos: (0, 0)),
                pl.BlockSpec((rows, cols), lambda i, pos: (0, 0)),
            ],
            out_specs=pl.BlockSpec((block, cols), lambda i, pos: (i, 0)),
        ),
        compiler_params=params("arbitrary"),
        cost_estimate=pl.CostEstimate(
            flops=4 * rows * width * cols,
            bytes_accessed=4 * rows * width + 4 * rows * cols + 2 * width * cols,
            transcendentals=0,
        ),
        name="head_grad",
    )(pos, hidden, hidden_oth, g, g_oth)


def body(teacher, hidden, head, ids, assignment, row_scale):
    c, x, y, z = (lax.axis_index(a) for a in ("c", "x", "y", "z"))
    rows, depth = hidden.shape
    cols = head.shape[1]
    block = lax.axis_index(("y", "z", "x"))
    pos = jnp.stack([c, block * cols, y, x, z]).astype(jnp.int32)

    teacher_oth = shift(teacher, "c", 1)
    width = depth // 2
    hidden_oth = shift(lax.dynamic_slice(hidden, (0, (1 - c) * width), (rows, width)), "c", 1)
    assign = lax.dynamic_slice(assignment, (c * rows,), (rows,)).reshape(rows, 1)
    ids = ids.reshape(rows, 1)
    scale = row_scale.reshape(rows, 1)

    logits = student_logits(hidden, head)
    stats, teacher_rows = local_stats(pos, logits, teacher, teacher_oth, assign, ids)
    for axis in ("x", "y"):
        stats = merge_stats([stats] + [shift(stats, axis, d) for d in (1, 2, 3)])
    parts = [stats] + [shift(stats, "z", d) for d in range(1, 8)]
    g, loss_part = grad_logits(pos, logits, teacher_rows, ids, scale, parts)
    g_oth = shift(g, "c", 1)

    ny, nz, nx = (lax.axis_size(a) for a in ("y", "z", "x"))
    sub = depth // (ny * nz * nx) // 2
    head6 = head.reshape(ny, nz, nx, 2, sub, cols)

    def first_level(half, axis):
        *far, own = hidden_part(pos, head6, g, axis == "x", half)
        far = [shift(f.astype(F16), axis, d + 1) for d, f in enumerate(far)]
        return own, far

    own_a, far_a = first_level(0, "x")
    own_b, far_b = first_level(1, "y")
    add = lambda own, far: own + sum(f.astype(F32) for f in far) * (1.0 / SEND_SCALE)
    sum_a, sum_b = add(own_a, far_a), add(own_b, far_b)
    sum_a = sum_a[0] + sum(shift(sum_a[d], "y", d) for d in (1, 2, 3))
    sum_b = sum_b[0] + sum(shift(sum_b[d], "x", d) for d in (1, 2, 3))
    both = jnp.concatenate([sum_a, sum_b], axis=1)
    hidden_sum = both[0] + sum(shift(both[d], "z", d) for d in range(1, 8))
    hidden_grad = hidden_sum.T.astype(BF16)

    head_out = head_grad(pos, hidden, hidden_oth, g, g_oth)
    loss_all = loss_part + shift(loss_part, "c", 1)
    loss = loss_all[0, :1] / (2 * rows)
    return loss, hidden_grad, head_out


def solution(mesh):
    ny, nzx, nc = mesh.devices.shape
    nx = 4
    fine = Mesh(mesh.devices.reshape(ny, nzx // nx, nx, nc), ("y", "z", "x", "c"))
    vocab = ("y", "z", "x")
    in_specs = (
        P(None, vocab + ("c",)),
        P("c", None),
        P(None, vocab),
        P("c"),
        P(),
        P("c"),
    )
    out_specs = (P(), P("c", vocab), P("c", vocab))
    return jax.shard_map(body, mesh=fine, in_specs=in_specs, out_specs=out_specs, check_vma=False)
```

time: 1590 us -> 159 us (0.10)
  waiting for transfers between devices: 828 us -> 39.3 us
  blocking collectives: 691 us -> 0 us
  starting transfers between devices: 4.31 us -> 63.5 us
  Pallas kernels: 0 us -> 41.5 us
  matrix products: 25 us -> 0 us
    reduce_scatter x2 -> x0, waiting for transfers between devices: 827 us -> none  [the longest x1 799 us: body(): lax.psum_scatter(partial_hidden, ('group', 'vocab'), scatter_dimension=1,...]
    psum x2 -> x0, blocking collectives: 349 us -> none  [the longest x1 346 us: body(): lax.psum(local_sums(logits, teacher, sampled_hot, top_student, top_teache...]
    pmax x1 -> x0, blocking collectives: 342 us -> none  [body(): lax.pmax((jnp.max(logits, axis=1), jnp.max(teacher, axis=1)), ('group', '...]
    ppermute x0 -> x36, starting transfers between devices: none -> 63.5 us  [shift(): return lax.ppermute(a, axis, [(i, (i + by) % n) for i in range(n)])]
    pallas_call x0 -> x8, Pallas kernels: none -> 41.5 us  [the longest x2 23.5 us: hidden_part(): pl.pallas_call(functools.partial(hidden_kernel, nz), out_shape=[jax.Shape...]
    ppermute x0 -> x36, waiting for transfers between devices: none -> 39.3 us  [shift(): return lax.ppermute(a, axis, [(i, (i + by) % n) for i in range(n)])]
    dot_general x3 -> x0, matrix products: 25 us -> none  [the longest x1 9.9 us: body(): lax.dot_general(grad_logits, head_weight, (((1,), (1,)), ((), ())), prefe...]
  transfers between devices with their start and end apart: 3 -> 36, of which waited for: 3 -> 15; matrix products, arithmetic and copies ran while one was open for 1% -> 4% of each run, Pallas kernels for 0% -> 12%
where the time goes in v1:
time: 159 us; the launch traced here: 157 us
  starting transfers between devices  63.5 us (40%)
  Pallas kernels  41.5 us (26%)
  waiting for transfers between devices  39.3 us (25%)
  local copies, waits for them, and re-layouts  5.33 us (3%)
  other arithmetic  4.22 us (3%)
  between operations  2.72 us (2%)
    ppermute x36, starting transfers between devices, shift(): return lax.ppermute(a, axis, [(i, (i + by) % n) for i in range(n)])  63.5 us
    ppermute x36, waiting for transfers between devices, shift(): return lax.ppermute(a, axis, [(i, (i + by) % n) for i in range(n)])  39.3 us
    pallas_call x2, Pallas kernels, hidden_part(): pl.pallas_call(functools.partial(hidden_kernel, nz), out_shape=[jax.Shape...  23.5 us
    pallas_call x1, Pallas kernels, student_logits(): pl.pallas_call(logits_kernel, out_shape=jax.ShapeDtypeStruct((rows, cols)...  7.79 us
    pallas_call x1, Pallas kernels, head_grad(): pl.pallas_call(head_kernel, out_shape=jax.ShapeDtypeStruct((width, cols),...  6.87 us
  transfers between devices with their start and end apart: 36, of which 15 were waited for; matrix products, arithmetic and copies ran while one was open for 4% of the time, Pallas kernels for 12%

profile of v1, /device:TPU:32, one launch (start us, length us, event | category | flops | bytes accessed | tf_op | source)
XLA Modules:
  0.0 156.5 jit_solution(10858667933046311883)
XLA Ops:
  2.5 1.9 %copy-done = bf16[384,4096]{1,0:T(8,128)(2,1)S(1)} copy-done((bf16[384,4096]{1,0:T(8,128)(2,1)S(1)}, bf16[384,4096]{1,0:T(8,128)(2,1)}, u32[]{:S(2)}) %copy-start) | copy-done | bytes 3145752
  4.4 7.8 %student_logits.1.l_ref = f32[384,768]{1,0:T(8,128)S(1)} custom-call(bf16[384,4096]{1,0:T(8,128)(2,1)S(1)} %copy-done, bf16[4096,768]{1,0:T(8,128)(2,1)} %w_ref.1), custom_call_target="tpu_custom_call" | custom-call | flops 2415919104 | bytes 10616832 | tf_op jit(solution)/shard_map/student_logits/pallas_call | solution.py:44
  12.2 2.0 %local_stats.1 = (f32[8,384]{1,0:T(8,128)S(1)}, bf16[384,768]{1,0:T(8,128)(2,1)S(1)}) custom-call(s32[5]{0:T(128)S(1)} %stack.23.pos_ref, f32[384,768]{1,0:T(8,128)S(1)} %student_logits.1.l_ref, bf16[768,384]{1,0:T(8,128)(2,1)S(1)} %copy-done.6, bf16[768,384]{1,0:T(8,128)(2,1)S(1)} %collective-permute-done.oth_ref, s32[384,1]{1,0:T(8,128)S(1)} %reshape.24.assign_ref, ...), custom_call_target="tpu_custom_call" | custom-call | flops 452984832 | bytes 2949120 | tf_op jit(solution)/shard_map/local_stats/pallas_call | solution.py:92
  14.2 1.5 collective-permute-start.1
  15.8 2.7 %collective-permute-start.2 = (f32[8,384]{1,0:T(8,128)S(1)}, f32[8,384]{1,0:T(8,128)S(1)}, u32[]{:S(2)}, u32[]{:S(2)}) collective-permute-start(f32[8,384]{1,0:T(8,128)S(1)} %get-tuple-element.16.refs_0_), channel_id=1, source_target_pairs={{0,4},{2,6},{4,0},{6,2},{1,5},{3,7},{5,1},{7,3},{8,12},{10,14},{12... | collective-permute-start | bytes 36872 | tf_op jit(solution)/shard_map/ppermute | solution.py:24
  18.5 1.4 collective-permute-start.3
  20.0 1.0 collective-permute-done.2.refs_2_
  21.0 1.2 collective-permute-done.3.refs_3_
  22.3 1.7 %collective-permute-start.4 = (f32[8,384]{1,0:T(8,128)S(1)}, f32[8,384]{1,0:T(8,128)S(1)}, u32[]{:S(2)}, u32[]{:S(2)}) collective-permute-start(f32[8,384]{1,0:T(8,128)S(1)} %merge_stats.2.refs_0_), channel_id=1, source_target_pairs={{0,64},{64,128},{128,192},{192,0},{1,65},{65,129},{129,193},{193,1... | collective-permute-start | bytes 36872 | tf_op jit(solution)/shard_map/ppermute | solution.py:24
  23.9 2.9 %collective-permute-start.5 = (f32[8,384]{1,0:T(8,128)S(1)}, f32[8,384]{1,0:T(8,128)S(1)}, u32[]{:S(2)}, u32[]{:S(2)}) collective-permute-start(f32[8,384]{1,0:T(8,128)S(1)} %merge_stats.2.refs_0_), channel_id=1, source_target_pairs={{0,128},{64,192},{128,0},{192,64},{1,129},{65,193},{129,1},{193,65... | collective-permute-start | bytes 36872 | tf_op jit(solution)/shard_map/ppermute | solution.py:24
  26.8 1.3 collective-permute-start.6
  28.2 1.0 collective-permute-done.5.refs_2_
  29.1 1.4 collective-permute-done.6.refs_3_
  30.5 2.0 %collective-permute-start.7 = (f32[8,384]{1,0:T(8,128)S(1)}, f32[8,384]{1,0:T(8,128)S(1)}, u32[]{:S(2)}, u32[]{:S(2)}) collective-permute-start(f32[8,384]{1,0:T(8,128)S(1)} %merge_stats.3.refs_0_), channel_id=1, source_target_pairs={{0,8},{8,16},{16,24},{24,32},{32,40},{40,48},{48,56},{56,0},{1,9},... | collective-permute-start | bytes 36872 | tf_op jit(solution)/shard_map/ppermute | solution.py:24
  32.5 4.5 %collective-permute-start.8 = (f32[8,384]{1,0:T(8,128)S(1)}, f32[8,384]{1,0:T(8,128)S(1)}, u32[]{:S(2)}, u32[]{:S(2)}) collective-permute-start(f32[8,384]{1,0:T(8,128)S(1)} %merge_stats.3.refs_0_), channel_id=1, source_target_pairs={{0,16},{8,24},{16,32},{24,40},{32,48},{40,56},{48,0},{56,8},{1,17}... | collective-permute-start | bytes 36872 | tf_op jit(solution)/shard_map/ppermute | solution.py:24
  37.0 1.9 %collective-permute-start.9 = (f32[8,384]{1,0:T(8,128)S(1)}, f32[8,384]{1,0:T(8,128)S(1)}, u32[]{:S(2)}, u32[]{:S(2)}) collective-permute-start(f32[8,384]{1,0:T(8,128)S(1)} %merge_stats.3.refs_0_), channel_id=1, source_target_pairs={{0,24},{8,32},{16,40},{24,48},{32,56},{40,0},{48,8},{56,16},{1,25}... | collective-permute-start | bytes 36872 | tf_op jit(solution)/shard_map/ppermute | solution.py:24
  38.9 1.4 collective-permute-start.10
  40.4 3.1 %collective-permute-start.11 = (f32[8,384]{1,0:T(8,128)S(1)}, f32[8,384]{1,0:T(8,128)S(1)}, u32[]{:S(2)}, u32[]{:S(2)}) collective-permute-start(f32[8,384]{1,0:T(8,128)S(1)} %merge_stats.3.refs_0_), channel_id=1, source_target_pairs={{0,40},{8,48},{16,56},{24,0},{32,8},{40,16},{48,24},{56,32},{1,41}... | collective-permute-start | bytes 36872 | tf_op jit(solution)/shard_map/ppermute | solution.py:24
  43.5 2.4 %collective-permute-start.12 = (f32[8,384]{1,0:T(8,128)S(1)}, f32[8,384]{1,0:T(8,128)S(1)}, u32[]{:S(2)}, u32[]{:S(2)}) collective-permute-start(f32[8,384]{1,0:T(8,128)S(1)} %merge_stats.3.refs_0_), channel_id=1, source_target_pairs={{0,48},{8,56},{16,0},{24,8},{32,16},{40,24},{48,32},{56,40},{1,49}... | collective-permute-start | bytes 36872 | tf_op jit(solution)/shard_map/ppermute | solution.py:24
  45.9 2.2 %collective-permute-start.13 = (f32[8,384]{1,0:T(8,128)S(1)}, f32[8,384]{1,0:T(8,128)S(1)}, u32[]{:S(2)}, u32[]{:S(2)}) collective-permute-start(f32[8,384]{1,0:T(8,128)S(1)} %merge_stats.3.refs_0_), channel_id=1, source_target_pairs={{0,56},{8,0},{16,8},{24,16},{32,24},{40,32},{48,40},{56,48},{1,57}... | collective-permute-start | bytes 36872 | tf_op jit(solution)/shard_map/ppermute | solution.py:24
  48.3 1.3 collective-permute-done.13.refs_7_
  49.6 1.3 grad_logits.1
  50.9 11.7 %hidden_part.2 = (f32[4,8,16,384]{3,2,1,0:T(8,128)S(1)}, f32[4,8,16,384]{3,2,1,0:T(8,128)S(1)}, f32[4,8,16,384]{3,2,1,0:T(8,128)S(1)}, f32[4,8,16,384]{3,2,1,0:T(8,128)S(1)}) custom-call(s32[5]{0:T(128)S(1)} %stack.23.pos_ref, bf16[4,8,4,2,16,768]{5,4,3,2,1,0:T(8,128)(2,1)} %bitcast.51, bf16[384,768]{1,0:T(8,128)(2,1)S(1)} %get-tuple-element.18.g_ref.g_own_ref), custom_call_target="tpu_custom_call" | custom-call | flops 1207959552 | bytes 9437184 | tf_op jit(solution)/shard_map/hidden_part/pallas_call | solution.py:219
  63.5 2.6 %collective-permute-start.17 = (f16[4,8,16,384]{3,2,1,0:T(8,128)(2,1)}, f16[4,8,16,384]{3,2,1,0:T(8,128)(2,1)}, u32[]{:S(2)}, u32[]{:S(2)}) collective-permute-start(f16[4,8,16,384]{3,2,1,0:T(8,128)(2,1)} %convert_element_type.46), channel_id=1, source_target_pairs={{0,6},{2,0},{4,2},{6,4},{1,7},{3,1},{5,3},{7,5},{8,14},{10,8},{12,... | collective-permute-start | bytes 1179656 | tf_op jit(solution)/shard_map/ppermute | solution.py:24
  69.1 11.7 %hidden_part.3 = (f32[4,8,16,384]{3,2,1,0:T(8,128)S(1)}, f32[4,8,16,384]{3,2,1,0:T(8,128)S(1)}, f32[4,8,16,384]{3,2,1,0:T(8,128)S(1)}, f32[4,8,16,384]{3,2,1,0:T(8,128)S(1)}) custom-call(s32[5]{0:T(128)S(1)} %stack.23.pos_ref, bf16[4,8,4,2,16,768]{5,4,3,2,1,0:T(8,128)(2,1)} %bitcast.52, bf16[384,768]{1,0:T(8,128)(2,1)S(1)} %copy-done.3), custom_call_target="tpu_custom_call" | custom-call | flops 1207959552 | bytes 9437184 | tf_op jit(solution)/shard_map/hidden_part/pallas_call | solution.py:219
  81.0 2.6 %collective-permute-start.23 = (f16[4,8,16,384]{3,2,1,0:T(8,128)(2,1)S(1)}, f16[4,8,16,384]{3,2,1,0:T(8,128)(2,1)S(1)}, u32[]{:S(2)}, u32[]{:S(2)}) collective-permute-start(f16[4,8,16,384]{3,2,1,0:T(8,128)(2,1)S(1)} %convert_element_type.52), channel_id=1, source_target_pairs={{0,192},{64,0},{128,64},{192,128},{1,193},{65,1},{129,65},{193,129... | collective-permute-start | bytes 1179656 | tf_op jit(solution)/shard_map/ppermute | solution.py:24
  83.7 1.0 collective-permute-start.21
  84.6 1.4 multiply_add_fusion.1
  86.1 15.0 %collective-permute-done.23 = f16[4,8,16,384]{3,2,1,0:T(8,128)(2,1)S(1)} collective-permute-done((f16[4,8,16,384]{3,2,1,0:T(8,128)(2,1)S(1)}, f16[4,8,16,384]{3,2,1,0:T(8,128)(2,1)S(1)}, u32[]{:S(2)}, u32[]{:S(2)}) %collective-permute-start.23) | collective-permute-done | bytes 393248 | tf_op jit(solution)/shard_map/ppermute | solution.py:24
  101.2 3.7 %collective-permute-start.20 = (f32[8,16,384]{2,1,0:T(8,128)S(1)}, f32[8,16,384]{2,1,0:T(8,128)S(1)}, u32[]{:S(2)}, u32[]{:S(2)}) collective-permute-start(f32[8,16,384]{2,1,0:T(8,128)S(1)} %get-tuple-element.28), channel_id=1, source_target_pairs={{0,192},{64,0},{128,64},{192,128},{1,193},{65,1},{129,65},{193,129... | collective-permute-start | bytes 589832 | tf_op jit(solution)/shard_map/ppermute | solution.py:24
  104.8 1.5 collective-permute-start.19
  106.5 6.6 %collective-permute-done.20 = f32[8,16,384]{2,1,0:T(8,128)S(1)} collective-permute-done((f32[8,16,384]{2,1,0:T(8,128)S(1)}, f32[8,16,384]{2,1,0:T(8,128)S(1)}, u32[]{:S(2)}, u32[]{:S(2)}) %collective-permute-start.20) | collective-permute-done | bytes 196640 | tf_op jit(solution)/shard_map/ppermute | solution.py:24
  113.1 2.4 %collective-permute-start.26 = (f32[8,16,384]{2,1,0:T(8,128)S(1)}, f32[8,16,384]{2,1,0:T(8,128)S(1)}, u32[]{:S(2)}, u32[]{:S(2)}) collective-permute-start(f32[8,16,384]{2,1,0:T(8,128)S(1)} %get-tuple-element.31), channel_id=1, source_target_pairs={{0,6},{2,0},{4,2},{6,4},{1,7},{3,1},{5,3},{7,5},{8,14},{10,8},{12,... | collective-permute-start | bytes 589832 | tf_op jit(solution)/shard_map/ppermute | solution.py:24
  115.5 1.0 collective-permute-done.18
  116.5 2.6 %collective-permute-start.24 = (f32[8,16,384]{2,1,0:T(8,128)S(1)}, f32[8,16,384]{2,1,0:T(8,128)S(1)}, u32[]{:S(2)}, u32[]{:S(2)}) collective-permute-start(f32[8,16,384]{2,1,0:T(8,128)S(1)} %get-tuple-element.32), channel_id=1, source_target_pairs={{0,2},{2,4},{4,6},{6,0},{1,3},{3,5},{5,7},{7,1},{8,10},{10,12},{12... | collective-permute-start | bytes 589832 | tf_op jit(solution)/shard_map/ppermute | solution.py:24
  119.1 1.2 collective-permute-start.25
  121.1 2.2 %collective-permute-done.24 = f32[8,16,384]{2,1,0:T(8,128)S(1)} collective-permute-done((f32[8,16,384]{2,1,0:T(8,128)S(1)}, f32[8,16,384]{2,1,0:T(8,128)S(1)}, u32[]{:S(2)}, u32[]{:S(2)}) %collective-permute-start.24) | collective-permute-done | bytes 196640 | tf_op jit(solution)/shard_map/ppermute | solution.py:24
  123.4 2.9 %collective-permute-done.25 = f32[8,16,384]{2,1,0:T(8,128)S(1)} collective-permute-done((f32[8,16,384]{2,1,0:T(8,128)S(1)}, f32[8,16,384]{2,1,0:T(8,128)S(1)}, u32[]{:S(2)}, u32[]{:S(2)}) %collective-permute-start.25) | collective-permute-done | bytes 196640 | tf_op jit(solution)/shard_map/ppermute | solution.py:24
  126.4 2.5 %collective-permute-start.33 = (f32[32,384]{1,0:T(8,128)S(1)}, f32[32,384]{1,0:T(8,128)S(1)}, u32[]{:S(2)}, u32[]{:S(2)}) collective-permute-start(f32[32,384]{1,0:T(8,128)S(1)} %get-tuple-element.38), channel_id=1, source_target_pairs={{0,56},{8,0},{16,8},{24,16},{32,24},{40,32},{48,40},{56,48},{1,57}... | collective-permute-start | bytes 147464 | tf_op jit(solution)/shard_map/ppermute | solution.py:24
  128.9 2.1 %collective-permute-start.32 = (f32[32,384]{1,0:T(8,128)S(1)}, f32[32,384]{1,0:T(8,128)S(1)}, u32[]{:S(2)}, u32[]{:S(2)}) collective-permute-start(f32[32,384]{1,0:T(8,128)S(1)} %get-tuple-element.39), channel_id=1, source_target_pairs={{0,48},{8,56},{16,0},{24,8},{32,16},{40,24},{48,32},{56,40},{1,49}... | collective-permute-start | bytes 147464 | tf_op jit(solution)/shard_map/ppermute | solution.py:24
  131.0 1.6 %collective-permute-start.31 = (f32[32,384]{1,0:T(8,128)S(1)}, f32[32,384]{1,0:T(8,128)S(1)}, u32[]{:S(2)}, u32[]{:S(2)}) collective-permute-start(f32[32,384]{1,0:T(8,128)S(1)} %get-tuple-element.37), channel_id=1, source_target_pairs={{0,40},{8,48},{16,56},{24,0},{32,8},{40,16},{48,24},{56,32},{1,41}... | collective-permute-start | bytes 147464 | tf_op jit(solution)/shard_map/ppermute | solution.py:24
  132.6 4.5 %collective-permute-start.30 = (f32[32,384]{1,0:T(8,128)S(1)}, f32[32,384]{1,0:T(8,128)S(1)}, u32[]{:S(2)}, u32[]{:S(2)}) collective-permute-start(f32[32,384]{1,0:T(8,128)S(1)} %get-tuple-element.36), channel_id=1, source_target_pairs={{0,32},{8,40},{16,48},{24,56},{32,0},{40,8},{48,16},{56,24},{1,33}... | collective-permute-start | bytes 147464 | tf_op jit(solution)/shard_map/ppermute | solution.py:24
  138.1 2.5 %collective-permute-start.27 = (f32[32,384]{1,0:T(8,128)S(1)}, f32[32,384]{1,0:T(8,128)S(1)}, u32[]{:S(2)}, u32[]{:S(2)}) collective-permute-start(f32[32,384]{1,0:T(8,128)S(1)} %get-tuple-element.34), channel_id=1, source_target_pairs={{0,8},{8,16},{16,24},{24,32},{32,40},{40,48},{48,56},{56,0},{1,9},... | collective-permute-start | bytes 147464 | tf_op jit(solution)/shard_map/ppermute | solution.py:24
  140.7 0.9 collective-permute-done.30
  141.6 1.7 %collective-permute-start.28 = (f32[32,384]{1,0:T(8,128)S(1)}, f32[32,384]{1,0:T(8,128)S(1)}, u32[]{:S(2)}, u32[]{:S(2)}) collective-permute-start(f32[32,384]{1,0:T(8,128)S(1)} %get-tuple-element.33), channel_id=1, source_target_pairs={{0,16},{8,24},{16,32},{24,40},{32,48},{40,56},{48,0},{56,8},{1,17}... | collective-permute-start | bytes 147464 | tf_op jit(solution)/shard_map/ppermute | solution.py:24
  144.5 1.1 collective-permute-done.29
  145.5 2.4 %collective-permute-done.28 = f32[32,384]{1,0:T(8,128)S(1)} collective-permute-done((f32[32,384]{1,0:T(8,128)S(1)}, f32[32,384]{1,0:T(8,128)S(1)}, u32[]{:S(2)}, u32[]{:S(2)}) %collective-permute-start.28) | collective-permute-done | bytes 49184 | tf_op jit(solution)/shard_map/ppermute | solution.py:24
  148.5 6.9 %head_grad.1 = bf16[2048,768]{1,0:T(8,128)(2,1)} custom-call(s32[5]{0:T(128)S(1)} %stack.23.pos_ref, bf16[384,4096]{1,0:T(8,128)(2,1)S(1)} %copy-done.1, bf16[384,2048]{1,0:T(8,128)(2,1)S(1)} %collective-permute-done.34.oth_ref, bf16[384,768]{1,0:T(8,128)(2,1)S(1)} %copy-done.3, bf16[384,768]{1,0:T(8,128)(2,1)S(1)} %collective-permute-done.35.g_oth_ref), custom_call_target="tpu_custom_call" | custom-call | flops 2415919104 | bytes 7471104 | tf_op jit(solution)/shard_map/head_grad/pallas_call | solution.py:253
  (70 shorter events, 9.3 us)
Async XLA Ops:
  0.6 11.6 %collective-permute-start = (bf16[768,384]{1,0:T(8,128)(2,1)}, bf16[768,384]{1,0:T(8,128)(2,1)S(1)}, u32[]{:S(2)}, u32[]{:S(2)}) collective-permute-start(bf16[768,384]{1,0:T(8,128)(2,1)} %own_ref.2), channel_id=1, source_target_pairs={{0,1},{1,0},{2,3},{3,2},{4,5},{5,4},{6,7},{7,6},{8,9},{9,8},{10,11... | collective-permute-start | bytes 1769480 | tf_op jit(solution)/shard_map/ppermute | solution.py:24
  2.5 1.9 %copy-start = (bf16[384,4096]{1,0:T(8,128)(2,1)S(1)}, bf16[384,4096]{1,0:T(8,128)(2,1)}, u32[]{:S(2)}) copy-start(bf16[384,4096]{1,0:T(8,128)(2,1)} %own_ref.3) | copy-start | bytes 9437188
  4.4 7.8 %copy-start.6 = (bf16[768,384]{1,0:T(8,128)(2,1)S(1)}, bf16[768,384]{1,0:T(8,128)(2,1)}, u32[]{:S(2)}) copy-start(bf16[768,384]{1,0:T(8,128)(2,1)} %own_ref.2) | copy-start | bytes 1769476
  4.4 43.7 %copy-start.7 = (f32[384]{0:T(512)S(1)}, f32[384]{0:T(512)}, u32[]{:S(2)}) copy-start(f32[384]{0:T(512)} %param.11) | copy-start | bytes 4612
  14.2 5.7 %collective-permute-start.1 = (f32[8,384]{1,0:T(8,128)S(1)}, f32[8,384]{1,0:T(8,128)S(1)}, u32[]{:S(2)}, u32[]{:S(2)}) collective-permute-start(f32[8,384]{1,0:T(8,128)S(1)} %get-tuple-element.16.refs_0_), channel_id=1, source_target_pairs={{0,2},{2,4},{4,6},{6,0},{1,3},{3,5},{5,7},{7,1},{8,10},{10,12},{12... | collective-permute-start | bytes 36872 | tf_op jit(solution)/shard_map/ppermute | solution.py:24
  15.8 5.2 %collective-permute-start.2 = (f32[8,384]{1,0:T(8,128)S(1)}, f32[8,384]{1,0:T(8,128)S(1)}, u32[]{:S(2)}, u32[]{:S(2)}) collective-permute-start(f32[8,384]{1,0:T(8,128)S(1)} %get-tuple-element.16.refs_0_), channel_id=1, source_target_pairs={{0,4},{2,6},{4,0},{6,2},{1,5},{3,7},{5,1},{7,3},{8,12},{10,14},{12... | collective-permute-start | bytes 36872 | tf_op jit(solution)/shard_map/ppermute | solution.py:24
  18.5 3.7 %collective-permute-start.3 = (f32[8,384]{1,0:T(8,128)S(1)}, f32[8,384]{1,0:T(8,128)S(1)}, u32[]{:S(2)}, u32[]{:S(2)}) collective-permute-start(f32[8,384]{1,0:T(8,128)S(1)} %get-tuple-element.16.refs_0_), channel_id=1, source_target_pairs={{0,6},{2,0},{4,2},{6,4},{1,7},{3,1},{5,3},{7,5},{8,14},{10,8},{12,... | collective-permute-start | bytes 36872 | tf_op jit(solution)/shard_map/ppermute | solution.py:24
  22.3 5.9 %collective-permute-start.4 = (f32[8,384]{1,0:T(8,128)S(1)}, f32[8,384]{1,0:T(8,128)S(1)}, u32[]{:S(2)}, u32[]{:S(2)}) collective-permute-start(f32[8,384]{1,0:T(8,128)S(1)} %merge_stats.2.refs_0_), channel_id=1, source_target_pairs={{0,64},{64,128},{128,192},{192,0},{1,65},{65,129},{129,193},{193,1... | collective-permute-start | bytes 36872 | tf_op jit(solution)/shard_map/ppermute | solution.py:24
  23.9 5.2 %collective-permute-start.5 = (f32[8,384]{1,0:T(8,128)S(1)}, f32[8,384]{1,0:T(8,128)S(1)}, u32[]{:S(2)}, u32[]{:S(2)}) collective-permute-start(f32[8,384]{1,0:T(8,128)S(1)} %merge_stats.2.refs_0_), channel_id=1, source_target_pairs={{0,128},{64,192},{128,0},{192,64},{1,129},{65,193},{129,1},{193,65... | collective-permute-start | bytes 36872 | tf_op jit(solution)/shard_map/ppermute | solution.py:24
  26.8 3.7 %collective-permute-start.6 = (f32[8,384]{1,0:T(8,128)S(1)}, f32[8,384]{1,0:T(8,128)S(1)}, u32[]{:S(2)}, u32[]{:S(2)}) collective-permute-start(f32[8,384]{1,0:T(8,128)S(1)} %merge_stats.2.refs_0_), channel_id=1, source_target_pairs={{0,192},{64,0},{128,64},{192,128},{1,193},{65,1},{129,65},{193,129... | collective-permute-start | bytes 36872 | tf_op jit(solution)/shard_map/ppermute | solution.py:24
  30.5 13.0 %collective-permute-start.7 = (f32[8,384]{1,0:T(8,128)S(1)}, f32[8,384]{1,0:T(8,128)S(1)}, u32[]{:S(2)}, u32[]{:S(2)}) collective-permute-start(f32[8,384]{1,0:T(8,128)S(1)} %merge_stats.3.refs_0_), channel_id=1, source_target_pairs={{0,8},{8,16},{16,24},{24,32},{32,40},{40,48},{48,56},{56,0},{1,9},... | collective-permute-start | bytes 36872 | tf_op jit(solution)/shard_map/ppermute | solution.py:24
  32.5 13.4 %collective-permute-start.8 = (f32[8,384]{1,0:T(8,128)S(1)}, f32[8,384]{1,0:T(8,128)S(1)}, u32[]{:S(2)}, u32[]{:S(2)}) collective-permute-start(f32[8,384]{1,0:T(8,128)S(1)} %merge_stats.3.refs_0_), channel_id=1, source_target_pairs={{0,16},{8,24},{16,32},{24,40},{32,48},{40,56},{48,0},{56,8},{1,17}... | collective-permute-start | bytes 36872 | tf_op jit(solution)/shard_map/ppermute | solution.py:24
  37.0 11.2 %collective-permute-start.9 = (f32[8,384]{1,0:T(8,128)S(1)}, f32[8,384]{1,0:T(8,128)S(1)}, u32[]{:S(2)}, u32[]{:S(2)}) collective-permute-start(f32[8,384]{1,0:T(8,128)S(1)} %merge_stats.3.refs_0_), channel_id=1, source_target_pairs={{0,24},{8,32},{16,40},{24,48},{32,56},{40,0},{48,8},{56,16},{1,25}... | collective-permute-start | bytes 36872 | tf_op jit(solution)/shard_map/ppermute | solution.py:24
  38.9 9.3 %collective-permute-start.10 = (f32[8,384]{1,0:T(8,128)S(1)}, f32[8,384]{1,0:T(8,128)S(1)}, u32[]{:S(2)}, u32[]{:S(2)}) collective-permute-start(f32[8,384]{1,0:T(8,128)S(1)} %merge_stats.3.refs_0_), channel_id=1, source_target_pairs={{0,32},{8,40},{16,48},{24,56},{32,0},{40,8},{48,16},{56,24},{1,33}... | collective-permute-start | bytes 36872 | tf_op jit(solution)/shard_map/ppermute | solution.py:24
  40.4 7.9 %collective-permute-start.11 = (f32[8,384]{1,0:T(8,128)S(1)}, f32[8,384]{1,0:T(8,128)S(1)}, u32[]{:S(2)}, u32[]{:S(2)}) collective-permute-start(f32[8,384]{1,0:T(8,128)S(1)} %merge_stats.3.refs_0_), channel_id=1, source_target_pairs={{0,40},{8,48},{16,56},{24,0},{32,8},{40,16},{48,24},{56,32},{1,41}... | collective-permute-start | bytes 36872 | tf_op jit(solution)/shard_map/ppermute | solution.py:24
  43.5 4.8 %collective-permute-start.12 = (f32[8,384]{1,0:T(8,128)S(1)}, f32[8,384]{1,0:T(8,128)S(1)}, u32[]{:S(2)}, u32[]{:S(2)}) collective-permute-start(f32[8,384]{1,0:T(8,128)S(1)} %merge_stats.3.refs_0_), channel_id=1, source_target_pairs={{0,48},{8,56},{16,0},{24,8},{32,16},{40,24},{48,32},{56,40},{1,49}... | collective-permute-start | bytes 36872 | tf_op jit(solution)/shard_map/ppermute | solution.py:24
  45.9 3.7 %collective-permute-start.13 = (f32[8,384]{1,0:T(8,128)S(1)}, f32[8,384]{1,0:T(8,128)S(1)}, u32[]{:S(2)}, u32[]{:S(2)}) collective-permute-start(f32[8,384]{1,0:T(8,128)S(1)} %merge_stats.3.refs_0_), channel_id=1, source_target_pairs={{0,56},{8,0},{16,8},{24,16},{32,24},{40,32},{48,40},{56,48},{1,57}... | collective-permute-start | bytes 36872 | tf_op jit(solution)/shard_map/ppermute | solution.py:24
  50.9 11.7 %copy-start.2 = (bf16[384,768]{1,0:T(8,128)(2,1)}, bf16[384,768]{1,0:T(8,128)(2,1)S(1)}, u32[]{:S(2)}) copy-start(bf16[384,768]{1,0:T(8,128)(2,1)S(1)} %get-tuple-element.18.g_ref.g_own_ref) | copy-start | bytes 1769476
  62.7 4.4 %copy-start.4 = (f32[4,8,16,384]{3,2,1,0:T(8,128)}, f32[4,8,16,384]{3,2,1,0:T(8,128)S(1)}, u32[]{:S(2)}) copy-start(f32[4,8,16,384]{3,2,1,0:T(8,128)S(1)} %get-tuple-element.19) | copy-start | bytes 2359300
  62.7 5.3 %copy-start.1 = (bf16[384,4096]{1,0:T(8,128)(2,1)S(1)}, bf16[384,4096]{1,0:T(8,128)(2,1)}, u32[]{:S(2)}) copy-start(bf16[384,4096]{1,0:T(8,128)(2,1)} %own_ref.3) | copy-start | bytes 9437188
  63.5 17.5 %collective-permute-start.17 = (f16[4,8,16,384]{3,2,1,0:T(8,128)(2,1)}, f16[4,8,16,384]{3,2,1,0:T(8,128)(2,1)}, u32[]{:S(2)}, u32[]{:S(2)}) collective-permute-start(f16[4,8,16,384]{3,2,1,0:T(8,128)(2,1)} %convert_element_type.46), channel_id=1, source_target_pairs={{0,6},{2,0},{4,2},{6,4},{1,7},{3,1},{5,3},{7,5},{8,14},{10,8},{12,... | collective-permute-start | bytes 1179656 | tf_op jit(solution)/shard_map/ppermute | solution.py:24
  67.0 16.7 %collective-permute-start.16 = (f16[4,8,16,384]{3,2,1,0:T(8,128)(2,1)}, f16[4,8,16,384]{3,2,1,0:T(8,128)(2,1)}, u32[]{:S(2)}, u32[]{:S(2)}) collective-permute-start(f16[4,8,16,384]{3,2,1,0:T(8,128)(2,1)} %convert_element_type.44), channel_id=1, source_target_pairs={{0,4},{2,6},{4,0},{6,2},{1,5},{3,7},{5,1},{7,3},{8,12},{10,14},{12... | collective-permute-start | bytes 1179656 | tf_op jit(solution)/shard_map/ppermute | solution.py:24
  67.0 16.6 %collective-permute-start.15 = (f16[4,8,16,384]{3,2,1,0:T(8,128)(2,1)S(1)}, f16[4,8,16,384]{3,2,1,0:T(8,128)(2,1)}, u32[]{:S(2)}, u32[]{:S(2)}) collective-permute-start(f16[4,8,16,384]{3,2,1,0:T(8,128)(2,1)S(1)} %convert_element_type.42), channel_id=1, source_target_pairs={{0,2},{2,4},{4,6},{6,0},{1,3},{3,5},{5,7},{7,1},{8,10},{10,12},{12... | collective-permute-start | bytes 1179656 | tf_op jit(solution)/shard_map/ppermute | solution.py:24
  68.0 1.1 copy-start.3
  68.1 80.4 %collective-permute-start.34 = (bf16[384,2048]{1,0:T(8,128)(2,1)S(1)}, bf16[384,2048]{1,0:T(8,128)(2,1)S(1)}, u32[]{:S(2)}, u32[]{:S(2)}) collective-permute-start(bf16[384,2048]{1,0:T(8,128)(2,1)S(1)} %constant_dynamic-slice_fusion), channel_id=1, source_target_pairs={{0,1},{1,0},{2,3},{3,2},{4,5},{5,4},{6,7},{7,6},{8,9},{9,8},{10,11... | collective-permute-start | bytes 4718600 | tf_op jit(solution)/shard_map/ppermute | solution.py:24
  69.0 79.5 %collective-permute-start.35 = (bf16[384,768]{1,0:T(8,128)(2,1)S(1)}, bf16[384,768]{1,0:T(8,128)(2,1)S(1)}, u32[]{:S(2)}, u32[]{:S(2)}) collective-permute-start(bf16[384,768]{1,0:T(8,128)(2,1)S(1)} %copy-done.3), channel_id=1, source_target_pairs={{0,1},{1,0},{2,3},{3,2},{4,5},{5,4},{6,7},{7,6},{8,9},{9,8},{10,11... | collective-permute-start | bytes 1769480 | tf_op jit(solution)/shard_map/ppermute | solution.py:24
  80.8 3.8 %copy-start.5 = (f32[4,8,16,384]{3,2,1,0:T(8,128)S(1)}, f32[4,8,16,384]{3,2,1,0:T(8,128)}, u32[]{:S(2)}) copy-start(f32[4,8,16,384]{3,2,1,0:T(8,128)} %copy-done.4) | copy-start | bytes 2359300
  81.0 20.1 %collective-permute-start.23 = (f16[4,8,16,384]{3,2,1,0:T(8,128)(2,1)S(1)}, f16[4,8,16,384]{3,2,1,0:T(8,128)(2,1)S(1)}, u32[]{:S(2)}, u32[]{:S(2)}) collective-permute-start(f16[4,8,16,384]{3,2,1,0:T(8,128)(2,1)S(1)} %convert_element_type.52), channel_id=1, source_target_pairs={{0,192},{64,0},{128,64},{192,128},{1,193},{65,1},{129,65},{193,129... | collective-permute-start | bytes 1179656 | tf_op jit(solution)/shard_map/ppermute | solution.py:24
  83.7 21.2 %collective-permute-start.22 = (f16[4,8,16,384]{3,2,1,0:T(8,128)(2,1)S(1)}, f16[4,8,16,384]{3,2,1,0:T(8,128)(2,1)S(1)}, u32[]{:S(2)}, u32[]{:S(2)}) collective-permute-start(f16[4,8,16,384]{3,2,1,0:T(8,128)(2,1)S(1)} %convert_element_type.50), channel_id=1, source_target_pairs={{0,128},{64,192},{128,0},{192,64},{1,129},{65,193},{129,1},{193,65... | collective-permute-start | bytes 1179656 | tf_op jit(solution)/shard_map/ppermute | solution.py:24
  83.7 21.2 %collective-permute-start.21 = (f16[4,8,16,384]{3,2,1,0:T(8,128)(2,1)S(1)}, f16[4,8,16,384]{3,2,1,0:T(8,128)(2,1)S(1)}, u32[]{:S(2)}, u32[]{:S(2)}) collective-permute-start(f16[4,8,16,384]{3,2,1,0:T(8,128)(2,1)S(1)} %convert_element_type.48), channel_id=1, source_target_pairs={{0,64},{64,128},{128,192},{192,0},{1,65},{65,129},{129,193},{193,1... | collective-permute-start | bytes 1179656 | tf_op jit(solution)/shard_map/ppermute | solution.py:24
  101.2 12.0 %collective-permute-start.20 = (f32[8,16,384]{2,1,0:T(8,128)S(1)}, f32[8,16,384]{2,1,0:T(8,128)S(1)}, u32[]{:S(2)}, u32[]{:S(2)}) collective-permute-start(f32[8,16,384]{2,1,0:T(8,128)S(1)} %get-tuple-element.28), channel_id=1, source_target_pairs={{0,192},{64,0},{128,64},{192,128},{1,193},{65,1},{129,65},{193,129... | collective-permute-start | bytes 589832 | tf_op jit(solution)/shard_map/ppermute | solution.py:24
  104.8 11.7 %collective-permute-start.18 = (f32[8,16,384]{2,1,0:T(8,128)S(1)}, f32[8,16,384]{2,1,0:T(8,128)S(1)}, u32[]{:S(2)}, u32[]{:S(2)}) collective-permute-start(f32[8,16,384]{2,1,0:T(8,128)S(1)} %get-tuple-element.29), channel_id=1, source_target_pairs={{0,64},{64,128},{128,192},{192,0},{1,65},{65,129},{129,193},{193,1... | collective-permute-start | bytes 589832 | tf_op jit(solution)/shard_map/ppermute | solution.py:24
  104.8 14.3 %collective-permute-start.19 = (f32[8,16,384]{2,1,0:T(8,128)S(1)}, f32[8,16,384]{2,1,0:T(8,128)S(1)}, u32[]{:S(2)}, u32[]{:S(2)}) collective-permute-start(f32[8,16,384]{2,1,0:T(8,128)S(1)} %get-tuple-element.27), channel_id=1, source_target_pairs={{0,128},{64,192},{128,0},{192,64},{1,129},{65,193},{129,1},{193,65... | collective-permute-start | bytes 589832 | tf_op jit(solution)/shard_map/ppermute | solution.py:24
  113.1 8.0 %collective-permute-start.26 = (f32[8,16,384]{2,1,0:T(8,128)S(1)}, f32[8,16,384]{2,1,0:T(8,128)S(1)}, u32[]{:S(2)}, u32[]{:S(2)}) collective-permute-start(f32[8,16,384]{2,1,0:T(8,128)S(1)} %get-tuple-element.31), channel_id=1, source_target_pairs={{0,6},{2,0},{4,2},{6,4},{1,7},{3,1},{5,3},{7,5},{8,14},{10,8},{12,... | collective-permute-start | bytes 589832 | tf_op jit(solution)/shard_map/ppermute | solution.py:24
  116.5 6.9 %collective-permute-start.24 = (f32[8,16,384]{2,1,0:T(8,128)S(1)}, f32[8,16,384]{2,1,0:T(8,128)S(1)}, u32[]{:S(2)}, u32[]{:S(2)}) collective-permute-start(f32[8,16,384]{2,1,0:T(8,128)S(1)} %get-tuple-element.32), channel_id=1, source_target_pairs={{0,2},{2,4},{4,6},{6,0},{1,3},{3,5},{5,7},{7,1},{8,10},{10,12},{12... | collective-permute-start | bytes 589832 | tf_op jit(solution)/shard_map/ppermute | solution.py:24
  119.1 7.2 %collective-permute-start.25 = (f32[8,16,384]{2,1,0:T(8,128)S(1)}, f32[8,16,384]{2,1,0:T(8,128)S(1)}, u32[]{:S(2)}, u32[]{:S(2)}) collective-permute-start(f32[8,16,384]{2,1,0:T(8,128)S(1)} %get-tuple-element.30), channel_id=1, source_target_pairs={{0,4},{2,6},{4,0},{6,2},{1,5},{3,7},{5,1},{7,3},{8,12},{10,14},{12... | collective-permute-start | bytes 589832 | tf_op jit(solution)/shard_map/ppermute | solution.py:24
  126.4 6.2 %collective-permute-start.33 = (f32[32,384]{1,0:T(8,128)S(1)}, f32[32,384]{1,0:T(8,128)S(1)}, u32[]{:S(2)}, u32[]{:S(2)}) collective-permute-start(f32[32,384]{1,0:T(8,128)S(1)} %get-tuple-element.38), channel_id=1, source_target_pairs={{0,56},{8,0},{16,8},{24,16},{32,24},{40,32},{48,40},{56,48},{1,57}... | collective-permute-start | bytes 147464 | tf_op jit(solution)/shard_map/ppermute | solution.py:24
  128.9 2.1 %collective-permute-start.14 = (f32[8,128]{1,0:T(8,128)S(1)}, f32[8,128]{1,0:T(8,128)S(1)}, u32[]{:S(2)}, u32[]{:S(2)}) collective-permute-start(f32[8,128]{1,0:T(8,128)S(1)} %get-tuple-element.17), channel_id=1, source_target_pairs={{0,1},{1,0},{2,3},{3,2},{4,5},{5,4},{6,7},{7,6},{8,9},{9,8},{10,11... | collective-permute-start | bytes 12296 | tf_op jit(solution)/shard_map/ppermute | solution.py:24
  128.9 8.2 %collective-permute-start.32 = (f32[32,384]{1,0:T(8,128)S(1)}, f32[32,384]{1,0:T(8,128)S(1)}, u32[]{:S(2)}, u32[]{:S(2)}) collective-permute-start(f32[32,384]{1,0:T(8,128)S(1)} %get-tuple-element.39), channel_id=1, source_target_pairs={{0,48},{8,56},{16,0},{24,8},{32,16},{40,24},{48,32},{56,40},{1,49}... | collective-permute-start | bytes 147464 | tf_op jit(solution)/shard_map/ppermute | solution.py:24
  131.0 7.1 %collective-permute-start.31 = (f32[32,384]{1,0:T(8,128)S(1)}, f32[32,384]{1,0:T(8,128)S(1)}, u32[]{:S(2)}, u32[]{:S(2)}) collective-permute-start(f32[32,384]{1,0:T(8,128)S(1)} %get-tuple-element.37), channel_id=1, source_target_pairs={{0,40},{8,48},{16,56},{24,0},{32,8},{40,16},{48,24},{56,32},{1,41}... | collective-permute-start | bytes 147464 | tf_op jit(solution)/shard_map/ppermute | solution.py:24
  132.6 9.0 %collective-permute-start.30 = (f32[32,384]{1,0:T(8,128)S(1)}, f32[32,384]{1,0:T(8,128)S(1)}, u32[]{:S(2)}, u32[]{:S(2)}) collective-permute-start(f32[32,384]{1,0:T(8,128)S(1)} %get-tuple-element.36), channel_id=1, source_target_pairs={{0,32},{8,40},{16,48},{24,56},{32,0},{40,8},{48,16},{56,24},{1,33}... | collective-permute-start | bytes 147464 | tf_op jit(solution)/shard_map/ppermute | solution.py:24
  137.1 8.4 %collective-permute-start.29 = (f32[32,384]{1,0:T(8,128)S(1)}, f32[32,384]{1,0:T(8,128)S(1)}, u32[]{:S(2)}, u32[]{:S(2)}) collective-permute-start(f32[32,384]{1,0:T(8,128)S(1)} %get-tuple-element.35), channel_id=1, source_target_pairs={{0,24},{8,32},{16,40},{24,48},{32,56},{40,0},{48,8},{56,16},{1,25}... | collective-permute-start | bytes 147464 | tf_op jit(solution)/shard_map/ppermute | solution.py:24
  138.1 7.4 %collective-permute-start.27 = (f32[32,384]{1,0:T(8,128)S(1)}, f32[32,384]{1,0:T(8,128)S(1)}, u32[]{:S(2)}, u32[]{:S(2)}) collective-permute-start(f32[32,384]{1,0:T(8,128)S(1)} %get-tuple-element.34), channel_id=1, source_target_pairs={{0,8},{8,16},{16,24},{24,32},{32,40},{40,48},{48,56},{56,0},{1,9},... | collective-permute-start | bytes 147464 | tf_op jit(solution)/shard_map/ppermute | solution.py:24
  141.6 6.3 %collective-permute-start.28 = (f32[32,384]{1,0:T(8,128)S(1)}, f32[32,384]{1,0:T(8,128)S(1)}, u32[]{:S(2)}, u32[]{:S(2)}) collective-permute-start(f32[32,384]{1,0:T(8,128)S(1)} %get-tuple-element.33), channel_id=1, source_target_pairs={{0,16},{8,24},{16,32},{24,40},{32,48},{40,56},{48,0},{56,8},{1,17}... | collective-permute-start | bytes 147464 | tf_op jit(solution)/shard_map/ppermute | solution.py:24

commit v2 on v1

v2 whole, which is shorter than its diff:
```python
import functools

import jax
import jax.numpy as jnp
from jax import lax
from jax.experimental import pallas as pl
from jax.experimental.pallas import tpu as pltpu
from jax.sharding import Mesh, PartitionSpec as P

CE_WEIGHT = 0.5
SEND_SCALE = 64.0
F32 = jnp.float32
BF16 = jnp.bfloat16
F16 = jnp.float16


WHOLE = pl.BlockSpec(memory_space=pltpu.VMEM)


def params(mib, *semantics):
    return pltpu.CompilerParams(
        vmem_limit_bytes=mib * 1024 * 1024, dimension_semantics=semantics or None
    )


def shift(a, axis, by):
    n = lax.axis_size(axis)
    return lax.ppermute(a, axis, [(i, (i + by) % n) for i in range(n)])


def logits_kernel(steps, h_ref, w_ref, out_ref, h_buf, w_buf, h_sem, w_sem):
    kb = w_buf.shape[1]

    def copies(k):
        at = pl.ds(k * kb, kb)
        return (
            pltpu.make_async_copy(h_ref.at[:, at], h_buf.at[k], h_sem.at[k]),
            pltpu.make_async_copy(w_ref.at[at], w_buf.at[k], w_sem.at[k]),
        )

    for k in range(steps):
        for copy in copies(k):
            copy.start()
    out_ref[...] = jnp.zeros_like(out_ref)

    def step(k, carry):
        for copy in copies(k):
            copy.wait()
        out_ref[...] += jnp.dot(h_buf[k], w_buf[k], preferred_element_type=F32)
        return carry

    lax.fori_loop(0, steps, step, 0)


def student_logits(hidden, head, steps=4):
    rows, depth = hidden.shape
    cols = head.shape[1]
    kb = depth // steps
    return pl.pallas_call(
        functools.partial(logits_kernel, steps),
        out_shape=jax.ShapeDtypeStruct((rows, cols), F32),
        in_specs=[pl.BlockSpec(memory_space=pl.ANY)] * 2,
        out_specs=WHOLE,
        scratch_shapes=[
            pltpu.VMEM((steps, rows, kb), BF16),
            pltpu.VMEM((steps, kb, cols), BF16),
            pltpu.SemaphoreType.DMA((steps,)),
            pltpu.SemaphoreType.DMA((steps,)),
        ],
        compiler_params=params(56),
        cost_estimate=pl.CostEstimate(
            flops=2 * rows * depth * cols,
            bytes_accessed=2 * (rows * depth + depth * cols) + 4 * rows * cols,
            transcendentals=0,
        ),
        name="student_logits",
    )(hidden, head)


def columns_of(*rows):
    n = rows[0].shape[1]
    sub = lax.broadcasted_iota(jnp.int32, (128, n), 0)
    packed = jnp.zeros((128, n), F32)
    for at, row in enumerate(rows):
        packed = jnp.where(sub == at, row.astype(F32), packed)
    turned = packed.T
    return [turned[:, at : at + 1] for at in range(len(rows))]


def stats_kernel(pos_ref, l_ref, own_ref, oth_ref, assign_ref, ids_ref, stats_ref, t_ref):
    rows, cols = l_ref.shape
    total = own_ref.shape[0]
    first = pos_ref[0] == 0
    assign = assign_ref[...]
    assign = jnp.where(first, assign[:, :rows], assign[:, rows:])
    assign, ids = columns_of(assign, ids_ref[...])
    lanes = lax.broadcasted_iota(jnp.int32, (rows, total), 1).astype(F32)
    pick = (lanes == assign).astype(BF16)
    own = jnp.dot(pick, own_ref[...], preferred_element_type=F32)
    oth = jnp.dot(pick, oth_ref[...], preferred_element_type=F32)
    teacher = jnp.concatenate([jnp.where(first, own, oth), jnp.where(first, oth, own)], axis=1)
    t_ref[...] = teacher.astype(BF16)
    logits = l_ref[...]
    top_s = jnp.max(logits, axis=1, keepdims=True)
    sum_s = jnp.sum(jnp.exp(logits - top_s), axis=1, keepdims=True)
    top_t = jnp.max(teacher, axis=1, keepdims=True)
    exp_t = jnp.exp(teacher - top_t)
    sum_t = jnp.sum(exp_t, axis=1, keepdims=True)
    cross = jnp.sum(exp_t * (teacher - logits), axis=1, keepdims=True)
    columns = pos_ref[1] + lax.broadcasted_iota(jnp.int32, (rows, cols), 1)
    hot = columns.astype(F32) == ids
    picked = jnp.sum(jnp.where(hot, logits, 0.0), axis=1, keepdims=True)
    lane = lax.broadcasted_iota(jnp.int32, (rows, 128), 1)
    packed = jnp.zeros((rows, 128), F32)
    for at, value in enumerate((top_s, sum_s, top_t, sum_t, cross, picked)):
        packed = jnp.where(lane == at, value, packed)
    stats_ref[...] = packed.T[:8, :]


def local_stats(pos, logits, own, oth, assign, ids):
    rows, cols = logits.shape
    return pl.pallas_call(
        stats_kernel,
        out_shape=(
            jax.ShapeDtypeStruct((8, rows), F32),
            jax.ShapeDtypeStruct((rows, cols), BF16),
        ),
        in_specs=[pl.BlockSpec(memory_space=pltpu.SMEM)] + [WHOLE] * 5,
        out_specs=(WHOLE, WHOLE),
        compiler_params=params(16),
        cost_estimate=pl.CostEstimate(
            flops=2 * rows * cols * own.shape[0],
            bytes_accessed=4 * rows * cols + 4 * own.size + 2 * rows * cols,
            transcendentals=2 * rows * cols,
        ),
        name="local_stats",
    )(pos, logits, own, oth, assign, ids)


def merge(refs):
    def row(at):
        return [r[:, at, :] if len(r.shape) == 3 else r[at : at + 1, :] for r in refs]

    def over(fold, reduce, values):
        return functools.reduce(fold, [reduce(v, axis=0, keepdims=True) for v in values])

    tops_s, sums_s, tops_t, sums_t, crosses, pickeds = (row(at) for at in range(6))
    top_s = over(jnp.maximum, jnp.max, tops_s)
    top_t = over(jnp.maximum, jnp.max, tops_t)
    scale_s = [jnp.exp(t - top_s) for t in tops_s]
    scale_t = [jnp.exp(t - top_t) for t in tops_t]
    total = lambda xs: over(jnp.add, jnp.sum, xs)
    times = lambda xs, ys: [a * b for a, b in zip(xs, ys)]
    return (
        top_s,
        total(times(sums_s, scale_s)),
        top_t,
        total(times(sums_t, scale_t)),
        total(times(crosses, scale_t)),
        total(pickeds),
    )


def merge_kernel(*refs):
    out = refs[-1]
    merged = merge(refs[:-1])
    out[...] = jnp.zeros_like(out)
    for at, value in enumerate(merged):
        out[at : at + 1, :] = value


def merge_stats(*parts):
    return pl.pallas_call(
        merge_kernel,
        out_shape=jax.ShapeDtypeStruct(parts[0].shape[-2:], F32),
        in_specs=[WHOLE] * len(parts),
        out_specs=WHOLE,
        compiler_params=params(16),
        name="merge_stats",
    )(*parts)


def grad_kernel(n_parts, pos_ref, l_ref, t_ref, ids_ref, scale_ref, *refs):
    parts, (g_ref, loss_ref) = refs[:n_parts], refs[n_parts:]
    rows, cols = l_ref.shape
    top_s, sum_s, top_t, sum_t, cross, picked = merge(parts)
    norm_s = top_s + jnp.log(sum_s)
    norm_t = top_t + jnp.log(sum_t)
    terms = cross / sum_t - norm_t + norm_s + CE_WEIGHT * (norm_s - picked)
    loss_ref[...] = jnp.broadcast_to(jnp.sum(terms, axis=1, keepdims=True), loss_ref.shape)
    norm_s, norm_t, ids, scale = columns_of(norm_s, norm_t, ids_ref[...], scale_ref[...])
    columns = pos_ref[1] + lax.broadcasted_iota(jnp.int32, (rows, cols), 1)
    hot = jnp.where(columns.astype(F32) == ids, CE_WEIGHT, 0.0)
    prob_s = jnp.exp(l_ref[...] - norm_s)
    prob_t = jnp.exp(t_ref[...].astype(F32) - norm_t)
    g_ref[...] = (scale * ((1.0 + CE_WEIGHT) * prob_s - prob_t - hot)).astype(BF16)


def grad_logits(pos, logits, teacher, ids, scale, parts):
    rows, cols = logits.shape
    return pl.pallas_call(
        functools.partial(grad_kernel, len(parts)),
        out_shape=(
            jax.ShapeDtypeStruct((rows, cols), BF16),
            jax.ShapeDtypeStruct((8, 128), F32),
        ),
        in_specs=[pl.BlockSpec(memory_space=pltpu.SMEM)] + [WHOLE] * (4 + len(parts)),
        out_specs=(WHOLE, WHOLE),
        compiler_params=params(16),
        cost_estimate=pl.CostEstimate(
            flops=8 * rows * cols,
            bytes_accessed=8 * rows * cols,
            transcendentals=2 * rows * cols,
        ),
        name="grad_logits",
    )(pos, logits, teacher, ids, scale, *parts)


def hidden_kernel(first_x, half, pos_ref, w_ref, g_ref, *outs):
    ny, nz, nx, _, sub, cols = w_ref.shape
    y, x, z = pos_ref[2], pos_ref[3], pos_ref[4]
    g = g_ref[...]
    first, second = (nx, ny) if first_x else (ny, nx)
    for k, out in enumerate(outs):
        far = (k + 1) % first
        if first_x:
            w = w_ref[:, :, lax.rem(x + far, nx), half]
        else:
            w = w_ref[lax.rem(y + far, ny), :, :, half]
        part = lax.dot_general(
            w.reshape(-1, cols), g, (((1,), (1,)), ((), ())), preferred_element_type=F32
        )
        if far:
            part = part * SEND_SCALE
        for a in range(second):
            for b in range(nz):
                at = (a * nz + b if first_x else b * nx + a) * sub
                near = lax.rem(a - (y if first_x else x) + second, second)
                out[near, lax.rem(b - z + nz, nz)] = part[at : at + sub]


def hidden_part(pos, head6, g, first_x, half):
    ny, nz, nx, _, sub, cols = head6.shape
    rows = g.shape[0]
    first, second = (nx, ny) if first_x else (ny, nx)
    shape = jax.ShapeDtypeStruct((second, nz, sub, rows), F32)
    return pl.pallas_call(
        functools.partial(hidden_kernel, first_x, half),
        out_shape=[shape] * first,
        in_specs=[pl.BlockSpec(memory_space=pltpu.SMEM), WHOLE, WHOLE],
        out_specs=[WHOLE] * first,
        compiler_params=params(16),
        cost_estimate=pl.CostEstimate(
            flops=rows * head6.size,
            bytes_accessed=head6.size + 4 * rows * first * second * nz * sub,
            transcendentals=0,
        ),
        name="hidden_part",
    )(pos, head6, g)


def head_kernel(pos_ref, own_ref, oth_ref, g_own_ref, g_oth_ref, out_ref):
    dims = (((0,), (0,)), ((), ()))
    total = lax.dot_general(own_ref[...], g_own_ref[...], dims, preferred_element_type=F32)
    total += lax.dot_general(oth_ref[...], g_oth_ref[...], dims, preferred_element_type=F32)
    out_ref[...] = total.astype(BF16)


def head_grad(pos, hidden, hidden_oth, g, g_oth, block=512):
    rows, depth = hidden.shape
    cols = g.shape[1]
    width = hidden_oth.shape[1]
    steps = width // block
    return pl.pallas_call(
        head_kernel,
        out_shape=jax.ShapeDtypeStruct((width, cols), BF16),
        grid_spec=pltpu.PrefetchScalarGridSpec(
            num_scalar_prefetch=1,
            grid=(steps,),
            in_specs=[
                pl.BlockSpec((rows, block), lambda i, pos: (0, pos[0] * steps + i)),
                pl.BlockSpec((rows, block), lambda i, pos: (0, i)),
                pl.BlockSpec((rows, cols), lambda i, pos: (0, 0)),
                pl.BlockSpec((rows, cols), lambda i, pos: (0, 0)),
            ],
            out_specs=pl.BlockSpec((block, cols), lambda i, pos: (i, 0)),
        ),
        compiler_params=params(24, "arbitrary"),
        cost_estimate=pl.CostEstimate(
            flops=4 * rows * width * cols,
            bytes_accessed=4 * rows * width + 4 * rows * cols + 2 * width * cols,
            transcendentals=0,
        ),
        name="head_grad",
    )(pos, hidden, hidden_oth, g, g_oth)


def body(teacher, hidden, head, ids, assignment, row_scale):
    c, x, y, z = (lax.axis_index(a) for a in ("c", "x", "y", "z"))
    rows, depth = hidden.shape
    cols = head.shape[1]
    block = lax.axis_index(("y", "z", "x"))
    pos = jnp.stack([c, block * cols, y, x, z]).astype(jnp.int32)

    teacher_oth = shift(teacher, "c", 1)
    width = depth // 2
    hidden_oth = shift(lax.dynamic_slice(hidden, (0, (1 - c) * width), (rows, width)), "c", 1)
    assign = assignment.reshape(1, -1)
    ids = ids.reshape(1, rows)
    scale = row_scale.reshape(1, rows)

    logits = student_logits(hidden, head)
    stats, teacher_rows = local_stats(pos, logits, teacher, teacher_oth, assign, ids)
    stats, hidden_oth = lax.optimization_barrier((stats, hidden_oth))
    ny, nz, nx = (lax.axis_size(a) for a in ("y", "z", "x"))
    stats = jnp.broadcast_to(stats[None], (nz * nx,) + stats.shape)
    stats = merge_stats(lax.all_to_all(stats, ("z", "x"), 0, 0, tiled=True))
    parts = [stats] + [shift(stats, "y", d) for d in range(1, ny)]
    g, loss_part = grad_logits(pos, logits, teacher_rows, ids, scale, parts)
    g_oth = shift(g, "c", 1)

    sub = depth // (ny * nz * nx) // 2
    head6 = head.reshape(ny, nz, nx, 2, sub, cols)

    def first_level(half, axis):
        *far, own = hidden_part(pos, head6, g, axis == "x", half)
        far = [shift(f.astype(F16), axis, d + 1) for d, f in enumerate(far)]
        return own, far

    own_a, far_a = first_level(0, "x")
    own_b, far_b = first_level(1, "y")
    head_out = head_grad(pos, hidden, hidden_oth, g, g_oth)
    far_a, far_b, head_out = lax.optimization_barrier((far_a, far_b, head_out))

    def add(own, far):
        return own + sum(f.astype(F32) for f in far) * (1.0 / SEND_SCALE)

    def level(chunks, axis):
        sent = [(chunks[d] * SEND_SCALE).astype(F16) for d in range(1, chunks.shape[0])]
        return add(chunks[0], [shift(f, axis, d + 1) for d, f in enumerate(sent)])

    sum_a = level(add(own_a, far_a), "y")
    sum_b = level(add(own_b, far_b), "x")
    hidden_sum = level(jnp.concatenate([sum_a, sum_b], axis=1), "z")
    hidden_grad = hidden_sum.T.astype(BF16)

    loss_all = loss_part + shift(loss_part, "c", 1)
    loss = loss_all[0, :1] / (2 * rows)
    return loss, hidden_grad, head_out


def solution(mesh):
    ny, nzx, nc = mesh.devices.shape
    nx = 4
    fine = Mesh(mesh.devices.reshape(ny, nzx // nx, nx, nc), ("y", "z", "x", "c"))
    vocab = ("y", "z", "x")
    in_specs = (
        P(None, vocab + ("c",)),
        P("c", None),
        P(None, vocab),
        P("c"),
        P(),
        P("c"),
    )
    out_specs = (P(), P("c", vocab), P("c", vocab))
    return jax.shard_map(body, mesh=fine, in_specs=in_specs, out_specs=out_specs, check_vma=False)
```

time: 159 us -> 118 us (0.74)
  starting transfers between devices: 63.5 us -> 31.9 us
  blocking collectives: 0 us -> 25.9 us
  Pallas kernels: 41.5 us -> 21.4 us
  waiting for transfers between devices: 39.3 us -> 27.8 us
  other arithmetic: 4.22 us -> 1.63 us
    ppermute x36 -> x26, starting transfers between devices: 63.5 us -> 31.9 us  [shift(): return lax.ppermute(a, axis, [(i, (i + by) % n) for i in range(n)])]
    all_to_all x0 -> x1, blocking collectives: none -> 25.9 us  [body(): stats = merge_stats(lax.all_to_all(stats, ('z', 'x'), 0, 0, tiled=True))]
    pallas_call x3, Pallas kernels: 31.3 us -> 10.8 us  [the longest x1 6 us: student_logits(): pl.pallas_call(functools.partial(logits_kernel, steps), out_shape=jax.Sha...]
    ppermute x36 -> x26, waiting for transfers between devices: 39.3 us -> 27.8 us  [shift(): return lax.ppermute(a, axis, [(i, (i + by) % n) for i in range(n)])]
    dynamic_slice x1, local copies, waits for them, and re-layouts: 0.1 us -> 2.79 us  [body(): lax.dynamic_slice(hidden, (0, (1 - c) * width), (rows, width))]
  transfers between devices with their start and end apart: 36 -> 26, of which waited for: 15 -> 12; matrix products, arithmetic and copies ran while one was open for 4% -> 1% of each run, Pallas kernels for 12% -> 17%
where the time goes in v2:
time: 118 us; the launch traced here: 116 us
  starting transfers between devices  31.9 us (27%)
  waiting for transfers between devices  27.8 us (24%)
  blocking collectives  25.9 us (22%)
  Pallas kernels  21.4 us (18%)
  local copies, waits for them, and re-layouts  4.74 us (4%)
  between operations  2.7 us (2%)
  other arithmetic  1.63 us (1%)
    ppermute x26, starting transfers between devices, shift(): return lax.ppermute(a, axis, [(i, (i + by) % n) for i in range(n)])  31.9 us
    ppermute x26, waiting for transfers between devices, shift(): return lax.ppermute(a, axis, [(i, (i + by) % n) for i in range(n)])  27.8 us
    all_to_all x1, blocking collectives, body(): stats = merge_stats(lax.all_to_all(stats, ('z', 'x'), 0, 0, tiled=True))  25.9 us
    pallas_call x1, Pallas kernels, head_grad(): pl.pallas_call(head_kernel, out_shape=jax.ShapeDtypeStruct((width, cols),...  6.86 us
    pallas_call x1, Pallas kernels, student_logits(): pl.pallas_call(functools.partial(logits_kernel, steps), out_shape=jax.Sha...  6 us
    pallas_call x2, Pallas kernels, hidden_part(): pl.pallas_call(functools.partial(hidden_kernel, first_x, half), out_shape...  4.79 us
    dynamic_slice x1, local copies, waits for them, and re-layouts, body(): lax.dynamic_slice(hidden, (0, (1 - c) * width), (rows, width))  2.79 us
  transfers between devices with their start and end apart: 26, of which 12 were waited for; matrix products, arithmetic and copies ran while one was open for 1% of the time, Pallas kernels for 17%

profile of v2, /device:TPU:32, one launch (start us, length us, event | category | flops | bytes accessed | tf_op | source)
XLA Modules:
  0.0 116.0 jit_solution(79026407170607726)
XLA Ops:
  0.7 2.8 %constant_dynamic-slice_fusion = bf16[384,2048]{1,0:T(8,128)(2,1)} fusion(bf16[384,4096]{1,0:T(8,128)(2,1)} %own_ref.3, s32[]{:T(128)S(6)} %select_n.3), kind=kLoop, calls=%fused_computation.71 | loop fusion | bytes 3145732 | tf_op jit(solution)/shard_map/dynamic_slice | solution.py:307
  3.5 0.5 collective-permute-start
  4.1 6.0 %student_logits.1.l_ref = f32[384,768]{1,0:T(8,128)} custom-call(bf16[384,4096]{1,0:T(8,128)(2,1)} %own_ref.3, bf16[4096,768]{1,0:T(8,128)(2,1)} %w_ref.1), custom_call_target="tpu_custom_call" | custom-call | flops 2415919104 | bytes 10616832 | tf_op jit(solution)/shard_map/student_logits/pallas_call | solution.py:59
  10.1 1.3 %copy-done.1 = f32[384,768]{1,0:T(8,128)S(1)} copy-done((f32[384,768]{1,0:T(8,128)S(1)}, f32[384,768]{1,0:T(8,128)}, u32[]{:S(2)}) %copy-start.1) | copy-done | bytes 1179672
  11.4 2.2 %local_stats.1 = (f32[8,384]{1,0:T(8,128)S(1)}, bf16[384,768]{1,0:T(8,128)(2,1)S(1)}) custom-call(s32[5]{0:T(128)S(1)} %stack.23.pos_ref, f32[384,768]{1,0:T(8,128)S(1)} %copy-done.1, bf16[768,384]{1,0:T(8,128)(2,1)S(1)} %copy-done.3, bf16[768,384]{1,0:T(8,128)(2,1)S(1)} %collective-permute-done.oth_ref, s32[1,768]{1,0:T(1,128)S(1)} %reshape.60.assign_ref, ...), custom_call_target="tpu_custom_call" | custom-call | flops 452984832 | bytes 2949120 | tf_op jit(solution)/shard_map/local_stats/pallas_call | solution.py:122
  13.6 25.9 %all_to_all.5.refs_0_ = f32[32,8,384]{2,1,0:T(8,128)S(1)} all-to-all(f32[32,8,384]{2,1,0:T(8,128)S(1)} %broadcast_in_dim.2), channel_id=1, replica_groups=mesh['y'=4,'z'=8,'x'=4,'c'=2] {'z','x'}, dimensions={0} | all-to-all | bytes 786432 | tf_op jit(solution)/shard_map/all_to_all | solution.py:317
  39.5 0.1 merge_stats.1.refs_0_
  39.7 3.1 %collective-permute-start.4 = (f32[8,384]{1,0:T(8,128)S(1)}, f32[8,384]{1,0:T(8,128)S(1)}, u32[]{:S(2)}, u32[]{:S(2)}) collective-permute-start(f32[8,384]{1,0:T(8,128)S(1)} %merge_stats.1.refs_0_), channel_id=1, source_target_pairs={{0,192},{64,0},{128,64},{192,128},{1,193},{65,1},{129,65},{193,129... | collective-permute-start | bytes 36872 | tf_op jit(solution)/shard_map/ppermute | solution.py:28
  42.7 0.6 collective-permute-start.3
  43.4 1.0 collective-permute-start.2
  44.4 3.6 %collective-permute-done.3.refs_2_ = f32[8,384]{1,0:T(8,128)S(1)} collective-permute-done((f32[8,384]{1,0:T(8,128)S(1)}, f32[8,384]{1,0:T(8,128)S(1)}, u32[]{:S(2)}, u32[]{:S(2)}) %collective-permute-start.3) | collective-permute-done | bytes 12320 | tf_op jit(solution)/shard_map/ppermute | solution.py:28
  47.9 0.3 collective-permute-done.2.refs_1_
  48.3 1.4 %grad_logits.1 = (bf16[384,768]{1,0:T(8,128)(2,1)S(1)}, f32[8,128]{1,0:T(8,128)S(1)}) custom-call(s32[5]{0:T(128)S(1)} %stack.23.pos_ref, f32[384,768]{1,0:T(8,128)S(1)} %copy-done.2, bf16[384,768]{1,0:T(8,128)(2,1)S(1)} %get-tuple-element.24.t_ref, s32[1,384]{1,0:T(1,128)S(1)} %reshape.61.ids_ref, f32[1,384]{1,0:T(1,128)S(1)} %reshape.62.scale_ref, ...), custom_call_target="tpu_custom_call" | custom-call | flops 2359296 | bytes 2359296 | tf_op jit(solution)/shard_map/grad_logits/pallas_call | solution.py:201
  49.7 0.1 collective-permute-start.12
  49.8 2.5 %hidden_part.3 = (f32[4,8,16,384]{3,2,1,0:T(8,128)S(1)}, f32[4,8,16,384]{3,2,1,0:T(8,128)S(1)}, f32[4,8,16,384]{3,2,1,0:T(8,128)S(1)}, f32[4,8,16,384]{3,2,1,0:T(8,128)S(1)}) custom-call(s32[5]{0:T(128)S(1)} %stack.23.pos_ref, bf16[4,8,4,2,16,768]{5,4,3,2,1,0:T(8,128)(2,1)S(1)} %bitcast.53, bf16[384,768]{1,0:T(8,128)(2,1)S(1)} %get-tuple-element.28.g_ref.g_own_ref), custom_call_target="tpu_custom_call" | custom-call | flops 1207959552 | bytes 6291456 | tf_op jit(solution)/shard_map/hidden_part/pallas_call | solution.py:247
  52.3 0.5 collective-permute-start.11
  52.9 1.5 %collective-permute-start.10 = (f16[4,8,16,384]{3,2,1,0:T(8,128)(2,1)S(1)}, f16[4,8,16,384]{3,2,1,0:T(8,128)(2,1)S(1)}, u32[]{:S(2)}, u32[]{:S(2)}) collective-permute-start(f16[4,8,16,384]{3,2,1,0:T(8,128)(2,1)S(1)} %convert_element_type.163), channel_id=1, source_target_pairs={{0,128},{64,192},{128,0},{192,64},{1,129},{65,193},{129,1},{193,65... | collective-permute-start | bytes 1179656 | tf_op jit(solution)/shard_map/ppermute | solution.py:28
  54.4 1.3 %collective-permute-start.9 = (f16[4,8,16,384]{3,2,1,0:T(8,128)(2,1)S(1)}, f16[4,8,16,384]{3,2,1,0:T(8,128)(2,1)S(1)}, u32[]{:S(2)}, u32[]{:S(2)}) collective-permute-start(f16[4,8,16,384]{3,2,1,0:T(8,128)(2,1)S(1)} %convert_element_type.162), channel_id=1, source_target_pairs={{0,64},{64,128},{128,192},{192,0},{1,65},{65,129},{129,193},{193,1... | collective-permute-start | bytes 1179656 | tf_op jit(solution)/shard_map/ppermute | solution.py:28
  55.7 2.3 %hidden_part.2 = (f32[4,8,16,384]{3,2,1,0:T(8,128)S(1)}, f32[4,8,16,384]{3,2,1,0:T(8,128)S(1)}, f32[4,8,16,384]{3,2,1,0:T(8,128)S(1)}, f32[4,8,16,384]{3,2,1,0:T(8,128)S(1)}) custom-call(s32[5]{0:T(128)S(1)} %stack.23.pos_ref, bf16[4,8,4,2,16,768]{5,4,3,2,1,0:T(8,128)(2,1)S(1)} %bitcast.54, bf16[384,768]{1,0:T(8,128)(2,1)S(1)} %get-tuple-element.28.g_ref.g_own_ref), custom_call_target="tpu_custom_call" | custom-call | flops 1207959552 | bytes 6291456 | tf_op jit(solution)/shard_map/hidden_part/pallas_call | solution.py:247
  58.3 1.3 %collective-permute-start.8 = (f16[4,8,16,384]{3,2,1,0:T(8,128)(2,1)S(1)}, f16[4,8,16,384]{3,2,1,0:T(8,128)(2,1)S(1)}, u32[]{:S(2)}, u32[]{:S(2)}) collective-permute-start(f16[4,8,16,384]{3,2,1,0:T(8,128)(2,1)S(1)} %convert_element_type.161), channel_id=1, source_target_pairs={{0,6},{2,0},{4,2},{6,4},{1,7},{3,1},{5,3},{7,5},{8,14},{10,8},{12,... | collective-permute-start | bytes 1179656 | tf_op jit(solution)/shard_map/ppermute | solution.py:28
  59.6 4.8 %collective-permute-done.11 = f16[4,8,16,384]{3,2,1,0:T(8,128)(2,1)S(1)} collective-permute-done((f16[4,8,16,384]{3,2,1,0:T(8,128)(2,1)S(1)}, f16[4,8,16,384]{3,2,1,0:T(8,128)(2,1)S(1)}, u32[]{:S(2)}, u32[]{:S(2)}) %collective-permute-start.11) | collective-permute-done | bytes 393248 | tf_op jit(solution)/shard_map/ppermute | solution.py:28
  64.3 1.4 %collective-permute-start.7 = (f16[4,8,16,384]{3,2,1,0:T(8,128)(2,1)S(1)}, f16[4,8,16,384]{3,2,1,0:T(8,128)(2,1)S(1)}, u32[]{:S(2)}, u32[]{:S(2)}) collective-permute-start(f16[4,8,16,384]{3,2,1,0:T(8,128)(2,1)S(1)} %convert_element_type.160), channel_id=1, source_target_pairs={{0,4},{2,6},{4,0},{6,2},{1,5},{3,7},{5,1},{7,3},{8,12},{10,14},{12... | collective-permute-start | bytes 1179656 | tf_op jit(solution)/shard_map/ppermute | solution.py:28
  65.7 0.7 collective-permute-start.6
  66.4 6.9 %head_grad.1 = bf16[2048,768]{1,0:T(8,128)(2,1)} custom-call(s32[5]{0:T(128)S(1)} %stack.23.pos_ref, bf16[384,4096]{1,0:T(8,128)(2,1)S(1)} %copy-done, bf16[384,2048]{1,0:T(8,128)(2,1)} %collective-permute-done.1.oth_ref, bf16[384,768]{1,0:T(8,128)(2,1)S(1)} %get-tuple-element.28.g_ref.g_own_ref, bf16[384,768]{1,0:T(8,128)(2,1)S(1)} %collective-permute-done.12.g_oth_ref), custom_call_target="tpu_custom_call" | custom-call | flops 2415919104 | bytes 7471104 | tf_op jit(solution)/shard_map/head_grad/pallas_call | solution.py:274
  73.3 0.9 collective-permute-done.9
  74.2 3.8 %collective-permute-done.7 = f16[4,8,16,384]{3,2,1,0:T(8,128)(2,1)S(1)} collective-permute-done((f16[4,8,16,384]{3,2,1,0:T(8,128)(2,1)S(1)}, f16[4,8,16,384]{3,2,1,0:T(8,128)(2,1)S(1)}, u32[]{:S(2)}, u32[]{:S(2)}) %collective-permute-start.7) | collective-permute-done | bytes 393248 | tf_op jit(solution)/shard_map/ppermute | solution.py:28
  77.9 6.6 %collective-permute-done.6 = f16[4,8,16,384]{3,2,1,0:T(8,128)(2,1)S(1)} collective-permute-done((f16[4,8,16,384]{3,2,1,0:T(8,128)(2,1)S(1)}, f16[4,8,16,384]{3,2,1,0:T(8,128)(2,1)S(1)}, u32[]{:S(2)}, u32[]{:S(2)}) %collective-permute-start.6) | collective-permute-done | bytes 393248 | tf_op jit(solution)/shard_map/ppermute | solution.py:28
  84.5 0.2 multiply_add_fusion.1
  84.8 0.2 collective-permute-start.13
  85.0 3.2 %collective-permute-start.15 = (f16[8,16,384]{2,1,0:T(8,128)(2,1)S(1)}, f16[8,16,384]{2,1,0:T(8,128)(2,1)S(1)}, u32[]{:S(2)}, u32[]{:S(2)}) collective-permute-start(f16[8,16,384]{2,1,0:T(8,128)(2,1)S(1)} %get-tuple-element.46), channel_id=1, source_target_pairs={{0,192},{64,0},{128,64},{192,128},{1,193},{65,1},{129,65},{193,129... | collective-permute-start | bytes 294920 | tf_op jit(solution)/shard_map/ppermute | solution.py:28
  88.1 0.5 collective-permute-start.14
  88.6 0.2 multiply_add_fusion
  89.0 3.2 %collective-permute-start.18 = (f16[8,16,384]{2,1,0:T(8,128)(2,1)S(1)}, f16[8,16,384]{2,1,0:T(8,128)(2,1)S(1)}, u32[]{:S(2)}, u32[]{:S(2)}) collective-permute-start(f16[8,16,384]{2,1,0:T(8,128)(2,1)S(1)} %get-tuple-element.49), channel_id=1, source_target_pairs={{0,6},{2,0},{4,2},{6,4},{1,7},{3,1},{5,3},{7,5},{8,14},{10,8},{12,... | collective-permute-start | bytes 294920 | tf_op jit(solution)/shard_map/ppermute | solution.py:28
  92.2 0.2 collective-permute-start.17
  92.4 1.9 %collective-permute-done.14 = f16[8,16,384]{2,1,0:T(8,128)(2,1)S(1)} collective-permute-done((f16[8,16,384]{2,1,0:T(8,128)(2,1)S(1)}, f16[8,16,384]{2,1,0:T(8,128)(2,1)S(1)}, u32[]{:S(2)}, u32[]{:S(2)}) %collective-permute-start.14) | collective-permute-done | bytes 98336 | tf_op jit(solution)/shard_map/ppermute | solution.py:28
  94.3 0.5 collective-permute-done.16
  94.8 0.8 collective-permute-done.18
  95.5 2.8 %collective-permute-done.17 = f16[8,16,384]{2,1,0:T(8,128)(2,1)S(1)} collective-permute-done((f16[8,16,384]{2,1,0:T(8,128)(2,1)S(1)}, f16[8,16,384]{2,1,0:T(8,128)(2,1)S(1)}, u32[]{:S(2)}, u32[]{:S(2)}) %collective-permute-start.17) | collective-permute-done | bytes 98336 | tf_op jit(solution)/shard_map/ppermute | solution.py:28
  98.4 0.9 collective-permute-start.19
  99.3 0.6 collective-permute-start.20
  99.9 2.3 %collective-permute-start.21 = (f16[32,384]{1,0:T(8,128)(2,1)S(1)}, f16[32,384]{1,0:T(8,128)(2,1)S(1)}, u32[]{:S(2)}, u32[]{:S(2)}) collective-permute-start(f16[32,384]{1,0:T(8,128)(2,1)S(1)} %get-tuple-element.53), channel_id=1, source_target_pairs={{0,24},{8,32},{16,40},{24,48},{32,56},{40,0},{48,8},{56,16},{1,25}... | collective-permute-start | bytes 73736 | tf_op jit(solution)/shard_map/ppermute | solution.py:28
  102.2 3.8 %collective-permute-start.22 = (f16[32,384]{1,0:T(8,128)(2,1)S(1)}, f16[32,384]{1,0:T(8,128)(2,1)S(1)}, u32[]{:S(2)}, u32[]{:S(2)}) collective-permute-start(f16[32,384]{1,0:T(8,128)(2,1)S(1)} %get-tuple-element.54), channel_id=1, source_target_pairs={{0,32},{8,40},{16,48},{24,56},{32,0},{40,8},{48,16},{56,24},{1,33}... | collective-permute-start | bytes 73736 | tf_op jit(solution)/shard_map/ppermute | solution.py:28
  106.0 3.4 %collective-permute-start.23 = (f16[32,384]{1,0:T(8,128)(2,1)S(1)}, f16[32,384]{1,0:T(8,128)(2,1)S(1)}, u32[]{:S(2)}, u32[]{:S(2)}) collective-permute-start(f16[32,384]{1,0:T(8,128)(2,1)S(1)} %get-tuple-element.55), channel_id=1, source_target_pairs={{0,40},{8,48},{16,56},{24,0},{32,8},{40,16},{48,24},{56,32},{1,41}... | collective-permute-start | bytes 73736 | tf_op jit(solution)/shard_map/ppermute | solution.py:28
  109.4 1.7 %collective-permute-start.24 = (f16[32,384]{1,0:T(8,128)(2,1)S(1)}, f16[32,384]{1,0:T(8,128)(2,1)S(1)}, u32[]{:S(2)}, u32[]{:S(2)}) collective-permute-start(f16[32,384]{1,0:T(8,128)(2,1)S(1)} %get-tuple-element.57), channel_id=1, source_target_pairs={{0,48},{8,56},{16,0},{24,8},{32,16},{40,24},{48,32},{56,40},{1,49}... | collective-permute-start | bytes 73736 | tf_op jit(solution)/shard_map/ppermute | solution.py:28
  111.1 0.5 slice.51
  112.3 1.3 %collective-permute-done.23 = f16[32,384]{1,0:T(8,128)(2,1)S(1)} collective-permute-done((f16[32,384]{1,0:T(8,128)(2,1)S(1)}, f16[32,384]{1,0:T(8,128)(2,1)S(1)}, u32[]{:S(2)}, u32[]{:S(2)}) %collective-permute-start.23) | collective-permute-done | bytes 24608 | tf_op jit(solution)/shard_map/ppermute | solution.py:28
  113.6 0.6 collective-permute-done.24
  114.2 0.6 fusion.45
  (53 shorter events, 0.9 us)
Async XLA Ops:
  0.6 2.8 %copy-start.3 = (bf16[768,384]{1,0:T(8,128)(2,1)S(1)}, bf16[768,384]{1,0:T(8,128)(2,1)}, u32[]{:S(2)}) copy-start(bf16[768,384]{1,0:T(8,128)(2,1)} %own_ref.2) | copy-start | bytes 1769476
  0.6 3.3 %copy-start.5 = (s32[384]{0:T(512)S(1)}, s32[384]{0:T(512)}, u32[]{:S(2)}) copy-start(s32[384]{0:T(512)} %param.9) | copy-start | bytes 4612
  0.7 3.3 %copy-start.4 = (s32[768]{0:T(1024)S(1)}, s32[768]{0:T(1024)}, u32[]{:S(2)}) copy-start(s32[768]{0:T(1024)} %param.10) | copy-start | bytes 9220
  3.5 10.1 %collective-permute-start.1 = (bf16[384,2048]{1,0:T(8,128)(2,1)}, bf16[384,2048]{1,0:T(8,128)(2,1)}, u32[]{:S(2)}, u32[]{:S(2)}) collective-permute-start(bf16[384,2048]{1,0:T(8,128)(2,1)} %constant_dynamic-slice_fusion), channel_id=1, source_target_pairs={{0,1},{1,0},{2,3},{3,2},{4,5},{5,4},{6,7},{7,6},{8,9},{9,8},{10,11... | collective-permute-start | bytes 4718600 | tf_op jit(solution)/shard_map/ppermute | solution.py:28
  3.5 6.7 %collective-permute-start = (bf16[768,384]{1,0:T(8,128)(2,1)S(1)}, bf16[768,384]{1,0:T(8,128)(2,1)S(1)}, u32[]{:S(2)}, u32[]{:S(2)}) collective-permute-start(bf16[768,384]{1,0:T(8,128)(2,1)S(1)} %copy-done.3), channel_id=1, source_target_pairs={{0,1},{1,0},{2,3},{3,2},{4,5},{5,4},{6,7},{7,6},{8,9},{9,8},{10,11... | collective-permute-start | bytes 1769480 | tf_op jit(solution)/shard_map/ppermute | solution.py:28
  4.0 45.8 %slice-start = ((s8[6291456]{0:T(1024)(128)(4,1)}), s8[2097152]{0:T(1024)(128)(4,1)S(1)}, s32[]{:S(2)}) async-start(s8[6291456]{0:T(1024)(128)(4,1)} %bitcast.51), calls=%async_computation.1 | async-start | bytes 4194304
  4.1 45.7 %slice-start.1 = ((s8[6291456]{0:T(1024)(128)(4,1)}), s8[4194304]{0:T(1024)(128)(4,1)S(1)}, s32[]{:S(2)}) async-start(s8[6291456]{0:T(1024)(128)(4,1)} %bitcast.51), calls=%async_computation.2 | async-start | bytes 8388608
  10.1 1.3 %copy-start.1 = (f32[384,768]{1,0:T(8,128)S(1)}, f32[384,768]{1,0:T(8,128)}, u32[]{:S(2)}) copy-start(f32[384,768]{1,0:T(8,128)} %student_logits.1.l_ref) | copy-start | bytes 3538948
  11.4 33.0 %copy-start.6 = (f32[384]{0:T(512)S(1)}, f32[384]{0:T(512)}, u32[]{:S(2)}) copy-start(f32[384]{0:T(512)} %param.11) | copy-start | bytes 4612
  11.4 36.9 %copy-start.2 = (f32[384,768]{1,0:T(8,128)S(1)}, f32[384,768]{1,0:T(8,128)}, u32[]{:S(2)}) copy-start(f32[384,768]{1,0:T(8,128)} %student_logits.1.l_ref) | copy-start | bytes 3538948
  39.7 4.7 %collective-permute-start.4 = (f32[8,384]{1,0:T(8,128)S(1)}, f32[8,384]{1,0:T(8,128)S(1)}, u32[]{:S(2)}, u32[]{:S(2)}) collective-permute-start(f32[8,384]{1,0:T(8,128)S(1)} %merge_stats.1.refs_0_), channel_id=1, source_target_pairs={{0,192},{64,0},{128,64},{192,128},{1,193},{65,1},{129,65},{193,129... | collective-permute-start | bytes 36872 | tf_op jit(solution)/shard_map/ppermute | solution.py:28
  42.7 5.2 %collective-permute-start.3 = (f32[8,384]{1,0:T(8,128)S(1)}, f32[8,384]{1,0:T(8,128)S(1)}, u32[]{:S(2)}, u32[]{:S(2)}) collective-permute-start(f32[8,384]{1,0:T(8,128)S(1)} %merge_stats.1.refs_0_), channel_id=1, source_target_pairs={{0,128},{64,192},{128,0},{192,64},{1,129},{65,193},{129,1},{193,65... | collective-permute-start | bytes 36872 | tf_op jit(solution)/shard_map/ppermute | solution.py:28
  43.4 4.9 %collective-permute-start.2 = (f32[8,384]{1,0:T(8,128)S(1)}, f32[8,384]{1,0:T(8,128)S(1)}, u32[]{:S(2)}, u32[]{:S(2)}) collective-permute-start(f32[8,384]{1,0:T(8,128)S(1)} %merge_stats.1.refs_0_), channel_id=1, source_target_pairs={{0,64},{64,128},{128,192},{192,0},{1,65},{65,129},{129,193},{193,1... | collective-permute-start | bytes 36872 | tf_op jit(solution)/shard_map/ppermute | solution.py:28
  49.7 16.0 %collective-permute-start.12 = (bf16[384,768]{1,0:T(8,128)(2,1)S(1)}, bf16[384,768]{1,0:T(8,128)(2,1)S(1)}, u32[]{:S(2)}, u32[]{:S(2)}) collective-permute-start(bf16[384,768]{1,0:T(8,128)(2,1)S(1)} %get-tuple-element.28.g_ref.g_own_ref), channel_id=1, source_target_pairs={{0,1},{1,0},{2,3},{3,2},{4,5},{5,4},{6,7},{7,6},{8,9},{9,8},{10,11... | collective-permute-start | bytes 1769480 | tf_op jit(solution)/shard_map/ppermute | solution.py:28
  52.3 12.0 %collective-permute-start.11 = (f16[4,8,16,384]{3,2,1,0:T(8,128)(2,1)S(1)}, f16[4,8,16,384]{3,2,1,0:T(8,128)(2,1)S(1)}, u32[]{:S(2)}, u32[]{:S(2)}) collective-permute-start(f16[4,8,16,384]{3,2,1,0:T(8,128)(2,1)S(1)} %convert_element_type.164), channel_id=1, source_target_pairs={{0,192},{64,0},{128,64},{192,128},{1,193},{65,1},{129,65},{193,129... | collective-permute-start | bytes 1179656 | tf_op jit(solution)/shard_map/ppermute | solution.py:28
  52.9 20.3 %collective-permute-start.10 = (f16[4,8,16,384]{3,2,1,0:T(8,128)(2,1)S(1)}, f16[4,8,16,384]{3,2,1,0:T(8,128)(2,1)S(1)}, u32[]{:S(2)}, u32[]{:S(2)}) collective-permute-start(f16[4,8,16,384]{3,2,1,0:T(8,128)(2,1)S(1)} %convert_element_type.163), channel_id=1, source_target_pairs={{0,128},{64,192},{128,0},{192,64},{1,129},{65,193},{129,1},{193,65... | collective-permute-start | bytes 1179656 | tf_op jit(solution)/shard_map/ppermute | solution.py:28
  54.4 19.7 %collective-permute-start.9 = (f16[4,8,16,384]{3,2,1,0:T(8,128)(2,1)S(1)}, f16[4,8,16,384]{3,2,1,0:T(8,128)(2,1)S(1)}, u32[]{:S(2)}, u32[]{:S(2)}) collective-permute-start(f16[4,8,16,384]{3,2,1,0:T(8,128)(2,1)S(1)} %convert_element_type.162), channel_id=1, source_target_pairs={{0,64},{64,128},{128,192},{192,0},{1,65},{65,129},{129,193},{193,1... | collective-permute-start | bytes 1179656 | tf_op jit(solution)/shard_map/ppermute | solution.py:28
  58.1 8.3 %copy-start = (bf16[384,4096]{1,0:T(8,128)(2,1)S(1)}, bf16[384,4096]{1,0:T(8,128)(2,1)}, u32[]{:S(2)}) copy-start(bf16[384,4096]{1,0:T(8,128)(2,1)} %own_ref.3) | copy-start | bytes 9437188
  58.3 15.9 %collective-permute-start.8 = (f16[4,8,16,384]{3,2,1,0:T(8,128)(2,1)S(1)}, f16[4,8,16,384]{3,2,1,0:T(8,128)(2,1)S(1)}, u32[]{:S(2)}, u32[]{:S(2)}) collective-permute-start(f16[4,8,16,384]{3,2,1,0:T(8,128)(2,1)S(1)} %convert_element_type.161), channel_id=1, source_target_pairs={{0,6},{2,0},{4,2},{6,4},{1,7},{3,1},{5,3},{7,5},{8,14},{10,8},{12,... | collective-permute-start | bytes 1179656 | tf_op jit(solution)/shard_map/ppermute | solution.py:28
  64.3 13.6 %collective-permute-start.7 = (f16[4,8,16,384]{3,2,1,0:T(8,128)(2,1)S(1)}, f16[4,8,16,384]{3,2,1,0:T(8,128)(2,1)S(1)}, u32[]{:S(2)}, u32[]{:S(2)}) collective-permute-start(f16[4,8,16,384]{3,2,1,0:T(8,128)(2,1)S(1)} %convert_element_type.160), channel_id=1, source_target_pairs={{0,4},{2,6},{4,0},{6,2},{1,5},{3,7},{5,1},{7,3},{8,12},{10,14},{12... | collective-permute-start | bytes 1179656 | tf_op jit(solution)/shard_map/ppermute | solution.py:28
  65.7 18.8 %collective-permute-start.6 = (f16[4,8,16,384]{3,2,1,0:T(8,128)(2,1)S(1)}, f16[4,8,16,384]{3,2,1,0:T(8,128)(2,1)S(1)}, u32[]{:S(2)}, u32[]{:S(2)}) collective-permute-start(f16[4,8,16,384]{3,2,1,0:T(8,128)(2,1)S(1)} %convert_element_type.159), channel_id=1, source_target_pairs={{0,2},{2,4},{4,6},{6,0},{1,3},{3,5},{5,7},{7,1},{8,10},{10,12},{12... | collective-permute-start | bytes 1179656 | tf_op jit(solution)/shard_map/ppermute | solution.py:28
  84.8 7.4 %collective-permute-start.13 = (f16[8,16,384]{2,1,0:T(8,128)(2,1)S(1)}, f16[8,16,384]{2,1,0:T(8,128)(2,1)S(1)}, u32[]{:S(2)}, u32[]{:S(2)}) collective-permute-start(f16[8,16,384]{2,1,0:T(8,128)(2,1)S(1)} %get-tuple-element.45), channel_id=1, source_target_pairs={{0,64},{64,128},{128,192},{192,0},{1,65},{65,129},{129,193},{193,1... | collective-permute-start | bytes 294920 | tf_op jit(solution)/shard_map/ppermute | solution.py:28
  85.0 7.4 %collective-permute-start.15 = (f16[8,16,384]{2,1,0:T(8,128)(2,1)S(1)}, f16[8,16,384]{2,1,0:T(8,128)(2,1)S(1)}, u32[]{:S(2)}, u32[]{:S(2)}) collective-permute-start(f16[8,16,384]{2,1,0:T(8,128)(2,1)S(1)} %get-tuple-element.46), channel_id=1, source_target_pairs={{0,192},{64,0},{128,64},{192,128},{1,193},{65,1},{129,65},{193,129... | collective-permute-start | bytes 294920 | tf_op jit(solution)/shard_map/ppermute | solution.py:28
  88.1 6.1 %collective-permute-start.14 = (f16[8,16,384]{2,1,0:T(8,128)(2,1)S(1)}, f16[8,16,384]{2,1,0:T(8,128)(2,1)S(1)}, u32[]{:S(2)}, u32[]{:S(2)}) collective-permute-start(f16[8,16,384]{2,1,0:T(8,128)(2,1)S(1)} %get-tuple-element.47), channel_id=1, source_target_pairs={{0,128},{64,192},{128,0},{192,64},{1,129},{65,193},{129,1},{193,65... | collective-permute-start | bytes 294920 | tf_op jit(solution)/shard_map/ppermute | solution.py:28
  88.9 5.9 %collective-permute-start.16 = (f16[8,16,384]{2,1,0:T(8,128)(2,1)S(1)}, f16[8,16,384]{2,1,0:T(8,128)(2,1)S(1)}, u32[]{:S(2)}, u32[]{:S(2)}) collective-permute-start(f16[8,16,384]{2,1,0:T(8,128)(2,1)S(1)} %get-tuple-element.48), channel_id=1, source_target_pairs={{0,2},{2,4},{4,6},{6,0},{1,3},{3,5},{5,7},{7,1},{8,10},{10,12},{12... | collective-permute-start | bytes 294920 | tf_op jit(solution)/shard_map/ppermute | solution.py:28
  89.0 6.6 %collective-permute-start.18 = (f16[8,16,384]{2,1,0:T(8,128)(2,1)S(1)}, f16[8,16,384]{2,1,0:T(8,128)(2,1)S(1)}, u32[]{:S(2)}, u32[]{:S(2)}) collective-permute-start(f16[8,16,384]{2,1,0:T(8,128)(2,1)S(1)} %get-tuple-element.49), channel_id=1, source_target_pairs={{0,6},{2,0},{4,2},{6,4},{1,7},{3,1},{5,3},{7,5},{8,14},{10,8},{12,... | collective-permute-start | bytes 294920 | tf_op jit(solution)/shard_map/ppermute | solution.py:28
  92.2 6.1 %collective-permute-start.17 = (f16[8,16,384]{2,1,0:T(8,128)(2,1)S(1)}, f16[8,16,384]{2,1,0:T(8,128)(2,1)S(1)}, u32[]{:S(2)}, u32[]{:S(2)}) collective-permute-start(f16[8,16,384]{2,1,0:T(8,128)(2,1)S(1)} %get-tuple-element.50), channel_id=1, source_target_pairs={{0,4},{2,6},{4,0},{6,2},{1,5},{3,7},{5,1},{7,3},{8,12},{10,14},{12... | collective-permute-start | bytes 294920 | tf_op jit(solution)/shard_map/ppermute | solution.py:28
  98.4 11.0 %collective-permute-start.19 = (f16[32,384]{1,0:T(8,128)(2,1)S(1)}, f16[32,384]{1,0:T(8,128)(2,1)S(1)}, u32[]{:S(2)}, u32[]{:S(2)}) collective-permute-start(f16[32,384]{1,0:T(8,128)(2,1)S(1)} %get-tuple-element.51), channel_id=1, source_target_pairs={{0,8},{8,16},{16,24},{24,32},{32,40},{40,48},{48,56},{56,0},{1,9},... | collective-permute-start | bytes 73736 | tf_op jit(solution)/shard_map/ppermute | solution.py:28
  99.3 10.1 %collective-permute-start.20 = (f16[32,384]{1,0:T(8,128)(2,1)S(1)}, f16[32,384]{1,0:T(8,128)(2,1)S(1)}, u32[]{:S(2)}, u32[]{:S(2)}) collective-permute-start(f16[32,384]{1,0:T(8,128)(2,1)S(1)} %get-tuple-element.52), channel_id=1, source_target_pairs={{0,16},{8,24},{16,32},{24,40},{32,48},{40,56},{48,0},{56,8},{1,17}... | collective-permute-start | bytes 73736 | tf_op jit(solution)/shard_map/ppermute | solution.py:28
  99.9 6.1 %collective-permute-start.5 = (f32[8,128]{1,0:T(8,128)S(1)}, f32[8,128]{1,0:T(8,128)S(1)}, u32[]{:S(2)}, u32[]{:S(2)}) collective-permute-start(f32[8,128]{1,0:T(8,128)S(1)} %get-tuple-element.27), channel_id=1, source_target_pairs={{0,1},{1,0},{2,3},{3,2},{4,5},{5,4},{6,7},{7,6},{8,9},{9,8},{10,11... | collective-permute-start | bytes 12296 | tf_op jit(solution)/shard_map/ppermute | solution.py:28
  99.9 12.4 %collective-permute-start.21 = (f16[32,384]{1,0:T(8,128)(2,1)S(1)}, f16[32,384]{1,0:T(8,128)(2,1)S(1)}, u32[]{:S(2)}, u32[]{:S(2)}) collective-permute-start(f16[32,384]{1,0:T(8,128)(2,1)S(1)} %get-tuple-element.53), channel_id=1, source_target_pairs={{0,24},{8,32},{16,40},{24,48},{32,56},{40,0},{48,8},{56,16},{1,25}... | collective-permute-start | bytes 73736 | tf_op jit(solution)/shard_map/ppermute | solution.py:28
  102.2 10.1 %collective-permute-start.22 = (f16[32,384]{1,0:T(8,128)(2,1)S(1)}, f16[32,384]{1,0:T(8,128)(2,1)S(1)}, u32[]{:S(2)}, u32[]{:S(2)}) collective-permute-start(f16[32,384]{1,0:T(8,128)(2,1)S(1)} %get-tuple-element.54), channel_id=1, source_target_pairs={{0,32},{8,40},{16,48},{24,56},{32,0},{40,8},{48,16},{56,24},{1,33}... | collective-permute-start | bytes 73736 | tf_op jit(solution)/shard_map/ppermute | solution.py:28
  106.0 7.7 %collective-permute-start.23 = (f16[32,384]{1,0:T(8,128)(2,1)S(1)}, f16[32,384]{1,0:T(8,128)(2,1)S(1)}, u32[]{:S(2)}, u32[]{:S(2)}) collective-permute-start(f16[32,384]{1,0:T(8,128)(2,1)S(1)} %get-tuple-element.55), channel_id=1, source_target_pairs={{0,40},{8,48},{16,56},{24,0},{32,8},{40,16},{48,24},{56,32},{1,41}... | collective-permute-start | bytes 73736 | tf_op jit(solution)/shard_map/ppermute | solution.py:28
  109.4 4.2 %collective-permute-start.25 = (f16[32,384]{1,0:T(8,128)(2,1)S(1)}, f16[32,384]{1,0:T(8,128)(2,1)S(1)}, u32[]{:S(2)}, u32[]{:S(2)}) collective-permute-start(f16[32,384]{1,0:T(8,128)(2,1)S(1)} %get-tuple-element.56), channel_id=1, source_target_pairs={{0,56},{8,0},{16,8},{24,16},{32,24},{40,32},{48,40},{56,48},{1,57}... | collective-permute-start | bytes 73736 | tf_op jit(solution)/shard_map/ppermute | solution.py:28
  109.4 4.8 %collective-permute-start.24 = (f16[32,384]{1,0:T(8,128)(2,1)S(1)}, f16[32,384]{1,0:T(8,128)(2,1)S(1)}, u32[]{:S(2)}, u32[]{:S(2)}) collective-permute-start(f16[32,384]{1,0:T(8,128)(2,1)S(1)} %get-tuple-element.57), channel_id=1, source_target_pairs={{0,48},{8,56},{16,0},{24,8},{32,16},{40,24},{48,32},{56,40},{1,49}... | collective-permute-start | bytes 73736 | tf_op jit(solution)/shard_map/ppermute | solution.py:28

commit v3 on v2

v3 whole, which is shorter than its diff:
```python
import functools

import jax
import jax.numpy as jnp
from jax import lax
from jax.experimental import pallas as pl
from jax.experimental.pallas import tpu as pltpu
from jax.sharding import Mesh, PartitionSpec as P

CE_WEIGHT = 0.5
SEND_SCALE = 64.0
SPARE = 256
F32 = jnp.float32
BF16 = jnp.bfloat16
F16 = jnp.float16


WHOLE = pl.BlockSpec(memory_space=pltpu.VMEM)


def params(mib, *semantics):
    return pltpu.CompilerParams(
        vmem_limit_bytes=mib * 1024 * 1024, dimension_semantics=semantics or None
    )


def shift(a, axis, by):
    n = lax.axis_size(axis)
    return lax.ppermute(a, axis, [(i, (i + by) % n) for i in range(n)])


def logits_kernel(steps, h_ref, w_ref, out_ref, h_buf, w_buf, h_sem, w_sem):
    kb = w_buf.shape[1]

    def copies(k):
        at = pl.ds(k * kb, kb)
        return (
            pltpu.make_async_copy(h_ref.at[:, at], h_buf.at[k], h_sem.at[k]),
            pltpu.make_async_copy(w_ref.at[at], w_buf.at[k], w_sem.at[k]),
        )

    for k in range(steps):
        for copy in copies(k):
            copy.start()
    out_ref[...] = jnp.zeros_like(out_ref)

    def step(k, carry):
        for copy in copies(k):
            copy.wait()
        out_ref[...] += jnp.dot(h_buf[k], w_buf[k], preferred_element_type=F32)
        return carry

    lax.fori_loop(0, steps, step, 0)


def student_logits(hidden, head, steps=4):
    rows, depth = hidden.shape
    cols = head.shape[1]
    kb = depth // steps
    return pl.pallas_call(
        functools.partial(logits_kernel, steps),
        out_shape=jax.ShapeDtypeStruct((rows, cols), F32),
        in_specs=[pl.BlockSpec(memory_space=pl.ANY)] * 2,
        out_specs=WHOLE,
        scratch_shapes=[
            pltpu.VMEM((steps, rows, kb), BF16),
            pltpu.VMEM((steps, kb, cols), BF16),
            pltpu.SemaphoreType.DMA((steps,)),
            pltpu.SemaphoreType.DMA((steps,)),
        ],
        compiler_params=params(52),
        cost_estimate=pl.CostEstimate(
            flops=2 * rows * depth * cols,
            bytes_accessed=2 * (rows * depth + depth * cols) + 4 * rows * cols,
            transcendentals=0,
        ),
        name="student_logits",
    )(hidden, head)


def columns_of(*rows):
    n = rows[0].shape[1]
    sub = lax.broadcasted_iota(jnp.int32, (128, n), 0)
    packed = jnp.zeros((128, n), F32)
    for at, row in enumerate(rows):
        packed = jnp.where(sub == at, row.astype(F32), packed)
    turned = packed.T
    return [turned[:, at : at + 1] for at in range(len(rows))]


def stats_kernel(
    pos_ref, l_hbm, own_ref, oth_ref, assign_ref, ids_ref, stats_ref, t_ref, l_ref, l_sem
):
    rows, cols = l_ref.shape
    copy = pltpu.make_async_copy(l_hbm, l_ref, l_sem)
    copy.start()
    total = own_ref.shape[0]
    first = pos_ref[0] == 0
    assign = assign_ref[...]
    assign = jnp.where(first, assign[:, :rows], assign[:, rows:])
    assign, ids = columns_of(assign, ids_ref[...])
    lanes = lax.broadcasted_iota(jnp.int32, (rows, total), 1).astype(F32)
    pick = (lanes == assign).astype(BF16)
    own = jnp.dot(pick, own_ref[...], preferred_element_type=F32)
    oth = jnp.dot(pick, oth_ref[...], preferred_element_type=F32)
    teacher = jnp.concatenate([jnp.where(first, own, oth), jnp.where(first, oth, own)], axis=1)
    t_ref[...] = teacher.astype(BF16)
    copy.wait()
    logits = l_ref[...]
    top_s = jnp.max(logits, axis=1, keepdims=True)
    sum_s = jnp.sum(jnp.exp(logits - top_s), axis=1, keepdims=True)
    top_t = jnp.max(teacher, axis=1, keepdims=True)
    exp_t = jnp.exp(teacher - top_t)
    sum_t = jnp.sum(exp_t, axis=1, keepdims=True)
    cross = jnp.sum(exp_t * (teacher - logits), axis=1, keepdims=True)
    columns = pos_ref[1] + lax.broadcasted_iota(jnp.int32, (rows, cols), 1)
    hot = columns.astype(F32) == ids
    picked = jnp.sum(jnp.where(hot, logits, 0.0), axis=1, keepdims=True)
    lane = lax.broadcasted_iota(jnp.int32, (rows, 128), 1)
    packed = jnp.zeros((rows, 128), F32)
    for at, value in enumerate((top_s, sum_s, top_t, sum_t, cross, picked)):
        packed = jnp.where(lane == at, value, packed)
    packed = packed.T
    top_s, sum_s, top_t, sum_t, cross, picked = (packed[at : at + 1] for at in range(6))
    cross = cross / sum_t
    picked = jnp.sum(picked, axis=1, keepdims=True)
    spare = stats_ref.shape[1] - rows
    stats_ref[0:1, :rows] = top_s + jnp.log(sum_s)
    stats_ref[1:2, :rows] = top_t + jnp.log(sum_t)
    stats_ref[0:1, rows:] = cross[:, :spare]
    stats_ref[1:2, rows : 2 * rows - spare] = cross[:, spare:]
    lane = lax.broadcasted_iota(jnp.int32, (1, 2 * (spare - rows // 2)), 1)
    stats_ref[1:2, 2 * rows - spare :] = jnp.where(lane == 0, picked, 0.0)


def local_stats(pos, logits, own, oth, assign, ids):
    rows, cols = logits.shape
    return pl.pallas_call(
        stats_kernel,
        out_shape=(
            jax.ShapeDtypeStruct((2, rows + SPARE), F32),
            jax.ShapeDtypeStruct((rows, cols), BF16),
        ),
        in_specs=[pl.BlockSpec(memory_space=pltpu.SMEM), pl.BlockSpec(memory_space=pl.ANY)]
        + [WHOLE] * 4,
        out_specs=(WHOLE, WHOLE),
        scratch_shapes=[pltpu.VMEM((rows, cols), F32), pltpu.SemaphoreType.DMA],
        compiler_params=params(16),
        cost_estimate=pl.CostEstimate(
            flops=2 * rows * cols * own.shape[0],
            bytes_accessed=4 * rows * cols + 4 * own.size + 2 * rows * cols,
            transcendentals=2 * rows * cols,
        ),
        name="local_stats",
    )(pos, logits, own, oth, assign, ids)


def logsumexp(values):
    top = jnp.max(values, axis=0, keepdims=True)
    return top + jnp.log(jnp.sum(jnp.exp(values - top), axis=0, keepdims=True))


def grad_kernel(pos_ref, l_ref, t_ref, ids_ref, scale_ref, stats_ref, g_ref, loss_ref):
    rows, cols = l_ref.shape
    spare = stats_ref.shape[2] - rows
    norm_s = logsumexp(stats_ref[:, 0, :rows])
    block_t = stats_ref[:, 1, :rows]
    norm_t = logsumexp(block_t)
    share_t = jnp.exp(block_t - norm_t)
    far = 2 * rows - spare
    picked = jnp.sum(stats_ref[:, 1, far:], axis=0, keepdims=True)
    cross = jnp.concatenate([stats_ref[:, 0, rows:], stats_ref[:, 1, rows:far]], axis=1)
    cross = jnp.sum(cross * share_t, axis=0, keepdims=True)
    terms = cross - norm_t + (1.0 + CE_WEIGHT) * norm_s
    terms = jnp.sum(terms, axis=1, keepdims=True)
    terms -= CE_WEIGHT * jnp.sum(picked, axis=1, keepdims=True)
    loss_ref[...] = jnp.broadcast_to(terms, loss_ref.shape)
    norm_s, norm_t, ids, scale = columns_of(norm_s, norm_t, ids_ref[...], scale_ref[...])
    columns = pos_ref[1] + lax.broadcasted_iota(jnp.int32, (rows, cols), 1)
    hot = jnp.where(columns.astype(F32) == ids, CE_WEIGHT, 0.0)
    prob_s = jnp.exp(l_ref[...] - norm_s)
    prob_t = jnp.exp(t_ref[...].astype(F32) - norm_t)
    g_ref[...] = (scale * ((1.0 + CE_WEIGHT) * prob_s - prob_t - hot)).astype(BF16)


def grad_logits(pos, logits, teacher, ids, scale, stats):
    rows, cols = logits.shape
    return pl.pallas_call(
        grad_kernel,
        out_shape=(
            jax.ShapeDtypeStruct((rows, cols), BF16),
            jax.ShapeDtypeStruct((8, 128), F32),
        ),
        in_specs=[pl.BlockSpec(memory_space=pltpu.SMEM)] + [WHOLE] * 5,
        out_specs=(WHOLE, WHOLE),
        compiler_params=params(16),
        cost_estimate=pl.CostEstimate(
            flops=8 * rows * cols,
            bytes_accessed=8 * rows * cols,
            transcendentals=2 * rows * cols,
        ),
        name="grad_logits",
    )(pos, logits, teacher, ids, scale, stats)


def hidden_kernel(first_x, half, pos_ref, w_ref, g_ref, up, down, keep1, keep3, own):
    ny, nz, nx, _, sub, cols = w_ref.shape
    y, x = pos_ref[2], pos_ref[3]
    g = g_ref[...]
    slots = {
        1: (keep1.at[0], keep1.at[1], up.at[2], up.at[3]),
        2: (up.at[0], up.at[1], down.at[0], down.at[1]),
        3: (down.at[2], down.at[3], keep3.at[0], keep3.at[1]),
        0: tuple(own.at[near] for near in range(4)),
    }
    for far, places in slots.items():

        def block(near):
            dx, dy = (far, near) if first_x else (near, far)
            w = w_ref[lax.rem(y + dy, ny), :, lax.rem(x + dx, nx), half]
            return w.reshape(nz * sub, cols)

        w = jnp.concatenate([block(near) for near in range(4)], axis=0)
        part = lax.dot_general(
            w, g, (((1,), (1,)), ((), ())), preferred_element_type=F32
        )
        for near, place in enumerate(places):
            place[...] = part[near * nz * sub : (near + 1) * nz * sub].reshape(place.shape)


def hidden_part(pos, head6, g, first_x, half):
    ny, nz, nx, _, sub, cols = head6.shape
    rows = g.shape[0]
    shape = lambda n: jax.ShapeDtypeStruct((n, nz, sub, rows), F32)
    return pl.pallas_call(
        functools.partial(hidden_kernel, first_x, half),
        out_shape=[shape(4), shape(4), shape(2), shape(2), shape(4)],
        in_specs=[pl.BlockSpec(memory_space=pltpu.SMEM), WHOLE, WHOLE],
        out_specs=[WHOLE] * 5,
        compiler_params=params(16),
        cost_estimate=pl.CostEstimate(
            flops=rows * head6.size,
            bytes_accessed=head6.size + 2 * rows * ny * nz * nx * sub,
            transcendentals=0,
        ),
        name="hidden_part",
    )(pos, head6, g)


def head_kernel(pos_ref, own_ref, oth_ref, g_own_ref, g_oth_ref, out_ref, buf, sem):
    steps, block, _ = buf.shape
    g = jnp.concatenate([g_own_ref[...], g_oth_ref[...]], axis=0)
    copies = []
    for i in range(steps):
        at = pl.ds(pl.multiple_of(pos_ref[0] * (steps * block) + i * block, block), block)
        h = jnp.concatenate([own_ref[:, at], oth_ref[:, at]], axis=0)
        total = lax.dot_general(h, g, (((0,), (0,)), ((), ())), preferred_element_type=F32)
        buf[i] = total.astype(BF16)
        copy = pltpu.make_async_copy(buf.at[i], out_ref.at[pl.ds(i * block, block)], sem.at[i])
        copy.start()
        copies.append(copy)
    for copy in copies:
        copy.wait()


def head_grad(pos, hidden, hidden_oth, g, g_oth, steps=2):
    rows, depth = hidden.shape
    cols = g.shape[1]
    width = depth // 2
    return pl.pallas_call(
        head_kernel,
        out_shape=jax.ShapeDtypeStruct((width, cols), BF16),
        in_specs=[pl.BlockSpec(memory_space=pltpu.SMEM)] + [WHOLE] * 4,
        out_specs=pl.BlockSpec(memory_space=pl.ANY),
        scratch_shapes=[
            pltpu.VMEM((steps, width // steps, cols), BF16),
            pltpu.SemaphoreType.DMA((steps,)),
        ],
        compiler_params=params(20),
        cost_estimate=pl.CostEstimate(
            flops=4 * rows * width * cols,
            bytes_accessed=4 * rows * width + 4 * rows * cols + 2 * width * cols,
            transcendentals=0,
        ),
        name="head_grad",
    )(pos, hidden, hidden_oth, g, g_oth)


def body(teacher, hidden, head, ids, assignment, row_scale):
    c, x, y = (lax.axis_index(a) for a in ("c", "x", "y"))
    rows, depth = hidden.shape
    cols = head.shape[1]
    chips = ("y", "z", "x")
    ny, nz, nx = (lax.axis_size(a) for a in chips)
    pos = jnp.stack([c, lax.axis_index(chips) * cols, y, x]).astype(jnp.int32)
    assign = assignment.reshape(1, -1)
    ids = ids.reshape(1, rows)
    scale = row_scale.reshape(1, rows)

    teacher_oth = shift(teacher, "c", 1)
    logits = student_logits(hidden, head)
    stats, teacher_rows = local_stats(pos, logits, teacher, teacher_oth, assign, ids)
    hidden, head, stats = lax.optimization_barrier((hidden, head, stats))
    hidden_oth = shift(hidden, "c", 1)
    stats = jnp.broadcast_to(stats[None], (ny * nz * nx,) + stats.shape)
    stats = lax.all_to_all(stats, chips, 0, 0, tiled=True)
    stats, hidden_oth = lax.optimization_barrier((stats, hidden_oth))
    g, loss_part = grad_logits(pos, logits, teacher_rows, ids, scale, stats)
    g_oth = shift(g, "c", 1)

    sub = depth // (ny * nz * nx) // 2
    head6 = head.reshape(ny, nz, nx, 2, sub, cols)

    def send(value, axis, by):
        return shift((value * SEND_SCALE).astype(F16), axis, by)

    def taken(value):
        return value.astype(F32) * (1.0 / SEND_SCALE)

    def first_step(g, half, axis):
        up, down, c1, c3, c0 = hidden_part(pos, head6, g, axis == "x", half)
        up, down = ((v * SEND_SCALE).astype(F16) for v in (up, down))
        g, up, down = lax.optimization_barrier((g, up, down))
        return g, (c0, c1, c3), (shift(up, axis, 1), shift(down, axis, -1))

    def second_step(kept, got, axis):
        (c0, c1, c3), (up, down) = kept, got
        up2 = send(c1 + taken(up[:2]), axis, 1)
        down2 = send(c3 + taken(down[:2]), axis, -1)
        return c0[:2] + taken(down[2:]) + taken(up2), c0[2:] + taken(up[2:]) + taken(down2)

    g_then, kept_a, got_a = first_step(g, 0, "x")
    _, kept_b, got_b = first_step(g_then, 1, "y")
    head_out = head_grad(pos, hidden, hidden_oth, g, g_oth)
    got_a, got_b, head_out = lax.optimization_barrier((got_a, got_b, head_out))
    low_a, high_a = second_step(kept_a, got_a, "x")
    low_b, high_b = second_step(kept_b, got_b, "y")

    def second_level(low, high, axis):
        far = [send(f, axis, d) for d, f in ((2, high[0]), (1, low[1]), (3, high[1]))]
        return low[0] + sum(taken(f) for f in far)

    both = jnp.concatenate(
        [second_level(low_a, high_a, "y"), second_level(low_b, high_b, "x")], axis=1
    )
    both = lax.all_to_all((both * SEND_SCALE).astype(F16), "z", 0, 0, tiled=True)
    hidden_grad = jnp.sum(taken(both), axis=0).T.astype(BF16)

    loss_all = loss_part + shift(loss_part, "c", 1)
    loss = loss_all[0, :1] / (2 * rows)
    return loss, hidden_grad, head_out


def solution(mesh):
    ny, nzx, nc = mesh.devices.shape
    nx = 4
    fine = Mesh(mesh.devices.reshape(ny, nzx // nx, nx, nc), ("y", "z", "x", "c"))
    vocab = ("y", "z", "x")
    in_specs = (
        P(None, vocab + ("c",)),
        P("c", None),
        P(None, vocab),
        P("c"),
        P(),
        P("c"),
    )
    out_specs = (P(), P("c", vocab), P("c", vocab))
    return jax.shard_map(body, mesh=fine, in_specs=in_specs, out_specs=out_specs, check_vma=False)
```

time: 118 us -> 119 us (level)
  blocking collectives: 25.9 us -> 0 us
  waiting for transfers between devices: 27.8 us -> 39.7 us
  starting transfers between devices: 31.9 us -> 41.8 us
  local copies, waits for them, and re-layouts: 4.74 us -> 8.88 us
    all_to_all x0 -> x2, waiting for transfers between devices: none -> 27.8 us  [the longest x1 21.8 us: body(): stats = lax.all_to_all(stats, chips, 0, 0, tiled=True)]
    all_to_all x1 -> x0, blocking collectives: 25.9 us -> none  [body(): stats = merge_stats(lax.all_to_all(stats, ('z', 'x'), 0, 0, tiled=True))]
    all_to_all x0 -> x2, starting transfers between devices: none -> 20.8 us  [the longest x1 15.4 us: body(): stats = lax.all_to_all(stats, chips, 0, 0, tiled=True)]
    ppermute x26 -> x18, waiting for transfers between devices: 27.8 us -> 11.9 us  [shift(): return lax.ppermute(a, axis, [(i, (i + by) % n) for i in range(n)])]
    ppermute x26 -> x18, starting transfers between devices: 31.9 us -> 20.9 us  [shift(): return lax.ppermute(a, axis, [(i, (i + by) % n) for i in range(n)])]
    unnamed x18 -> x16, local copies, waits for them, and re-layouts: 1.3 us -> 5.98 us
    dynamic_slice x1 -> x0, local copies, waits for them, and re-layouts: 2.79 us -> none  [body(): lax.dynamic_slice(hidden, (0, (1 - c) * width), (rows, width))]
    pallas_call x3 -> x2, Pallas kernels: 3.69 us -> 6.06 us  [the longest x1 3.87 us: local_stats(): pl.pallas_call(stats_kernel, out_shape=(jax.ShapeDtypeStruct((2, rows + S...]
  transfers between devices with their start and end apart: 26 -> 20, of which waited for: 12 -> 10; matrix products, arithmetic and copies ran while one was open for 1% -> 3% of each run, Pallas kernels for 17% -> 14%
where the time goes in v3:
time: 119 us; the launch traced here: 118 us
  starting transfers between devices  41.8 us (35%)
  waiting for transfers between devices  39.7 us (33%)
  Pallas kernels  22.4 us (19%)
  local copies, waits for them, and re-layouts  8.88 us (7%)
  between operations  2.69 us (2%)
  other arithmetic  2.64 us (2%)
    all_to_all x1, waiting for transfers between devices, body(): stats = lax.all_to_all(stats, chips, 0, 0, tiled=True)  21.8 us
    ppermute x18, starting transfers between devices, shift(): return lax.ppermute(a, axis, [(i, (i + by) % n) for i in range(n)])  20.9 us
    all_to_all x1, starting transfers between devices, body(): stats = lax.all_to_all(stats, chips, 0, 0, tiled=True)  15.4 us
    ppermute x18, waiting for transfers between devices, shift(): return lax.ppermute(a, axis, [(i, (i + by) % n) for i in range(n)])  11.9 us
    all_to_all x1, waiting for transfers between devices, body(): lax.all_to_all((both * SEND_SCALE).astype(F16), 'z', 0, 0, tiled=True)  5.99 us
    unnamed x16, local copies, waits for them, and re-layouts  5.98 us
    pallas_call x1, Pallas kernels, student_logits(): pl.pallas_call(functools.partial(logits_kernel, steps), out_shape=jax.Sha...  5.93 us
    pallas_call x1, Pallas kernels, head_grad(): pl.pallas_call(head_kernel, out_shape=jax.ShapeDtypeStruct((width, cols),...  5.78 us
  transfers between devices with their start and end apart: 20, of which 10 were waited for; matrix products, arithmetic and copies ran while one was open for 3% of the time, Pallas kernels for 14%

profile of v3, /device:TPU:32, one launch (start us, length us, event | category | flops | bytes accessed | tf_op | source)
XLA Modules:
  0.0 118.1 jit_solution(14588807062161632909)
XLA Ops:
  0.6 0.1 collective-permute-start
  0.7 0.7 reshape.40.ids_ref
  1.4 0.7 reshape.39.assign_ref
  2.2 5.9 %student_logits.1.l_hbm.l_ref = f32[384,768]{1,0:T(8,128)S(1)} custom-call(bf16[384,4096]{1,0:T(8,128)(2,1)} %own_ref.2, bf16[4096,768]{1,0:T(8,128)(2,1)} %w_ref.1), custom_call_target="tpu_custom_call" | custom-call | flops 2415919104 | bytes 10616832 | tf_op jit(solution)/shard_map/student_logits/pallas_call | solution.py:60
  8.2 3.9 %local_stats.1 = (f32[2,640]{1,0:T(2,128)S(1)}, bf16[384,768]{1,0:T(8,128)(2,1)S(1)}) custom-call(s32[4]{0:T(128)S(1)} %pad_add_fusion.pos_ref, f32[384,768]{1,0:T(8,128)S(1)} %student_logits.1.l_hbm.l_ref, bf16[768,384]{1,0:T(8,128)(2,1)S(1)} %copy-done.4, bf16[768,384]{1,0:T(8,128)(2,1)} %collective-permute-done.oth_ref, s32[1,768]{1,0:T(1,128)S(1)} %reshape.39.assign_ref, ...), custom_call_target="tpu_custom_call" | custom-call | flops 452984832 | bytes 2949120 | tf_op jit(solution)/shard_map/local_stats/pallas_call | solution.py:138
  12.1 0.8 copy-done.5
  12.9 0.5 collective-permute-start.1
  13.4 1.0 broadcast_in_dim.2
  14.4 15.4 %all-to-all-start = ((f32[128,2,640]{2,1,0:T(2,128)}), f32[128,2,640]{2,1,0:T(2,128)}, u32[]{:S(2)}, u32[]{:S(2)}) async-start(f32[128,2,640]{2,1,0:T(2,128)} %broadcast_in_dim.2), calls=%async_computation | async-start | bytes 1310720 | tf_op jit(solution)/shard_map/all_to_all | solution.py:306
  29.9 21.8 %all-to-all-done.stats_ref = f32[128,2,640]{2,1,0:T(2,128)} async-done(((f32[128,2,640]{2,1,0:T(2,128)}), f32[128,2,640]{2,1,0:T(2,128)}, u32[]{:S(2)}, u32[]{:S(2)}) %all-to-all-start) | async-done | bytes 655392 | tf_op jit(solution)/shard_map/all_to_all | solution.py:306
  51.6 1.3 %copy-done.3 = f32[384,768]{1,0:T(8,128)S(1)} copy-done((f32[384,768]{1,0:T(8,128)S(1)}, f32[384,768]{1,0:T(8,128)}, u32[]{:S(2)}) %copy-start.3) | copy-done | bytes 1179672
  52.9 1.1 copy-done.6
  54.0 2.2 %grad_logits.1 = (bf16[384,768]{1,0:T(8,128)(2,1)S(1)}, f32[8,128]{1,0:T(8,128)S(1)}) custom-call(s32[4]{0:T(128)S(1)} %pad_add_fusion.pos_ref, f32[384,768]{1,0:T(8,128)S(1)} %copy-done.3, bf16[384,768]{1,0:T(8,128)(2,1)S(1)} %copy-done.6, s32[1,384]{1,0:T(1,128)S(1)} %reshape.40.ids_ref, f32[1,384]{1,0:T(1,128)S(1)} %reshape.41.scale_ref, ...), custom_call_target="tpu_custom_call" | custom-call | flops 2359296 | bytes 2359296 | tf_op jit(solution)/shard_map/grad_logits/pallas_call | solution.py:188
  56.2 0.1 collective-permute-start.7
  56.3 2.8 %copy-done = bf16[4096,768]{1,0:T(8,128)(2,1)S(1)} copy-done((bf16[4096,768]{1,0:T(8,128)(2,1)S(1)}, bf16[4096,768]{1,0:T(8,128)(2,1)}, u32[]{:S(2)}) %copy-start) | copy-done | bytes 6291480
  59.0 2.3 %hidden_part.2 = (f32[4,8,16,384]{3,2,1,0:T(8,128)S(1)}, f32[4,8,16,384]{3,2,1,0:T(8,128)S(1)}, f32[2,8,16,384]{3,2,1,0:T(8,128)S(1)}, f32[2,8,16,384]{3,2,1,0:T(8,128)S(1)}, f32[4,8,16,384]{3,2,1,0:T(8,128)S(1)}) custom-call(s32[4]{0:T(128)S(1)} %pad_add_fusion.pos_ref, bf16[4,8,4,2,16,768]{5,4,3,2,1,0:T(8,128)(2,1)S(1)} %bitcast.29, ...), custom_call_target="tpu_custom_call" | custom-call | flops 1207959552 | bytes 4718592 | tf_op jit(solution)/shard_map/hidden_part/pallas_call | solution.py:235
  61.4 0.2 multiply_convert_fusion.2
  61.6 0.6 collective-permute-start.3
  62.2 2.7 %collective-permute-start.4 = (f16[4,8,16,384]{3,2,1,0:T(8,128)(2,1)S(1)}, f16[4,8,16,384]{3,2,1,0:T(8,128)(2,1)S(1)}, u32[]{:S(2)}, u32[]{:S(2)}) collective-permute-start(f16[4,8,16,384]{3,2,1,0:T(8,128)(2,1)S(1)} %get-tuple-element.44), channel_id=1, source_target_pairs={{0,6},{2,0},{4,2},{6,4},{1,7},{3,1},{5,3},{7,5},{8,14},{10,8},{12,... | collective-permute-start | bytes 1179656 | tf_op jit(solution)/shard_map/ppermute | solution.py:29
  64.9 2.3 %hidden_part.3 = (f32[4,8,16,384]{3,2,1,0:T(8,128)S(1)}, f32[4,8,16,384]{3,2,1,0:T(8,128)S(1)}, f32[2,8,16,384]{3,2,1,0:T(8,128)S(1)}, f32[2,8,16,384]{3,2,1,0:T(8,128)S(1)}, f32[4,8,16,384]{3,2,1,0:T(8,128)S(1)}) custom-call(s32[4]{0:T(128)S(1)} %pad_add_fusion.pos_ref, bf16[4,8,4,2,16,768]{5,4,3,2,1,0:T(8,128)(2,1)S(1)} %bitcast.30, ...), custom_call_target="tpu_custom_call" | custom-call | flops 1207959552 | bytes 4718592 | tf_op jit(solution)/shard_map/hidden_part/pallas_call | solution.py:235
  67.4 1.0 collective-permute-start.5
  68.4 2.5 %collective-permute-start.6 = (f16[4,8,16,384]{3,2,1,0:T(8,128)(2,1)S(1)}, f16[4,8,16,384]{3,2,1,0:T(8,128)(2,1)S(1)}, u32[]{:S(2)}, u32[]{:S(2)}) collective-permute-start(f16[4,8,16,384]{3,2,1,0:T(8,128)(2,1)S(1)} %multiply_convert_fusion), channel_id=1, source_target_pairs={{0,192},{64,0},{128,64},{192,128},{1,193},{65,1},{129,65},{193,129... | collective-permute-start | bytes 1179656 | tf_op jit(solution)/shard_map/ppermute | solution.py:29
  70.9 5.8 %head_grad.1 = bf16[2048,768]{1,0:T(8,128)(2,1)} custom-call(s32[4]{0:T(128)S(1)} %pad_add_fusion.pos_ref, bf16[384,4096]{1,0:T(8,128)(2,1)S(1)} %copy-done.1, bf16[384,4096]{1,0:T(8,128)(2,1)} %collective-permute-done.1.oth_ref, bf16[384,768]{1,0:T(8,128)(2,1)S(1)} %get-tuple-element.45.g_ref.g_own_ref, bf16[384,768]{1,0:T(8,128)(2,1)S(1)} %collective-permute-done.7.g_oth_ref), custom_call_target="tpu_custom_call" | custom-call | flops 2415919104 | bytes 7471104 | tf_op jit(solution)/shard_map/head_grad/pallas_call | solution.py:270
  76.7 3.1 %collective-permute-done.5 = f16[4,8,16,384]{3,2,1,0:T(8,128)(2,1)S(1)} collective-permute-done((f16[4,8,16,384]{3,2,1,0:T(8,128)(2,1)S(1)}, f16[4,8,16,384]{3,2,1,0:T(8,128)(2,1)S(1)}, u32[]{:S(2)}, u32[]{:S(2)}) %collective-permute-start.5) | collective-permute-done | bytes 393248 | tf_op jit(solution)/shard_map/ppermute | solution.py:29
  79.9 0.8 collective-permute-start.9
  80.8 1.4 %collective-permute-start.8 = (f16[2,8,16,384]{3,2,1,0:T(8,128)(2,1)S(1)}, f16[2,8,16,384]{3,2,1,0:T(8,128)(2,1)S(1)}, u32[]{:S(2)}, u32[]{:S(2)}) collective-permute-start(f16[2,8,16,384]{3,2,1,0:T(8,128)(2,1)S(1)} %multiply_convert_fusion.7), channel_id=1, source_target_pairs={{0,2},{2,4},{4,6},{6,0},{1,3},{3,5},{5,7},{7,1},{8,10},{10,12},{12... | collective-permute-start | bytes 589832 | tf_op jit(solution)/shard_map/ppermute | solution.py:29
  82.2 3.0 %collective-permute-start.14 = (f16[2,8,16,384]{3,2,1,0:T(8,128)(2,1)S(1)}, f16[2,8,16,384]{3,2,1,0:T(8,128)(2,1)S(1)}, u32[]{:S(2)}, u32[]{:S(2)}) collective-permute-start(f16[2,8,16,384]{3,2,1,0:T(8,128)(2,1)S(1)} %multiply_convert_fusion.4), channel_id=1, source_target_pairs={{0,192},{64,0},{128,64},{192,128},{1,193},{65,1},{129,65},{193,129... | collective-permute-start | bytes 589832 | tf_op jit(solution)/shard_map/ppermute | solution.py:29
  85.3 0.1 multiply_convert_fusion.5
  85.3 0.1 collective-permute-start.13
  85.4 0.4 collective-permute-done.9
  85.8 1.9 %collective-permute-done.8 = f16[2,8,16,384]{3,2,1,0:T(8,128)(2,1)S(1)} collective-permute-done((f16[2,8,16,384]{3,2,1,0:T(8,128)(2,1)S(1)}, f16[2,8,16,384]{3,2,1,0:T(8,128)(2,1)S(1)}, u32[]{:S(2)}, u32[]{:S(2)}) %collective-permute-start.8) | collective-permute-done | bytes 196640 | tf_op jit(solution)/shard_map/ppermute | solution.py:29
  87.7 0.2 multiply_add_fusion.2
  87.9 0.1 collective-permute-start.11
  88.0 4.5 %collective-permute-start.10 = (f16[8,16,384]{2,1,0:T(8,128)(2,1)S(1)}, f16[8,16,384]{2,1,0:T(8,128)(2,1)S(1)}, u32[]{:S(2)}, u32[]{:S(2)}) collective-permute-start(f16[8,16,384]{2,1,0:T(8,128)(2,1)S(1)} %get-tuple-element.65), channel_id=1, source_target_pairs={{0,128},{64,192},{128,0},{192,64},{1,129},{65,193},{129,1},{193,65... | collective-permute-start | bytes 294920 | tf_op jit(solution)/shard_map/ppermute | solution.py:29
  92.5 1.1 collective-permute-done.13
  93.6 0.2 multiply_add_fusion
  93.9 0.2 collective-permute-start.16
  94.1 3.1 %collective-permute-start.15 = (f16[8,16,384]{2,1,0:T(8,128)(2,1)S(1)}, f16[8,16,384]{2,1,0:T(8,128)(2,1)S(1)}, u32[]{:S(2)}, u32[]{:S(2)}) collective-permute-start(f16[8,16,384]{2,1,0:T(8,128)(2,1)S(1)} %get-tuple-element.67), channel_id=1, source_target_pairs={{0,4},{2,6},{4,0},{6,2},{1,5},{3,7},{5,1},{7,3},{8,12},{10,14},{12... | collective-permute-start | bytes 294920 | tf_op jit(solution)/shard_map/ppermute | solution.py:29
  97.2 0.3 collective-permute-start.17
  97.5 2.3 %collective-permute-done.16 = f16[8,16,384]{2,1,0:T(8,128)(2,1)S(1)} collective-permute-done((f16[8,16,384]{2,1,0:T(8,128)(2,1)S(1)}, f16[8,16,384]{2,1,0:T(8,128)(2,1)S(1)}, u32[]{:S(2)}, u32[]{:S(2)}) %collective-permute-start.16) | collective-permute-done | bytes 98336 | tf_op jit(solution)/shard_map/ppermute | solution.py:29
  99.8 1.0 collective-permute-done.15
  100.8 0.9 collective-permute-done.17
  101.9 0.7 fusion
  102.6 5.4 %all-to-all-start.1 = ((f16[8,32,384]{2,1,0:T(8,128)(2,1)}), f16[8,32,384]{2,1,0:T(8,128)(2,1)S(1)}, u32[]{:S(2)}, u32[]{:S(2)}) async-start(f16[8,32,384]{2,1,0:T(8,128)(2,1)} %fusion), calls=%async_computation.1 | async-start | bytes 393216 | tf_op jit(solution)/shard_map/all_to_all | solution.py:346
  108.0 1.2 collective-permute-done.2
  109.2 0.5 slice.63
  110.3 6.0 %all-to-all-done.1 = f16[8,32,384]{2,1,0:T(8,128)(2,1)S(1)} async-done(((f16[8,32,384]{2,1,0:T(8,128)(2,1)}), f16[8,32,384]{2,1,0:T(8,128)(2,1)S(1)}, u32[]{:S(2)}, u32[]{:S(2)}) %all-to-all-start.1) | async-done | bytes 196640 | tf_op jit(solution)/shard_map/all_to_all | solution.py:346
  116.3 0.7 multiply_reduce_fusion
  (38 shorter events, 0.8 us)
Async XLA Ops:
  0.6 7.5 %collective-permute-start = (bf16[768,384]{1,0:T(8,128)(2,1)}, bf16[768,384]{1,0:T(8,128)(2,1)}, u32[]{:S(2)}, u32[]{:S(2)}) collective-permute-start(bf16[768,384]{1,0:T(8,128)(2,1)} %own_ref.1), channel_id=1, source_target_pairs={{0,1},{1,0},{2,3},{3,2},{4,5},{5,4},{6,7},{7,6},{8,9},{9,8},{10,11... | collective-permute-start | bytes 1769480 | tf_op jit(solution)/shard_map/ppermute | solution.py:29
  2.2 6.0 %copy-start.4 = (bf16[768,384]{1,0:T(8,128)(2,1)S(1)}, bf16[768,384]{1,0:T(8,128)(2,1)}, u32[]{:S(2)}) copy-start(bf16[768,384]{1,0:T(8,128)(2,1)} %own_ref.1) | copy-start | bytes 1769476
  2.2 10.7 %copy-start.1 = (bf16[384,4096]{1,0:T(8,128)(2,1)S(1)}, bf16[384,4096]{1,0:T(8,128)(2,1)}, u32[]{:S(2)}) copy-start(bf16[384,4096]{1,0:T(8,128)(2,1)} %own_ref.2) | copy-start | bytes 9437188
  8.1 3.9 %copy-start.2 = (f32[384,768]{1,0:T(8,128)}, f32[384,768]{1,0:T(8,128)S(1)}, u32[]{:S(2)}) copy-start(f32[384,768]{1,0:T(8,128)S(1)} %student_logits.1.l_hbm.l_ref) | copy-start | bytes 3538948
  8.1 21.7 %copy-start.7 = (f32[384]{0:T(512)S(1)}, f32[384]{0:T(512)}, u32[]{:S(2)}) copy-start(f32[384]{0:T(512)} %param.11) | copy-start | bytes 4612
  12.1 0.9 copy-start.5
  12.9 38.7 %collective-permute-start.1 = (bf16[384,4096]{1,0:T(8,128)(2,1)S(1)}, bf16[384,4096]{1,0:T(8,128)(2,1)}, u32[]{:S(2)}, u32[]{:S(2)}) collective-permute-start(bf16[384,4096]{1,0:T(8,128)(2,1)S(1)} %copy-done.1), channel_id=1, source_target_pairs={{0,1},{1,0},{2,3},{3,2},{4,5},{5,4},{6,7},{7,6},{8,9},{9,8},{10,11... | collective-permute-start | bytes 9437192 | tf_op jit(solution)/shard_map/ppermute | solution.py:29
  14.4 37.2 %all-to-all-start = ((f32[128,2,640]{2,1,0:T(2,128)}), f32[128,2,640]{2,1,0:T(2,128)}, u32[]{:S(2)}, u32[]{:S(2)}) async-start(f32[128,2,640]{2,1,0:T(2,128)} %broadcast_in_dim.2), calls=%async_computation | async-start | bytes 1310720 | tf_op jit(solution)/shard_map/all_to_all | solution.py:306
  51.6 1.3 %copy-start.3 = (f32[384,768]{1,0:T(8,128)S(1)}, f32[384,768]{1,0:T(8,128)}, u32[]{:S(2)}) copy-start(f32[384,768]{1,0:T(8,128)} %copy-done.2) | copy-start | bytes 3538948
  52.9 1.1 copy-start.6
  56.2 14.7 %collective-permute-start.7 = (bf16[384,768]{1,0:T(8,128)(2,1)S(1)}, bf16[384,768]{1,0:T(8,128)(2,1)S(1)}, u32[]{:S(2)}, u32[]{:S(2)}) collective-permute-start(bf16[384,768]{1,0:T(8,128)(2,1)S(1)} %get-tuple-element.45.g_ref.g_own_ref), channel_id=1, source_target_pairs={{0,1},{1,0},{2,3},{3,2},{4,5},{5,4},{6,7},{7,6},{8,9},{9,8},{10,11... | collective-permute-start | bytes 1769480 | tf_op jit(solution)/shard_map/ppermute | solution.py:29
  56.3 2.8 %copy-start = (bf16[4096,768]{1,0:T(8,128)(2,1)S(1)}, bf16[4096,768]{1,0:T(8,128)(2,1)}, u32[]{:S(2)}) copy-start(bf16[4096,768]{1,0:T(8,128)(2,1)} %w_ref.1) | copy-start | bytes 18874372
  61.6 15.1 %collective-permute-start.3 = (f16[4,8,16,384]{3,2,1,0:T(8,128)(2,1)S(1)}, f16[4,8,16,384]{3,2,1,0:T(8,128)(2,1)S(1)}, u32[]{:S(2)}, u32[]{:S(2)}) collective-permute-start(f16[4,8,16,384]{3,2,1,0:T(8,128)(2,1)S(1)} %get-tuple-element.43), channel_id=1, source_target_pairs={{0,2},{2,4},{4,6},{6,0},{1,3},{3,5},{5,7},{7,1},{8,10},{10,12},{12... | collective-permute-start | bytes 1179656 | tf_op jit(solution)/shard_map/ppermute | solution.py:29
  62.2 14.5 %collective-permute-start.4 = (f16[4,8,16,384]{3,2,1,0:T(8,128)(2,1)S(1)}, f16[4,8,16,384]{3,2,1,0:T(8,128)(2,1)S(1)}, u32[]{:S(2)}, u32[]{:S(2)}) collective-permute-start(f16[4,8,16,384]{3,2,1,0:T(8,128)(2,1)S(1)} %get-tuple-element.44), channel_id=1, source_target_pairs={{0,6},{2,0},{4,2},{6,4},{1,7},{3,1},{5,3},{7,5},{8,14},{10,8},{12,... | collective-permute-start | bytes 1179656 | tf_op jit(solution)/shard_map/ppermute | solution.py:29
  67.4 12.4 %collective-permute-start.5 = (f16[4,8,16,384]{3,2,1,0:T(8,128)(2,1)S(1)}, f16[4,8,16,384]{3,2,1,0:T(8,128)(2,1)S(1)}, u32[]{:S(2)}, u32[]{:S(2)}) collective-permute-start(f16[4,8,16,384]{3,2,1,0:T(8,128)(2,1)S(1)} %multiply_convert_fusion.1), channel_id=1, source_target_pairs={{0,64},{64,128},{128,192},{192,0},{1,65},{65,129},{129,193},{193,1... | collective-permute-start | bytes 1179656 | tf_op jit(solution)/shard_map/ppermute | solution.py:29
  68.4 11.4 %collective-permute-start.6 = (f16[4,8,16,384]{3,2,1,0:T(8,128)(2,1)S(1)}, f16[4,8,16,384]{3,2,1,0:T(8,128)(2,1)S(1)}, u32[]{:S(2)}, u32[]{:S(2)}) collective-permute-start(f16[4,8,16,384]{3,2,1,0:T(8,128)(2,1)S(1)} %multiply_convert_fusion), channel_id=1, source_target_pairs={{0,192},{64,0},{128,64},{192,128},{1,193},{65,1},{129,65},{193,129... | collective-permute-start | bytes 1179656 | tf_op jit(solution)/shard_map/ppermute | solution.py:29
  79.9 6.0 %collective-permute-start.9 = (f16[2,8,16,384]{3,2,1,0:T(8,128)(2,1)S(1)}, f16[2,8,16,384]{3,2,1,0:T(8,128)(2,1)S(1)}, u32[]{:S(2)}, u32[]{:S(2)}) collective-permute-start(f16[2,8,16,384]{3,2,1,0:T(8,128)(2,1)S(1)} %multiply_convert_fusion.6), channel_id=1, source_target_pairs={{0,6},{2,0},{4,2},{6,4},{1,7},{3,1},{5,3},{7,5},{8,14},{10,8},{12,... | collective-permute-start | bytes 589832 | tf_op jit(solution)/shard_map/ppermute | solution.py:29
  80.8 7.0 %collective-permute-start.8 = (f16[2,8,16,384]{3,2,1,0:T(8,128)(2,1)S(1)}, f16[2,8,16,384]{3,2,1,0:T(8,128)(2,1)S(1)}, u32[]{:S(2)}, u32[]{:S(2)}) collective-permute-start(f16[2,8,16,384]{3,2,1,0:T(8,128)(2,1)S(1)} %multiply_convert_fusion.7), channel_id=1, source_target_pairs={{0,2},{2,4},{4,6},{6,0},{1,3},{3,5},{5,7},{7,1},{8,10},{10,12},{12... | collective-permute-start | bytes 589832 | tf_op jit(solution)/shard_map/ppermute | solution.py:29
  82.2 10.3 %collective-permute-start.14 = (f16[2,8,16,384]{3,2,1,0:T(8,128)(2,1)S(1)}, f16[2,8,16,384]{3,2,1,0:T(8,128)(2,1)S(1)}, u32[]{:S(2)}, u32[]{:S(2)}) collective-permute-start(f16[2,8,16,384]{3,2,1,0:T(8,128)(2,1)S(1)} %multiply_convert_fusion.4), channel_id=1, source_target_pairs={{0,192},{64,0},{128,64},{192,128},{1,193},{65,1},{129,65},{193,129... | collective-permute-start | bytes 589832 | tf_op jit(solution)/shard_map/ppermute | solution.py:29
  85.3 8.3 %collective-permute-start.13 = (f16[2,8,16,384]{3,2,1,0:T(8,128)(2,1)S(1)}, f16[2,8,16,384]{3,2,1,0:T(8,128)(2,1)S(1)}, u32[]{:S(2)}, u32[]{:S(2)}) collective-permute-start(f16[2,8,16,384]{3,2,1,0:T(8,128)(2,1)S(1)} %multiply_convert_fusion.5), channel_id=1, source_target_pairs={{0,64},{64,128},{128,192},{192,0},{1,65},{65,129},{129,193},{193,1... | collective-permute-start | bytes 589832 | tf_op jit(solution)/shard_map/ppermute | solution.py:29
  87.9 9.2 %collective-permute-start.11 = (f16[8,16,384]{2,1,0:T(8,128)(2,1)S(1)}, f16[8,16,384]{2,1,0:T(8,128)(2,1)S(1)}, u32[]{:S(2)}, u32[]{:S(2)}) collective-permute-start(f16[8,16,384]{2,1,0:T(8,128)(2,1)S(1)} %fusion.10), channel_id=1, source_target_pairs={{0,64},{64,128},{128,192},{192,0},{1,65},{65,129},{129,193},{193,1... | collective-permute-start | bytes 294920 | tf_op jit(solution)/shard_map/ppermute | solution.py:29
  88.0 9.4 %collective-permute-start.10 = (f16[8,16,384]{2,1,0:T(8,128)(2,1)S(1)}, f16[8,16,384]{2,1,0:T(8,128)(2,1)S(1)}, u32[]{:S(2)}, u32[]{:S(2)}) collective-permute-start(f16[8,16,384]{2,1,0:T(8,128)(2,1)S(1)} %get-tuple-element.65), channel_id=1, source_target_pairs={{0,128},{64,192},{128,0},{192,64},{1,129},{65,193},{129,1},{193,65... | collective-permute-start | bytes 294920 | tf_op jit(solution)/shard_map/ppermute | solution.py:29
  92.5 5.0 %collective-permute-start.12 = (f16[8,16,384]{2,1,0:T(8,128)(2,1)S(1)}, f16[8,16,384]{2,1,0:T(8,128)(2,1)S(1)}, u32[]{:S(2)}, u32[]{:S(2)}) collective-permute-start(f16[8,16,384]{2,1,0:T(8,128)(2,1)S(1)} %get-tuple-element.66), channel_id=1, source_target_pairs={{0,192},{64,0},{128,64},{192,128},{1,193},{65,1},{129,65},{193,129... | collective-permute-start | bytes 294920 | tf_op jit(solution)/shard_map/ppermute | solution.py:29
  93.9 5.9 %collective-permute-start.16 = (f16[8,16,384]{2,1,0:T(8,128)(2,1)S(1)}, f16[8,16,384]{2,1,0:T(8,128)(2,1)S(1)}, u32[]{:S(2)}, u32[]{:S(2)}) collective-permute-start(f16[8,16,384]{2,1,0:T(8,128)(2,1)S(1)} %fusion.13), channel_id=1, source_target_pairs={{0,2},{2,4},{4,6},{6,0},{1,3},{3,5},{5,7},{7,1},{8,10},{10,12},{12... | collective-permute-start | bytes 294920 | tf_op jit(solution)/shard_map/ppermute | solution.py:29
  94.1 6.8 %collective-permute-start.15 = (f16[8,16,384]{2,1,0:T(8,128)(2,1)S(1)}, f16[8,16,384]{2,1,0:T(8,128)(2,1)S(1)}, u32[]{:S(2)}, u32[]{:S(2)}) collective-permute-start(f16[8,16,384]{2,1,0:T(8,128)(2,1)S(1)} %get-tuple-element.67), channel_id=1, source_target_pairs={{0,4},{2,6},{4,0},{6,2},{1,5},{3,7},{5,1},{7,3},{8,12},{10,14},{12... | collective-permute-start | bytes 294920 | tf_op jit(solution)/shard_map/ppermute | solution.py:29
  97.2 4.6 %collective-permute-start.17 = (f16[8,16,384]{2,1,0:T(8,128)(2,1)S(1)}, f16[8,16,384]{2,1,0:T(8,128)(2,1)S(1)}, u32[]{:S(2)}, u32[]{:S(2)}) collective-permute-start(f16[8,16,384]{2,1,0:T(8,128)(2,1)S(1)} %get-tuple-element.68), channel_id=1, source_target_pairs={{0,6},{2,0},{4,2},{6,4},{1,7},{3,1},{5,3},{7,5},{8,14},{10,8},{12,... | collective-permute-start | bytes 294920 | tf_op jit(solution)/shard_map/ppermute | solution.py:29
  102.6 13.8 %all-to-all-start.1 = ((f16[8,32,384]{2,1,0:T(8,128)(2,1)}), f16[8,32,384]{2,1,0:T(8,128)(2,1)S(1)}, u32[]{:S(2)}, u32[]{:S(2)}) async-start(f16[8,32,384]{2,1,0:T(8,128)(2,1)} %fusion), calls=%async_computation.1 | async-start | bytes 393216 | tf_op jit(solution)/shard_map/all_to_all | solution.py:346
  108.0 1.2 collective-permute-start.2

commit v4 on v3

--- a/solution.py
+++ b/solution.py
@@ -88,24 +88,67 @@
     return [turned[:, at : at + 1] for at in range(len(rows))]
 
 
-def stats_kernel(
-    pos_ref, l_hbm, own_ref, oth_ref, assign_ref, ids_ref, stats_ref, t_ref, l_ref, l_sem
-):
+def in_row(ref):
+    return jnp.concatenate([ref[i : i + 1, :] for i in range(ref.shape[0])], axis=1)
+
+
+def pack_stats(out_ref, lse_s, lse_t, cross, picked):
+    rows = lse_s.shape[1]
+    spare = out_ref.shape[1] - rows
+    far = 2 * rows - spare
+    out_ref[0:1, :rows] = lse_s
+    out_ref[1:2, :rows] = lse_t
+    out_ref[0:1, rows:] = cross[:, :spare]
+    out_ref[1:2, rows:far] = cross[:, spare:]
+    lane = lax.broadcasted_iota(jnp.int32, (1, out_ref.shape[1] - far), 1)
+    out_ref[1:2, far:] = jnp.where(lane == 0, picked, 0.0)
+
+
+def logsumexp(values):
+    top = jnp.max(values, axis=0, keepdims=True)
+    return top + jnp.log(jnp.sum(jnp.exp(values - top), axis=0, keepdims=True))
+
+
+def merge(first, second):
+    rows = first.shape[1] - SPARE
+    far = 2 * rows - SPARE
+    lse_s = logsumexp(first[:, :rows])
+    lse_t = logsumexp(second[:, :rows])
+    share_t = jnp.exp(second[:, :rows] - lse_t)
+    cross = jnp.concatenate([first[:, rows:], second[:, rows:far]], axis=1)
+    cross = jnp.sum(cross * share_t, axis=0, keepdims=True)
+    picked = jnp.sum(second[:, far:], axis=0, keepdims=True)
+    return lse_s, lse_t, cross, jnp.sum(picked, axis=1, keepdims=True)
+
+
+def merge_kernel(in_ref, out_ref):
+    pack_stats(out_ref, *merge(in_ref[:, 0, :], in_ref[:, 1, :]))
+
+
+def merge_stats(stats):
+    return pl.pallas_call(
+        merge_kernel,
+        out_shape=jax.ShapeDtypeStruct(stats.shape[1:], F32),
+        in_specs=[WHOLE],
+        out_specs=WHOLE,
+        compiler_params=params(16),
+        name="merge_stats",
+    )(stats)
+
+
+def stats_kernel(pos_ref, l_ref, own_ref, oth_ref, assign_ref, ids_ref, stats_ref, t_ref):
     rows, cols = l_ref.shape
-    copy = pltpu.make_async_copy(l_hbm, l_ref, l_sem)
-    copy.start()
     total = own_ref.shape[0]
     first = pos_ref[0] == 0
-    assign = assign_ref[...]
+    assign = in_row(assign_ref)
     assign = jnp.where(first, assign[:, :rows], assign[:, rows:])
-    assign, ids = columns_of(assign, ids_ref[...])
+    assign, ids = columns_of(assign, in_row(ids_ref))
     lanes = lax.broadcasted_iota(jnp.int32, (rows, total), 1).astype(F32)
     pick = (lanes == assign).astype(BF16)
     own = jnp.dot(pick, own_ref[...], preferred_element_type=F32)
     oth = jnp.dot(pick, oth_ref[...], preferred_element_type=F32)
     teacher = jnp.concatenate([jnp.where(first, own, oth), jnp.where(first, oth, own)], axis=1)
     t_ref[...] = teacher.astype(BF16)
-    copy.wait()
     logits = l_ref[...]
     top_s = jnp.max(logits, axis=1, keepdims=True)
     sum_s = jnp.sum(jnp.exp(logits - top_s), axis=1, keepdims=True)
@@ -124,13 +167,7 @@
     top_s, sum_s, top_t, sum_t, cross, picked = (packed[at : at + 1] for at in range(6))
     cross = cross / sum_t
     picked = jnp.sum(picked, axis=1, keepdims=True)
-    spare = stats_ref.shape[1] - rows
-    stats_ref[0:1, :rows] = top_s + jnp.log(sum_s)
-    stats_ref[1:2, :rows] = top_t + jnp.log(sum_t)
-    stats_ref[0:1, rows:] = cross[:, :spare]
-    stats_ref[1:2, rows : 2 * rows - spare] = cross[:, spare:]
-    lane = lax.broadcasted_iota(jnp.int32, (1, 2 * (spare - rows // 2)), 1)
-    stats_ref[1:2, 2 * rows - spare :] = jnp.where(lane == 0, picked, 0.0)
+    pack_stats(stats_ref, top_s + jnp.log(sum_s), top_t + jnp.log(sum_t), cross, picked)
 
 
 def local_stats(pos, logits, own, oth, assign, ids):
@@ -141,10 +178,8 @@
             jax.ShapeDtypeStruct((2, rows + SPARE), F32),
             jax.ShapeDtypeStruct((rows, cols), BF16),
         ),
-        in_specs=[pl.BlockSpec(memory_space=pltpu.SMEM), pl.BlockSpec(memory_space=pl.ANY)]
-        + [WHOLE] * 4,
+        in_specs=[pl.BlockSpec(memory_space=pltpu.SMEM)] + [WHOLE] * 5,
         out_specs=(WHOLE, WHOLE),
-        scratch_shapes=[pltpu.VMEM((rows, cols), F32), pltpu.SemaphoreType.DMA],
         compiler_params=params(16),
         cost_estimate=pl.CostEstimate(
             flops=2 * rows * cols * own.shape[0],
@@ -155,27 +190,17 @@
     )(pos, logits, own, oth, assign, ids)
 
 
-def logsumexp(values):
-    top = jnp.max(values, axis=0, keepdims=True)
-    return top + jnp.log(jnp.sum(jnp.exp(values - top), axis=0, keepdims=True))
-
-
-def grad_kernel(pos_ref, l_ref, t_ref, ids_ref, scale_ref, stats_ref, g_ref, loss_ref):
+def grad_kernel(pos_ref, l_ref, t_ref, ids_ref, scale_ref, s0, s1, s2, s3, g_ref, loss_ref):
     rows, cols = l_ref.shape
-    spare = stats_ref.shape[2] - rows
-    norm_s = logsumexp(stats_ref[:, 0, :rows])
-    block_t = stats_ref[:, 1, :rows]
-    norm_t = logsumexp(block_t)
-    share_t = jnp.exp(block_t - norm_t)
-    far = 2 * rows - spare
-    picked = jnp.sum(stats_ref[:, 1, far:], axis=0, keepdims=True)
-    cross = jnp.concatenate([stats_ref[:, 0, rows:], stats_ref[:, 1, rows:far]], axis=1)
-    cross = jnp.sum(cross * share_t, axis=0, keepdims=True)
+    parts = (s0, s1, s2, s3)
+    first, second = (
+        jnp.concatenate([part[at : at + 1, :] for part in parts], axis=0) for at in (0, 1)
+    )
+    norm_s, norm_t, cross, picked = merge(first, second)
     terms = cross - norm_t + (1.0 + CE_WEIGHT) * norm_s
-    terms = jnp.sum(terms, axis=1, keepdims=True)
-    terms -= CE_WEIGHT * jnp.sum(picked, axis=1, keepdims=True)
+    terms = jnp.sum(terms, axis=1, keepdims=True) - CE_WEIGHT * picked
     loss_ref[...] = jnp.broadcast_to(terms, loss_ref.shape)
-    norm_s, norm_t, ids, scale = columns_of(norm_s, norm_t, ids_ref[...], scale_ref[...])
+    norm_s, norm_t, ids, scale = columns_of(norm_s, norm_t, in_row(ids_ref), in_row(scale_ref))
     columns = pos_ref[1] + lax.broadcasted_iota(jnp.int32, (rows, cols), 1)
     hot = jnp.where(columns.astype(F32) == ids, CE_WEIGHT, 0.0)
     prob_s = jnp.exp(l_ref[...] - norm_s)
@@ -183,7 +208,7 @@
     g_ref[...] = (scale * ((1.0 + CE_WEIGHT) * prob_s - prob_t - hot)).astype(BF16)
 
 
-def grad_logits(pos, logits, teacher, ids, scale, stats):
+def grad_logits(pos, logits, teacher, ids, scale, parts):
     rows, cols = logits.shape
     return pl.pallas_call(
         grad_kernel,
@@ -191,7 +216,7 @@
             jax.ShapeDtypeStruct((rows, cols), BF16),
             jax.ShapeDtypeStruct((8, 128), F32),
         ),
-        in_specs=[pl.BlockSpec(memory_space=pltpu.SMEM)] + [WHOLE] * 5,
+        in_specs=[pl.BlockSpec(memory_space=pltpu.SMEM)] + [WHOLE] * 8,
         out_specs=(WHOLE, WHOLE),
         compiler_params=params(16),
         cost_estimate=pl.CostEstimate(
@@ -200,7 +225,7 @@
             transcendentals=2 * rows * cols,
         ),
         name="grad_logits",
-    )(pos, logits, teacher, ids, scale, stats)
+    )(pos, logits, teacher, ids, scale, *parts)
 
 
 def hidden_kernel(first_x, half, pos_ref, w_ref, g_ref, up, down, keep1, keep3, own):
@@ -293,19 +318,19 @@
     chips = ("y", "z", "x")
     ny, nz, nx = (lax.axis_size(a) for a in chips)
     pos = jnp.stack([c, lax.axis_index(chips) * cols, y, x]).astype(jnp.int32)
-    assign = assignment.reshape(1, -1)
-    ids = ids.reshape(1, rows)
-    scale = row_scale.reshape(1, rows)
+    assign = assignment.reshape(-1, 128)
+    ids = ids.reshape(-1, 128)
+    scale = row_scale.reshape(-1, 128)
 
     teacher_oth = shift(teacher, "c", 1)
     logits = student_logits(hidden, head)
     stats, teacher_rows = local_stats(pos, logits, teacher, teacher_oth, assign, ids)
-    hidden, head, stats = lax.optimization_barrier((hidden, head, stats))
-    hidden_oth = shift(hidden, "c", 1)
-    stats = jnp.broadcast_to(stats[None], (ny * nz * nx,) + stats.shape)
-    stats = lax.all_to_all(stats, chips, 0, 0, tiled=True)
-    stats, hidden_oth = lax.optimization_barrier((stats, hidden_oth))
-    g, loss_part = grad_logits(pos, logits, teacher_rows, ids, scale, stats)
+    stats, scale = lax.optimization_barrier((stats, scale))
+    stats = jnp.broadcast_to(stats[None], (nz * nx,) + stats.shape)
+    stats = merge_stats(lax.all_to_all(stats, ("z", "x"), 0, 0, tiled=True))
+    parts = [stats] + [shift(stats, "y", d) for d in (2, 1, 3)]
+    hidden_oth = shift(lax.optimization_barrier((hidden, stats))[0], "c", 1)
+    g, loss_part = grad_logits(pos, logits, teacher_rows, ids, scale, parts)
     g_oth = shift(g, "c", 1)
 
     sub = depth // (ny * nz * nx) // 2
@@ -332,7 +357,9 @@
     g_then, kept_a, got_a = first_step(g, 0, "x")
     _, kept_b, got_b = first_step(g_then, 1, "y")
     head_out = head_grad(pos, hidden, hidden_oth, g, g_oth)
-    got_a, got_b, head_out = lax.optimization_barrier((got_a, got_b, head_out))
+    loss_all = loss_part + shift(loss_part, "c", 1)
+    got_a, _, loss_all = lax.optimization_barrier((got_a, head_out, loss_all))
+    got_b, head_out = lax.optimization_barrier((got_b, head_out))
     low_a, high_a = second_step(kept_a, got_a, "x")
     low_b, high_b = second_step(kept_b, got_b, "y")
 
@@ -346,7 +373,6 @@
     both = lax.all_to_all((both * SEND_SCALE).astype(F16), "z", 0, 0, tiled=True)
     hidden_grad = jnp.sum(taken(both), axis=0).T.astype(BF16)
 
-    loss_all = loss_part + shift(loss_part, "c", 1)
     loss = loss_all[0, :1] / (2 * rows)
     return loss, hidden_grad, head_out
 

time: 119 us -> 98 us (0.82)
  the two profiles are of different devices: /device:TPU:32 before, /device:TPU:24 now
where the time goes in v4:
time: 98 us; the launch traced here: 97.8 us
  waiting for transfers between devices  26.5 us (27%)
  starting transfers between devices  23.6 us (24%)
  blocking collectives  22.8 us (23%)
  Pallas kernels  18.8 us (19%)
  between operations  2.73 us (3%)
  other arithmetic  2.7 us (3%)
    all_to_all x1, blocking collectives, body(): stats = merge_stats(lax.all_to_all(stats, ('z', 'x'), 0, 0, tiled=True))  22.8 us
    ppermute x21, starting transfers between devices, shift(): return lax.ppermute(a, axis, [(i, (i + by) % n) for i in range(n)])  20.2 us
    ppermute x21, waiting for transfers between devices, shift(): return lax.ppermute(a, axis, [(i, (i + by) % n) for i in range(n)])  18 us
    all_to_all x1, waiting for transfers between devices, body(): lax.all_to_all((both * SEND_SCALE).astype(F16), 'z', 0, 0, tiled=True)  8.52 us
    pallas_call x1, Pallas kernels, student_logits(): pl.pallas_call(functools.partial(logits_kernel, steps), out_shape=jax.Sha...  5.9 us
    pallas_call x2, Pallas kernels, hidden_part(): pl.pallas_call(functools.partial(hidden_kernel, first_x, half), out_shape...  4.67 us
    pallas_call x1, Pallas kernels, head_grad(): pl.pallas_call(head_kernel, out_shape=jax.ShapeDtypeStruct((width, cols),...  4.4 us
    all_to_all x1, starting transfers between devices, body(): lax.all_to_all((both * SEND_SCALE).astype(F16), 'z', 0, 0, tiled=True)  3.39 us
  transfers between devices with their start and end apart: 22, of which 10 were waited for; matrix products, arithmetic and copies ran while one was open for 2% of the time, Pallas kernels for 17%

profile of v4, /device:TPU:24, one launch (start us, length us, event | category | flops | bytes accessed | tf_op | source)
XLA Modules:
  0.0 97.8 jit_solution(14125731583141178535)
XLA Ops:
  0.6 0.1 collective-permute-start
  0.8 0.1 pad_add_fusion.pos_ref
  0.9 5.9 %student_logits.1.l_ref = f32[384,768]{1,0:T(8,128)S(1)} custom-call(bf16[384,4096]{1,0:T(8,128)(2,1)} %own_ref.3, bf16[4096,768]{1,0:T(8,128)(2,1)} %w_ref.1), custom_call_target="tpu_custom_call" | custom-call | flops 2415919104 | bytes 10616832 | tf_op jit(solution)/shard_map/student_logits/pallas_call | solution.py:60
  6.8 2.3 %local_stats.1 = (f32[2,640]{1,0:T(2,128)S(1)}, bf16[384,768]{1,0:T(8,128)(2,1)S(1)}) custom-call(s32[4]{0:T(128)S(1)} %pad_add_fusion.pos_ref, f32[384,768]{1,0:T(8,128)S(1)} %student_logits.1.l_ref, bf16[768,384]{1,0:T(8,128)(2,1)S(1)} %copy-done.1, bf16[768,384]{1,0:T(8,128)(2,1)S(1)} %collective-permute-done.oth_ref, s32[6,128]{1,0:T(8,128)S(1)} %bitcast.38, ...), custom_call_target="tpu_custom_call" | custom-call | flops 452984832 | bytes 2949120 | tf_op jit(solution)/shard_map/local_stats/pallas_call | solution.py:175
  9.2 22.8 %all_to_all.10.in_ref = f32[32,2,640]{2,1,0:T(2,128)S(1)} all-to-all(f32[32,2,640]{2,1,0:T(2,128)S(1)} %broadcast_in_dim.2), channel_id=1, replica_groups=mesh['y'=4,'z'=8,'x'=4,'c'=2] {'z','x'}, dimensions={0} | all-to-all | bytes 327680 | tf_op jit(solution)/shard_map/all_to_all | solution.py:330
  31.9 0.2 merge_stats.1.s0
  32.2 1.3 %collective-permute-start.1 = (f32[2,640]{1,0:T(2,128)S(1)}, f32[2,640]{1,0:T(2,128)S(1)}, u32[]{:S(2)}, u32[]{:S(2)}) collective-permute-start(f32[2,640]{1,0:T(2,128)S(1)} %merge_stats.1.s0), channel_id=1, source_target_pairs={{0,128},{64,192},{128,0},{192,64},{1,129},{65,193},{129,1},{193,65... | collective-permute-start | bytes 15368 | tf_op jit(solution)/shard_map/ppermute | solution.py:29
  33.5 2.2 %collective-permute-start.2 = (f32[2,640]{1,0:T(2,128)S(1)}, f32[2,640]{1,0:T(2,128)S(1)}, u32[]{:S(2)}, u32[]{:S(2)}) collective-permute-start(f32[2,640]{1,0:T(2,128)S(1)} %merge_stats.1.s0), channel_id=1, source_target_pairs={{0,64},{64,128},{128,192},{192,0},{1,65},{65,129},{129,193},{193,1... | collective-permute-start | bytes 15368 | tf_op jit(solution)/shard_map/ppermute | solution.py:29
  35.7 1.7 %collective-permute-done.1.s1 = f32[2,640]{1,0:T(2,128)S(1)} collective-permute-done((f32[2,640]{1,0:T(2,128)S(1)}, f32[2,640]{1,0:T(2,128)S(1)}, u32[]{:S(2)}, u32[]{:S(2)}) %collective-permute-start.1) | collective-permute-done | bytes 5152 | tf_op jit(solution)/shard_map/ppermute | solution.py:29
  37.4 3.1 %collective-permute-done.3.s3 = f32[2,640]{1,0:T(2,128)S(1)} collective-permute-done((f32[2,640]{1,0:T(2,128)S(1)}, f32[2,640]{1,0:T(2,128)S(1)}, u32[]{:S(2)}, u32[]{:S(2)}) %collective-permute-start.3) | collective-permute-done | bytes 5152 | tf_op jit(solution)/shard_map/ppermute | solution.py:29
  40.5 1.4 %grad_logits.1 = (bf16[384,768]{1,0:T(8,128)(2,1)S(1)}, f32[8,128]{1,0:T(8,128)S(1)}) custom-call(s32[4]{0:T(128)S(1)} %pad_add_fusion.pos_ref, f32[384,768]{1,0:T(8,128)S(1)} %student_logits.1.l_ref, bf16[384,768]{1,0:T(8,128)(2,1)S(1)} %get-tuple-element.31.t_ref, s32[3,128]{1,0:T(4,128)S(1)} %bitcast.37, f32[3,128]{1,0:T(4,128)S(1)} %bitcast.39, ...), custom_call_target="tpu_custom_call" | custom-call | flops 2359296 | bytes 2359296 | tf_op jit(solution)/shard_map/grad_logits/pallas_call | solution.py:213
  41.9 0.1 collective-permute-start.7
  42.0 2.3 %hidden_part.2 = (f32[4,8,16,384]{3,2,1,0:T(8,128)S(1)}, f32[4,8,16,384]{3,2,1,0:T(8,128)S(1)}, f32[2,8,16,384]{3,2,1,0:T(8,128)S(1)}, f32[2,8,16,384]{3,2,1,0:T(8,128)S(1)}, f32[4,8,16,384]{3,2,1,0:T(8,128)S(1)}) custom-call(s32[4]{0:T(128)S(1)} %pad_add_fusion.pos_ref, bf16[4,8,4,2,16,768]{5,4,3,2,1,0:T(8,128)(2,1)S(1)} %bitcast.34, ...), custom_call_target="tpu_custom_call" | custom-call | flops 1207959552 | bytes 4718592 | tf_op jit(solution)/shard_map/hidden_part/pallas_call | solution.py:260
  44.4 0.2 multiply_convert_fusion.2
  44.6 0.1 collective-permute-start.4
  44.7 3.2 %collective-permute-start.5 = (f16[4,8,16,384]{3,2,1,0:T(8,128)(2,1)S(1)}, f16[4,8,16,384]{3,2,1,0:T(8,128)(2,1)S(1)}, u32[]{:S(2)}, u32[]{:S(2)}) collective-permute-start(f16[4,8,16,384]{3,2,1,0:T(8,128)(2,1)S(1)} %get-tuple-element.39), channel_id=1, source_target_pairs={{0,6},{2,0},{4,2},{6,4},{1,7},{3,1},{5,3},{7,5},{8,14},{10,8},{12,... | collective-permute-start | bytes 1179656 | tf_op jit(solution)/shard_map/ppermute | solution.py:29
  47.9 2.3 %hidden_part.3 = (f32[4,8,16,384]{3,2,1,0:T(8,128)S(1)}, f32[4,8,16,384]{3,2,1,0:T(8,128)S(1)}, f32[2,8,16,384]{3,2,1,0:T(8,128)S(1)}, f32[2,8,16,384]{3,2,1,0:T(8,128)S(1)}, f32[4,8,16,384]{3,2,1,0:T(8,128)S(1)}) custom-call(s32[4]{0:T(128)S(1)} %pad_add_fusion.pos_ref, bf16[4,8,4,2,16,768]{5,4,3,2,1,0:T(8,128)(2,1)S(1)} %bitcast.35, ...), custom_call_target="tpu_custom_call" | custom-call | flops 1207959552 | bytes 4718592 | tf_op jit(solution)/shard_map/hidden_part/pallas_call | solution.py:260
  50.2 0.1 multiply_convert_fusion
  50.4 0.1 collective-permute-start.14
  50.5 2.0 %collective-permute-start.15 = (f16[4,8,16,384]{3,2,1,0:T(8,128)(2,1)S(1)}, f16[4,8,16,384]{3,2,1,0:T(8,128)(2,1)S(1)}, u32[]{:S(2)}, u32[]{:S(2)}) collective-permute-start(f16[4,8,16,384]{3,2,1,0:T(8,128)(2,1)S(1)} %multiply_convert_fusion), channel_id=1, source_target_pairs={{0,192},{64,0},{128,64},{192,128},{1,193},{65,1},{129,65},{193,129... | collective-permute-start | bytes 1179656 | tf_op jit(solution)/shard_map/ppermute | solution.py:29
  52.5 4.4 %head_grad.1 = bf16[2048,768]{1,0:T(8,128)(2,1)} custom-call(s32[4]{0:T(128)S(1)} %pad_add_fusion.pos_ref, bf16[384,4096]{1,0:T(8,128)(2,1)S(1)} %copy-done, bf16[384,4096]{1,0:T(8,128)(2,1)S(1)} %collective-permute-done.6.oth_ref, bf16[384,768]{1,0:T(8,128)(2,1)S(1)} %get-tuple-element.48.g_ref.g_own_ref, bf16[384,768]{1,0:T(8,128)(2,1)S(1)} %collective-permute-done.7.g_oth_ref), custom_call_target="tpu_custom_call" | custom-call | flops 2415919104 | bytes 7471104 | tf_op jit(solution)/shard_map/head_grad/pallas_call | solution.py:295
  56.9 0.4 collective-permute-done.4
  57.4 0.1 multiply_convert_fusion.6
  57.4 3.0 %collective-permute-start.10 = (f16[2,8,16,384]{3,2,1,0:T(8,128)(2,1)S(1)}, f16[2,8,16,384]{3,2,1,0:T(8,128)(2,1)S(1)}, u32[]{:S(2)}, u32[]{:S(2)}) collective-permute-start(f16[2,8,16,384]{3,2,1,0:T(8,128)(2,1)S(1)} %multiply_convert_fusion.6), channel_id=1, source_target_pairs={{0,6},{2,0},{4,2},{6,4},{1,7},{3,1},{5,3},{7,5},{8,14},{10,8},{12,... | collective-permute-start | bytes 589832 | tf_op jit(solution)/shard_map/ppermute | solution.py:29
  60.5 0.1 multiply_convert_fusion.7
  60.6 0.1 collective-permute-start.9
  60.6 1.4 %collective-permute-done.14 = f16[4,8,16,384]{3,2,1,0:T(8,128)(2,1)S(1)} collective-permute-done((f16[4,8,16,384]{3,2,1,0:T(8,128)(2,1)S(1)}, f16[4,8,16,384]{3,2,1,0:T(8,128)(2,1)S(1)}, u32[]{:S(2)}, u32[]{:S(2)}) %collective-permute-start.14) | collective-permute-done | bytes 393248 | tf_op jit(solution)/shard_map/ppermute | solution.py:29
  62.0 1.3 %collective-permute-done.15 = f16[4,8,16,384]{3,2,1,0:T(8,128)(2,1)S(1)} collective-permute-done((f16[4,8,16,384]{3,2,1,0:T(8,128)(2,1)S(1)}, f16[4,8,16,384]{3,2,1,0:T(8,128)(2,1)S(1)}, u32[]{:S(2)}, u32[]{:S(2)}) %collective-permute-start.15) | collective-permute-done | bytes 393248 | tf_op jit(solution)/shard_map/ppermute | solution.py:29
  63.3 0.1 multiply_convert_fusion.5
  63.4 0.3 collective-permute-start.16
  63.7 0.1 multiply_convert_fusion.4
  63.8 1.9 %collective-permute-start.17 = (f16[2,8,16,384]{3,2,1,0:T(8,128)(2,1)S(1)}, f16[2,8,16,384]{3,2,1,0:T(8,128)(2,1)S(1)}, u32[]{:S(2)}, u32[]{:S(2)}) collective-permute-start(f16[2,8,16,384]{3,2,1,0:T(8,128)(2,1)S(1)} %multiply_convert_fusion.4), channel_id=1, source_target_pairs={{0,192},{64,0},{128,64},{192,128},{1,193},{65,1},{129,65},{193,129... | collective-permute-start | bytes 589832 | tf_op jit(solution)/shard_map/ppermute | solution.py:29
  65.7 2.1 %collective-permute-done.9 = f16[2,8,16,384]{3,2,1,0:T(8,128)(2,1)S(1)} collective-permute-done((f16[2,8,16,384]{3,2,1,0:T(8,128)(2,1)S(1)}, f16[2,8,16,384]{3,2,1,0:T(8,128)(2,1)S(1)}, u32[]{:S(2)}, u32[]{:S(2)}) %collective-permute-start.9) | collective-permute-done | bytes 196640 | tf_op jit(solution)/shard_map/ppermute | solution.py:29
  67.7 0.2 multiply_add_fusion.2
  68.0 0.1 collective-permute-start.11
  68.1 0.8 collective-permute-start.13
  68.9 2.6 %collective-permute-start.12 = (f16[8,16,384]{2,1,0:T(8,128)(2,1)S(1)}, f16[8,16,384]{2,1,0:T(8,128)(2,1)S(1)}, u32[]{:S(2)}, u32[]{:S(2)}) collective-permute-start(f16[8,16,384]{2,1,0:T(8,128)(2,1)S(1)} %fusion.10), channel_id=1, source_target_pairs={{0,64},{64,128},{128,192},{192,0},{1,65},{65,129},{129,193},{193,1... | collective-permute-start | bytes 294920 | tf_op jit(solution)/shard_map/ppermute | solution.py:29
  71.5 3.2 %collective-permute-done.17 = f16[2,8,16,384]{3,2,1,0:T(8,128)(2,1)S(1)} collective-permute-done((f16[2,8,16,384]{3,2,1,0:T(8,128)(2,1)S(1)}, f16[2,8,16,384]{3,2,1,0:T(8,128)(2,1)S(1)}, u32[]{:S(2)}, u32[]{:S(2)}) %collective-permute-start.17) | collective-permute-done | bytes 196640 | tf_op jit(solution)/shard_map/ppermute | solution.py:29
  74.7 0.2 multiply_add_fusion
  74.9 0.2 collective-permute-start.18
  75.2 2.1 %collective-permute-start.19 = (f16[8,16,384]{2,1,0:T(8,128)(2,1)S(1)}, f16[8,16,384]{2,1,0:T(8,128)(2,1)S(1)}, u32[]{:S(2)}, u32[]{:S(2)}) collective-permute-start(f16[8,16,384]{2,1,0:T(8,128)(2,1)S(1)} %fusion.13), channel_id=1, source_target_pairs={{0,2},{2,4},{4,6},{6,0},{1,3},{3,5},{5,7},{7,1},{8,10},{10,12},{12... | collective-permute-start | bytes 294920 | tf_op jit(solution)/shard_map/ppermute | solution.py:29
  77.3 3.8 %collective-permute-done.18 = f16[8,16,384]{2,1,0:T(8,128)(2,1)S(1)} collective-permute-done((f16[8,16,384]{2,1,0:T(8,128)(2,1)S(1)}, f16[8,16,384]{2,1,0:T(8,128)(2,1)S(1)}, u32[]{:S(2)}, u32[]{:S(2)}) %collective-permute-start.18) | collective-permute-done | bytes 98336 | tf_op jit(solution)/shard_map/ppermute | solution.py:29
  81.2 1.0 %collective-permute-done.19 = f16[8,16,384]{2,1,0:T(8,128)(2,1)S(1)} collective-permute-done((f16[8,16,384]{2,1,0:T(8,128)(2,1)S(1)}, f16[8,16,384]{2,1,0:T(8,128)(2,1)S(1)}, u32[]{:S(2)}, u32[]{:S(2)}) %collective-permute-start.19) | collective-permute-done | bytes 98336 | tf_op jit(solution)/shard_map/ppermute | solution.py:29
  82.2 0.7 fusion
  82.9 3.4 %all-to-all-start.1 = ((f16[8,32,384]{2,1,0:T(8,128)(2,1)}), f16[8,32,384]{2,1,0:T(8,128)(2,1)S(1)}, u32[]{:S(2)}, u32[]{:S(2)}) async-start(f16[8,32,384]{2,1,0:T(8,128)(2,1)} %fusion), calls=%async_computation.1 | async-start | bytes 393216 | tf_op jit(solution)/shard_map/all_to_all | solution.py:373
  86.3 0.5 slice.63
  87.5 8.5 %all-to-all-done.1 = f16[8,32,384]{2,1,0:T(8,128)(2,1)S(1)} async-done(((f16[8,32,384]{2,1,0:T(8,128)(2,1)}), f16[8,32,384]{2,1,0:T(8,128)(2,1)S(1)}, u32[]{:S(2)}, u32[]{:S(2)}) %all-to-all-start.1) | async-done | bytes 196640 | tf_op jit(solution)/shard_map/all_to_all | solution.py:373
  96.0 0.7 multiply_reduce_fusion
  (40 shorter events, 0.5 us)
Async XLA Ops:
  0.6 6.2 %collective-permute-start = (bf16[768,384]{1,0:T(8,128)(2,1)}, bf16[768,384]{1,0:T(8,128)(2,1)S(1)}, u32[]{:S(2)}, u32[]{:S(2)}) collective-permute-start(bf16[768,384]{1,0:T(8,128)(2,1)} %own_ref.2), channel_id=1, source_target_pairs={{0,1},{1,0},{2,3},{3,2},{4,5},{5,4},{6,7},{7,6},{8,9},{9,8},{10,11... | collective-permute-start | bytes 1769480 | tf_op jit(solution)/shard_map/ppermute | solution.py:29
  0.7 41.3 %slice-start = ((s8[6291456]{0:T(1024)(128)(4,1)}), s8[4194304]{0:T(1024)(128)(4,1)S(1)}, s32[]{:S(2)}) async-start(s8[6291456]{0:T(1024)(128)(4,1)} %bitcast.32), calls=%async_computation.2 | async-start | bytes 8388608
  0.8 6.0 %copy-start.1 = (bf16[768,384]{1,0:T(8,128)(2,1)S(1)}, bf16[768,384]{1,0:T(8,128)(2,1)}, u32[]{:S(2)}) copy-start(bf16[768,384]{1,0:T(8,128)(2,1)} %own_ref.2) | copy-start | bytes 1769476
  0.8 6.0 %copy-start.2 = (s32[384]{0:T(512)S(1)}, s32[384]{0:T(512)}, u32[]{:S(2)}) copy-start(s32[384]{0:T(512)} %param.9) | copy-start | bytes 4612
  0.8 6.0 %copy-start.3 = (s32[768]{0:T(1024)S(1)}, s32[768]{0:T(1024)}, u32[]{:S(2)}) copy-start(s32[768]{0:T(1024)} %param.10) | copy-start | bytes 9220
  0.8 31.3 %copy-start = (bf16[384,4096]{1,0:T(8,128)(2,1)S(1)}, bf16[384,4096]{1,0:T(8,128)(2,1)}, u32[]{:S(2)}) copy-start(bf16[384,4096]{1,0:T(8,128)(2,1)} %own_ref.3) | copy-start | bytes 9437188
  0.8 39.7 %copy-start.4 = (f32[384]{0:T(512)S(1)}, f32[384]{0:T(512)}, u32[]{:S(2)}) copy-start(f32[384]{0:T(512)} %param.11) | copy-start | bytes 4612
  0.9 41.2 %slice-start.1 = ((s8[6291456]{0:T(1024)(128)(4,1)}), s8[2097152]{0:T(1024)(128)(4,1)S(1)}, s32[]{:S(2)}) async-start(s8[6291456]{0:T(1024)(128)(4,1)} %bitcast.32), calls=%async_computation.3 | async-start | bytes 4194304
  32.1 20.4 %collective-permute-start.6 = (bf16[384,4096]{1,0:T(8,128)(2,1)S(1)}, bf16[384,4096]{1,0:T(8,128)(2,1)S(1)}, u32[]{:S(2)}, u32[]{:S(2)}) collective-permute-start(bf16[384,4096]{1,0:T(8,128)(2,1)S(1)} %copy-done), channel_id=1, source_target_pairs={{0,1},{1,0},{2,3},{3,2},{4,5},{5,4},{6,7},{7,6},{8,9},{9,8},{10,11... | collective-permute-start | bytes 9437192 | tf_op jit(solution)/shard_map/ppermute | solution.py:29
  32.2 5.2 %collective-permute-start.1 = (f32[2,640]{1,0:T(2,128)S(1)}, f32[2,640]{1,0:T(2,128)S(1)}, u32[]{:S(2)}, u32[]{:S(2)}) collective-permute-start(f32[2,640]{1,0:T(2,128)S(1)} %merge_stats.1.s0), channel_id=1, source_target_pairs={{0,128},{64,192},{128,0},{192,64},{1,129},{65,193},{129,1},{193,65... | collective-permute-start | bytes 15368 | tf_op jit(solution)/shard_map/ppermute | solution.py:29
  33.5 3.9 %collective-permute-start.2 = (f32[2,640]{1,0:T(2,128)S(1)}, f32[2,640]{1,0:T(2,128)S(1)}, u32[]{:S(2)}, u32[]{:S(2)}) collective-permute-start(f32[2,640]{1,0:T(2,128)S(1)} %merge_stats.1.s0), channel_id=1, source_target_pairs={{0,64},{64,128},{128,192},{192,0},{1,65},{65,129},{129,193},{193,1... | collective-permute-start | bytes 15368 | tf_op jit(solution)/shard_map/ppermute | solution.py:29
  35.7 4.8 %collective-permute-start.3 = (f32[2,640]{1,0:T(2,128)S(1)}, f32[2,640]{1,0:T(2,128)S(1)}, u32[]{:S(2)}, u32[]{:S(2)}) collective-permute-start(f32[2,640]{1,0:T(2,128)S(1)} %merge_stats.1.s0), channel_id=1, source_target_pairs={{0,192},{64,0},{128,64},{192,128},{1,193},{65,1},{129,65},{193,129... | collective-permute-start | bytes 15368 | tf_op jit(solution)/shard_map/ppermute | solution.py:29
  41.9 8.6 %collective-permute-start.7 = (bf16[384,768]{1,0:T(8,128)(2,1)S(1)}, bf16[384,768]{1,0:T(8,128)(2,1)S(1)}, u32[]{:S(2)}, u32[]{:S(2)}) collective-permute-start(bf16[384,768]{1,0:T(8,128)(2,1)S(1)} %get-tuple-element.48.g_ref.g_own_ref), channel_id=1, source_target_pairs={{0,1},{1,0},{2,3},{3,2},{4,5},{5,4},{6,7},{7,6},{8,9},{9,8},{10,11... | collective-permute-start | bytes 1769480 | tf_op jit(solution)/shard_map/ppermute | solution.py:29
  44.6 12.8 %collective-permute-start.4 = (f16[4,8,16,384]{3,2,1,0:T(8,128)(2,1)S(1)}, f16[4,8,16,384]{3,2,1,0:T(8,128)(2,1)S(1)}, u32[]{:S(2)}, u32[]{:S(2)}) collective-permute-start(f16[4,8,16,384]{3,2,1,0:T(8,128)(2,1)S(1)} %get-tuple-element.38), channel_id=1, source_target_pairs={{0,2},{2,4},{4,6},{6,0},{1,3},{3,5},{5,7},{7,1},{8,10},{10,12},{12... | collective-permute-start | bytes 1179656 | tf_op jit(solution)/shard_map/ppermute | solution.py:29
  44.7 12.7 %collective-permute-start.5 = (f16[4,8,16,384]{3,2,1,0:T(8,128)(2,1)S(1)}, f16[4,8,16,384]{3,2,1,0:T(8,128)(2,1)S(1)}, u32[]{:S(2)}, u32[]{:S(2)}) collective-permute-start(f16[4,8,16,384]{3,2,1,0:T(8,128)(2,1)S(1)} %get-tuple-element.39), channel_id=1, source_target_pairs={{0,6},{2,0},{4,2},{6,4},{1,7},{3,1},{5,3},{7,5},{8,14},{10,8},{12,... | collective-permute-start | bytes 1179656 | tf_op jit(solution)/shard_map/ppermute | solution.py:29
  47.9 2.5 %collective-permute-start.8 = (f32[8,128]{1,0:T(8,128)S(1)}, f32[8,128]{1,0:T(8,128)S(1)}, u32[]{:S(2)}, u32[]{:S(2)}) collective-permute-start(f32[8,128]{1,0:T(8,128)S(1)} %get-tuple-element.41), channel_id=1, source_target_pairs={{0,1},{1,0},{2,3},{3,2},{4,5},{5,4},{6,7},{7,6},{8,9},{9,8},{10,11... | collective-permute-start | bytes 12296 | tf_op jit(solution)/shard_map/ppermute | solution.py:29
  50.4 11.6 %collective-permute-start.14 = (f16[4,8,16,384]{3,2,1,0:T(8,128)(2,1)S(1)}, f16[4,8,16,384]{3,2,1,0:T(8,128)(2,1)S(1)}, u32[]{:S(2)}, u32[]{:S(2)}) collective-permute-start(f16[4,8,16,384]{3,2,1,0:T(8,128)(2,1)S(1)} %multiply_convert_fusion.1), channel_id=1, source_target_pairs={{0,64},{64,128},{128,192},{192,0},{1,65},{65,129},{129,193},{193,1... | collective-permute-start | bytes 1179656 | tf_op jit(solution)/shard_map/ppermute | solution.py:29
  50.5 12.8 %collective-permute-start.15 = (f16[4,8,16,384]{3,2,1,0:T(8,128)(2,1)S(1)}, f16[4,8,16,384]{3,2,1,0:T(8,128)(2,1)S(1)}, u32[]{:S(2)}, u32[]{:S(2)}) collective-permute-start(f16[4,8,16,384]{3,2,1,0:T(8,128)(2,1)S(1)} %multiply_convert_fusion), channel_id=1, source_target_pairs={{0,192},{64,0},{128,64},{192,128},{1,193},{65,1},{129,65},{193,129... | collective-permute-start | bytes 1179656 | tf_op jit(solution)/shard_map/ppermute | solution.py:29
  57.4 8.2 %collective-permute-start.10 = (f16[2,8,16,384]{3,2,1,0:T(8,128)(2,1)S(1)}, f16[2,8,16,384]{3,2,1,0:T(8,128)(2,1)S(1)}, u32[]{:S(2)}, u32[]{:S(2)}) collective-permute-start(f16[2,8,16,384]{3,2,1,0:T(8,128)(2,1)S(1)} %multiply_convert_fusion.6), channel_id=1, source_target_pairs={{0,6},{2,0},{4,2},{6,4},{1,7},{3,1},{5,3},{7,5},{8,14},{10,8},{12,... | collective-permute-start | bytes 589832 | tf_op jit(solution)/shard_map/ppermute | solution.py:29
  60.6 7.2 %collective-permute-start.9 = (f16[2,8,16,384]{3,2,1,0:T(8,128)(2,1)S(1)}, f16[2,8,16,384]{3,2,1,0:T(8,128)(2,1)S(1)}, u32[]{:S(2)}, u32[]{:S(2)}) collective-permute-start(f16[2,8,16,384]{3,2,1,0:T(8,128)(2,1)S(1)} %multiply_convert_fusion.7), channel_id=1, source_target_pairs={{0,2},{2,4},{4,6},{6,0},{1,3},{3,5},{5,7},{7,1},{8,10},{10,12},{12... | collective-permute-start | bytes 589832 | tf_op jit(solution)/shard_map/ppermute | solution.py:29
  63.4 8.1 %collective-permute-start.16 = (f16[2,8,16,384]{3,2,1,0:T(8,128)(2,1)S(1)}, f16[2,8,16,384]{3,2,1,0:T(8,128)(2,1)S(1)}, u32[]{:S(2)}, u32[]{:S(2)}) collective-permute-start(f16[2,8,16,384]{3,2,1,0:T(8,128)(2,1)S(1)} %multiply_convert_fusion.5), channel_id=1, source_target_pairs={{0,64},{64,128},{128,192},{192,0},{1,65},{65,129},{129,193},{193,1... | collective-permute-start | bytes 589832 | tf_op jit(solution)/shard_map/ppermute | solution.py:29
  63.8 10.9 %collective-permute-start.17 = (f16[2,8,16,384]{3,2,1,0:T(8,128)(2,1)S(1)}, f16[2,8,16,384]{3,2,1,0:T(8,128)(2,1)S(1)}, u32[]{:S(2)}, u32[]{:S(2)}) collective-permute-start(f16[2,8,16,384]{3,2,1,0:T(8,128)(2,1)S(1)} %multiply_convert_fusion.4), channel_id=1, source_target_pairs={{0,192},{64,0},{128,64},{192,128},{1,193},{65,1},{129,65},{193,129... | collective-permute-start | bytes 589832 | tf_op jit(solution)/shard_map/ppermute | solution.py:29
  68.0 7.2 %collective-permute-start.11 = (f16[8,16,384]{2,1,0:T(8,128)(2,1)S(1)}, f16[8,16,384]{2,1,0:T(8,128)(2,1)S(1)}, u32[]{:S(2)}, u32[]{:S(2)}) collective-permute-start(f16[8,16,384]{2,1,0:T(8,128)(2,1)S(1)} %get-tuple-element.63), channel_id=1, source_target_pairs={{0,128},{64,192},{128,0},{192,64},{1,129},{65,193},{129,1},{193,65... | collective-permute-start | bytes 294920 | tf_op jit(solution)/shard_map/ppermute | solution.py:29
  68.1 9.2 %collective-permute-start.13 = (f16[8,16,384]{2,1,0:T(8,128)(2,1)S(1)}, f16[8,16,384]{2,1,0:T(8,128)(2,1)S(1)}, u32[]{:S(2)}, u32[]{:S(2)}) collective-permute-start(f16[8,16,384]{2,1,0:T(8,128)(2,1)S(1)} %get-tuple-element.64), channel_id=1, source_target_pairs={{0,192},{64,0},{128,64},{192,128},{1,193},{65,1},{129,65},{193,129... | collective-permute-start | bytes 294920 | tf_op jit(solution)/shard_map/ppermute | solution.py:29
  68.9 8.3 %collective-permute-start.12 = (f16[8,16,384]{2,1,0:T(8,128)(2,1)S(1)}, f16[8,16,384]{2,1,0:T(8,128)(2,1)S(1)}, u32[]{:S(2)}, u32[]{:S(2)}) collective-permute-start(f16[8,16,384]{2,1,0:T(8,128)(2,1)S(1)} %fusion.10), channel_id=1, source_target_pairs={{0,64},{64,128},{128,192},{192,0},{1,65},{65,129},{129,193},{193,1... | collective-permute-start | bytes 294920 | tf_op jit(solution)/shard_map/ppermute | solution.py:29
  74.9 6.2 %collective-permute-start.18 = (f16[8,16,384]{2,1,0:T(8,128)(2,1)S(1)}, f16[8,16,384]{2,1,0:T(8,128)(2,1)S(1)}, u32[]{:S(2)}, u32[]{:S(2)}) collective-permute-start(f16[8,16,384]{2,1,0:T(8,128)(2,1)S(1)} %get-tuple-element.65), channel_id=1, source_target_pairs={{0,4},{2,6},{4,0},{6,2},{1,5},{3,7},{5,1},{7,3},{8,12},{10,14},{12... | collective-permute-start | bytes 294920 | tf_op jit(solution)/shard_map/ppermute | solution.py:29
  75.1 6.0 %collective-permute-start.20 = (f16[8,16,384]{2,1,0:T(8,128)(2,1)S(1)}, f16[8,16,384]{2,1,0:T(8,128)(2,1)S(1)}, u32[]{:S(2)}, u32[]{:S(2)}) collective-permute-start(f16[8,16,384]{2,1,0:T(8,128)(2,1)S(1)} %get-tuple-element.66), channel_id=1, source_target_pairs={{0,6},{2,0},{4,2},{6,4},{1,7},{3,1},{5,3},{7,5},{8,14},{10,8},{12,... | collective-permute-start | bytes 294920 | tf_op jit(solution)/shard_map/ppermute | solution.py:29
  75.2 7.0 %collective-permute-start.19 = (f16[8,16,384]{2,1,0:T(8,128)(2,1)S(1)}, f16[8,16,384]{2,1,0:T(8,128)(2,1)S(1)}, u32[]{:S(2)}, u32[]{:S(2)}) collective-permute-start(f16[8,16,384]{2,1,0:T(8,128)(2,1)S(1)} %fusion.13), channel_id=1, source_target_pairs={{0,2},{2,4},{4,6},{6,0},{1,3},{3,5},{5,7},{7,1},{8,10},{10,12},{12... | collective-permute-start | bytes 294920 | tf_op jit(solution)/shard_map/ppermute | solution.py:29
  82.9 13.1 %all-to-all-start.1 = ((f16[8,32,384]{2,1,0:T(8,128)(2,1)}), f16[8,32,384]{2,1,0:T(8,128)(2,1)S(1)}, u32[]{:S(2)}, u32[]{:S(2)}) async-start(f16[8,32,384]{2,1,0:T(8,128)(2,1)} %fusion), calls=%async_computation.1 | async-start | bytes 393216 | tf_op jit(solution)/shard_map/all_to_all | solution.py:373

commit v5 on v4

--- a/solution.py
+++ b/solution.py
@@ -10,11 +10,13 @@
 CE_WEIGHT = 0.5
 SEND_SCALE = 64.0
 SPARE = 256
+LOSS_ROWS = 16
 F32 = jnp.float32
 BF16 = jnp.bfloat16
 F16 = jnp.float16
 
 
+LIGHT = pl.CostEstimate(flops=1, bytes_accessed=1, transcendentals=0)
 WHOLE = pl.BlockSpec(memory_space=pltpu.VMEM)
 
 
@@ -190,7 +192,7 @@
     )(pos, logits, own, oth, assign, ids)
 
 
-def grad_kernel(pos_ref, l_ref, t_ref, ids_ref, scale_ref, s0, s1, s2, s3, g_ref, loss_ref):
+def grad_kernel(pos_ref, l_ref, t_ref, ids_ref, scale_ref, s0, s1, s2, s3, g_ref):
     rows, cols = l_ref.shape
     parts = (s0, s1, s2, s3)
     first, second = (
@@ -199,25 +201,27 @@
     norm_s, norm_t, cross, picked = merge(first, second)
     terms = cross - norm_t + (1.0 + CE_WEIGHT) * norm_s
     terms = jnp.sum(terms, axis=1, keepdims=True) - CE_WEIGHT * picked
-    loss_ref[...] = jnp.broadcast_to(terms, loss_ref.shape)
+    high = terms.astype(BF16).astype(F32)
+    middle = (terms - high).astype(BF16).astype(F32)
+    low = terms - high - middle
+    at = lax.broadcasted_iota(jnp.int32, (LOSS_ROWS, cols), 0)
+    tail = jnp.where(at == 0, high, jnp.where(at == 1, middle, jnp.where(at == 2, low, 0.0)))
+    g_ref[rows:, :] = tail.astype(BF16)
     norm_s, norm_t, ids, scale = columns_of(norm_s, norm_t, in_row(ids_ref), in_row(scale_ref))
     columns = pos_ref[1] + lax.broadcasted_iota(jnp.int32, (rows, cols), 1)
     hot = jnp.where(columns.astype(F32) == ids, CE_WEIGHT, 0.0)
     prob_s = jnp.exp(l_ref[...] - norm_s)
     prob_t = jnp.exp(t_ref[...].astype(F32) - norm_t)
-    g_ref[...] = (scale * ((1.0 + CE_WEIGHT) * prob_s - prob_t - hot)).astype(BF16)
+    g_ref[:rows, :] = (scale * ((1.0 + CE_WEIGHT) * prob_s - prob_t - hot)).astype(BF16)
 
 
 def grad_logits(pos, logits, teacher, ids, scale, parts):
     rows, cols = logits.shape
     return pl.pallas_call(
         grad_kernel,
-        out_shape=(
-            jax.ShapeDtypeStruct((rows, cols), BF16),
-            jax.ShapeDtypeStruct((8, 128), F32),
-        ),
+        out_shape=jax.ShapeDtypeStruct((rows + LOSS_ROWS, cols), BF16),
         in_specs=[pl.BlockSpec(memory_space=pltpu.SMEM)] + [WHOLE] * 8,
-        out_specs=(WHOLE, WHOLE),
+        out_specs=WHOLE,
         compiler_params=params(16),
         cost_estimate=pl.CostEstimate(
             flops=8 * rows * cols,
@@ -228,53 +232,49 @@
     )(pos, logits, teacher, ids, scale, *parts)
 
 
-def hidden_kernel(first_x, half, pos_ref, w_ref, g_ref, up, down, keep1, keep3, own):
+SENT = (((2, 0), (2, 1), (1, 2), (1, 3)), ((2, 2), (2, 3), (3, 0), (3, 1)))
+KEPT = (((1, 0), (1, 1)), ((3, 2), (3, 3)), ((0, 0), (0, 1), (0, 2), (0, 3)))
+
+
+def hidden_kernel(groups, pos_ref, w_ref, g_ref, *outs):
     ny, nz, nx, _, sub, cols = w_ref.shape
     y, x = pos_ref[2], pos_ref[3]
-    g = g_ref[...]
-    slots = {
-        1: (keep1.at[0], keep1.at[1], up.at[2], up.at[3]),
-        2: (up.at[0], up.at[1], down.at[0], down.at[1]),
-        3: (down.at[2], down.at[3], keep3.at[0], keep3.at[1]),
-        0: tuple(own.at[near] for near in range(4)),
-    }
-    for far, places in slots.items():
-
-        def block(near):
-            dx, dy = (far, near) if first_x else (near, far)
-            w = w_ref[lax.rem(y + dy, ny), :, lax.rem(x + dx, nx), half]
-            return w.reshape(nz * sub, cols)
-
-        w = jnp.concatenate([block(near) for near in range(4)], axis=0)
-        part = lax.dot_general(
-            w, g, (((1,), (1,)), ((), ())), preferred_element_type=F32
-        )
-        for near, place in enumerate(places):
-            place[...] = part[near * nz * sub : (near + 1) * nz * sub].reshape(place.shape)
-
-
-def hidden_part(pos, head6, g, first_x, half):
-    ny, nz, nx, _, sub, cols = head6.shape
-    rows = g.shape[0]
-    shape = lambda n: jax.ShapeDtypeStruct((n, nz, sub, rows), F32)
-    return pl.pallas_call(
-        functools.partial(hidden_kernel, first_x, half),
-        out_shape=[shape(4), shape(4), shape(2), shape(2), shape(4)],
+    g = g_ref[: outs[0].shape[-1], :]
+
+    def block(part, far, near):
+        dy, dx = (near, far) if part == 0 else (far, near)
+        w = w_ref[lax.rem(y + dy, ny), :, lax.rem(x + dx, nx), part]
+        return w.reshape(nz * sub, cols)
+
+    for at, out in enumerate(outs):
+        part, names = divmod(at, len(groups))
+        names = groups[names]
+        w = jnp.concatenate([block(part, *name) for name in names], axis=0)
+        product = lax.dot_general(w, g, (((1,), (1,)), ((), ())), preferred_element_type=F32)
+        out[...] = product.reshape(out.shape)
+
+
+def hidden_part(pos, head6, g, groups):
+    _, nz, _, _, sub, cols = head6.shape
+    rows = g.shape[0] - LOSS_ROWS
+    out_shape = [
+        jax.ShapeDtypeStruct((len(names), nz, sub, rows), F32) for _ in range(2) for names in groups
+    ]
+    return pl.pallas_call(
+        functools.partial(hidden_kernel, groups),
+        out_shape=out_shape,
         in_specs=[pl.BlockSpec(memory_space=pltpu.SMEM), WHOLE, WHOLE],
-        out_specs=[WHOLE] * 5,
+        out_specs=[WHOLE] * len(out_shape),
         compiler_params=params(16),
-        cost_estimate=pl.CostEstimate(
-            flops=rows * head6.size,
-            bytes_accessed=head6.size + 2 * rows * ny * nz * nx * sub,
-            transcendentals=0,
-        ),
+        cost_estimate=LIGHT,
         name="hidden_part",
     )(pos, head6, g)
 
 
-def head_kernel(pos_ref, own_ref, oth_ref, g_own_ref, g_oth_ref, out_ref, buf, sem):
+def head_kernel(pos_ref, own_ref, oth_ref, g_own_ref, g_oth_ref, out_ref, loss_ref, buf, sem):
     steps, block, _ = buf.shape
-    g = jnp.concatenate([g_own_ref[...], g_oth_ref[...]], axis=0)
+    rows = own_ref.shape[0]
+    g = jnp.concatenate([g_own_ref[:rows, :], g_oth_ref[:rows, :]], axis=0)
     copies = []
     for i in range(steps):
         at = pl.ds(pl.multiple_of(pos_ref[0] * (steps * block) + i * block, block), block)
@@ -284,6 +284,12 @@
         copy = pltpu.make_async_copy(buf.at[i], out_ref.at[pl.ds(i * block, block)], sem.at[i])
         copy.start()
         copies.append(copy)
+
+    def loss(ref):
+        parts = ref[rows:, :128].astype(F32)
+        return (parts[0:1] + parts[1:2]) + parts[2:3]
+
+    loss_ref[...] = (loss(g_own_ref) + loss(g_oth_ref)) * (1.0 / (2 * rows))
     for copy in copies:
         copy.wait()
 
@@ -294,19 +300,18 @@
     width = depth // 2
     return pl.pallas_call(
         head_kernel,
-        out_shape=jax.ShapeDtypeStruct((width, cols), BF16),
+        out_shape=(
+            jax.ShapeDtypeStruct((width, cols), BF16),
+            jax.ShapeDtypeStruct((1, 128), F32),
+        ),
         in_specs=[pl.BlockSpec(memory_space=pltpu.SMEM)] + [WHOLE] * 4,
-        out_specs=pl.BlockSpec(memory_space=pl.ANY),
+        out_specs=(pl.BlockSpec(memory_space=pl.ANY), WHOLE),
         scratch_shapes=[
             pltpu.VMEM((steps, width // steps, cols), BF16),
             pltpu.SemaphoreType.DMA((steps,)),
         ],
         compiler_params=params(20),
-        cost_estimate=pl.CostEstimate(
-            flops=4 * rows * width * cols,
-            bytes_accessed=4 * rows * width + 4 * rows * cols + 2 * width * cols,
-            transcendentals=0,
-        ),
+        cost_estimate=LIGHT,
         name="head_grad",
     )(pos, hidden, hidden_oth, g, g_oth)
 
@@ -330,9 +335,8 @@
     stats = merge_stats(lax.all_to_all(stats, ("z", "x"), 0, 0, tiled=True))
     parts = [stats] + [shift(stats, "y", d) for d in (2, 1, 3)]
     hidden_oth = shift(lax.optimization_barrier((hidden, stats))[0], "c", 1)
-    g, loss_part = grad_logits(pos, logits, teacher_rows, ids, scale, parts)
-    g_oth = shift(g, "c", 1)
-
+    g = grad_logits(pos, logits, teacher_rows, ids, scale, parts)
+    g, hidden_oth = lax.optimization_barrier((g, hidden_oth))
     sub = depth // (ny * nz * nx) // 2
     head6 = head.reshape(ny, nz, nx, 2, sub, cols)
 
@@ -342,24 +346,25 @@
     def taken(value):
         return value.astype(F32) * (1.0 / SEND_SCALE)
 
-    def first_step(g, half, axis):
-        up, down, c1, c3, c0 = hidden_part(pos, head6, g, axis == "x", half)
-        up, down = ((v * SEND_SCALE).astype(F16) for v in (up, down))
-        g, up, down = lax.optimization_barrier((g, up, down))
-        return g, (c0, c1, c3), (shift(up, axis, 1), shift(down, axis, -1))
+    sent = [(v * SEND_SCALE).astype(F16) for v in hidden_part(pos, head6, g, SENT)]
+    *sent, g = lax.optimization_barrier((*sent, g))
+    up_a, down_a, up_b, down_b = sent
+    got_a = shift(up_a, "x", 1), shift(down_a, "x", -1)
+    got_b = shift(up_b, "y", 1), shift(down_b, "y", -1)
+    g_oth = shift(g, "c", 1)
+    kept = hidden_part(pos, head6, g, KEPT)
+    kept_a, kept_b = kept[:3], kept[3:]
+    head_out, loss = head_grad(pos, hidden, hidden_oth, g, g_oth)
+    loss = loss[0, :1]
+    got_a, loss, _ = lax.optimization_barrier((got_a, loss, head_out))
+    got_b, head_out = lax.optimization_barrier((got_b, head_out))
 
     def second_step(kept, got, axis):
-        (c0, c1, c3), (up, down) = kept, got
+        (c1, c3, c0), (up, down) = kept, got
         up2 = send(c1 + taken(up[:2]), axis, 1)
         down2 = send(c3 + taken(down[:2]), axis, -1)
         return c0[:2] + taken(down[2:]) + taken(up2), c0[2:] + taken(up[2:]) + taken(down2)
 
-    g_then, kept_a, got_a = first_step(g, 0, "x")
-    _, kept_b, got_b = first_step(g_then, 1, "y")
-    head_out = head_grad(pos, hidden, hidden_oth, g, g_oth)
-    loss_all = loss_part + shift(loss_part, "c", 1)
-    got_a, _, loss_all = lax.optimization_barrier((got_a, head_out, loss_all))
-    got_b, head_out = lax.optimization_barrier((got_b, head_out))
     low_a, high_a = second_step(kept_a, got_a, "x")
     low_b, high_b = second_step(kept_b, got_b, "y")
 
@@ -367,13 +372,10 @@
         far = [send(f, axis, d) for d, f in ((2, high[0]), (1, low[1]), (3, high[1]))]
         return low[0] + sum(taken(f) for f in far)
 
-    both = jnp.concatenate(
-        [second_level(low_a, high_a, "y"), second_level(low_b, high_b, "x")], axis=1
-    )
-    both = lax.all_to_all((both * SEND_SCALE).astype(F16), "z", 0, 0, tiled=True)
+    both = (second_level(low_a, high_a, "y"), second_level(low_b, high_b, "x"))
+    both = (jnp.concatenate(both, axis=1) * SEND_SCALE).astype(F16)
+    both = lax.all_to_all(both, "z", 0, 0, tiled=True)
     hidden_grad = jnp.sum(taken(both), axis=0).T.astype(BF16)
-
-    loss = loss_all[0, :1] / (2 * rows)
     return loss, hidden_grad, head_out
 
 

time: 98 us -> 95.6 us (0.976)
  the two profiles are of different devices: /device:TPU:24 before, /device:TPU:32 now
where the time goes in v5:
time: 95.6 us; the launch traced here: 95.5 us
  blocking collectives  33.6 us (35%)
  starting transfers between devices  25.6 us (27%)
  Pallas kernels  19.3 us (20%)
  waiting for transfers between devices  13.8 us (14%)
  other arithmetic  2.05 us (2%)
    ppermute x20, starting transfers between devices, shift(): return lax.ppermute(a, axis, [(i, (i + by) % n) for i in range(n)])  25.6 us
    all_to_all x1, blocking collectives, body(): stats = merge_stats(lax.all_to_all(stats, ('z', 'x'), 0, 0, tiled=True))  21.9 us
    ppermute x20, waiting for transfers between devices, shift(): return lax.ppermute(a, axis, [(i, (i + by) % n) for i in range(n)])  13.8 us
    all_to_all x1, blocking collectives, body(): both = lax.all_to_all(both, 'z', 0, 0, tiled=True)  11.8 us
    pallas_call x1, Pallas kernels, student_logits(): pl.pallas_call(functools.partial(logits_kernel, steps), out_shape=jax.Sha...  5.91 us
    pallas_call x1, Pallas kernels, head_grad(): pl.pallas_call(head_kernel, out_shape=(jax.ShapeDtypeStruct((width, cols)...  4.91 us
    pallas_call x2, Pallas kernels, hidden_part(): pl.pallas_call(functools.partial(hidden_kernel, groups), out_shape=out_sh...  4.67 us
    pallas_call x1, Pallas kernels, local_stats(): pl.pallas_call(stats_kernel, out_shape=(jax.ShapeDtypeStruct((2, rows + S...  2.26 us
  transfers between devices with their start and end apart: 20, of which 8 were waited for; matrix products, arithmetic and copies ran while one was open for 1% of the time, Pallas kernels for 15%

profile of v5, /device:TPU:32, one launch (start us, length us, event | category | flops | bytes accessed | tf_op | source)
XLA Modules:
  0.0 95.5 jit_solution(5711913085992241295)
XLA Ops:
  0.6 0.1 collective-permute-start
  0.8 0.1 pad_add_fusion.pos_ref
  0.9 5.9 %student_logits.1.l_ref = f32[384,768]{1,0:T(8,128)S(1)} custom-call(bf16[384,4096]{1,0:T(8,128)(2,1)} %own_ref.3, bf16[4096,768]{1,0:T(8,128)(2,1)} %w_ref.1), custom_call_target="tpu_custom_call" | custom-call | flops 2415919104 | bytes 10616832 | tf_op jit(solution)/shard_map/student_logits/pallas_call | solution.py:62
  6.8 2.3 %local_stats.1 = (f32[2,640]{1,0:T(2,128)S(1)}, bf16[384,768]{1,0:T(8,128)(2,1)S(1)}) custom-call(s32[4]{0:T(128)S(1)} %pad_add_fusion.pos_ref, f32[384,768]{1,0:T(8,128)S(1)} %student_logits.1.l_ref, bf16[768,384]{1,0:T(8,128)(2,1)S(1)} %copy-done.1, bf16[768,384]{1,0:T(8,128)(2,1)S(1)} %collective-permute-done.oth_ref, s32[6,128]{1,0:T(8,128)S(1)} %bitcast.39, ...), custom_call_target="tpu_custom_call" | custom-call | flops 452984832 | bytes 2949120 | tf_op jit(solution)/shard_map/local_stats/pallas_call | solution.py:177
  9.1 0.1 broadcast_in_dim.2
  9.1 21.9 %all_to_all.10.in_ref = f32[32,2,640]{2,1,0:T(2,128)S(1)} all-to-all(f32[32,2,640]{2,1,0:T(2,128)S(1)} %broadcast_in_dim.2), channel_id=1, replica_groups=mesh['y'=4,'z'=8,'x'=4,'c'=2] {'z','x'}, dimensions={0} | all-to-all | bytes 327680 | tf_op jit(solution)/shard_map/all_to_all | solution.py:335
  31.0 0.2 merge_stats.1.s0
  31.2 0.0 collective-permute-start.4
  31.2 3.1 %collective-permute-start.3 = (f32[2,640]{1,0:T(2,128)S(1)}, f32[2,640]{1,0:T(2,128)S(1)}, u32[]{:S(2)}, u32[]{:S(2)}) collective-permute-start(f32[2,640]{1,0:T(2,128)S(1)} %merge_stats.1.s0), channel_id=1, source_target_pairs={{0,192},{64,0},{128,64},{192,128},{1,193},{65,1},{129,65},{193,129... | collective-permute-start | bytes 15368 | tf_op jit(solution)/shard_map/ppermute | solution.py:31
  34.3 2.2 %collective-permute-start.1 = (f32[2,640]{1,0:T(2,128)S(1)}, f32[2,640]{1,0:T(2,128)S(1)}, u32[]{:S(2)}, u32[]{:S(2)}) collective-permute-start(f32[2,640]{1,0:T(2,128)S(1)} %merge_stats.1.s0), channel_id=1, source_target_pairs={{0,128},{64,192},{128,0},{192,64},{1,129},{65,193},{129,1},{193,65... | collective-permute-start | bytes 15368 | tf_op jit(solution)/shard_map/ppermute | solution.py:31
  36.5 2.6 %collective-permute-done.2.s2 = f32[2,640]{1,0:T(2,128)S(1)} collective-permute-done((f32[2,640]{1,0:T(2,128)S(1)}, f32[2,640]{1,0:T(2,128)S(1)}, u32[]{:S(2)}, u32[]{:S(2)}) %collective-permute-start.2) | collective-permute-done | bytes 5152 | tf_op jit(solution)/shard_map/ppermute | solution.py:31
  39.1 0.3 collective-permute-done.1.s1
  39.4 1.4 %grad_logits.1.g_ref.g_own_ref = bf16[400,768]{1,0:T(8,128)(2,1)S(1)} custom-call(s32[4]{0:T(128)S(1)} %pad_add_fusion.pos_ref, f32[384,768]{1,0:T(8,128)S(1)} %student_logits.1.l_ref, bf16[384,768]{1,0:T(8,128)(2,1)S(1)} %get-tuple-element.33.t_ref, s32[3,128]{1,0:T(4,128)S(1)} %bitcast.38, f32[3,128]{1,0:T(4,128)S(1)} %bitcast.40, ...), custom_call_target="tpu_custom_call" | custom-call | flops 2359296 | bytes 2359296 | tf_op jit(solution)/shard_map/grad_logits/pallas_call | solution.py:220
  40.9 2.3 %hidden_part.2 = (f32[4,8,16,384]{3,2,1,0:T(8,128)S(1)}, f32[4,8,16,384]{3,2,1,0:T(8,128)S(1)}, f32[4,8,16,384]{3,2,1,0:T(8,128)S(1)}, f32[4,8,16,384]{3,2,1,0:T(8,128)S(1)}) custom-call(s32[4]{0:T(128)S(1)} %pad_add_fusion.pos_ref, bf16[4,8,4,2,16,768]{5,4,3,2,1,0:T(8,128)(2,1)S(1)} %bitcast.35, bf16[400,768]{1,0:T(8,128)(2,1)S(1)} %grad_logits.1.g_ref.g_own_ref), custom_call_target="tpu_custom_call" | custom-call | flops 1 | bytes 1 | tf_op jit(solution)/shard_map/hidden_part/pallas_call | solution.py:263
  43.2 0.2 multiply_convert_fusion.2
  43.4 0.2 multiply_convert_fusion
  43.6 0.1 collective-permute-start.7
  43.7 0.6 collective-permute-start.5
  44.3 2.7 %collective-permute-start.6 = (f16[4,8,16,384]{3,2,1,0:T(8,128)(2,1)S(1)}, f16[4,8,16,384]{3,2,1,0:T(8,128)(2,1)S(1)}, u32[]{:S(2)}, u32[]{:S(2)}) collective-permute-start(f16[4,8,16,384]{3,2,1,0:T(8,128)(2,1)S(1)} %get-tuple-element.44), channel_id=1, source_target_pairs={{0,6},{2,0},{4,2},{6,4},{1,7},{3,1},{5,3},{7,5},{8,14},{10,8},{12,... | collective-permute-start | bytes 1179656 | tf_op jit(solution)/shard_map/ppermute | solution.py:31
  47.0 0.6 collective-permute-start.13
  47.6 2.6 %collective-permute-start.14 = (f16[4,8,16,384]{3,2,1,0:T(8,128)(2,1)S(1)}, f16[4,8,16,384]{3,2,1,0:T(8,128)(2,1)S(1)}, u32[]{:S(2)}, u32[]{:S(2)}) collective-permute-start(f16[4,8,16,384]{3,2,1,0:T(8,128)(2,1)S(1)} %get-tuple-element.57), channel_id=1, source_target_pairs={{0,192},{64,0},{128,64},{192,128},{1,193},{65,1},{129,65},{193,129... | collective-permute-start | bytes 1179656 | tf_op jit(solution)/shard_map/ppermute | solution.py:31
  50.3 2.3 %hidden_part.3 = (f32[2,8,16,384]{3,2,1,0:T(8,128)S(1)}, f32[2,8,16,384]{3,2,1,0:T(8,128)S(1)}, f32[4,8,16,384]{3,2,1,0:T(8,128)S(1)}, f32[2,8,16,384]{3,2,1,0:T...) custom-call(s32[4]{0:T(128)S(1)} %pad_add_fusion.pos_ref, ...), custom_call_target="tpu_custom_call" | custom-call | flops 1 | bytes 1 | tf_op jit(solution)/shard_map/hidden_part/pallas_call | solution.py:263
  52.6 4.9 %head_grad.1 = (bf16[2048,768]{1,0:T(8,128)(2,1)}, f32[1,128]{1,0:T(1,128)}) custom-call(s32[4]{0:T(128)S(1)} %pad_add_fusion.pos_ref, bf16[384,4096]{1,0:T(8,128)(2,1)S(1)} %copy-done, bf16[384,4096]{1,0:T(8,128)(2,1)S(1)} %collective-permute-done.4.oth_ref, bf16[400,768]{1,0:T(8,128)(2,1)S(1)} %grad_logits.1.g_ref.g_own_ref, ...), custom_call_target="tpu_custom_call" | custom-call | flops 1 | bytes 1 | tf_op jit(solution)/shard_map/head_grad/pallas_call | solution.py:301
  57.5 1.9 %collective-permute-done.13 = f16[4,8,16,384]{3,2,1,0:T(8,128)(2,1)S(1)} collective-permute-done((f16[4,8,16,384]{3,2,1,0:T(8,128)(2,1)S(1)}, f16[4,8,16,384]{3,2,1,0:T(8,128)(2,1)S(1)}, u32[]{:S(2)}, u32[]{:S(2)}) %collective-permute-start.13) | collective-permute-done | bytes 393248 | tf_op jit(solution)/shard_map/ppermute | solution.py:31
  59.4 0.1 multiply_convert_fusion.4
  59.5 3.0 %collective-permute-start.16 = (f16[2,8,16,384]{3,2,1,0:T(8,128)(2,1)S(1)}, f16[2,8,16,384]{3,2,1,0:T(8,128)(2,1)S(1)}, u32[]{:S(2)}, u32[]{:S(2)}) collective-permute-start(f16[2,8,16,384]{3,2,1,0:T(8,128)(2,1)S(1)} %multiply_convert_fusion.4), channel_id=1, source_target_pairs={{0,192},{64,0},{128,64},{192,128},{1,193},{65,1},{129,65},{193,129... | collective-permute-start | bytes 589832 | tf_op jit(solution)/shard_map/ppermute | solution.py:31
  62.5 0.1 multiply_convert_fusion.5
  62.6 0.1 collective-permute-start.15
  62.7 0.1 multiply_convert_fusion.6
  62.8 0.4 collective-permute-start.9
  63.1 0.1 multiply_convert_fusion.7
  63.2 1.8 %collective-permute-start.8 = (f16[2,8,16,384]{3,2,1,0:T(8,128)(2,1)S(1)}, f16[2,8,16,384]{3,2,1,0:T(8,128)(2,1)S(1)}, u32[]{:S(2)}, u32[]{:S(2)}) collective-permute-start(f16[2,8,16,384]{3,2,1,0:T(8,128)(2,1)S(1)} %multiply_convert_fusion.7), channel_id=1, source_target_pairs={{0,2},{2,4},{4,6},{6,0},{1,3},{3,5},{5,7},{7,1},{8,10},{10,12},{12... | collective-permute-start | bytes 589832 | tf_op jit(solution)/shard_map/ppermute | solution.py:31
  65.0 0.8 collective-permute-done.16
  65.8 3.7 %collective-permute-done.15 = f16[2,8,16,384]{3,2,1,0:T(8,128)(2,1)S(1)} collective-permute-done((f16[2,8,16,384]{3,2,1,0:T(8,128)(2,1)S(1)}, f16[2,8,16,384]{3,2,1,0:T(8,128)(2,1)S(1)}, u32[]{:S(2)}, u32[]{:S(2)}) %collective-permute-start.15) | collective-permute-done | bytes 196640 | tf_op jit(solution)/shard_map/ppermute | solution.py:31
  69.6 0.2 multiply_add_fusion
  69.8 0.1 collective-permute-start.18
  69.9 2.0 %collective-permute-start.17 = (f16[8,16,384]{2,1,0:T(8,128)(2,1)S(1)}, f16[8,16,384]{2,1,0:T(8,128)(2,1)S(1)}, u32[]{:S(2)}, u32[]{:S(2)}) collective-permute-start(f16[8,16,384]{2,1,0:T(8,128)(2,1)S(1)} %get-tuple-element.69), channel_id=1, source_target_pairs={{0,4},{2,6},{4,0},{6,2},{1,5},{3,7},{5,1},{7,3},{8,12},{10,14},{12... | collective-permute-start | bytes 294920 | tf_op jit(solution)/shard_map/ppermute | solution.py:31
  71.9 1.4 %collective-permute-start.19 = (f16[8,16,384]{2,1,0:T(8,128)(2,1)S(1)}, f16[8,16,384]{2,1,0:T(8,128)(2,1)S(1)}, u32[]{:S(2)}, u32[]{:S(2)}) collective-permute-start(f16[8,16,384]{2,1,0:T(8,128)(2,1)S(1)} %get-tuple-element.70), channel_id=1, source_target_pairs={{0,6},{2,0},{4,2},{6,4},{1,7},{3,1},{5,3},{7,5},{8,14},{10,8},{12,... | collective-permute-start | bytes 294920 | tf_op jit(solution)/shard_map/ppermute | solution.py:31
  73.3 0.2 multiply_add_fusion.2
  73.6 0.1 collective-permute-start.11
  73.7 4.7 %collective-permute-start.10 = (f16[8,16,384]{2,1,0:T(8,128)(2,1)S(1)}, f16[8,16,384]{2,1,0:T(8,128)(2,1)S(1)}, u32[]{:S(2)}, u32[]{:S(2)}) collective-permute-start(f16[8,16,384]{2,1,0:T(8,128)(2,1)S(1)} %get-tuple-element.67), channel_id=1, source_target_pairs={{0,128},{64,192},{128,0},{192,64},{1,129},{65,193},{129,1},{193,65... | collective-permute-start | bytes 294920 | tf_op jit(solution)/shard_map/ppermute | solution.py:31
  78.4 0.1 fusion.4
  78.4 1.0 %collective-permute-done.11 = f16[8,16,384]{2,1,0:T(8,128)(2,1)S(1)} collective-permute-done((f16[8,16,384]{2,1,0:T(8,128)(2,1)S(1)}, f16[8,16,384]{2,1,0:T(8,128)(2,1)S(1)}, u32[]{:S(2)}, u32[]{:S(2)}) %collective-permute-start.11) | collective-permute-done | bytes 98336 | tf_op jit(solution)/shard_map/ppermute | solution.py:31
  79.5 2.5 %collective-permute-done.10 = f16[8,16,384]{2,1,0:T(8,128)(2,1)S(1)} collective-permute-done((f16[8,16,384]{2,1,0:T(8,128)(2,1)S(1)}, f16[8,16,384]{2,1,0:T(8,128)(2,1)S(1)}, u32[]{:S(2)}, u32[]{:S(2)}) %collective-permute-start.10) | collective-permute-done | bytes 98336 | tf_op jit(solution)/shard_map/ppermute | solution.py:31
  82.0 1.0 %collective-permute-done.12 = f16[8,16,384]{2,1,0:T(8,128)(2,1)S(1)} collective-permute-done((f16[8,16,384]{2,1,0:T(8,128)(2,1)S(1)}, f16[8,16,384]{2,1,0:T(8,128)(2,1)S(1)}, u32[]{:S(2)}, u32[]{:S(2)}) %collective-permute-start.12) | collective-permute-done | bytes 98336 | tf_op jit(solution)/shard_map/ppermute | solution.py:31
  83.0 0.1 fusion.8
  83.1 11.8 %all_to_all.11 = f16[8,32,384]{2,1,0:T(8,128)(2,1)S(1)} all-to-all(f16[8,32,384]{2,1,0:T(8,128)(2,1)S(1)} %fusion), channel_id=1, replica_groups=mesh['y'=4,'z'=8,'x'=4,'c'=2] {'z'}, dimensions={0} | all-to-all | bytes 393216 | tf_op jit(solution)/shard_map/all_to_all | solution.py:377
  94.8 0.7 multiply_reduce_fusion
  (34 shorter events, 0.2 us)
Async XLA Ops:
  0.6 6.2 %collective-permute-start = (bf16[768,384]{1,0:T(8,128)(2,1)}, bf16[768,384]{1,0:T(8,128)(2,1)S(1)}, u32[]{:S(2)}, u32[]{:S(2)}) collective-permute-start(bf16[768,384]{1,0:T(8,128)(2,1)} %own_ref.2), channel_id=1, source_target_pairs={{0,1},{1,0},{2,3},{3,2},{4,5},{5,4},{6,7},{7,6},{8,9},{9,8},{10,11... | collective-permute-start | bytes 1769480 | tf_op jit(solution)/shard_map/ppermute | solution.py:31
  0.7 40.1 %slice-start = ((s8[6291456]{0:T(1024)(128)(4,1)}), s8[4194304]{0:T(1024)(128)(4,1)S(1)}, s32[]{:S(2)}) async-start(s8[6291456]{0:T(1024)(128)(4,1)} %bitcast.33), calls=%async_computation.2 | async-start | bytes 8388608
  0.8 6.0 %copy-start.1 = (bf16[768,384]{1,0:T(8,128)(2,1)S(1)}, bf16[768,384]{1,0:T(8,128)(2,1)}, u32[]{:S(2)}) copy-start(bf16[768,384]{1,0:T(8,128)(2,1)} %own_ref.2) | copy-start | bytes 1769476
  0.8 6.0 %copy-start.2 = (s32[384]{0:T(512)S(1)}, s32[384]{0:T(512)}, u32[]{:S(2)}) copy-start(s32[384]{0:T(512)} %param.9) | copy-start | bytes 4612
  0.8 6.0 %copy-start.3 = (s32[768]{0:T(1024)S(1)}, s32[768]{0:T(1024)}, u32[]{:S(2)}) copy-start(s32[768]{0:T(1024)} %param.10) | copy-start | bytes 9220
  0.8 30.3 %copy-start = (bf16[384,4096]{1,0:T(8,128)(2,1)S(1)}, bf16[384,4096]{1,0:T(8,128)(2,1)}, u32[]{:S(2)}) copy-start(bf16[384,4096]{1,0:T(8,128)(2,1)} %own_ref.3) | copy-start | bytes 9437188
  0.8 38.6 %copy-start.4 = (f32[384]{0:T(512)S(1)}, f32[384]{0:T(512)}, u32[]{:S(2)}) copy-start(f32[384]{0:T(512)} %param.11) | copy-start | bytes 4612
  0.9 40.0 %slice-start.1 = ((s8[6291456]{0:T(1024)(128)(4,1)}), s8[2097152]{0:T(1024)(128)(4,1)S(1)}, s32[]{:S(2)}) async-start(s8[6291456]{0:T(1024)(128)(4,1)} %bitcast.33), calls=%async_computation.3 | async-start | bytes 4194304
  31.2 9.7 %collective-permute-start.4 = (bf16[384,4096]{1,0:T(8,128)(2,1)S(1)}, bf16[384,4096]{1,0:T(8,128)(2,1)S(1)}, u32[]{:S(2)}, u32[]{:S(2)}) collective-permute-start(bf16[384,4096]{1,0:T(8,128)(2,1)S(1)} %copy-done), channel_id=1, source_target_pairs={{0,1},{1,0},{2,3},{3,2},{4,5},{5,4},{6,7},{7,6},{8,9},{9,8},{10,11... | collective-permute-start | bytes 9437192 | tf_op jit(solution)/shard_map/ppermute | solution.py:31
  31.2 5.3 %collective-permute-start.3 = (f32[2,640]{1,0:T(2,128)S(1)}, f32[2,640]{1,0:T(2,128)S(1)}, u32[]{:S(2)}, u32[]{:S(2)}) collective-permute-start(f32[2,640]{1,0:T(2,128)S(1)} %merge_stats.1.s0), channel_id=1, source_target_pairs={{0,192},{64,0},{128,64},{192,128},{1,193},{65,1},{129,65},{193,129... | collective-permute-start | bytes 15368 | tf_op jit(solution)/shard_map/ppermute | solution.py:31
  34.3 4.8 %collective-permute-start.2 = (f32[2,640]{1,0:T(2,128)S(1)}, f32[2,640]{1,0:T(2,128)S(1)}, u32[]{:S(2)}, u32[]{:S(2)}) collective-permute-start(f32[2,640]{1,0:T(2,128)S(1)} %merge_stats.1.s0), channel_id=1, source_target_pairs={{0,64},{64,128},{128,192},{192,0},{1,65},{65,129},{129,193},{193,1... | collective-permute-start | bytes 15368 | tf_op jit(solution)/shard_map/ppermute | solution.py:31
  34.3 5.1 %collective-permute-start.1 = (f32[2,640]{1,0:T(2,128)S(1)}, f32[2,640]{1,0:T(2,128)S(1)}, u32[]{:S(2)}, u32[]{:S(2)}) collective-permute-start(f32[2,640]{1,0:T(2,128)S(1)} %merge_stats.1.s0), channel_id=1, source_target_pairs={{0,128},{64,192},{128,0},{192,64},{1,129},{65,193},{129,1},{193,65... | collective-permute-start | bytes 15368 | tf_op jit(solution)/shard_map/ppermute | solution.py:31
  43.6 9.0 %collective-permute-start.7 = (bf16[400,768]{1,0:T(8,128)(2,1)S(1)}, bf16[400,768]{1,0:T(8,128)(2,1)S(1)}, u32[]{:S(2)}, u32[]{:S(2)}) collective-permute-start(bf16[400,768]{1,0:T(8,128)(2,1)S(1)} %grad_logits.1.g_ref.g_own_ref), channel_id=1, source_target_pairs={{0,1},{1,0},{2,3},{3,2},{4,5},{5,4},{6,7},{7,6},{8,9},{9,8},{10,11... | collective-permute-start | bytes 1843208 | tf_op jit(solution)/shard_map/ppermute | solution.py:31
  43.7 13.8 %collective-permute-start.5 = (f16[4,8,16,384]{3,2,1,0:T(8,128)(2,1)S(1)}, f16[4,8,16,384]{3,2,1,0:T(8,128)(2,1)S(1)}, u32[]{:S(2)}, u32[]{:S(2)}) collective-permute-start(f16[4,8,16,384]{3,2,1,0:T(8,128)(2,1)S(1)} %get-tuple-element.43), channel_id=1, source_target_pairs={{0,2},{2,4},{4,6},{6,0},{1,3},{3,5},{5,7},{7,1},{8,10},{10,12},{12... | collective-permute-start | bytes 1179656 | tf_op jit(solution)/shard_map/ppermute | solution.py:31
  44.3 13.2 %collective-permute-start.6 = (f16[4,8,16,384]{3,2,1,0:T(8,128)(2,1)S(1)}, f16[4,8,16,384]{3,2,1,0:T(8,128)(2,1)S(1)}, u32[]{:S(2)}, u32[]{:S(2)}) collective-permute-start(f16[4,8,16,384]{3,2,1,0:T(8,128)(2,1)S(1)} %get-tuple-element.44), channel_id=1, source_target_pairs={{0,6},{2,0},{4,2},{6,4},{1,7},{3,1},{5,3},{7,5},{8,14},{10,8},{12,... | collective-permute-start | bytes 1179656 | tf_op jit(solution)/shard_map/ppermute | solution.py:31
  47.0 12.4 %collective-permute-start.13 = (f16[4,8,16,384]{3,2,1,0:T(8,128)(2,1)S(1)}, f16[4,8,16,384]{3,2,1,0:T(8,128)(2,1)S(1)}, u32[]{:S(2)}, u32[]{:S(2)}) collective-permute-start(f16[4,8,16,384]{3,2,1,0:T(8,128)(2,1)S(1)} %get-tuple-element.56), channel_id=1, source_target_pairs={{0,64},{64,128},{128,192},{192,0},{1,65},{65,129},{129,193},{193,1... | collective-permute-start | bytes 1179656 | tf_op jit(solution)/shard_map/ppermute | solution.py:31
  47.6 11.8 %collective-permute-start.14 = (f16[4,8,16,384]{3,2,1,0:T(8,128)(2,1)S(1)}, f16[4,8,16,384]{3,2,1,0:T(8,128)(2,1)S(1)}, u32[]{:S(2)}, u32[]{:S(2)}) collective-permute-start(f16[4,8,16,384]{3,2,1,0:T(8,128)(2,1)S(1)} %get-tuple-element.57), channel_id=1, source_target_pairs={{0,192},{64,0},{128,64},{192,128},{1,193},{65,1},{129,65},{193,129... | collective-permute-start | bytes 1179656 | tf_op jit(solution)/shard_map/ppermute | solution.py:31
  59.5 6.4 %collective-permute-start.16 = (f16[2,8,16,384]{3,2,1,0:T(8,128)(2,1)S(1)}, f16[2,8,16,384]{3,2,1,0:T(8,128)(2,1)S(1)}, u32[]{:S(2)}, u32[]{:S(2)}) collective-permute-start(f16[2,8,16,384]{3,2,1,0:T(8,128)(2,1)S(1)} %multiply_convert_fusion.4), channel_id=1, source_target_pairs={{0,192},{64,0},{128,64},{192,128},{1,193},{65,1},{129,65},{193,129... | collective-permute-start | bytes 589832 | tf_op jit(solution)/shard_map/ppermute | solution.py:31
  62.6 7.0 %collective-permute-start.15 = (f16[2,8,16,384]{3,2,1,0:T(8,128)(2,1)S(1)}, f16[2,8,16,384]{3,2,1,0:T(8,128)(2,1)S(1)}, u32[]{:S(2)}, u32[]{:S(2)}) collective-permute-start(f16[2,8,16,384]{3,2,1,0:T(8,128)(2,1)S(1)} %multiply_convert_fusion.5), channel_id=1, source_target_pairs={{0,64},{64,128},{128,192},{192,0},{1,65},{65,129},{129,193},{193,1... | collective-permute-start | bytes 589832 | tf_op jit(solution)/shard_map/ppermute | solution.py:31
  62.8 10.5 %collective-permute-start.9 = (f16[2,8,16,384]{3,2,1,0:T(8,128)(2,1)S(1)}, f16[2,8,16,384]{3,2,1,0:T(8,128)(2,1)S(1)}, u32[]{:S(2)}, u32[]{:S(2)}) collective-permute-start(f16[2,8,16,384]{3,2,1,0:T(8,128)(2,1)S(1)} %multiply_convert_fusion.6), channel_id=1, source_target_pairs={{0,6},{2,0},{4,2},{6,4},{1,7},{3,1},{5,3},{7,5},{8,14},{10,8},{12,... | collective-permute-start | bytes 589832 | tf_op jit(solution)/shard_map/ppermute | solution.py:31
  63.2 10.1 %collective-permute-start.8 = (f16[2,8,16,384]{3,2,1,0:T(8,128)(2,1)S(1)}, f16[2,8,16,384]{3,2,1,0:T(8,128)(2,1)S(1)}, u32[]{:S(2)}, u32[]{:S(2)}) collective-permute-start(f16[2,8,16,384]{3,2,1,0:T(8,128)(2,1)S(1)} %multiply_convert_fusion.7), channel_id=1, source_target_pairs={{0,2},{2,4},{4,6},{6,0},{1,3},{3,5},{5,7},{7,1},{8,10},{10,12},{12... | collective-permute-start | bytes 589832 | tf_op jit(solution)/shard_map/ppermute | solution.py:31
  69.8 8.5 %collective-permute-start.18 = (f16[8,16,384]{2,1,0:T(8,128)(2,1)S(1)}, f16[8,16,384]{2,1,0:T(8,128)(2,1)S(1)}, u32[]{:S(2)}, u32[]{:S(2)}) collective-permute-start(f16[8,16,384]{2,1,0:T(8,128)(2,1)S(1)} %fusion.13), channel_id=1, source_target_pairs={{0,2},{2,4},{4,6},{6,0},{1,3},{3,5},{5,7},{7,1},{8,10},{10,12},{12... | collective-permute-start | bytes 294920 | tf_op jit(solution)/shard_map/ppermute | solution.py:31
  69.9 8.4 %collective-permute-start.17 = (f16[8,16,384]{2,1,0:T(8,128)(2,1)S(1)}, f16[8,16,384]{2,1,0:T(8,128)(2,1)S(1)}, u32[]{:S(2)}, u32[]{:S(2)}) collective-permute-start(f16[8,16,384]{2,1,0:T(8,128)(2,1)S(1)} %get-tuple-element.69), channel_id=1, source_target_pairs={{0,4},{2,6},{4,0},{6,2},{1,5},{3,7},{5,1},{7,3},{8,12},{10,14},{12... | collective-permute-start | bytes 294920 | tf_op jit(solution)/shard_map/ppermute | solution.py:31
  71.9 6.4 %collective-permute-start.19 = (f16[8,16,384]{2,1,0:T(8,128)(2,1)S(1)}, f16[8,16,384]{2,1,0:T(8,128)(2,1)S(1)}, u32[]{:S(2)}, u32[]{:S(2)}) collective-permute-start(f16[8,16,384]{2,1,0:T(8,128)(2,1)S(1)} %get-tuple-element.70), channel_id=1, source_target_pairs={{0,6},{2,0},{4,2},{6,4},{1,7},{3,1},{5,3},{7,5},{8,14},{10,8},{12,... | collective-permute-start | bytes 294920 | tf_op jit(solution)/shard_map/ppermute | solution.py:31
  73.6 5.9 %collective-permute-start.11 = (f16[8,16,384]{2,1,0:T(8,128)(2,1)S(1)}, f16[8,16,384]{2,1,0:T(8,128)(2,1)S(1)}, u32[]{:S(2)}, u32[]{:S(2)}) collective-permute-start(f16[8,16,384]{2,1,0:T(8,128)(2,1)S(1)} %fusion.10), channel_id=1, source_target_pairs={{0,64},{64,128},{128,192},{192,0},{1,65},{65,129},{129,193},{193,1... | collective-permute-start | bytes 294920 | tf_op jit(solution)/shard_map/ppermute | solution.py:31
  73.7 8.3 %collective-permute-start.10 = (f16[8,16,384]{2,1,0:T(8,128)(2,1)S(1)}, f16[8,16,384]{2,1,0:T(8,128)(2,1)S(1)}, u32[]{:S(2)}, u32[]{:S(2)}) collective-permute-start(f16[8,16,384]{2,1,0:T(8,128)(2,1)S(1)} %get-tuple-element.67), channel_id=1, source_target_pairs={{0,128},{64,192},{128,0},{192,64},{1,129},{65,193},{129,1},{193,65... | collective-permute-start | bytes 294920 | tf_op jit(solution)/shard_map/ppermute | solution.py:31
  78.3 4.6 %collective-permute-start.12 = (f16[8,16,384]{2,1,0:T(8,128)(2,1)S(1)}, f16[8,16,384]{2,1,0:T(8,128)(2,1)S(1)}, u32[]{:S(2)}, u32[]{:S(2)}) collective-permute-start(f16[8,16,384]{2,1,0:T(8,128)(2,1)S(1)} %get-tuple-element.68), channel_id=1, source_target_pairs={{0,192},{64,0},{128,64},{192,128},{1,193},{65,1},{129,65},{193,129... | collective-permute-start | bytes 294920 | tf_op jit(solution)/shard_map/ppermute | solution.py:31

commit v6 on v5

--- a/solution.py
+++ b/solution.py
@@ -2,6 +2,7 @@
 
 import jax
 import jax.numpy as jnp
+import numpy as np
 from jax import lax
 from jax.experimental import pallas as pl
 from jax.experimental.pallas import tpu as pltpu
@@ -29,6 +30,18 @@
 def shift(a, axis, by):
     n = lax.axis_size(axis)
     return lax.ppermute(a, axis, [(i, (i + by) % n) for i in range(n)])
+
+
+def shift_by_core(a, by, first):
+    axes = ("y", "z", "x", "c")
+    shape = tuple(lax.axis_size(axis) for axis in axes)
+    pairs = []
+    for source in np.ndindex(shape):
+        target = list(source)
+        axis = 2 if (source[3] == 0) == first else 0
+        target[axis] = (target[axis] + by) % shape[axis]
+        pairs.append(tuple(int(np.ravel_multi_index(at, shape)) for at in (source, target)))
+    return lax.ppermute(a, axes, pairs)
 
 
 def logits_kernel(steps, h_ref, w_ref, out_ref, h_buf, w_buf, h_sem, w_sem):
@@ -237,29 +250,26 @@
 
 
 def hidden_kernel(groups, pos_ref, w_ref, g_ref, *outs):
-    ny, nz, nx, _, sub, cols = w_ref.shape
-    y, x = pos_ref[2], pos_ref[3]
+    ny, nz, nx, sub, cols = w_ref.shape
+    x_first, y, x = pos_ref[0] == 0, pos_ref[2], pos_ref[3]
     g = g_ref[: outs[0].shape[-1], :]
 
-    def block(part, far, near):
-        dy, dx = (near, far) if part == 0 else (far, near)
-        w = w_ref[lax.rem(y + dy, ny), :, lax.rem(x + dx, nx), part]
+    def block(far, near):
+        dx = jnp.where(x_first, far, near)
+        dy = jnp.where(x_first, near, far)
+        w = w_ref[lax.rem(y + dy, ny), :, lax.rem(x + dx, nx)]
         return w.reshape(nz * sub, cols)
 
-    for at, out in enumerate(outs):
-        part, names = divmod(at, len(groups))
-        names = groups[names]
-        w = jnp.concatenate([block(part, *name) for name in names], axis=0)
+    for names, out in zip(groups, outs):
+        w = jnp.concatenate([block(*name) for name in names], axis=0)
         product = lax.dot_general(w, g, (((1,), (1,)), ((), ())), preferred_element_type=F32)
         out[...] = product.reshape(out.shape)
 
 
-def hidden_part(pos, head6, g, groups):
-    _, nz, _, _, sub, cols = head6.shape
+def hidden_part(pos, head5, g, groups):
+    nz, sub = head5.shape[1], head5.shape[3]
     rows = g.shape[0] - LOSS_ROWS
-    out_shape = [
-        jax.ShapeDtypeStruct((len(names), nz, sub, rows), F32) for _ in range(2) for names in groups
-    ]
+    out_shape = [jax.ShapeDtypeStruct((len(names), nz, sub, rows), F32) for names in groups]
     return pl.pallas_call(
         functools.partial(hidden_kernel, groups),
         out_shape=out_shape,
@@ -268,7 +278,7 @@
         compiler_params=params(16),
         cost_estimate=LIGHT,
         name="hidden_part",
-    )(pos, head6, g)
+    )(pos, head5, g)
 
 
 def head_kernel(pos_ref, own_ref, oth_ref, g_own_ref, g_oth_ref, out_ref, loss_ref, buf, sem):
@@ -337,43 +347,30 @@
     hidden_oth = shift(lax.optimization_barrier((hidden, stats))[0], "c", 1)
     g = grad_logits(pos, logits, teacher_rows, ids, scale, parts)
     g, hidden_oth = lax.optimization_barrier((g, hidden_oth))
-    sub = depth // (ny * nz * nx) // 2
-    head6 = head.reshape(ny, nz, nx, 2, sub, cols)
-
-    def send(value, axis, by):
-        return shift((value * SEND_SCALE).astype(F16), axis, by)
+    head5 = head.reshape(ny, nz, nx, depth // (ny * nz * nx), cols)
+
+    def coded(value):
+        return (value * SEND_SCALE).astype(F16)
 
     def taken(value):
         return value.astype(F32) * (1.0 / SEND_SCALE)
 
-    sent = [(v * SEND_SCALE).astype(F16) for v in hidden_part(pos, head6, g, SENT)]
-    *sent, g = lax.optimization_barrier((*sent, g))
-    up_a, down_a, up_b, down_b = sent
-    got_a = shift(up_a, "x", 1), shift(down_a, "x", -1)
-    got_b = shift(up_b, "y", 1), shift(down_b, "y", -1)
+    up, down = (coded(v) for v in hidden_part(pos, head5, g, SENT))
+    up, down, g = lax.optimization_barrier((up, down, g))
+    up, down = shift_by_core(up, 1, True), shift_by_core(down, -1, True)
     g_oth = shift(g, "c", 1)
-    kept = hidden_part(pos, head6, g, KEPT)
-    kept_a, kept_b = kept[:3], kept[3:]
+    c1, c3, c0 = hidden_part(pos, head5, g, KEPT)
     head_out, loss = head_grad(pos, hidden, hidden_oth, g, g_oth)
     loss = loss[0, :1]
-    got_a, loss, _ = lax.optimization_barrier((got_a, loss, head_out))
-    got_b, head_out = lax.optimization_barrier((got_b, head_out))
-
-    def second_step(kept, got, axis):
-        (c1, c3, c0), (up, down) = kept, got
-        up2 = send(c1 + taken(up[:2]), axis, 1)
-        down2 = send(c3 + taken(down[:2]), axis, -1)
-        return c0[:2] + taken(down[2:]) + taken(up2), c0[2:] + taken(up[2:]) + taken(down2)
-
-    low_a, high_a = second_step(kept_a, got_a, "x")
-    low_b, high_b = second_step(kept_b, got_b, "y")
-
-    def second_level(low, high, axis):
-        far = [send(f, axis, d) for d, f in ((2, high[0]), (1, low[1]), (3, high[1]))]
-        return low[0] + sum(taken(f) for f in far)
-
-    both = (second_level(low_a, high_a, "y"), second_level(low_b, high_b, "x"))
-    both = (jnp.concatenate(both, axis=1) * SEND_SCALE).astype(F16)
+    up, down, loss, head_out = lax.optimization_barrier((up, down, loss, head_out))
+
+    up2 = shift_by_core(coded(c1 + taken(up[:2])), 1, True)
+    down2 = shift_by_core(coded(c3 + taken(down[:2])), -1, True)
+    low = c0[:2] + taken(down[2:]) + taken(up2)
+    high = c0[2:] + taken(up[2:]) + taken(down2)
+
+    far = [shift_by_core(coded(v), d, False) for d, v in ((2, high[0]), (1, low[1]), (3, high[1]))]
+    both = coded(low[0] + sum(taken(v) for v in far))
     both = lax.all_to_all(both, "z", 0, 0, tiled=True)
     hidden_grad = jnp.sum(taken(both), axis=0).T.astype(BF16)
     return loss, hidden_grad, head_out

time: 95.6 us -> 98.2 us (1.027)
  waiting for transfers between devices: 13.8 us -> 20.3 us
  starting transfers between devices: 25.6 us -> 21.1 us
    ppermute x20 -> x6, starting transfers between devices: 25.6 us -> 5.44 us  [shift(): return lax.ppermute(a, axis, [(i, (i + by) % n) for i in range(n)])]
    ppermute x0 -> x7, waiting for transfers between devices: none -> 17.4 us  [shift_by_core(): return lax.ppermute(a, axes, pairs)]
    ppermute x0 -> x7, starting transfers between devices: none -> 15.7 us  [shift_by_core(): return lax.ppermute(a, axes, pairs)]
    ppermute x20 -> x6, waiting for transfers between devices: 13.8 us -> 2.93 us  [shift(): return lax.ppermute(a, axis, [(i, (i + by) % n) for i in range(n)])]
  transfers between devices with their start and end apart: 20 -> 13, of which waited for: 8 -> 7; matrix products, arithmetic and copies ran while one was open for 1% -> 0% of each run, Pallas kernels for 15% -> 15%
where the time goes in v6:
time: 98.2 us; the launch traced here: 97.5 us
  blocking collectives  33.6 us (34%)
  starting transfers between devices  21.1 us (21%)
  waiting for transfers between devices  20.3 us (21%)
  Pallas kernels  19.3 us (20%)
  other arithmetic  2.12 us (2%)
    all_to_all x1, blocking collectives, body(): stats = merge_stats(lax.all_to_all(stats, ('z', 'x'), 0, 0, tiled=True))  21.9 us
    ppermute x7, waiting for transfers between devices, shift_by_core(): return lax.ppermute(a, axes, pairs)  17.4 us
    ppermute x7, starting transfers between devices, shift_by_core(): return lax.ppermute(a, axes, pairs)  15.7 us
    all_to_all x1, blocking collectives, body(): both = lax.all_to_all(both, 'z', 0, 0, tiled=True)  11.8 us
    pallas_call x1, Pallas kernels, student_logits(): pl.pallas_call(functools.partial(logits_kernel, steps), out_shape=jax.Sha...  5.91 us
    ppermute x6, starting transfers between devices, shift(): return lax.ppermute(a, axis, [(i, (i + by) % n) for i in range(n)])  5.44 us
    pallas_call x1, Pallas kernels, head_grad(): pl.pallas_call(head_kernel, out_shape=(jax.ShapeDtypeStruct((width, cols)...  4.92 us
    pallas_call x2, Pallas kernels, hidden_part(): pl.pallas_call(functools.partial(hidden_kernel, groups), out_shape=out_sh...  4.66 us
  transfers between devices with their start and end apart: 13, of which 7 were waited for; matrix products, arithmetic and copies ran while one was open for 0% of the time, Pallas kernels for 15%

profile of v6, /device:TPU:32, one launch (start us, length us, event | category | flops | bytes accessed | tf_op | source)
XLA Modules:
  0.0 97.5 jit_solution(7350332708403419154)
XLA Ops:
  0.6 0.1 collective-permute-start
  0.7 0.0 slice-start
  0.8 0.1 pad_add_fusion.pos_ref
  0.8 0.0 slice-start.1
  0.9 5.9 %student_logits.1.l_ref = f32[384,768]{1,0:T(8,128)S(1)} custom-call(bf16[384,4096]{1,0:T(8,128)(2,1)} %own_ref.3, bf16[4096,768]{1,0:T(8,128)(2,1)} %w_ref.1), custom_call_target="tpu_custom_call" | custom-call | flops 2415919104 | bytes 10616832 | tf_op jit(solution)/shard_map/student_logits/pallas_call | solution.py:75
  6.8 0.0 copy-start.4
  6.8 0.0 collective-permute-done.oth_ref
  6.8 0.0 copy-done.1
  6.8 2.3 %local_stats.1 = (f32[2,640]{1,0:T(2,128)S(1)}, bf16[384,768]{1,0:T(8,128)(2,1)S(1)}) custom-call(s32[4]{0:T(128)S(1)} %pad_add_fusion.pos_ref, f32[384,768]{1,0:T(8,128)S(1)} %student_logits.1.l_ref, bf16[768,384]{1,0:T(8,128)(2,1)S(1)} %copy-done.1, bf16[768,384]{1,0:T(8,128)(2,1)S(1)} %collective-permute-done.oth_ref, s32[6,128]{1,0:T(8,128)S(1)} %bitcast.33, ...), custom_call_target="tpu_custom_call" | custom-call | flops 452984832 | bytes 2949120 | tf_op jit(solution)/shard_map/local_stats/pallas_call | solution.py:190
  9.1 0.1 broadcast_in_dim.2
  9.1 21.9 %all_to_all.10.in_ref = f32[32,2,640]{2,1,0:T(2,128)S(1)} all-to-all(f32[32,2,640]{2,1,0:T(2,128)S(1)} %broadcast_in_dim.2), channel_id=1, replica_groups=mesh['y'=4,'z'=8,'x'=4,'c'=2] {'z','x'}, dimensions={0} | all-to-all | bytes 327680 | tf_op jit(solution)/shard_map/all_to_all | solution.py:345
  31.0 0.2 merge_stats.1.s0
  31.2 0.0 collective-permute-start.4
  31.2 3.1 %collective-permute-start.3 = (f32[2,640]{1,0:T(2,128)S(1)}, f32[2,640]{1,0:T(2,128)S(1)}, u32[]{:S(2)}, u32[]{:S(2)}) collective-permute-start(f32[2,640]{1,0:T(2,128)S(1)} %merge_stats.1.s0), channel_id=1, source_target_pairs={{0,192},{64,0},{128,64},{192,128},{1,193},{65,1},{129,65},{193,129... | collective-permute-start | bytes 15368 | tf_op jit(solution)/shard_map/ppermute | solution.py:32
  34.3 0.0 collective-permute-start.2
  34.3 2.2 %collective-permute-start.1 = (f32[2,640]{1,0:T(2,128)S(1)}, f32[2,640]{1,0:T(2,128)S(1)}, u32[]{:S(2)}, u32[]{:S(2)}) collective-permute-start(f32[2,640]{1,0:T(2,128)S(1)} %merge_stats.1.s0), channel_id=1, source_target_pairs={{0,128},{64,192},{128,0},{192,64},{1,129},{65,193},{129,1},{193,65... | collective-permute-start | bytes 15368 | tf_op jit(solution)/shard_map/ppermute | solution.py:32
  36.5 0.0 collective-permute-done.3.s3
  36.5 2.6 %collective-permute-done.2.s2 = f32[2,640]{1,0:T(2,128)S(1)} collective-permute-done((f32[2,640]{1,0:T(2,128)S(1)}, f32[2,640]{1,0:T(2,128)S(1)}, u32[]{:S(2)}, u32[]{:S(2)}) %collective-permute-start.2) | collective-permute-done | bytes 5152 | tf_op jit(solution)/shard_map/ppermute | solution.py:32
  39.2 0.3 collective-permute-done.1.s1
  39.5 1.4 %grad_logits.1.g_ref.g_own_ref = bf16[400,768]{1,0:T(8,128)(2,1)S(1)} custom-call(s32[4]{0:T(128)S(1)} %pad_add_fusion.pos_ref, f32[384,768]{1,0:T(8,128)S(1)} %student_logits.1.l_ref, bf16[384,768]{1,0:T(8,128)(2,1)S(1)} %get-tuple-element.24.t_ref, s32[3,128]{1,0:T(4,128)S(1)} %bitcast.32, f32[3,128]{1,0:T(4,128)S(1)} %bitcast.34, ...), custom_call_target="tpu_custom_call" | custom-call | flops 2359296 | bytes 2359296 | tf_op jit(solution)/shard_map/grad_logits/pallas_call | solution.py:233
  40.9 0.0 collective-permute-done.4.oth_ref
  40.9 2.3 %hidden_part.2 = (f32[4,8,32,384]{3,2,1,0:T(8,128)S(1)}, f32[4,8,32,384]{3,2,1,0:T(8,128)S(1)}) custom-call(s32[4]{0:T(128)S(1)} %pad_add_fusion.pos_ref, bf16[4,8,4,32,768]{4,3,2,1,0:T(8,128)(2,1)S(1)} %bitcast.29, bf16[400,768]{1,0:T(8,128)(2,1)S(1)} %grad_logits.1.g_ref.g_own_ref), custom_call_target="tpu_custom_call" | custom-call | flops 1 | bytes 1 | tf_op jit(solution)/shard_map/hidden_part/pallas_call | solution.py:273
  43.2 0.4 multiply_convert_fusion
  43.6 0.6 collective-permute-start.5
  44.3 2.7 %collective-permute-start.6 = (f16[4,8,32,384]{3,2,1,0:T(8,128)(2,1)S(1)}, f16[4,8,32,384]{3,2,1,0:T(8,128)(2,1)S(1)}, u32[]{:S(2)}, u32[]{:S(2)}) collective-permute-start(f16[4,8,32,384]{3,2,1,0:T(8,128)(2,1)S(1)} %get-tuple-element.33), channel_id=1, source_target_pairs={{0,6},{1,193},{2,0},{3,195},{4,2},{5,197},{6,4},{7,199},{8,14},{9,... | collective-permute-start | bytes 2359304 | tf_op jit(solution)/shard_map/ppermute | solution.py:44
  47.0 0.0 collective-permute-start.7
  47.0 2.3 %hidden_part.3 = (f32[2,8,32,384]{3,2,1,0:T(8,128)S(1)}, f32[2,8,32,384]{3,2,1,0:T(8,128)S(1)}, f32[4,8,32,384]{3,2,1,0:T(8,128)S(1)}) custom-call(s32[4]{0:T(128)S(1)} %pad_add_fusion.pos_ref, bf16[4,8,4,32,768]{4,3,2,1,0:T(8,128)(2,1)S(1)} %bitcast.30, bf16[400,768]{1,0:T(8,128)(2,1)S(1)} %grad_logits.1.g_ref.g_own_ref), custom_call_target="tpu_custom_call" | custom-call | flops 1 | bytes 1 | tf_op jit(solution)/shard_map/hidden_part/pallas_call | solution.py:273
  49.3 0.0 collective-permute-done.7.g_oth_ref
  49.3 4.9 %head_grad.1 = (bf16[2048,768]{1,0:T(8,128)(2,1)}, f32[1,128]{1,0:T(1,128)}) custom-call(s32[4]{0:T(128)S(1)} %pad_add_fusion.pos_ref, bf16[384,4096]{1,0:T(8,128)(2,1)S(1)} %copy-done, bf16[384,4096]{1,0:T(8,128)(2,1)S(1)} %collective-permute-done.4.oth_ref, bf16[400,768]{1,0:T(8,128)(2,1)S(1)} %grad_logits.1.g_ref.g_own_ref, ...), custom_call_target="tpu_custom_call" | custom-call | flops 1 | bytes 1 | tf_op jit(solution)/shard_map/head_grad/pallas_call | solution.py:311
  54.2 2.7 %collective-permute-done.5 = f16[4,8,32,384]{3,2,1,0:T(8,128)(2,1)S(1)} collective-permute-done((f16[4,8,32,384]{3,2,1,0:T(8,128)(2,1)S(1)}, f16[4,8,32,384]{3,2,1,0:T(8,128)(2,1)S(1)}, u32[]{:S(2)}, u32[]{:S(2)}) %collective-permute-start.5) | collective-permute-done | bytes 786464 | tf_op jit(solution)/shard_map/ppermute | solution.py:44
  56.9 0.0 collective-permute-done.6
  56.9 0.2 multiply_convert_fusion.2
  57.1 3.3 %collective-permute-start.9 = (f16[2,8,32,384]{3,2,1,0:T(8,128)(2,1)S(1)}, f16[2,8,32,384]{3,2,1,0:T(8,128)(2,1)S(1)}, u32[]{:S(2)}, u32[]{:S(2)}) collective-permute-start(f16[2,8,32,384]{3,2,1,0:T(8,128)(2,1)S(1)} %multiply_convert_fusion.2), channel_id=1, source_target_pairs={{0,6},{1,193},{2,0},{3,195},{4,2},{5,197},{6,4},{7,199},{8,14},{9,... | collective-permute-start | bytes 1179656 | tf_op jit(solution)/shard_map/ppermute | solution.py:44
  60.4 0.2 multiply_convert_fusion.3
  60.6 0.1 collective-permute-start.8
  60.7 5.0 %collective-permute-done.9 = f16[2,8,32,384]{3,2,1,0:T(8,128)(2,1)S(1)} collective-permute-done((f16[2,8,32,384]{3,2,1,0:T(8,128)(2,1)S(1)}, f16[2,8,32,384]{3,2,1,0:T(8,128)(2,1)S(1)}, u32[]{:S(2)}, u32[]{:S(2)}) %collective-permute-start.9) | collective-permute-done | bytes 393248 | tf_op jit(solution)/shard_map/ppermute | solution.py:44
  65.7 3.9 %collective-permute-done.8 = f16[2,8,32,384]{3,2,1,0:T(8,128)(2,1)S(1)} collective-permute-done((f16[2,8,32,384]{3,2,1,0:T(8,128)(2,1)S(1)}, f16[2,8,32,384]{3,2,1,0:T(8,128)(2,1)S(1)}, u32[]{:S(2)}, u32[]{:S(2)}) %collective-permute-start.8) | collective-permute-done | bytes 393248 | tf_op jit(solution)/shard_map/ppermute | solution.py:44
  69.6 0.4 multiply_add_fusion
  70.0 0.1 fusion.6
  70.2 0.9 collective-permute-start.11
  71.0 8.1 %collective-permute-start.10 = (f16[8,32,384]{2,1,0:T(8,128)(2,1)S(1)}, f16[8,32,384]{2,1,0:T(8,128)(2,1)S(1)}, u32[]{:S(2)}, u32[]{:S(2)}) collective-permute-start(f16[8,32,384]{2,1,0:T(8,128)(2,1)S(1)} %get-tuple-element.47), channel_id=1, source_target_pairs={{0,128},{1,5},{2,130},{3,7},{4,132},{5,1},{6,134},{7,3},{8,136},{9... | collective-permute-start | bytes 589832 | tf_op jit(solution)/shard_map/ppermute | solution.py:44
  79.2 0.0 collective-permute-start.12
  79.2 2.2 %collective-permute-done.11 = f16[8,32,384]{2,1,0:T(8,128)(2,1)S(1)} collective-permute-done((f16[8,32,384]{2,1,0:T(8,128)(2,1)S(1)}, f16[8,32,384]{2,1,0:T(8,128)(2,1)S(1)}, u32[]{:S(2)}, u32[]{:S(2)}) %collective-permute-start.11) | collective-permute-done | bytes 196640 | tf_op jit(solution)/shard_map/ppermute | solution.py:44
  81.3 3.6 %collective-permute-done.10 = f16[8,32,384]{2,1,0:T(8,128)(2,1)S(1)} collective-permute-done((f16[8,32,384]{2,1,0:T(8,128)(2,1)S(1)}, f16[8,32,384]{2,1,0:T(8,128)(2,1)S(1)}, u32[]{:S(2)}, u32[]{:S(2)}) %collective-permute-start.10) | collective-permute-done | bytes 196640 | tf_op jit(solution)/shard_map/ppermute | solution.py:44
  84.9 0.0 collective-permute-done.12
  84.9 0.1 fusion.5
  85.1 11.8 %all_to_all.11 = f16[8,32,384]{2,1,0:T(8,128)(2,1)S(1)} all-to-all(f16[8,32,384]{2,1,0:T(8,128)(2,1)S(1)} %fusion.5), channel_id=1, replica_groups=mesh['y'=4,'z'=8,'x'=4,'c'=2] {'z'}, dimensions={0} | all-to-all | bytes 393216 | tf_op jit(solution)/shard_map/all_to_all | solution.py:374
  96.8 0.7 multiply_reduce_fusion
  (12 shorter events, 0.1 us)
Async XLA Ops:
  0.6 6.2 %collective-permute-start = (bf16[768,384]{1,0:T(8,128)(2,1)}, bf16[768,384]{1,0:T(8,128)(2,1)S(1)}, u32[]{:S(2)}, u32[]{:S(2)}) collective-permute-start(bf16[768,384]{1,0:T(8,128)(2,1)} %own_ref.2), channel_id=1, source_target_pairs={{0,1},{1,0},{2,3},{3,2},{4,5},{5,4},{6,7},{7,6},{8,9},{9,8},{10,11... | collective-permute-start | bytes 1769480 | tf_op jit(solution)/shard_map/ppermute | solution.py:32
  0.7 40.1 %slice-start = ((s8[6291456]{0:T(1024)(128)(4,1)}), s8[4194304]{0:T(1024)(128)(4,1)S(1)}, s32[]{:S(2)}) async-start(s8[6291456]{0:T(1024)(128)(4,1)} %bitcast.27), calls=%async_computation.2 | async-start | bytes 8388608
  0.8 6.0 %copy-start.1 = (bf16[768,384]{1,0:T(8,128)(2,1)S(1)}, bf16[768,384]{1,0:T(8,128)(2,1)}, u32[]{:S(2)}) copy-start(bf16[768,384]{1,0:T(8,128)(2,1)} %own_ref.2) | copy-start | bytes 1769476
  0.8 6.0 %copy-start.2 = (s32[384]{0:T(512)S(1)}, s32[384]{0:T(512)}, u32[]{:S(2)}) copy-start(s32[384]{0:T(512)} %param.9) | copy-start | bytes 4612
  0.8 6.0 %copy-start.3 = (s32[768]{0:T(1024)S(1)}, s32[768]{0:T(1024)}, u32[]{:S(2)}) copy-start(s32[768]{0:T(1024)} %param.10) | copy-start | bytes 9220
  0.8 30.3 %copy-start = (bf16[384,4096]{1,0:T(8,128)(2,1)S(1)}, bf16[384,4096]{1,0:T(8,128)(2,1)}, u32[]{:S(2)}) copy-start(bf16[384,4096]{1,0:T(8,128)(2,1)} %own_ref.3) | copy-start | bytes 9437188
  0.8 40.0 %slice-start.1 = ((s8[6291456]{0:T(1024)(128)(4,1)}), s8[2097152]{0:T(1024)(128)(4,1)S(1)}, s32[]{:S(2)}) async-start(s8[6291456]{0:T(1024)(128)(4,1)} %bitcast.27), calls=%async_computation.3 | async-start | bytes 4194304
  6.8 32.7 %copy-start.4 = (f32[384]{0:T(512)S(1)}, f32[384]{0:T(512)}, u32[]{:S(2)}) copy-start(f32[384]{0:T(512)} %param.11) | copy-start | bytes 4612
  31.2 9.7 %collective-permute-start.4 = (bf16[384,4096]{1,0:T(8,128)(2,1)S(1)}, bf16[384,4096]{1,0:T(8,128)(2,1)S(1)}, u32[]{:S(2)}, u32[]{:S(2)}) collective-permute-start(bf16[384,4096]{1,0:T(8,128)(2,1)S(1)} %copy-done), channel_id=1, source_target_pairs={{0,1},{1,0},{2,3},{3,2},{4,5},{5,4},{6,7},{7,6},{8,9},{9,8},{10,11... | collective-permute-start | bytes 9437192 | tf_op jit(solution)/shard_map/ppermute | solution.py:32
  31.2 5.3 %collective-permute-start.3 = (f32[2,640]{1,0:T(2,128)S(1)}, f32[2,640]{1,0:T(2,128)S(1)}, u32[]{:S(2)}, u32[]{:S(2)}) collective-permute-start(f32[2,640]{1,0:T(2,128)S(1)} %merge_stats.1.s0), channel_id=1, source_target_pairs={{0,192},{64,0},{128,64},{192,128},{1,193},{65,1},{129,65},{193,129... | collective-permute-start | bytes 15368 | tf_op jit(solution)/shard_map/ppermute | solution.py:32
  34.3 4.8 %collective-permute-start.2 = (f32[2,640]{1,0:T(2,128)S(1)}, f32[2,640]{1,0:T(2,128)S(1)}, u32[]{:S(2)}, u32[]{:S(2)}) collective-permute-start(f32[2,640]{1,0:T(2,128)S(1)} %merge_stats.1.s0), channel_id=1, source_target_pairs={{0,64},{64,128},{128,192},{192,0},{1,65},{65,129},{129,193},{193,1... | collective-permute-start | bytes 15368 | tf_op jit(solution)/shard_map/ppermute | solution.py:32
  34.3 5.1 %collective-permute-start.1 = (f32[2,640]{1,0:T(2,128)S(1)}, f32[2,640]{1,0:T(2,128)S(1)}, u32[]{:S(2)}, u32[]{:S(2)}) collective-permute-start(f32[2,640]{1,0:T(2,128)S(1)} %merge_stats.1.s0), channel_id=1, source_target_pairs={{0,128},{64,192},{128,0},{192,64},{1,129},{65,193},{129,1},{193,65... | collective-permute-start | bytes 15368 | tf_op jit(solution)/shard_map/ppermute | solution.py:32
  43.6 13.3 %collective-permute-start.5 = (f16[4,8,32,384]{3,2,1,0:T(8,128)(2,1)S(1)}, f16[4,8,32,384]{3,2,1,0:T(8,128)(2,1)S(1)}, u32[]{:S(2)}, u32[]{:S(2)}) collective-permute-start(f16[4,8,32,384]{3,2,1,0:T(8,128)(2,1)S(1)} %get-tuple-element.32), channel_id=1, source_target_pairs={{0,2},{1,65},{2,4},{3,67},{4,6},{5,69},{6,0},{7,71},{8,10},{9,73},... | collective-permute-start | bytes 2359304 | tf_op jit(solution)/shard_map/ppermute | solution.py:44
  44.3 12.7 %collective-permute-start.6 = (f16[4,8,32,384]{3,2,1,0:T(8,128)(2,1)S(1)}, f16[4,8,32,384]{3,2,1,0:T(8,128)(2,1)S(1)}, u32[]{:S(2)}, u32[]{:S(2)}) collective-permute-start(f16[4,8,32,384]{3,2,1,0:T(8,128)(2,1)S(1)} %get-tuple-element.33), channel_id=1, source_target_pairs={{0,6},{1,193},{2,0},{3,195},{4,2},{5,197},{6,4},{7,199},{8,14},{9,... | collective-permute-start | bytes 2359304 | tf_op jit(solution)/shard_map/ppermute | solution.py:44
  47.0 2.3 %collective-permute-start.7 = (bf16[400,768]{1,0:T(8,128)(2,1)S(1)}, bf16[400,768]{1,0:T(8,128)(2,1)S(1)}, u32[]{:S(2)}, u32[]{:S(2)}) collective-permute-start(bf16[400,768]{1,0:T(8,128)(2,1)S(1)} %grad_logits.1.g_ref.g_own_ref), channel_id=1, source_target_pairs={{0,1},{1,0},{2,3},{3,2},{4,5},{5,4},{6,7},{7,6},{8,9},{9,8},{10,11... | collective-permute-start | bytes 1843208 | tf_op jit(solution)/shard_map/ppermute | solution.py:32
  57.1 8.6 %collective-permute-start.9 = (f16[2,8,32,384]{3,2,1,0:T(8,128)(2,1)S(1)}, f16[2,8,32,384]{3,2,1,0:T(8,128)(2,1)S(1)}, u32[]{:S(2)}, u32[]{:S(2)}) collective-permute-start(f16[2,8,32,384]{3,2,1,0:T(8,128)(2,1)S(1)} %multiply_convert_fusion.2), channel_id=1, source_target_pairs={{0,6},{1,193},{2,0},{3,195},{4,2},{5,197},{6,4},{7,199},{8,14},{9,... | collective-permute-start | bytes 1179656 | tf_op jit(solution)/shard_map/ppermute | solution.py:44
  60.6 9.1 %collective-permute-start.8 = (f16[2,8,32,384]{3,2,1,0:T(8,128)(2,1)S(1)}, f16[2,8,32,384]{3,2,1,0:T(8,128)(2,1)S(1)}, u32[]{:S(2)}, u32[]{:S(2)}) collective-permute-start(f16[2,8,32,384]{3,2,1,0:T(8,128)(2,1)S(1)} %multiply_convert_fusion.3), channel_id=1, source_target_pairs={{0,2},{1,65},{2,4},{3,67},{4,6},{5,69},{6,0},{7,71},{8,10},{9,73},... | collective-permute-start | bytes 1179656 | tf_op jit(solution)/shard_map/ppermute | solution.py:44
  70.2 11.2 %collective-permute-start.11 = (f16[8,32,384]{2,1,0:T(8,128)(2,1)S(1)}, f16[8,32,384]{2,1,0:T(8,128)(2,1)S(1)}, u32[]{:S(2)}, u32[]{:S(2)}) collective-permute-start(f16[8,32,384]{2,1,0:T(8,128)(2,1)S(1)} %fusion.7), channel_id=1, source_target_pairs={{0,64},{1,3},{2,66},{3,5},{4,68},{5,7},{6,70},{7,1},{8,72},{9,11},... | collective-permute-start | bytes 589832 | tf_op jit(solution)/shard_map/ppermute | solution.py:44
  71.0 13.9 %collective-permute-start.10 = (f16[8,32,384]{2,1,0:T(8,128)(2,1)S(1)}, f16[8,32,384]{2,1,0:T(8,128)(2,1)S(1)}, u32[]{:S(2)}, u32[]{:S(2)}) collective-permute-start(f16[8,32,384]{2,1,0:T(8,128)(2,1)S(1)} %get-tuple-element.47), channel_id=1, source_target_pairs={{0,128},{1,5},{2,130},{3,7},{4,132},{5,1},{6,134},{7,3},{8,136},{9... | collective-permute-start | bytes 589832 | tf_op jit(solution)/shard_map/ppermute | solution.py:44
  79.2 5.8 %collective-permute-start.12 = (f16[8,32,384]{2,1,0:T(8,128)(2,1)S(1)}, f16[8,32,384]{2,1,0:T(8,128)(2,1)S(1)}, u32[]{:S(2)}, u32[]{:S(2)}) collective-permute-start(f16[8,32,384]{2,1,0:T(8,128)(2,1)S(1)} %get-tuple-element.48), channel_id=1, source_target_pairs={{0,192},{1,7},{2,194},{3,1},{4,196},{5,3},{6,198},{7,5},{8,200},{9... | collective-permute-start | bytes 589832 | tf_op jit(solution)/shard_map/ppermute | solution.py:44

commit v7 on v6

--- a/solution.py
+++ b/solution.py
@@ -245,8 +245,8 @@
     )(pos, logits, teacher, ids, scale, *parts)
 
 
-SENT = (((2, 0), (2, 1), (1, 2), (1, 3)), ((2, 2), (2, 3), (3, 0), (3, 1)))
-KEPT = (((1, 0), (1, 1)), ((3, 2), (3, 3)), ((0, 0), (0, 1), (0, 2), (0, 3)))
+SENT = tuple(tuple((far, near) for near in range(4)) for far in (2, 1, 3))
+KEPT = (tuple((0, near) for near in range(4)),)
 
 
 def hidden_kernel(groups, pos_ref, w_ref, g_ref, *outs):
@@ -355,22 +355,20 @@
     def taken(value):
         return value.astype(F32) * (1.0 / SEND_SCALE)
 
-    up, down = (coded(v) for v in hidden_part(pos, head5, g, SENT))
-    up, down, g = lax.optimization_barrier((up, down, g))
-    up, down = shift_by_core(up, 1, True), shift_by_core(down, -1, True)
+    def exchange(chunks, first):
+        return [shift_by_core(v, d, first) for v, d in zip(chunks, (2, 1, 3))]
+
+    sent = [coded(v) for v in hidden_part(pos, head5, g, SENT)]
+    *sent, g = lax.optimization_barrier((*sent, g))
+    got = exchange(sent, True)
     g_oth = shift(g, "c", 1)
-    c1, c3, c0 = hidden_part(pos, head5, g, KEPT)
+    (own,) = hidden_part(pos, head5, g, KEPT)
     head_out, loss = head_grad(pos, hidden, hidden_oth, g, g_oth)
     loss = loss[0, :1]
-    up, down, loss, head_out = lax.optimization_barrier((up, down, loss, head_out))
-
-    up2 = shift_by_core(coded(c1 + taken(up[:2])), 1, True)
-    down2 = shift_by_core(coded(c3 + taken(down[:2])), -1, True)
-    low = c0[:2] + taken(down[2:]) + taken(up2)
-    high = c0[2:] + taken(up[2:]) + taken(down2)
-
-    far = [shift_by_core(coded(v), d, False) for d, v in ((2, high[0]), (1, low[1]), (3, high[1]))]
-    both = coded(low[0] + sum(taken(v) for v in far))
+    *got, loss, head_out = lax.optimization_barrier((*got, loss, head_out))
+    total = own + sum(taken(v) for v in got)
+    got = exchange([coded(total[d]) for d in (2, 1, 3)], False)
+    both = coded(total[0] + sum(taken(v) for v in got))
     both = lax.all_to_all(both, "z", 0, 0, tiled=True)
     hidden_grad = jnp.sum(taken(both), axis=0).T.astype(BF16)
     return loss, hidden_grad, head_out

time: 98.2 us -> 90.8 us (0.925)
  starting transfers between devices: 21.1 us -> 14.1 us
    ppermute x7 -> x6, starting transfers between devices: 15.7 us -> 8.61 us  [shift_by_core(): return lax.ppermute(a, axes, pairs)]
    ppermute x7 -> x6, waiting for transfers between devices: 17.4 us -> 16.7 us  [shift_by_core(): return lax.ppermute(a, axes, pairs)]
  transfers between devices with their start and end apart: 13 -> 12, of which waited for: 7 -> 8; matrix products, arithmetic and copies ran while one was open for 0% -> 0% of each run, Pallas kernels for 15% -> 15%
where the time goes in v7:
time: 90.8 us; the launch traced here: 90.2 us
  blocking collectives  33.6 us (37%)
  waiting for transfers between devices  20.1 us (22%)
  Pallas kernels  19.3 us (21%)
  starting transfers between devices  14.1 us (16%)
  other arithmetic  2.12 us (2%)
    all_to_all x1, blocking collectives, body(): stats = merge_stats(lax.all_to_all(stats, ('z', 'x'), 0, 0, tiled=True))  21.9 us
    ppermute x6, waiting for transfers between devices, shift_by_core(): return lax.ppermute(a, axes, pairs)  16.7 us
    all_to_all x1, blocking collectives, body(): both = lax.all_to_all(both, 'z', 0, 0, tiled=True)  11.8 us
    ppermute x6, starting transfers between devices, shift_by_core(): return lax.ppermute(a, axes, pairs)  8.61 us
    pallas_call x1, Pallas kernels, student_logits(): pl.pallas_call(functools.partial(logits_kernel, steps), out_shape=jax.Sha...  5.91 us
    ppermute x6, starting transfers between devices, shift(): return lax.ppermute(a, axis, [(i, (i + by) % n) for i in range(n)])  5.44 us
    pallas_call x1, Pallas kernels, head_grad(): pl.pallas_call(head_kernel, out_shape=(jax.ShapeDtypeStruct((width, cols)...  4.91 us
    pallas_call x2, Pallas kernels, hidden_part(): pl.pallas_call(functools.partial(hidden_kernel, groups), out_shape=out_sh...  4.68 us
  transfers between devices with their start and end apart: 12, of which 8 were waited for; matrix products, arithmetic and copies ran while one was open for 0% of the time, Pallas kernels for 15%

profile of v7, /device:TPU:32, one launch (start us, length us, event | category | flops | bytes accessed | tf_op | source)
XLA Modules:
  0.0 90.2 jit_solution(15025672220128701177)
XLA Ops:
  0.6 0.1 collective-permute-start
  0.7 0.0 slice-start
  0.8 0.1 pad_add_fusion.pos_ref
  0.8 0.0 slice-start.1
  0.9 5.9 %student_logits.1.l_ref = f32[384,768]{1,0:T(8,128)S(1)} custom-call(bf16[384,4096]{1,0:T(8,128)(2,1)} %own_ref.3, bf16[4096,768]{1,0:T(8,128)(2,1)} %w_ref.1), custom_call_target="tpu_custom_call" | custom-call | flops 2415919104 | bytes 10616832 | tf_op jit(solution)/shard_map/student_logits/pallas_call | solution.py:75
  6.8 0.0 copy-start.4
  6.8 0.0 collective-permute-done.oth_ref
  6.8 0.0 copy-done.1
  6.8 0.0 copy-done.2
  6.8 0.0 copy-done.3
  6.8 2.3 %local_stats.1 = (f32[2,640]{1,0:T(2,128)S(1)}, bf16[384,768]{1,0:T(8,128)(2,1)S(1)}) custom-call(s32[4]{0:T(128)S(1)} %pad_add_fusion.pos_ref, f32[384,768]{1,0:T(8,128)S(1)} %student_logits.1.l_ref, bf16[768,384]{1,0:T(8,128)(2,1)S(1)} %copy-done.1, bf16[768,384]{1,0:T(8,128)(2,1)S(1)} %collective-permute-done.oth_ref, s32[6,128]{1,0:T(8,128)S(1)} %bitcast.33, ...), custom_call_target="tpu_custom_call" | custom-call | flops 452984832 | bytes 2949120 | tf_op jit(solution)/shard_map/local_stats/pallas_call | solution.py:190
  9.1 0.1 broadcast_in_dim.2
  9.1 21.9 %all_to_all.10.in_ref = f32[32,2,640]{2,1,0:T(2,128)S(1)} all-to-all(f32[32,2,640]{2,1,0:T(2,128)S(1)} %broadcast_in_dim.2), channel_id=1, replica_groups=mesh['y'=4,'z'=8,'x'=4,'c'=2] {'z','x'}, dimensions={0} | all-to-all | bytes 327680 | tf_op jit(solution)/shard_map/all_to_all | solution.py:345
  31.0 0.2 merge_stats.1.s0
  31.2 0.0 copy-done
  31.2 0.0 collective-permute-start.4
  31.2 3.1 %collective-permute-start.3 = (f32[2,640]{1,0:T(2,128)S(1)}, f32[2,640]{1,0:T(2,128)S(1)}, u32[]{:S(2)}, u32[]{:S(2)}) collective-permute-start(f32[2,640]{1,0:T(2,128)S(1)} %merge_stats.1.s0), channel_id=1, source_target_pairs={{0,192},{64,0},{128,64},{192,128},{1,193},{65,1},{129,65},{193,129... | collective-permute-start | bytes 15368 | tf_op jit(solution)/shard_map/ppermute | solution.py:32
  34.3 0.0 collective-permute-start.2
  34.3 2.2 %collective-permute-start.1 = (f32[2,640]{1,0:T(2,128)S(1)}, f32[2,640]{1,0:T(2,128)S(1)}, u32[]{:S(2)}, u32[]{:S(2)}) collective-permute-start(f32[2,640]{1,0:T(2,128)S(1)} %merge_stats.1.s0), channel_id=1, source_target_pairs={{0,128},{64,192},{128,0},{192,64},{1,129},{65,193},{129,1},{193,65... | collective-permute-start | bytes 15368 | tf_op jit(solution)/shard_map/ppermute | solution.py:32
  36.5 0.0 collective-permute-done.3.s3
  36.5 2.6 %collective-permute-done.2.s2 = f32[2,640]{1,0:T(2,128)S(1)} collective-permute-done((f32[2,640]{1,0:T(2,128)S(1)}, f32[2,640]{1,0:T(2,128)S(1)}, u32[]{:S(2)}, u32[]{:S(2)}) %collective-permute-start.2) | collective-permute-done | bytes 5152 | tf_op jit(solution)/shard_map/ppermute | solution.py:32
  39.2 0.3 collective-permute-done.1.s1
  39.5 1.4 %grad_logits.1.g_ref.g_own_ref = bf16[400,768]{1,0:T(8,128)(2,1)S(1)} custom-call(s32[4]{0:T(128)S(1)} %pad_add_fusion.pos_ref, f32[384,768]{1,0:T(8,128)S(1)} %student_logits.1.l_ref, bf16[384,768]{1,0:T(8,128)(2,1)S(1)} %get-tuple-element.24.t_ref, s32[3,128]{1,0:T(4,128)S(1)} %bitcast.32, f32[3,128]{1,0:T(4,128)S(1)} %bitcast.34, ...), custom_call_target="tpu_custom_call" | custom-call | flops 2359296 | bytes 2359296 | tf_op jit(solution)/shard_map/grad_logits/pallas_call | solution.py:233
  40.9 0.0 collective-permute-done.4.oth_ref
  40.9 3.1 %hidden_part.2 = (f32[4,8,32,384]{3,2,1,0:T(8,128)S(1)}, f32[4,8,32,384]{3,2,1,0:T(8,128)S(1)}, f32[4,8,32,384]{3,2,1,0:T(8,128)S(1)}) custom-call(s32[4]{0:T(128)S(1)} %pad_add_fusion.pos_ref, bf16[4,8,4,32,768]{4,3,2,1,0:T(8,128)(2,1)S(1)} %bitcast.29, bf16[400,768]{1,0:T(8,128)(2,1)S(1)} %grad_logits.1.g_ref.g_own_ref), custom_call_target="tpu_custom_call" | custom-call | flops 1 | bytes 1 | tf_op jit(solution)/shard_map/hidden_part/pallas_call | solution.py:273
  44.0 0.2 multiply_convert_fusion.2
  44.2 0.4 multiply_convert_fusion
  44.7 1.1 %collective-permute-start.5 = (f16[4,8,32,384]{3,2,1,0:T(8,128)(2,1)S(1)}, f16[4,8,32,384]{3,2,1,0:T(8,128)(2,1)S(1)}, u32[]{:S(2)}, u32[]{:S(2)}) collective-permute-start(f16[4,8,32,384]{3,2,1,0:T(8,128)(2,1)S(1)} %multiply_convert_fusion.2), channel_id=1, source_target_pairs={{0,4},{1,129},{2,6},{3,131},{4,0},{5,133},{6,2},{7,135},{8,12},{9,... | collective-permute-start | bytes 2359304 | tf_op jit(solution)/shard_map/ppermute | solution.py:44
  45.7 1.1 %collective-permute-start.6 = (f16[4,8,32,384]{3,2,1,0:T(8,128)(2,1)S(1)}, f16[4,8,32,384]{3,2,1,0:T(8,128)(2,1)S(1)}, u32[]{:S(2)}, u32[]{:S(2)}) collective-permute-start(f16[4,8,32,384]{3,2,1,0:T(8,128)(2,1)S(1)} %get-tuple-element.34), channel_id=1, source_target_pairs={{0,2},{1,65},{2,4},{3,67},{4,6},{5,69},{6,0},{7,71},{8,10},{9,73},... | collective-permute-start | bytes 2359304 | tf_op jit(solution)/shard_map/ppermute | solution.py:44
  46.8 2.2 %collective-permute-start.7 = (f16[4,8,32,384]{3,2,1,0:T(8,128)(2,1)S(1)}, f16[4,8,32,384]{3,2,1,0:T(8,128)(2,1)S(1)}, u32[]{:S(2)}, u32[]{:S(2)}) collective-permute-start(f16[4,8,32,384]{3,2,1,0:T(8,128)(2,1)S(1)} %get-tuple-element.35), channel_id=1, source_target_pairs={{0,6},{1,193},{2,0},{3,195},{4,2},{5,197},{6,4},{7,199},{8,14},{9,... | collective-permute-start | bytes 2359304 | tf_op jit(solution)/shard_map/ppermute | solution.py:44
  49.0 0.0 collective-permute-start.8
  49.0 1.5 %hidden_part.3 = f32[4,8,32,384]{3,2,1,0:T(8,128)S(1)} custom-call(s32[4]{0:T(128)S(1)} %pad_add_fusion.pos_ref, bf16[4,8,4,32,768]{4,3,2,1,0:T(8,128)(2,1)S(1)} %bitcast.30, bf16[400,768]{1,0:T(8,128)(2,1)S(1)} %grad_logits.1.g_ref.g_own_ref), custom_call_target="tpu_custom_call" | custom-call | flops 1 | bytes 1 | tf_op jit(solution)/shard_map/hidden_part/pallas_call | solution.py:273
  50.5 0.5 collective-permute-done.8.g_oth_ref
  51.0 4.9 %head_grad.1 = (bf16[2048,768]{1,0:T(8,128)(2,1)}, f32[1,128]{1,0:T(1,128)}) custom-call(s32[4]{0:T(128)S(1)} %pad_add_fusion.pos_ref, bf16[384,4096]{1,0:T(8,128)(2,1)S(1)} %copy-done, bf16[384,4096]{1,0:T(8,128)(2,1)S(1)} %collective-permute-done.4.oth_ref, bf16[400,768]{1,0:T(8,128)(2,1)S(1)} %grad_logits.1.g_ref.g_own_ref, ...), custom_call_target="tpu_custom_call" | custom-call | flops 1 | bytes 1 | tf_op jit(solution)/shard_map/head_grad/pallas_call | solution.py:311
  55.9 2.4 %collective-permute-done.5 = f16[4,8,32,384]{3,2,1,0:T(8,128)(2,1)S(1)} collective-permute-done((f16[4,8,32,384]{3,2,1,0:T(8,128)(2,1)S(1)}, f16[4,8,32,384]{3,2,1,0:T(8,128)(2,1)S(1)}, u32[]{:S(2)}, u32[]{:S(2)}) %collective-permute-start.5) | collective-permute-done | bytes 786464 | tf_op jit(solution)/shard_map/ppermute | solution.py:44
  58.3 8.3 %collective-permute-done.6 = f16[4,8,32,384]{3,2,1,0:T(8,128)(2,1)S(1)} collective-permute-done((f16[4,8,32,384]{3,2,1,0:T(8,128)(2,1)S(1)}, f16[4,8,32,384]{3,2,1,0:T(8,128)(2,1)S(1)}, u32[]{:S(2)}, u32[]{:S(2)}) %collective-permute-start.6) | collective-permute-done | bytes 786464 | tf_op jit(solution)/shard_map/ppermute | solution.py:44
  66.7 0.0 collective-permute-done.7
  66.7 0.5 multiply_add_fusion
  67.2 0.1 fusion.6
  67.3 2.3 %collective-permute-start.9 = (f16[8,32,384]{2,1,0:T(8,128)(2,1)S(1)}, f16[8,32,384]{2,1,0:T(8,128)(2,1)S(1)}, u32[]{:S(2)}, u32[]{:S(2)}) collective-permute-start(f16[8,32,384]{2,1,0:T(8,128)(2,1)S(1)} %get-tuple-element.45), channel_id=1, source_target_pairs={{0,128},{1,5},{2,130},{3,7},{4,132},{5,1},{6,134},{7,3},{8,136},{9... | collective-permute-start | bytes 589832 | tf_op jit(solution)/shard_map/ppermute | solution.py:44
  69.6 1.1 %collective-permute-start.11 = (f16[8,32,384]{2,1,0:T(8,128)(2,1)S(1)}, f16[8,32,384]{2,1,0:T(8,128)(2,1)S(1)}, u32[]{:S(2)}, u32[]{:S(2)}) collective-permute-start(f16[8,32,384]{2,1,0:T(8,128)(2,1)S(1)} %get-tuple-element.46), channel_id=1, source_target_pairs={{0,192},{1,7},{2,194},{3,1},{4,196},{5,3},{6,198},{7,5},{8,200},{9... | collective-permute-start | bytes 589832 | tf_op jit(solution)/shard_map/ppermute | solution.py:44
  70.7 0.9 %collective-permute-start.10 = (f16[8,32,384]{2,1,0:T(8,128)(2,1)S(1)}, f16[8,32,384]{2,1,0:T(8,128)(2,1)S(1)}, u32[]{:S(2)}, u32[]{:S(2)}) collective-permute-start(f16[8,32,384]{2,1,0:T(8,128)(2,1)S(1)} %get-tuple-element.47), channel_id=1, source_target_pairs={{0,64},{1,3},{2,66},{3,5},{4,68},{5,7},{6,70},{7,1},{8,72},{9,11},... | collective-permute-start | bytes 589832 | tf_op jit(solution)/shard_map/ppermute | solution.py:44
  71.6 2.9 %collective-permute-done.9 = f16[8,32,384]{2,1,0:T(8,128)(2,1)S(1)} collective-permute-done((f16[8,32,384]{2,1,0:T(8,128)(2,1)S(1)}, f16[8,32,384]{2,1,0:T(8,128)(2,1)S(1)}, u32[]{:S(2)}, u32[]{:S(2)}) %collective-permute-start.9) | collective-permute-done | bytes 196640 | tf_op jit(solution)/shard_map/ppermute | solution.py:44
  74.6 2.7 %collective-permute-done.11 = f16[8,32,384]{2,1,0:T(8,128)(2,1)S(1)} collective-permute-done((f16[8,32,384]{2,1,0:T(8,128)(2,1)S(1)}, f16[8,32,384]{2,1,0:T(8,128)(2,1)S(1)}, u32[]{:S(2)}, u32[]{:S(2)}) %collective-permute-start.11) | collective-permute-done | bytes 196640 | tf_op jit(solution)/shard_map/ppermute | solution.py:44
  77.3 0.3 collective-permute-done.10
  77.6 0.1 fusion.5
  77.8 11.8 %all_to_all.11 = f16[8,32,384]{2,1,0:T(8,128)(2,1)S(1)} all-to-all(f16[8,32,384]{2,1,0:T(8,128)(2,1)S(1)} %fusion.5), channel_id=1, replica_groups=mesh['y'=4,'z'=8,'x'=4,'c'=2] {'z'}, dimensions={0} | all-to-all | bytes 393216 | tf_op jit(solution)/shard_map/all_to_all | solution.py:372
  89.5 0.7 multiply_reduce_fusion
  (8 shorter events, 0.0 us)
Async XLA Ops:
  0.6 6.2 %collective-permute-start = (bf16[768,384]{1,0:T(8,128)(2,1)}, bf16[768,384]{1,0:T(8,128)(2,1)S(1)}, u32[]{:S(2)}, u32[]{:S(2)}) collective-permute-start(bf16[768,384]{1,0:T(8,128)(2,1)} %own_ref.2), channel_id=1, source_target_pairs={{0,1},{1,0},{2,3},{3,2},{4,5},{5,4},{6,7},{7,6},{8,9},{9,8},{10,11... | collective-permute-start | bytes 1769480 | tf_op jit(solution)/shard_map/ppermute | solution.py:32
  0.7 40.1 %slice-start = ((s8[6291456]{0:T(1024)(128)(4,1)}), s8[4194304]{0:T(1024)(128)(4,1)S(1)}, s32[]{:S(2)}) async-start(s8[6291456]{0:T(1024)(128)(4,1)} %bitcast.27), calls=%async_computation.2 | async-start | bytes 8388608
  0.8 6.0 %copy-start.1 = (bf16[768,384]{1,0:T(8,128)(2,1)S(1)}, bf16[768,384]{1,0:T(8,128)(2,1)}, u32[]{:S(2)}) copy-start(bf16[768,384]{1,0:T(8,128)(2,1)} %own_ref.2) | copy-start | bytes 1769476
  0.8 6.0 %copy-start.2 = (s32[384]{0:T(512)S(1)}, s32[384]{0:T(512)}, u32[]{:S(2)}) copy-start(s32[384]{0:T(512)} %param.9) | copy-start | bytes 4612
  0.8 6.0 %copy-start.3 = (s32[768]{0:T(1024)S(1)}, s32[768]{0:T(1024)}, u32[]{:S(2)}) copy-start(s32[768]{0:T(1024)} %param.10) | copy-start | bytes 9220
  0.8 30.3 %copy-start = (bf16[384,4096]{1,0:T(8,128)(2,1)S(1)}, bf16[384,4096]{1,0:T(8,128)(2,1)}, u32[]{:S(2)}) copy-start(bf16[384,4096]{1,0:T(8,128)(2,1)} %own_ref.3) | copy-start | bytes 9437188
  0.8 40.0 %slice-start.1 = ((s8[6291456]{0:T(1024)(128)(4,1)}), s8[2097152]{0:T(1024)(128)(4,1)S(1)}, s32[]{:S(2)}) async-start(s8[6291456]{0:T(1024)(128)(4,1)} %bitcast.27), calls=%async_computation.3 | async-start | bytes 4194304
  6.8 32.7 %copy-start.4 = (f32[384]{0:T(512)S(1)}, f32[384]{0:T(512)}, u32[]{:S(2)}) copy-start(f32[384]{0:T(512)} %param.11) | copy-start | bytes 4612
  31.2 9.7 %collective-permute-start.4 = (bf16[384,4096]{1,0:T(8,128)(2,1)S(1)}, bf16[384,4096]{1,0:T(8,128)(2,1)S(1)}, u32[]{:S(2)}, u32[]{:S(2)}) collective-permute-start(bf16[384,4096]{1,0:T(8,128)(2,1)S(1)} %copy-done), channel_id=1, source_target_pairs={{0,1},{1,0},{2,3},{3,2},{4,5},{5,4},{6,7},{7,6},{8,9},{9,8},{10,11... | collective-permute-start | bytes 9437192 | tf_op jit(solution)/shard_map/ppermute | solution.py:32
  31.2 5.3 %collective-permute-start.3 = (f32[2,640]{1,0:T(2,128)S(1)}, f32[2,640]{1,0:T(2,128)S(1)}, u32[]{:S(2)}, u32[]{:S(2)}) collective-permute-start(f32[2,640]{1,0:T(2,128)S(1)} %merge_stats.1.s0), channel_id=1, source_target_pairs={{0,192},{64,0},{128,64},{192,128},{1,193},{65,1},{129,65},{193,129... | collective-permute-start | bytes 15368 | tf_op jit(solution)/shard_map/ppermute | solution.py:32
  34.3 4.8 %collective-permute-start.2 = (f32[2,640]{1,0:T(2,128)S(1)}, f32[2,640]{1,0:T(2,128)S(1)}, u32[]{:S(2)}, u32[]{:S(2)}) collective-permute-start(f32[2,640]{1,0:T(2,128)S(1)} %merge_stats.1.s0), channel_id=1, source_target_pairs={{0,64},{64,128},{128,192},{192,0},{1,65},{65,129},{129,193},{193,1... | collective-permute-start | bytes 15368 | tf_op jit(solution)/shard_map/ppermute | solution.py:32
  34.3 5.1 %collective-permute-start.1 = (f32[2,640]{1,0:T(2,128)S(1)}, f32[2,640]{1,0:T(2,128)S(1)}, u32[]{:S(2)}, u32[]{:S(2)}) collective-permute-start(f32[2,640]{1,0:T(2,128)S(1)} %merge_stats.1.s0), channel_id=1, source_target_pairs={{0,128},{64,192},{128,0},{192,64},{1,129},{65,193},{129,1},{193,65... | collective-permute-start | bytes 15368 | tf_op jit(solution)/shard_map/ppermute | solution.py:32
  44.7 13.7 %collective-permute-start.5 = (f16[4,8,32,384]{3,2,1,0:T(8,128)(2,1)S(1)}, f16[4,8,32,384]{3,2,1,0:T(8,128)(2,1)S(1)}, u32[]{:S(2)}, u32[]{:S(2)}) collective-permute-start(f16[4,8,32,384]{3,2,1,0:T(8,128)(2,1)S(1)} %multiply_convert_fusion.2), channel_id=1, source_target_pairs={{0,4},{1,129},{2,6},{3,131},{4,0},{5,133},{6,2},{7,135},{8,12},{9,... | collective-permute-start | bytes 2359304 | tf_op jit(solution)/shard_map/ppermute | solution.py:44
  45.7 20.9 %collective-permute-start.6 = (f16[4,8,32,384]{3,2,1,0:T(8,128)(2,1)S(1)}, f16[4,8,32,384]{3,2,1,0:T(8,128)(2,1)S(1)}, u32[]{:S(2)}, u32[]{:S(2)}) collective-permute-start(f16[4,8,32,384]{3,2,1,0:T(8,128)(2,1)S(1)} %get-tuple-element.34), channel_id=1, source_target_pairs={{0,2},{1,65},{2,4},{3,67},{4,6},{5,69},{6,0},{7,71},{8,10},{9,73},... | collective-permute-start | bytes 2359304 | tf_op jit(solution)/shard_map/ppermute | solution.py:44
  46.8 19.9 %collective-permute-start.7 = (f16[4,8,32,384]{3,2,1,0:T(8,128)(2,1)S(1)}, f16[4,8,32,384]{3,2,1,0:T(8,128)(2,1)S(1)}, u32[]{:S(2)}, u32[]{:S(2)}) collective-permute-start(f16[4,8,32,384]{3,2,1,0:T(8,128)(2,1)S(1)} %get-tuple-element.35), channel_id=1, source_target_pairs={{0,6},{1,193},{2,0},{3,195},{4,2},{5,197},{6,4},{7,199},{8,14},{9,... | collective-permute-start | bytes 2359304 | tf_op jit(solution)/shard_map/ppermute | solution.py:44
  49.0 2.0 %collective-permute-start.8 = (bf16[400,768]{1,0:T(8,128)(2,1)S(1)}, bf16[400,768]{1,0:T(8,128)(2,1)S(1)}, u32[]{:S(2)}, u32[]{:S(2)}) collective-permute-start(bf16[400,768]{1,0:T(8,128)(2,1)S(1)} %grad_logits.1.g_ref.g_own_ref), channel_id=1, source_target_pairs={{0,1},{1,0},{2,3},{3,2},{4,5},{5,4},{6,7},{7,6},{8,9},{9,8},{10,11... | collective-permute-start | bytes 1843208 | tf_op jit(solution)/shard_map/ppermute | solution.py:32
  67.3 7.3 %collective-permute-start.9 = (f16[8,32,384]{2,1,0:T(8,128)(2,1)S(1)}, f16[8,32,384]{2,1,0:T(8,128)(2,1)S(1)}, u32[]{:S(2)}, u32[]{:S(2)}) collective-permute-start(f16[8,32,384]{2,1,0:T(8,128)(2,1)S(1)} %get-tuple-element.45), channel_id=1, source_target_pairs={{0,128},{1,5},{2,130},{3,7},{4,132},{5,1},{6,134},{7,3},{8,136},{9... | collective-permute-start | bytes 589832 | tf_op jit(solution)/shard_map/ppermute | solution.py:44
  69.6 7.7 %collective-permute-start.11 = (f16[8,32,384]{2,1,0:T(8,128)(2,1)S(1)}, f16[8,32,384]{2,1,0:T(8,128)(2,1)S(1)}, u32[]{:S(2)}, u32[]{:S(2)}) collective-permute-start(f16[8,32,384]{2,1,0:T(8,128)(2,1)S(1)} %get-tuple-element.46), channel_id=1, source_target_pairs={{0,192},{1,7},{2,194},{3,1},{4,196},{5,3},{6,198},{7,5},{8,200},{9... | collective-permute-start | bytes 589832 | tf_op jit(solution)/shard_map/ppermute | solution.py:44
  70.7 6.9 %collective-permute-start.10 = (f16[8,32,384]{2,1,0:T(8,128)(2,1)S(1)}, f16[8,32,384]{2,1,0:T(8,128)(2,1)S(1)}, u32[]{:S(2)}, u32[]{:S(2)}) collective-permute-start(f16[8,32,384]{2,1,0:T(8,128)(2,1)S(1)} %get-tuple-element.47), channel_id=1, source_target_pairs={{0,64},{1,3},{2,66},{3,5},{4,68},{5,7},{6,70},{7,1},{8,72},{9,11},... | collective-permute-start | bytes 589832 | tf_op jit(solution)/shard_map/ppermute | solution.py:44

commit v8 on v7

--- a/solution.py
+++ b/solution.py
@@ -205,7 +205,48 @@
     )(pos, logits, own, oth, assign, ids)
 
 
-def grad_kernel(pos_ref, l_ref, t_ref, ids_ref, scale_ref, s0, s1, s2, s3, g_ref):
+def chunk(far):
+    return tuple((far, near) for near in range(4))
+
+
+def hidden_product(groups, pos_ref, w_ref, g, outs):
+    ny, nz, nx, sub, cols = w_ref.shape
+    x_first, y, x = pos_ref[0] == 0, pos_ref[2], pos_ref[3]
+
+    def block(far, near):
+        dx = jnp.where(x_first, far, near)
+        dy = jnp.where(x_first, near, far)
+        w = w_ref[lax.rem(y + dy, ny), :, lax.rem(x + dx, nx)]
+        return w.reshape(nz * sub, cols)
+
+    for names, out in zip(groups, outs):
+        w = jnp.concatenate([block(*name) for name in names], axis=0)
+        product = lax.dot_general(w, g, (((1,), (1,)), ((), ())), preferred_element_type=F32)
+        out[...] = product.reshape(out.shape)
+
+
+def hidden_kernel(groups, pos_ref, w_ref, g_ref, *outs):
+    hidden_product(groups, pos_ref, w_ref, g_ref[: outs[0].shape[-1], :], outs)
+
+
+def hidden_part(pos, head5, g, groups):
+    nz, sub = head5.shape[1], head5.shape[3]
+    rows = g.shape[0] - LOSS_ROWS
+    out_shape = [jax.ShapeDtypeStruct((len(names), nz, sub, rows), F32) for names in groups]
+    return pl.pallas_call(
+        functools.partial(hidden_kernel, groups),
+        out_shape=out_shape,
+        in_specs=[pl.BlockSpec(memory_space=pltpu.SMEM), WHOLE, WHOLE],
+        out_specs=[WHOLE] * len(out_shape),
+        compiler_params=params(16),
+        cost_estimate=LIGHT,
+        name="hidden_part",
+    )(pos, head5, g)
+
+
+def grad_kernel(
+    pos_ref, l_ref, t_ref, ids_ref, scale_ref, s0, s1, s2, s3, w_ref, g_ref, far_ref
+):
     rows, cols = l_ref.shape
     parts = (s0, s1, s2, s3)
     first, second = (
@@ -225,16 +266,22 @@
     hot = jnp.where(columns.astype(F32) == ids, CE_WEIGHT, 0.0)
     prob_s = jnp.exp(l_ref[...] - norm_s)
     prob_t = jnp.exp(t_ref[...].astype(F32) - norm_t)
-    g_ref[:rows, :] = (scale * ((1.0 + CE_WEIGHT) * prob_s - prob_t - hot)).astype(BF16)
-
-
-def grad_logits(pos, logits, teacher, ids, scale, parts):
+    g = (scale * ((1.0 + CE_WEIGHT) * prob_s - prob_t - hot)).astype(BF16)
+    g_ref[:rows, :] = g
+    hidden_product((chunk(2),), pos_ref, w_ref, g, (far_ref,))
+
+
+def grad_logits(pos, logits, teacher, ids, scale, parts, head5):
     rows, cols = logits.shape
+    _, nz, _, sub, _ = head5.shape
     return pl.pallas_call(
         grad_kernel,
-        out_shape=jax.ShapeDtypeStruct((rows + LOSS_ROWS, cols), BF16),
-        in_specs=[pl.BlockSpec(memory_space=pltpu.SMEM)] + [WHOLE] * 8,
-        out_specs=WHOLE,
+        out_shape=(
+            jax.ShapeDtypeStruct((rows + LOSS_ROWS, cols), BF16),
+            jax.ShapeDtypeStruct((4, nz, sub, rows), F32),
+        ),
+        in_specs=[pl.BlockSpec(memory_space=pltpu.SMEM)] + [WHOLE] * 9,
+        out_specs=(WHOLE, WHOLE),
         compiler_params=params(16),
         cost_estimate=pl.CostEstimate(
             flops=8 * rows * cols,
@@ -242,43 +289,7 @@
             transcendentals=2 * rows * cols,
         ),
         name="grad_logits",
-    )(pos, logits, teacher, ids, scale, *parts)
-
-
-SENT = tuple(tuple((far, near) for near in range(4)) for far in (2, 1, 3))
-KEPT = (tuple((0, near) for near in range(4)),)
-
-
-def hidden_kernel(groups, pos_ref, w_ref, g_ref, *outs):
-    ny, nz, nx, sub, cols = w_ref.shape
-    x_first, y, x = pos_ref[0] == 0, pos_ref[2], pos_ref[3]
-    g = g_ref[: outs[0].shape[-1], :]
-
-    def block(far, near):
-        dx = jnp.where(x_first, far, near)
-        dy = jnp.where(x_first, near, far)
-        w = w_ref[lax.rem(y + dy, ny), :, lax.rem(x + dx, nx)]
-        return w.reshape(nz * sub, cols)
-
-    for names, out in zip(groups, outs):
-        w = jnp.concatenate([block(*name) for name in names], axis=0)
-        product = lax.dot_general(w, g, (((1,), (1,)), ((), ())), preferred_element_type=F32)
-        out[...] = product.reshape(out.shape)
-
-
-def hidden_part(pos, head5, g, groups):
-    nz, sub = head5.shape[1], head5.shape[3]
-    rows = g.shape[0] - LOSS_ROWS
-    out_shape = [jax.ShapeDtypeStruct((len(names), nz, sub, rows), F32) for names in groups]
-    return pl.pallas_call(
-        functools.partial(hidden_kernel, groups),
-        out_shape=out_shape,
-        in_specs=[pl.BlockSpec(memory_space=pltpu.SMEM), WHOLE, WHOLE],
-        out_specs=[WHOLE] * len(out_shape),
-        compiler_params=params(16),
-        cost_estimate=LIGHT,
-        name="hidden_part",
-    )(pos, head5, g)
+    )(pos, logits, teacher, ids, scale, *parts, head5)
 
 
 def head_kernel(pos_ref, own_ref, oth_ref, g_own_ref, g_oth_ref, out_ref, loss_ref, buf, sem):
@@ -345,9 +356,9 @@
     stats = merge_stats(lax.all_to_all(stats, ("z", "x"), 0, 0, tiled=True))
     parts = [stats] + [shift(stats, "y", d) for d in (2, 1, 3)]
     hidden_oth = shift(lax.optimization_barrier((hidden, stats))[0], "c", 1)
-    g = grad_logits(pos, logits, teacher_rows, ids, scale, parts)
-    g, hidden_oth = lax.optimization_barrier((g, hidden_oth))
     head5 = head.reshape(ny, nz, nx, depth // (ny * nz * nx), cols)
+    g, far2 = grad_logits(pos, logits, teacher_rows, ids, scale, parts, head5)
+    g, far2, hidden_oth = lax.optimization_barrier((g, far2, hidden_oth))
 
     def coded(value):
         return (value * SEND_SCALE).astype(F16)
@@ -355,19 +366,18 @@
     def taken(value):
         return value.astype(F32) * (1.0 / SEND_SCALE)
 
-    def exchange(chunks, first):
-        return [shift_by_core(v, d, first) for v, d in zip(chunks, (2, 1, 3))]
-
-    sent = [coded(v) for v in hidden_part(pos, head5, g, SENT)]
-    *sent, g = lax.optimization_barrier((*sent, g))
-    got = exchange(sent, True)
+    far2, g = lax.optimization_barrier((coded(far2), g))
+    got2 = shift_by_core(far2, 2, True)
+    far1, far3 = hidden_part(pos, head5, g, (chunk(1), chunk(3)))
+    far1, far3, g = lax.optimization_barrier((coded(far1), coded(far3), g))
+    got = [got2, shift_by_core(far1, 1, True), shift_by_core(far3, 3, True)]
     g_oth = shift(g, "c", 1)
-    (own,) = hidden_part(pos, head5, g, KEPT)
+    (own,) = hidden_part(pos, head5, g, (chunk(0),))
     head_out, loss = head_grad(pos, hidden, hidden_oth, g, g_oth)
     loss = loss[0, :1]
     *got, loss, head_out = lax.optimization_barrier((*got, loss, head_out))
     total = own + sum(taken(v) for v in got)
-    got = exchange([coded(total[d]) for d in (2, 1, 3)], False)
+    got = [shift_by_core(coded(total[d]), d, False) for d in (2, 1, 3)]
     both = coded(total[0] + sum(taken(v) for v in got))
     both = lax.all_to_all(both, "z", 0, 0, tiled=True)
     hidden_grad = jnp.sum(taken(both), axis=0).T.astype(BF16)

time: 90.8 us -> 87.9 us (0.968)
  waiting for transfers between devices: 20.1 us -> 17.3 us
    ppermute x6, waiting for transfers between devices: 16.7 us -> 13.9 us  [shift_by_core(): return lax.ppermute(a, axes, pairs)]
  transfers between devices with their start and end apart: 12 -> 12, of which waited for: 8 -> 7; matrix products, arithmetic and copies ran while one was open for 0% -> 1% of each run, Pallas kernels for 15% -> 19%
where the time goes in v8:
time: 87.9 us; the launch traced here: 87.3 us
  blocking collectives  33.6 us (38%)
  Pallas kernels  19.2 us (22%)
  waiting for transfers between devices  17.3 us (20%)
  starting transfers between devices  14.1 us (16%)
  other arithmetic  2.08 us (2%)
    all_to_all x1, blocking collectives, body(): stats = merge_stats(lax.all_to_all(stats, ('z', 'x'), 0, 0, tiled=True))  21.9 us
    ppermute x6, waiting for transfers between devices, shift_by_core(): return lax.ppermute(a, axes, pairs)  13.9 us
    all_to_all x1, blocking collectives, body(): both = lax.all_to_all(both, 'z', 0, 0, tiled=True)  11.8 us
    ppermute x6, starting transfers between devices, shift_by_core(): return lax.ppermute(a, axes, pairs)  8.68 us
    pallas_call x1, Pallas kernels, student_logits(): pl.pallas_call(functools.partial(logits_kernel, steps), out_shape=jax.Sha...  5.91 us
    ppermute x6, starting transfers between devices, shift(): return lax.ppermute(a, axis, [(i, (i + by) % n) for i in range(n)])  5.44 us
    pallas_call x1, Pallas kernels, head_grad(): pl.pallas_call(head_kernel, out_shape=(jax.ShapeDtypeStruct((width, cols)...  4.93 us
    pallas_call x2, Pallas kernels, hidden_part(): pl.pallas_call(functools.partial(hidden_kernel, groups), out_shape=out_sh...  3.86 us
  transfers between devices with their start and end apart: 12, of which 7 were waited for; matrix products, arithmetic and copies ran while one was open for 1% of the time, Pallas kernels for 19%

profile of v8, /device:TPU:32, one launch (start us, length us, event | category | flops | bytes accessed | tf_op | source)
XLA Modules:
  0.0 87.3 jit_solution(17559433702907550199)
XLA Ops:
  0.6 0.1 collective-permute-start
  0.7 0.0 slice-start
  0.8 0.1 pad_add_fusion.pos_ref
  0.8 0.0 slice-start.1
  0.9 5.9 %student_logits.1.l_ref = f32[384,768]{1,0:T(8,128)S(1)} custom-call(bf16[384,4096]{1,0:T(8,128)(2,1)} %own_ref.3, bf16[4096,768]{1,0:T(8,128)(2,1)} %w_ref.1), custom_call_target="tpu_custom_call" | custom-call | flops 2415919104 | bytes 10616832 | tf_op jit(solution)/shard_map/student_logits/pallas_call | solution.py:75
  6.8 0.0 copy-start.4
  6.8 0.0 collective-permute-done.oth_ref
  6.8 0.0 copy-done.1
  6.8 0.0 copy-done.2
  6.8 0.0 copy-done.3
  6.8 2.3 %local_stats.1 = (f32[2,640]{1,0:T(2,128)S(1)}, bf16[384,768]{1,0:T(8,128)(2,1)S(1)}) custom-call(s32[4]{0:T(128)S(1)} %pad_add_fusion.pos_ref, f32[384,768]{1,0:T(8,128)S(1)} %student_logits.1.l_ref, bf16[768,384]{1,0:T(8,128)(2,1)S(1)} %copy-done.1, bf16[768,384]{1,0:T(8,128)(2,1)S(1)} %collective-permute-done.oth_ref, s32[6,128]{1,0:T(8,128)S(1)} %bitcast.34, ...), custom_call_target="tpu_custom_call" | custom-call | flops 452984832 | bytes 2949120 | tf_op jit(solution)/shard_map/local_stats/pallas_call | solution.py:190
  9.1 0.1 broadcast_in_dim.2
  9.1 21.9 %all_to_all.10.in_ref = f32[32,2,640]{2,1,0:T(2,128)S(1)} all-to-all(f32[32,2,640]{2,1,0:T(2,128)S(1)} %broadcast_in_dim.2), channel_id=1, replica_groups=mesh['y'=4,'z'=8,'x'=4,'c'=2] {'z','x'}, dimensions={0} | all-to-all | bytes 327680 | tf_op jit(solution)/shard_map/all_to_all | solution.py:356
  31.0 0.2 merge_stats.1.s0
  31.2 0.0 collective-permute-start.4
  31.2 3.1 %collective-permute-start.3 = (f32[2,640]{1,0:T(2,128)S(1)}, f32[2,640]{1,0:T(2,128)S(1)}, u32[]{:S(2)}, u32[]{:S(2)}) collective-permute-start(f32[2,640]{1,0:T(2,128)S(1)} %merge_stats.1.s0), channel_id=1, source_target_pairs={{0,192},{64,0},{128,64},{192,128},{1,193},{65,1},{129,65},{193,129... | collective-permute-start | bytes 15368 | tf_op jit(solution)/shard_map/ppermute | solution.py:32
  34.3 0.0 collective-permute-start.2
  34.3 2.2 %collective-permute-start.1 = (f32[2,640]{1,0:T(2,128)S(1)}, f32[2,640]{1,0:T(2,128)S(1)}, u32[]{:S(2)}, u32[]{:S(2)}) collective-permute-start(f32[2,640]{1,0:T(2,128)S(1)} %merge_stats.1.s0), channel_id=1, source_target_pairs={{0,128},{64,192},{128,0},{192,64},{1,129},{65,193},{129,1},{193,65... | collective-permute-start | bytes 15368 | tf_op jit(solution)/shard_map/ppermute | solution.py:32
  36.5 0.0 collective-permute-done.3.s3
  36.5 2.6 %collective-permute-done.2.s2 = f32[2,640]{1,0:T(2,128)S(1)} collective-permute-done((f32[2,640]{1,0:T(2,128)S(1)}, f32[2,640]{1,0:T(2,128)S(1)}, u32[]{:S(2)}, u32[]{:S(2)}) %collective-permute-start.2) | collective-permute-done | bytes 5152 | tf_op jit(solution)/shard_map/ppermute | solution.py:32
  39.2 0.3 collective-permute-done.1.s1
  39.5 0.0 slice-done.1
  39.5 2.1 %grad_logits.1 = (bf16[400,768]{1,0:T(8,128)(2,1)S(1)}, f32[4,8,32,384]{3,2,1,0:T(8,128)S(1)}) custom-call(s32[4]{0:T(128)S(1)} %pad_add_fusion.pos_ref, f32[384,768]{1,0:T(8,128)S(1)} %student_logits.1.l_ref, bf16[384,768]{1,0:T(8,128)(2,1)S(1)} %get-tuple-element.27.t_ref, s32[3,128]{1,0:T(4,128)S(1)} %bitcast.33, f32[3,128]{1,0:T(4,128)S(1)} %bitcast.35, ...), custom_call_target="tpu_custom_call" | custom-call | flops 2359296 | bytes 2359296 | tf_op jit(solution)/shard_map/grad_logits/pallas_call | solution.py:277
  41.6 0.0 collective-permute-done.4.oth_ref
  41.6 0.2 multiply_convert_fusion.2
  41.8 1.1 %collective-permute-start.5 = (f16[4,8,32,384]{3,2,1,0:T(8,128)(2,1)S(1)}, f16[4,8,32,384]{3,2,1,0:T(8,128)(2,1)S(1)}, u32[]{:S(2)}, u32[]{:S(2)}) collective-permute-start(f16[4,8,32,384]{3,2,1,0:T(8,128)(2,1)S(1)} %multiply_convert_fusion.2), channel_id=1, source_target_pairs={{0,4},{1,129},{2,6},{3,131},{4,0},{5,133},{6,2},{7,135},{8,12},{9,... | collective-permute-start | bytes 2359304 | tf_op jit(solution)/shard_map/ppermute | solution.py:44
  42.8 2.3 %hidden_part.2 = (f32[4,8,32,384]{3,2,1,0:T(8,128)S(1)}, f32[4,8,32,384]{3,2,1,0:T(8,128)S(1)}) custom-call(s32[4]{0:T(128)S(1)} %pad_add_fusion.pos_ref, bf16[4,8,4,32,768]{4,3,2,1,0:T(8,128)(2,1)S(1)} %bitcast.30, bf16[400,768]{1,0:T(8,128)(2,1)S(1)} %get-tuple-element.43.g_ref.g_own_ref), custom_call_target="tpu_custom_call" | custom-call | flops 1 | bytes 1 | tf_op jit(solution)/shard_map/hidden_part/pallas_call | solution.py:236
  45.2 0.4 multiply_convert_fusion
  45.6 1.2 %collective-permute-start.6 = (f16[4,8,32,384]{3,2,1,0:T(8,128)(2,1)S(1)}, f16[4,8,32,384]{3,2,1,0:T(8,128)(2,1)S(1)}, u32[]{:S(2)}, u32[]{:S(2)}) collective-permute-start(f16[4,8,32,384]{3,2,1,0:T(8,128)(2,1)S(1)} %get-tuple-element.40), channel_id=1, source_target_pairs={{0,2},{1,65},{2,4},{3,67},{4,6},{5,69},{6,0},{7,71},{8,10},{9,73},... | collective-permute-start | bytes 2359304 | tf_op jit(solution)/shard_map/ppermute | solution.py:44
  46.7 2.2 %collective-permute-start.7 = (f16[4,8,32,384]{3,2,1,0:T(8,128)(2,1)S(1)}, f16[4,8,32,384]{3,2,1,0:T(8,128)(2,1)S(1)}, u32[]{:S(2)}, u32[]{:S(2)}) collective-permute-start(f16[4,8,32,384]{3,2,1,0:T(8,128)(2,1)S(1)} %get-tuple-element.41), channel_id=1, source_target_pairs={{0,6},{1,193},{2,0},{3,195},{4,2},{5,197},{6,4},{7,199},{8,14},{9,... | collective-permute-start | bytes 2359304 | tf_op jit(solution)/shard_map/ppermute | solution.py:44
  48.9 0.0 collective-permute-start.8
  48.9 1.5 %hidden_part.3 = f32[4,8,32,384]{3,2,1,0:T(8,128)S(1)} custom-call(s32[4]{0:T(128)S(1)} %pad_add_fusion.pos_ref, bf16[4,8,4,32,768]{4,3,2,1,0:T(8,128)(2,1)S(1)} %bitcast.31, bf16[400,768]{1,0:T(8,128)(2,1)S(1)} %get-tuple-element.43.g_ref.g_own_ref), custom_call_target="tpu_custom_call" | custom-call | flops 1 | bytes 1 | tf_op jit(solution)/shard_map/hidden_part/pallas_call | solution.py:236
  50.4 0.5 collective-permute-done.8.g_oth_ref
  50.9 4.9 %head_grad.1 = (bf16[2048,768]{1,0:T(8,128)(2,1)}, f32[1,128]{1,0:T(1,128)}) custom-call(s32[4]{0:T(128)S(1)} %pad_add_fusion.pos_ref, bf16[384,4096]{1,0:T(8,128)(2,1)S(1)} %copy-done, bf16[384,4096]{1,0:T(8,128)(2,1)S(1)} %collective-permute-done.4.oth_ref, bf16[400,768]{1,0:T(8,128)(2,1)S(1)} %get-tuple-element.43.g_ref.g_own_ref, ...), custom_call_target="tpu_custom_call" | custom-call | flops 1 | bytes 1 | tf_op jit(solution)/shard_map/head_grad/pallas_call | solution.py:322
  55.9 0.0 collective-permute-done.5
  55.9 7.9 %collective-permute-done.6 = f16[4,8,32,384]{3,2,1,0:T(8,128)(2,1)S(1)} collective-permute-done((f16[4,8,32,384]{3,2,1,0:T(8,128)(2,1)S(1)}, f16[4,8,32,384]{3,2,1,0:T(8,128)(2,1)S(1)}, u32[]{:S(2)}, u32[]{:S(2)}) %collective-permute-start.6) | collective-permute-done | bytes 786464 | tf_op jit(solution)/shard_map/ppermute | solution.py:44
  63.8 0.0 collective-permute-done.7
  63.8 0.5 multiply_add_fusion
  64.3 0.1 fusion.6
  64.4 2.3 %collective-permute-start.9 = (f16[8,32,384]{2,1,0:T(8,128)(2,1)S(1)}, f16[8,32,384]{2,1,0:T(8,128)(2,1)S(1)}, u32[]{:S(2)}, u32[]{:S(2)}) collective-permute-start(f16[8,32,384]{2,1,0:T(8,128)(2,1)S(1)} %get-tuple-element.51), channel_id=1, source_target_pairs={{0,128},{1,5},{2,130},{3,7},{4,132},{5,1},{6,134},{7,3},{8,136},{9... | collective-permute-start | bytes 589832 | tf_op jit(solution)/shard_map/ppermute | solution.py:44
  66.7 1.1 %collective-permute-start.11 = (f16[8,32,384]{2,1,0:T(8,128)(2,1)S(1)}, f16[8,32,384]{2,1,0:T(8,128)(2,1)S(1)}, u32[]{:S(2)}, u32[]{:S(2)}) collective-permute-start(f16[8,32,384]{2,1,0:T(8,128)(2,1)S(1)} %get-tuple-element.52), channel_id=1, source_target_pairs={{0,192},{1,7},{2,194},{3,1},{4,196},{5,3},{6,198},{7,5},{8,200},{9... | collective-permute-start | bytes 589832 | tf_op jit(solution)/shard_map/ppermute | solution.py:44
  67.8 0.9 %collective-permute-start.10 = (f16[8,32,384]{2,1,0:T(8,128)(2,1)S(1)}, f16[8,32,384]{2,1,0:T(8,128)(2,1)S(1)}, u32[]{:S(2)}, u32[]{:S(2)}) collective-permute-start(f16[8,32,384]{2,1,0:T(8,128)(2,1)S(1)} %get-tuple-element.53), channel_id=1, source_target_pairs={{0,64},{1,3},{2,66},{3,5},{4,68},{5,7},{6,70},{7,1},{8,72},{9,11},... | collective-permute-start | bytes 589832 | tf_op jit(solution)/shard_map/ppermute | solution.py:44
  68.7 2.9 %collective-permute-done.9 = f16[8,32,384]{2,1,0:T(8,128)(2,1)S(1)} collective-permute-done((f16[8,32,384]{2,1,0:T(8,128)(2,1)S(1)}, f16[8,32,384]{2,1,0:T(8,128)(2,1)S(1)}, u32[]{:S(2)}, u32[]{:S(2)}) %collective-permute-start.9) | collective-permute-done | bytes 196640 | tf_op jit(solution)/shard_map/ppermute | solution.py:44
  71.7 2.7 %collective-permute-done.11 = f16[8,32,384]{2,1,0:T(8,128)(2,1)S(1)} collective-permute-done((f16[8,32,384]{2,1,0:T(8,128)(2,1)S(1)}, f16[8,32,384]{2,1,0:T(8,128)(2,1)S(1)}, u32[]{:S(2)}, u32[]{:S(2)}) %collective-permute-start.11) | collective-permute-done | bytes 196640 | tf_op jit(solution)/shard_map/ppermute | solution.py:44
  74.4 0.3 collective-permute-done.10
  74.7 0.1 fusion.5
  74.8 11.8 %all_to_all.11 = f16[8,32,384]{2,1,0:T(8,128)(2,1)S(1)} all-to-all(f16[8,32,384]{2,1,0:T(8,128)(2,1)S(1)} %fusion.5), channel_id=1, replica_groups=mesh['y'=4,'z'=8,'x'=4,'c'=2] {'z'}, dimensions={0} | all-to-all | bytes 393216 | tf_op jit(solution)/shard_map/all_to_all | solution.py:382
  86.6 0.7 multiply_reduce_fusion
  (8 shorter events, 0.0 us)
Async XLA Ops:
  0.6 6.2 %collective-permute-start = (bf16[768,384]{1,0:T(8,128)(2,1)}, bf16[768,384]{1,0:T(8,128)(2,1)S(1)}, u32[]{:S(2)}, u32[]{:S(2)}) collective-permute-start(bf16[768,384]{1,0:T(8,128)(2,1)} %own_ref.2), channel_id=1, source_target_pairs={{0,1},{1,0},{2,3},{3,2},{4,5},{5,4},{6,7},{7,6},{8,9},{9,8},{10,11... | collective-permute-start | bytes 1769480 | tf_op jit(solution)/shard_map/ppermute | solution.py:32
  0.7 38.7 %slice-start = ((s8[6291456]{0:T(1024)(128)(4,1)}), s8[4194304]{0:T(1024)(128)(4,1)S(1)}, s32[]{:S(2)}) async-start(s8[6291456]{0:T(1024)(128)(4,1)} %bitcast.27), calls=%async_computation.2 | async-start | bytes 8388608
  0.8 6.0 %copy-start.1 = (bf16[768,384]{1,0:T(8,128)(2,1)S(1)}, bf16[768,384]{1,0:T(8,128)(2,1)}, u32[]{:S(2)}) copy-start(bf16[768,384]{1,0:T(8,128)(2,1)} %own_ref.2) | copy-start | bytes 1769476
  0.8 6.0 %copy-start.2 = (s32[384]{0:T(512)S(1)}, s32[384]{0:T(512)}, u32[]{:S(2)}) copy-start(s32[384]{0:T(512)} %param.9) | copy-start | bytes 4612
  0.8 6.0 %copy-start.3 = (s32[768]{0:T(1024)S(1)}, s32[768]{0:T(1024)}, u32[]{:S(2)}) copy-start(s32[768]{0:T(1024)} %param.10) | copy-start | bytes 9220
  0.8 30.3 %copy-start = (bf16[384,4096]{1,0:T(8,128)(2,1)S(1)}, bf16[384,4096]{1,0:T(8,128)(2,1)}, u32[]{:S(2)}) copy-start(bf16[384,4096]{1,0:T(8,128)(2,1)} %own_ref.3) | copy-start | bytes 9437188
  0.8 38.6 %slice-start.1 = ((s8[6291456]{0:T(1024)(128)(4,1)}), s8[2097152]{0:T(1024)(128)(4,1)S(1)}, s32[]{:S(2)}) async-start(s8[6291456]{0:T(1024)(128)(4,1)} %bitcast.27), calls=%async_computation.3 | async-start | bytes 4194304
  6.8 32.7 %copy-start.4 = (f32[384]{0:T(512)S(1)}, f32[384]{0:T(512)}, u32[]{:S(2)}) copy-start(f32[384]{0:T(512)} %param.11) | copy-start | bytes 4612
  31.2 10.4 %collective-permute-start.4 = (bf16[384,4096]{1,0:T(8,128)(2,1)S(1)}, bf16[384,4096]{1,0:T(8,128)(2,1)S(1)}, u32[]{:S(2)}, u32[]{:S(2)}) collective-permute-start(bf16[384,4096]{1,0:T(8,128)(2,1)S(1)} %copy-done), channel_id=1, source_target_pairs={{0,1},{1,0},{2,3},{3,2},{4,5},{5,4},{6,7},{7,6},{8,9},{9,8},{10,11... | collective-permute-start | bytes 9437192 | tf_op jit(solution)/shard_map/ppermute | solution.py:32
  31.2 5.3 %collective-permute-start.3 = (f32[2,640]{1,0:T(2,128)S(1)}, f32[2,640]{1,0:T(2,128)S(1)}, u32[]{:S(2)}, u32[]{:S(2)}) collective-permute-start(f32[2,640]{1,0:T(2,128)S(1)} %merge_stats.1.s0), channel_id=1, source_target_pairs={{0,192},{64,0},{128,64},{192,128},{1,193},{65,1},{129,65},{193,129... | collective-permute-start | bytes 15368 | tf_op jit(solution)/shard_map/ppermute | solution.py:32
  34.3 4.8 %collective-permute-start.2 = (f32[2,640]{1,0:T(2,128)S(1)}, f32[2,640]{1,0:T(2,128)S(1)}, u32[]{:S(2)}, u32[]{:S(2)}) collective-permute-start(f32[2,640]{1,0:T(2,128)S(1)} %merge_stats.1.s0), channel_id=1, source_target_pairs={{0,64},{64,128},{128,192},{192,0},{1,65},{65,129},{129,193},{193,1... | collective-permute-start | bytes 15368 | tf_op jit(solution)/shard_map/ppermute | solution.py:32
  34.3 5.1 %collective-permute-start.1 = (f32[2,640]{1,0:T(2,128)S(1)}, f32[2,640]{1,0:T(2,128)S(1)}, u32[]{:S(2)}, u32[]{:S(2)}) collective-permute-start(f32[2,640]{1,0:T(2,128)S(1)} %merge_stats.1.s0), channel_id=1, source_target_pairs={{0,128},{64,192},{128,0},{192,64},{1,129},{65,193},{129,1},{193,65... | collective-permute-start | bytes 15368 | tf_op jit(solution)/shard_map/ppermute | solution.py:32
  41.8 14.1 %collective-permute-start.5 = (f16[4,8,32,384]{3,2,1,0:T(8,128)(2,1)S(1)}, f16[4,8,32,384]{3,2,1,0:T(8,128)(2,1)S(1)}, u32[]{:S(2)}, u32[]{:S(2)}) collective-permute-start(f16[4,8,32,384]{3,2,1,0:T(8,128)(2,1)S(1)} %multiply_convert_fusion.2), channel_id=1, source_target_pairs={{0,4},{1,129},{2,6},{3,131},{4,0},{5,133},{6,2},{7,135},{8,12},{9,... | collective-permute-start | bytes 2359304 | tf_op jit(solution)/shard_map/ppermute | solution.py:44
  45.6 18.2 %collective-permute-start.6 = (f16[4,8,32,384]{3,2,1,0:T(8,128)(2,1)S(1)}, f16[4,8,32,384]{3,2,1,0:T(8,128)(2,1)S(1)}, u32[]{:S(2)}, u32[]{:S(2)}) collective-permute-start(f16[4,8,32,384]{3,2,1,0:T(8,128)(2,1)S(1)} %get-tuple-element.40), channel_id=1, source_target_pairs={{0,2},{1,65},{2,4},{3,67},{4,6},{5,69},{6,0},{7,71},{8,10},{9,73},... | collective-permute-start | bytes 2359304 | tf_op jit(solution)/shard_map/ppermute | solution.py:44
  46.7 17.0 %collective-permute-start.7 = (f16[4,8,32,384]{3,2,1,0:T(8,128)(2,1)S(1)}, f16[4,8,32,384]{3,2,1,0:T(8,128)(2,1)S(1)}, u32[]{:S(2)}, u32[]{:S(2)}) collective-permute-start(f16[4,8,32,384]{3,2,1,0:T(8,128)(2,1)S(1)} %get-tuple-element.41), channel_id=1, source_target_pairs={{0,6},{1,193},{2,0},{3,195},{4,2},{5,197},{6,4},{7,199},{8,14},{9,... | collective-permute-start | bytes 2359304 | tf_op jit(solution)/shard_map/ppermute | solution.py:44
  48.9 2.0 %collective-permute-start.8 = (bf16[400,768]{1,0:T(8,128)(2,1)S(1)}, bf16[400,768]{1,0:T(8,128)(2,1)S(1)}, u32[]{:S(2)}, u32[]{:S(2)}) collective-permute-start(bf16[400,768]{1,0:T(8,128)(2,1)S(1)} %get-tuple-element.43.g_ref.g_own_ref), channel_id=1, source_target_pairs={{0,1},{1,0},{2,3},{3,2},{4,5},{5,4},{6,7},{7,6},{8,9},{9,8},{10,11... | collective-permute-start | bytes 1843208 | tf_op jit(solution)/shard_map/ppermute | solution.py:32
  64.4 7.3 %collective-permute-start.9 = (f16[8,32,384]{2,1,0:T(8,128)(2,1)S(1)}, f16[8,32,384]{2,1,0:T(8,128)(2,1)S(1)}, u32[]{:S(2)}, u32[]{:S(2)}) collective-permute-start(f16[8,32,384]{2,1,0:T(8,128)(2,1)S(1)} %get-tuple-element.51), channel_id=1, source_target_pairs={{0,128},{1,5},{2,130},{3,7},{4,132},{5,1},{6,134},{7,3},{8,136},{9... | collective-permute-start | bytes 589832 | tf_op jit(solution)/shard_map/ppermute | solution.py:44
  66.7 7.7 %collective-permute-start.11 = (f16[8,32,384]{2,1,0:T(8,128)(2,1)S(1)}, f16[8,32,384]{2,1,0:T(8,128)(2,1)S(1)}, u32[]{:S(2)}, u32[]{:S(2)}) collective-permute-start(f16[8,32,384]{2,1,0:T(8,128)(2,1)S(1)} %get-tuple-element.52), channel_id=1, source_target_pairs={{0,192},{1,7},{2,194},{3,1},{4,196},{5,3},{6,198},{7,5},{8,200},{9... | collective-permute-start | bytes 589832 | tf_op jit(solution)/shard_map/ppermute | solution.py:44
  67.8 6.9 %collective-permute-start.10 = (f16[8,32,384]{2,1,0:T(8,128)(2,1)S(1)}, f16[8,32,384]{2,1,0:T(8,128)(2,1)S(1)}, u32[]{:S(2)}, u32[]{:S(2)}) collective-permute-start(f16[8,32,384]{2,1,0:T(8,128)(2,1)S(1)} %get-tuple-element.53), channel_id=1, source_target_pairs={{0,64},{1,3},{2,66},{3,5},{4,68},{5,7},{6,70},{7,1},{8,72},{9,11},... | collective-permute-start | bytes 589832 | tf_op jit(solution)/shard_map/ppermute | solution.py:44

commit v9 on v8

--- a/solution.py
+++ b/solution.py
@@ -205,8 +205,8 @@
     )(pos, logits, own, oth, assign, ids)
 
 
-def chunk(far):
-    return tuple((far, near) for near in range(4))
+def half(far, at):
+    return ((far, 2 * at), (far, 2 * at + 1))
 
 
 def hidden_product(groups, pos_ref, w_ref, g, outs):
@@ -245,7 +245,7 @@
 
 
 def grad_kernel(
-    pos_ref, l_ref, t_ref, ids_ref, scale_ref, s0, s1, s2, s3, w_ref, g_ref, far_ref
+    pos_ref, l_ref, t_ref, ids_ref, scale_ref, s0, s1, s2, s3, w_ref, g_ref, low_ref, high_ref
 ):
     rows, cols = l_ref.shape
     parts = (s0, s1, s2, s3)
@@ -268,7 +268,7 @@
     prob_t = jnp.exp(t_ref[...].astype(F32) - norm_t)
     g = (scale * ((1.0 + CE_WEIGHT) * prob_s - prob_t - hot)).astype(BF16)
     g_ref[:rows, :] = g
-    hidden_product((chunk(2),), pos_ref, w_ref, g, (far_ref,))
+    hidden_product((half(2, 0), half(2, 1)), pos_ref, w_ref, g, (low_ref, high_ref))
 
 
 def grad_logits(pos, logits, teacher, ids, scale, parts, head5):
@@ -278,10 +278,11 @@
         grad_kernel,
         out_shape=(
             jax.ShapeDtypeStruct((rows + LOSS_ROWS, cols), BF16),
-            jax.ShapeDtypeStruct((4, nz, sub, rows), F32),
+            jax.ShapeDtypeStruct((2, nz, sub, rows), F32),
+            jax.ShapeDtypeStruct((2, nz, sub, rows), F32),
         ),
         in_specs=[pl.BlockSpec(memory_space=pltpu.SMEM)] + [WHOLE] * 9,
-        out_specs=(WHOLE, WHOLE),
+        out_specs=(WHOLE, WHOLE, WHOLE),
         compiler_params=params(16),
         cost_estimate=pl.CostEstimate(
             flops=8 * rows * cols,
@@ -357,8 +358,8 @@
     parts = [stats] + [shift(stats, "y", d) for d in (2, 1, 3)]
     hidden_oth = shift(lax.optimization_barrier((hidden, stats))[0], "c", 1)
     head5 = head.reshape(ny, nz, nx, depth // (ny * nz * nx), cols)
-    g, far2 = grad_logits(pos, logits, teacher_rows, ids, scale, parts, head5)
-    g, far2, hidden_oth = lax.optimization_barrier((g, far2, hidden_oth))
+    g, low2, high2 = grad_logits(pos, logits, teacher_rows, ids, scale, parts, head5)
+    g, low2, high2, hidden_oth = lax.optimization_barrier((g, low2, high2, hidden_oth))
 
     def coded(value):
         return (value * SEND_SCALE).astype(F16)
@@ -366,19 +367,25 @@
     def taken(value):
         return value.astype(F32) * (1.0 / SEND_SCALE)
 
-    far2, g = lax.optimization_barrier((coded(far2), g))
-    got2 = shift_by_core(far2, 2, True)
-    far1, far3 = hidden_part(pos, head5, g, (chunk(1), chunk(3)))
-    far1, far3, g = lax.optimization_barrier((coded(far1), coded(far3), g))
-    got = [got2, shift_by_core(far1, 1, True), shift_by_core(far3, 3, True)]
+    low2, high2, g = lax.optimization_barrier((coded(low2), coded(high2), g))
+    from_back, from_front = shift_by_core(low2, 1, True), shift_by_core(high2, -1, True)
+    groups = (half(1, 1), half(3, 0), half(1, 0), half(3, 1))
+    high1, low3, low1, high3 = hidden_part(pos, head5, g, groups)
+    high1, low3, low1, high3 = lax.optimization_barrier((coded(high1), coded(low3), low1, high3))
+    to_high, to_low = shift_by_core(high1, 1, True), shift_by_core(low3, -1, True)
+    low1, high3 = coded(low1 + taken(from_back)), coded(high3 + taken(from_front))
+    low1, high3, g = lax.optimization_barrier((low1, high3, g))
+    to_low = [to_low, shift_by_core(low1, 1, True)]
+    to_high = [to_high, shift_by_core(high3, -1, True)]
     g_oth = shift(g, "c", 1)
-    (own,) = hidden_part(pos, head5, g, (chunk(0),))
+    low, high = hidden_part(pos, head5, g, (half(0, 0), half(0, 1)))
     head_out, loss = head_grad(pos, hidden, hidden_oth, g, g_oth)
     loss = loss[0, :1]
-    *got, loss, head_out = lax.optimization_barrier((*got, loss, head_out))
-    total = own + sum(taken(v) for v in got)
-    got = [shift_by_core(coded(total[d]), d, False) for d in (2, 1, 3)]
-    both = coded(total[0] + sum(taken(v) for v in got))
+    *got, loss, head_out = lax.optimization_barrier((*to_low, *to_high, loss, head_out))
+    low = low + taken(got[0]) + taken(got[1])
+    high = high + taken(got[2]) + taken(got[3])
+    got = [shift_by_core(coded(v), d, False) for d, v in ((2, high[0]), (1, low[1]), (3, high[1]))]
+    both = coded(low[0] + sum(taken(v) for v in got))
     both = lax.all_to_all(both, "z", 0, 0, tiled=True)
     hidden_grad = jnp.sum(taken(both), axis=0).T.astype(BF16)
     return loss, hidden_grad, head_out

time: 87.9 us -> 92.4 us (1.051)
  starting transfers between devices: 14.1 us -> 20.5 us
  waiting for transfers between devices: 17.3 us -> 15.1 us
    ppermute x6 -> x9, starting transfers between devices: 8.68 us -> 15 us  [shift_by_core(): return lax.ppermute(a, axes, pairs)]
    ppermute x6 -> x9, waiting for transfers between devices: 13.9 us -> 12.1 us  [shift_by_core(): return lax.ppermute(a, axes, pairs)]
  transfers between devices with their start and end apart: 12 -> 15, of which waited for: 7 -> 7; matrix products, arithmetic and copies ran while one was open for 1% -> 0% of each run, Pallas kernels for 19% -> 18%
where the time goes in v9:
time: 92.4 us; the launch traced here: 91.4 us
  blocking collectives  33.6 us (36%)
  starting transfers between devices  20.5 us (22%)
  Pallas kernels  19.2 us (21%)
  waiting for transfers between devices  15.1 us (16%)
  other arithmetic  2.08 us (2%)
    all_to_all x1, blocking collectives, body(): stats = merge_stats(lax.all_to_all(stats, ('z', 'x'), 0, 0, tiled=True))  21.9 us
    ppermute x9, starting transfers between devices, shift_by_core(): return lax.ppermute(a, axes, pairs)  15 us
    ppermute x9, waiting for transfers between devices, shift_by_core(): return lax.ppermute(a, axes, pairs)  12.1 us
    all_to_all x1, blocking collectives, body(): both = lax.all_to_all(both, 'z', 0, 0, tiled=True)  11.7 us
    pallas_call x1, Pallas kernels, student_logits(): pl.pallas_call(functools.partial(logits_kernel, steps), out_shape=jax.Sha...  5.91 us
    ppermute x6, starting transfers between devices, shift(): return lax.ppermute(a, axis, [(i, (i + by) % n) for i in range(n)])  5.53 us
    pallas_call x1, Pallas kernels, head_grad(): pl.pallas_call(head_kernel, out_shape=(jax.ShapeDtypeStruct((width, cols)...  4.93 us
    pallas_call x2, Pallas kernels, hidden_part(): pl.pallas_call(functools.partial(hidden_kernel, groups), out_shape=out_sh...  3.85 us
  transfers between devices with their start and end apart: 15, of which 7 were waited for; matrix products, arithmetic and copies ran while one was open for 0% of the time, Pallas kernels for 18%

profile of v9, /device:TPU:32, one launch (start us, length us, event | category | flops | bytes accessed | tf_op | source)
XLA Modules:
  0.0 91.4 jit_solution(1022249994975466871)
XLA Ops:
  0.6 0.1 collective-permute-start
  0.7 0.0 slice-start
  0.8 0.1 pad_add_fusion.pos_ref
  0.8 0.0 slice-start.1
  0.9 0.0 copy-start.4
  0.9 5.9 %student_logits.1.l_ref = f32[384,768]{1,0:T(8,128)S(1)} custom-call(bf16[384,4096]{1,0:T(8,128)(2,1)} %own_ref.3, bf16[4096,768]{1,0:T(8,128)(2,1)} %w_ref.1), custom_call_target="tpu_custom_call" | custom-call | flops 2415919104 | bytes 10616832 | tf_op jit(solution)/shard_map/student_logits/pallas_call | solution.py:75
  6.8 2.3 %local_stats.1 = (f32[2,640]{1,0:T(2,128)S(1)}, bf16[384,768]{1,0:T(8,128)(2,1)S(1)}) custom-call(s32[4]{0:T(128)S(1)} %pad_add_fusion.pos_ref, f32[384,768]{1,0:T(8,128)S(1)} %student_logits.1.l_ref, bf16[768,384]{1,0:T(8,128)(2,1)S(1)} %copy-done.1, bf16[768,384]{1,0:T(8,128)(2,1)S(1)} %collective-permute-done.oth_ref, s32[6,128]{1,0:T(8,128)S(1)} %bitcast.34, ...), custom_call_target="tpu_custom_call" | custom-call | flops 452984832 | bytes 2949120 | tf_op jit(solution)/shard_map/local_stats/pallas_call | solution.py:190
  9.1 0.1 broadcast_in_dim.2
  9.1 21.9 %all_to_all.10.in_ref = f32[32,2,640]{2,1,0:T(2,128)S(1)} all-to-all(f32[32,2,640]{2,1,0:T(2,128)S(1)} %broadcast_in_dim.2), channel_id=1, replica_groups=mesh['y'=4,'z'=8,'x'=4,'c'=2] {'z','x'}, dimensions={0} | all-to-all | bytes 327680 | tf_op jit(solution)/shard_map/all_to_all | solution.py:357
  31.0 0.2 merge_stats.1.s0
  31.2 0.0 collective-permute-start.4
  31.2 3.1 %collective-permute-start.3 = (f32[2,640]{1,0:T(2,128)S(1)}, f32[2,640]{1,0:T(2,128)S(1)}, u32[]{:S(2)}, u32[]{:S(2)}) collective-permute-start(f32[2,640]{1,0:T(2,128)S(1)} %merge_stats.1.s0), channel_id=1, source_target_pairs={{0,192},{64,0},{128,64},{192,128},{1,193},{65,1},{129,65},{193,129... | collective-permute-start | bytes 15368 | tf_op jit(solution)/shard_map/ppermute | solution.py:32
  34.3 0.0 collective-permute-start.2
  34.3 2.2 %collective-permute-start.1 = (f32[2,640]{1,0:T(2,128)S(1)}, f32[2,640]{1,0:T(2,128)S(1)}, u32[]{:S(2)}, u32[]{:S(2)}) collective-permute-start(f32[2,640]{1,0:T(2,128)S(1)} %merge_stats.1.s0), channel_id=1, source_target_pairs={{0,128},{64,192},{128,0},{192,64},{1,129},{65,193},{129,1},{193,65... | collective-permute-start | bytes 15368 | tf_op jit(solution)/shard_map/ppermute | solution.py:32
  36.5 0.0 collective-permute-done.3.s3
  36.5 2.6 %collective-permute-done.2.s2 = f32[2,640]{1,0:T(2,128)S(1)} collective-permute-done((f32[2,640]{1,0:T(2,128)S(1)}, f32[2,640]{1,0:T(2,128)S(1)}, u32[]{:S(2)}, u32[]{:S(2)}) %collective-permute-start.2) | collective-permute-done | bytes 5152 | tf_op jit(solution)/shard_map/ppermute | solution.py:32
  39.1 0.3 collective-permute-done.1.s1
  39.5 2.1 %grad_logits.1 = (bf16[400,768]{1,0:T(8,128)(2,1)S(1)}, f32[2,8,32,384]{3,2,1,0:T(8,128)S(1)}, f32[2,8,32,384]{3,2,1,0:T(8,128)S(1)}) custom-call(s32[4]{0:T(128)S(1)} %pad_add_fusion.pos_ref, f32[384,768]{1,0:T(8,128)S(1)} %student_logits.1.l_ref, bf16[384,768]{1,0:T(8,128)(2,1)S(1)} %get-tuple-element.39.t_ref, s32[3,128]{1,0:T(4,128)S(1)} %bitcast.33, ...), custom_call_target="tpu_custom_call" | custom-call | flops 2359296 | bytes 2359296 | tf_op jit(solution)/shard_map/grad_logits/pallas_call | solution.py:277
  41.6 0.2 multiply_convert_fusion.4
  41.8 0.6 collective-permute-start.6
  42.4 2.7 %collective-permute-start.7 = (f16[2,8,32,384]{3,2,1,0:T(8,128)(2,1)S(1)}, f16[2,8,32,384]{3,2,1,0:T(8,128)(2,1)S(1)}, u32[]{:S(2)}, u32[]{:S(2)}) collective-permute-start(f16[2,8,32,384]{3,2,1,0:T(8,128)(2,1)S(1)} %get-tuple-element.59), channel_id=1, source_target_pairs={{0,6},{1,193},{2,0},{3,195},{4,2},{5,197},{6,4},{7,199},{8,14},{9,... | collective-permute-start | bytes 1179656 | tf_op jit(solution)/shard_map/ppermute | solution.py:44
  45.1 2.3 %hidden_part.2 = (f32[2,8,32,384]{3,2,1,0:T(8,128)S(1)}, f32[2,8,32,384]{3,2,1,0:T(8,128)S(1)}, f32[2,8,32,384]{3,2,1,0:T(8,128)S(1)}, f32[2,8,32,384]{3,2,1,0:T(8,128)S(1)}) custom-call(s32[4]{0:T(128)S(1)} %pad_add_fusion.pos_ref, bf16[4,8,4,32,768]{4,3,2,1,0:T(8,128)(2,1)S(1)} %bitcast.30, bf16[400,768]{1,0:T(8,128)(2,1)S(1)} %get-tuple-element.64.g_ref.g_own_ref), custom_call_target="tpu_custom_call" | custom-call | flops 1 | bytes 1 | tf_op jit(solution)/shard_map/hidden_part/pallas_call | solution.py:236
  47.5 0.1 multiply_convert_fusion.3
  47.6 0.1 multiply_convert_fusion.2
  47.6 2.8 %collective-permute-done.7 = f16[2,8,32,384]{3,2,1,0:T(8,128)(2,1)S(1)} collective-permute-done((f16[2,8,32,384]{3,2,1,0:T(8,128)(2,1)S(1)}, f16[2,8,32,384]{3,2,1,0:T(8,128)(2,1)S(1)}, u32[]{:S(2)}, u32[]{:S(2)}) %collective-permute-start.7) | collective-permute-done | bytes 393248 | tf_op jit(solution)/shard_map/ppermute | solution.py:44
  50.4 0.2 multiply_convert_fusion
  50.6 0.3 collective-permute-done.6
  50.9 0.2 multiply_convert_fusion.1
  51.0 0.1 collective-permute-start.11
  51.1 3.5 %collective-permute-start.5 = (f16[2,8,32,384]{3,2,1,0:T(8,128)(2,1)S(1)}, f16[2,8,32,384]{3,2,1,0:T(8,128)(2,1)S(1)}, u32[]{:S(2)}, u32[]{:S(2)}) collective-permute-start(f16[2,8,32,384]{3,2,1,0:T(8,128)(2,1)S(1)} %multiply_convert_fusion.2), channel_id=1, source_target_pairs={{0,6},{1,193},{2,0},{3,195},{4,2},{5,197},{6,4},{7,199},{8,14},{9,... | collective-permute-start | bytes 1179656 | tf_op jit(solution)/shard_map/ppermute | solution.py:44
  54.6 0.0 collective-permute-start.9
  54.7 3.3 %collective-permute-start.10 = (f16[2,8,32,384]{3,2,1,0:T(8,128)(2,1)S(1)}, f16[2,8,32,384]{3,2,1,0:T(8,128)(2,1)S(1)}, u32[]{:S(2)}, u32[]{:S(2)}) collective-permute-start(f16[2,8,32,384]{3,2,1,0:T(8,128)(2,1)S(1)} %multiply_convert_fusion), channel_id=1, source_target_pairs={{0,6},{1,193},{2,0},{3,195},{4,2},{5,197},{6,4},{7,199},{8,14},{9,... | collective-permute-start | bytes 1179656 | tf_op jit(solution)/shard_map/ppermute | solution.py:44
  57.9 1.5 %hidden_part.3 = (f32[2,8,32,384]{3,2,1,0:T(8,128)S(1)}, f32[2,8,32,384]{3,2,1,0:T(8,128)S(1)}) custom-call(s32[4]{0:T(128)S(1)} %pad_add_fusion.pos_ref, bf16[4,8,4,32,768]{4,3,2,1,0:T(8,128)(2,1)S(1)} %bitcast.31, bf16[400,768]{1,0:T(8,128)(2,1)S(1)} %get-tuple-element.64.g_ref.g_own_ref), custom_call_target="tpu_custom_call" | custom-call | flops 1 | bytes 1 | tf_op jit(solution)/shard_map/hidden_part/pallas_call | solution.py:236
  59.4 0.0 collective-permute-done.11.g_oth_ref
  59.5 4.9 %head_grad.1 = (bf16[2048,768]{1,0:T(8,128)(2,1)}, f32[1,128]{1,0:T(1,128)}) custom-call(s32[4]{0:T(128)S(1)} %pad_add_fusion.pos_ref, bf16[384,4096]{1,0:T(8,128)(2,1)S(1)} %copy-done, bf16[384,4096]{1,0:T(8,128)(2,1)S(1)} %collective-permute-done.4.oth_ref, bf16[400,768]{1,0:T(8,128)(2,1)S(1)} %get-tuple-element.64.g_ref.g_own_ref, ...), custom_call_target="tpu_custom_call" | custom-call | flops 1 | bytes 1 | tf_op jit(solution)/shard_map/head_grad/pallas_call | solution.py:323
  64.4 0.0 collective-permute-done.5
  64.4 3.4 %collective-permute-done.8 = f16[2,8,32,384]{3,2,1,0:T(8,128)(2,1)S(1)} collective-permute-done((f16[2,8,32,384]{3,2,1,0:T(8,128)(2,1)S(1)}, f16[2,8,32,384]{3,2,1,0:T(8,128)(2,1)S(1)}, u32[]{:S(2)}, u32[]{:S(2)}) %collective-permute-start.8) | collective-permute-done | bytes 393248 | tf_op jit(solution)/shard_map/ppermute | solution.py:44
  67.9 0.2 multiply_add_fusion
  68.0 0.1 fusion.6
  68.1 0.2 multiply_add_fusion.1
  68.4 0.7 collective-permute-start.13
  69.0 4.1 %collective-permute-start.12 = (f16[8,32,384]{2,1,0:T(8,128)(2,1)S(1)}, f16[8,32,384]{2,1,0:T(8,128)(2,1)S(1)}, u32[]{:S(2)}, u32[]{:S(2)}) collective-permute-start(f16[8,32,384]{2,1,0:T(8,128)(2,1)S(1)} %get-tuple-element.75), channel_id=1, source_target_pairs={{0,128},{1,5},{2,130},{3,7},{4,132},{5,1},{6,134},{7,3},{8,136},{9... | collective-permute-start | bytes 589832 | tf_op jit(solution)/shard_map/ppermute | solution.py:44
  73.2 0.1 collective-permute-start.14
  73.3 2.0 %collective-permute-done.13 = f16[8,32,384]{2,1,0:T(8,128)(2,1)S(1)} collective-permute-done((f16[8,32,384]{2,1,0:T(8,128)(2,1)S(1)}, f16[8,32,384]{2,1,0:T(8,128)(2,1)S(1)}, u32[]{:S(2)}, u32[]{:S(2)}) %collective-permute-start.13) | collective-permute-done | bytes 196640 | tf_op jit(solution)/shard_map/ppermute | solution.py:44
  75.3 3.6 %collective-permute-done.12 = f16[8,32,384]{2,1,0:T(8,128)(2,1)S(1)} collective-permute-done((f16[8,32,384]{2,1,0:T(8,128)(2,1)S(1)}, f16[8,32,384]{2,1,0:T(8,128)(2,1)S(1)}, u32[]{:S(2)}, u32[]{:S(2)}) %collective-permute-start.12) | collective-permute-done | bytes 196640 | tf_op jit(solution)/shard_map/ppermute | solution.py:44
  78.9 0.1 fusion.5
  79.1 11.7 %all_to_all.11 = f16[8,32,384]{2,1,0:T(8,128)(2,1)S(1)} all-to-all(f16[8,32,384]{2,1,0:T(8,128)(2,1)S(1)} %fusion.5), channel_id=1, replica_groups=mesh['y'=4,'z'=8,'x'=4,'c'=2] {'z'}, dimensions={0} | all-to-all | bytes 393216 | tf_op jit(solution)/shard_map/all_to_all | solution.py:389
  90.8 0.7 multiply_reduce_fusion
  (19 shorter events, 0.1 us)
Async XLA Ops:
  0.6 6.2 %collective-permute-start = (bf16[768,384]{1,0:T(8,128)(2,1)}, bf16[768,384]{1,0:T(8,128)(2,1)S(1)}, u32[]{:S(2)}, u32[]{:S(2)}) collective-permute-start(bf16[768,384]{1,0:T(8,128)(2,1)} %own_ref.2), channel_id=1, source_target_pairs={{0,1},{1,0},{2,3},{3,2},{4,5},{5,4},{6,7},{7,6},{8,9},{9,8},{10,11... | collective-permute-start | bytes 1769480 | tf_op jit(solution)/shard_map/ppermute | solution.py:32
  0.7 38.7 %slice-start = ((s8[6291456]{0:T(1024)(128)(4,1)}), s8[4194304]{0:T(1024)(128)(4,1)S(1)}, s32[]{:S(2)}) async-start(s8[6291456]{0:T(1024)(128)(4,1)} %bitcast.27), calls=%async_computation.2 | async-start | bytes 8388608
  0.8 6.0 %copy-start.1 = (bf16[768,384]{1,0:T(8,128)(2,1)S(1)}, bf16[768,384]{1,0:T(8,128)(2,1)}, u32[]{:S(2)}) copy-start(bf16[768,384]{1,0:T(8,128)(2,1)} %own_ref.2) | copy-start | bytes 1769476
  0.8 6.0 %copy-start.2 = (s32[384]{0:T(512)S(1)}, s32[384]{0:T(512)}, u32[]{:S(2)}) copy-start(s32[384]{0:T(512)} %param.9) | copy-start | bytes 4612
  0.8 6.0 %copy-start.3 = (s32[768]{0:T(1024)S(1)}, s32[768]{0:T(1024)}, u32[]{:S(2)}) copy-start(s32[768]{0:T(1024)} %param.10) | copy-start | bytes 9220
  0.8 30.3 %copy-start = (bf16[384,4096]{1,0:T(8,128)(2,1)S(1)}, bf16[384,4096]{1,0:T(8,128)(2,1)}, u32[]{:S(2)}) copy-start(bf16[384,4096]{1,0:T(8,128)(2,1)} %own_ref.3) | copy-start | bytes 9437188
  0.8 38.6 %slice-start.1 = ((s8[6291456]{0:T(1024)(128)(4,1)}), s8[2097152]{0:T(1024)(128)(4,1)S(1)}, s32[]{:S(2)}) async-start(s8[6291456]{0:T(1024)(128)(4,1)} %bitcast.27), calls=%async_computation.3 | async-start | bytes 4194304
  0.9 38.6 %copy-start.4 = (f32[384]{0:T(512)S(1)}, f32[384]{0:T(512)}, u32[]{:S(2)}) copy-start(f32[384]{0:T(512)} %param.11) | copy-start | bytes 4612
  31.2 10.4 %collective-permute-start.4 = (bf16[384,4096]{1,0:T(8,128)(2,1)S(1)}, bf16[384,4096]{1,0:T(8,128)(2,1)S(1)}, u32[]{:S(2)}, u32[]{:S(2)}) collective-permute-start(bf16[384,4096]{1,0:T(8,128)(2,1)S(1)} %copy-done), channel_id=1, source_target_pairs={{0,1},{1,0},{2,3},{3,2},{4,5},{5,4},{6,7},{7,6},{8,9},{9,8},{10,11... | collective-permute-start | bytes 9437192 | tf_op jit(solution)/shard_map/ppermute | solution.py:32
  31.2 5.3 %collective-permute-start.3 = (f32[2,640]{1,0:T(2,128)S(1)}, f32[2,640]{1,0:T(2,128)S(1)}, u32[]{:S(2)}, u32[]{:S(2)}) collective-permute-start(f32[2,640]{1,0:T(2,128)S(1)} %merge_stats.1.s0), channel_id=1, source_target_pairs={{0,192},{64,0},{128,64},{192,128},{1,193},{65,1},{129,65},{193,129... | collective-permute-start | bytes 15368 | tf_op jit(solution)/shard_map/ppermute | solution.py:32
  34.3 4.8 %collective-permute-start.2 = (f32[2,640]{1,0:T(2,128)S(1)}, f32[2,640]{1,0:T(2,128)S(1)}, u32[]{:S(2)}, u32[]{:S(2)}) collective-permute-start(f32[2,640]{1,0:T(2,128)S(1)} %merge_stats.1.s0), channel_id=1, source_target_pairs={{0,64},{64,128},{128,192},{192,0},{1,65},{65,129},{129,193},{193,1... | collective-permute-start | bytes 15368 | tf_op jit(solution)/shard_map/ppermute | solution.py:32
  34.3 5.1 %collective-permute-start.1 = (f32[2,640]{1,0:T(2,128)S(1)}, f32[2,640]{1,0:T(2,128)S(1)}, u32[]{:S(2)}, u32[]{:S(2)}) collective-permute-start(f32[2,640]{1,0:T(2,128)S(1)} %merge_stats.1.s0), channel_id=1, source_target_pairs={{0,128},{64,192},{128,0},{192,64},{1,129},{65,193},{129,1},{193,65... | collective-permute-start | bytes 15368 | tf_op jit(solution)/shard_map/ppermute | solution.py:32
  41.8 9.1 %collective-permute-start.6 = (f16[2,8,32,384]{3,2,1,0:T(8,128)(2,1)S(1)}, f16[2,8,32,384]{3,2,1,0:T(8,128)(2,1)S(1)}, u32[]{:S(2)}, u32[]{:S(2)}) collective-permute-start(f16[2,8,32,384]{3,2,1,0:T(8,128)(2,1)S(1)} %get-tuple-element.57), channel_id=1, source_target_pairs={{0,2},{1,65},{2,4},{3,67},{4,6},{5,69},{6,0},{7,71},{8,10},{9,73},... | collective-permute-start | bytes 1179656 | tf_op jit(solution)/shard_map/ppermute | solution.py:44
  42.4 8.0 %collective-permute-start.7 = (f16[2,8,32,384]{3,2,1,0:T(8,128)(2,1)S(1)}, f16[2,8,32,384]{3,2,1,0:T(8,128)(2,1)S(1)}, u32[]{:S(2)}, u32[]{:S(2)}) collective-permute-start(f16[2,8,32,384]{3,2,1,0:T(8,128)(2,1)S(1)} %get-tuple-element.59), channel_id=1, source_target_pairs={{0,6},{1,193},{2,0},{3,195},{4,2},{5,197},{6,4},{7,199},{8,14},{9,... | collective-permute-start | bytes 1179656 | tf_op jit(solution)/shard_map/ppermute | solution.py:44
  51.0 8.4 %collective-permute-start.11 = (bf16[400,768]{1,0:T(8,128)(2,1)S(1)}, bf16[400,768]{1,0:T(8,128)(2,1)S(1)}, u32[]{:S(2)}, u32[]{:S(2)}) collective-permute-start(bf16[400,768]{1,0:T(8,128)(2,1)S(1)} %get-tuple-element.64.g_ref.g_own_ref), channel_id=1, source_target_pairs={{0,1},{1,0},{2,3},{3,2},{4,5},{5,4},{6,7},{7,6},{8,9},{9,8},{10,11... | collective-permute-start | bytes 1843208 | tf_op jit(solution)/shard_map/ppermute | solution.py:32
  51.1 13.2 %collective-permute-start.5 = (f16[2,8,32,384]{3,2,1,0:T(8,128)(2,1)S(1)}, f16[2,8,32,384]{3,2,1,0:T(8,128)(2,1)S(1)}, u32[]{:S(2)}, u32[]{:S(2)}) collective-permute-start(f16[2,8,32,384]{3,2,1,0:T(8,128)(2,1)S(1)} %multiply_convert_fusion.2), channel_id=1, source_target_pairs={{0,6},{1,193},{2,0},{3,195},{4,2},{5,197},{6,4},{7,199},{8,14},{9,... | collective-permute-start | bytes 1179656 | tf_op jit(solution)/shard_map/ppermute | solution.py:44
  54.6 9.8 %collective-permute-start.9 = (f16[2,8,32,384]{3,2,1,0:T(8,128)(2,1)S(1)}, f16[2,8,32,384]{3,2,1,0:T(8,128)(2,1)S(1)}, u32[]{:S(2)}, u32[]{:S(2)}) collective-permute-start(f16[2,8,32,384]{3,2,1,0:T(8,128)(2,1)S(1)} %multiply_convert_fusion.3), channel_id=1, source_target_pairs={{0,2},{1,65},{2,4},{3,67},{4,6},{5,69},{6,0},{7,71},{8,10},{9,73},... | collective-permute-start | bytes 1179656 | tf_op jit(solution)/shard_map/ppermute | solution.py:44
  54.7 13.2 %collective-permute-start.8 = (f16[2,8,32,384]{3,2,1,0:T(8,128)(2,1)S(1)}, f16[2,8,32,384]{3,2,1,0:T(8,128)(2,1)S(1)}, u32[]{:S(2)}, u32[]{:S(2)}) collective-permute-start(f16[2,8,32,384]{3,2,1,0:T(8,128)(2,1)S(1)} %multiply_convert_fusion.1), channel_id=1, source_target_pairs={{0,2},{1,65},{2,4},{3,67},{4,6},{5,69},{6,0},{7,71},{8,10},{9,73},... | collective-permute-start | bytes 1179656 | tf_op jit(solution)/shard_map/ppermute | solution.py:44
  54.7 13.2 %collective-permute-start.10 = (f16[2,8,32,384]{3,2,1,0:T(8,128)(2,1)S(1)}, f16[2,8,32,384]{3,2,1,0:T(8,128)(2,1)S(1)}, u32[]{:S(2)}, u32[]{:S(2)}) collective-permute-start(f16[2,8,32,384]{3,2,1,0:T(8,128)(2,1)S(1)} %multiply_convert_fusion), channel_id=1, source_target_pairs={{0,6},{1,193},{2,0},{3,195},{4,2},{5,197},{6,4},{7,199},{8,14},{9,... | collective-permute-start | bytes 1179656 | tf_op jit(solution)/shard_map/ppermute | solution.py:44
  68.4 7.0 %collective-permute-start.13 = (f16[8,32,384]{2,1,0:T(8,128)(2,1)S(1)}, f16[8,32,384]{2,1,0:T(8,128)(2,1)S(1)}, u32[]{:S(2)}, u32[]{:S(2)}) collective-permute-start(f16[8,32,384]{2,1,0:T(8,128)(2,1)S(1)} %fusion.7), channel_id=1, source_target_pairs={{0,64},{1,3},{2,66},{3,5},{4,68},{5,7},{6,70},{7,1},{8,72},{9,11},... | collective-permute-start | bytes 589832 | tf_op jit(solution)/shard_map/ppermute | solution.py:44
  69.0 9.9 %collective-permute-start.12 = (f16[8,32,384]{2,1,0:T(8,128)(2,1)S(1)}, f16[8,32,384]{2,1,0:T(8,128)(2,1)S(1)}, u32[]{:S(2)}, u32[]{:S(2)}) collective-permute-start(f16[8,32,384]{2,1,0:T(8,128)(2,1)S(1)} %get-tuple-element.75), channel_id=1, source_target_pairs={{0,128},{1,5},{2,130},{3,7},{4,132},{5,1},{6,134},{7,3},{8,136},{9... | collective-permute-start | bytes 589832 | tf_op jit(solution)/shard_map/ppermute | solution.py:44
  73.2 5.8 %collective-permute-start.14 = (f16[8,32,384]{2,1,0:T(8,128)(2,1)S(1)}, f16[8,32,384]{2,1,0:T(8,128)(2,1)S(1)}, u32[]{:S(2)}, u32[]{:S(2)}) collective-permute-start(f16[8,32,384]{2,1,0:T(8,128)(2,1)S(1)} %get-tuple-element.76), channel_id=1, source_target_pairs={{0,192},{1,7},{2,194},{3,1},{4,196},{5,3},{6,198},{7,5},{8,200},{9... | collective-permute-start | bytes 589832 | tf_op jit(solution)/shard_map/ppermute | solution.py:44

commit v10 on v8

--- a/solution.py
+++ b/solution.py
@@ -244,15 +244,9 @@
     )(pos, head5, g)
 
 
-def grad_kernel(
-    pos_ref, l_ref, t_ref, ids_ref, scale_ref, s0, s1, s2, s3, w_ref, g_ref, far_ref
-):
+def grad_kernel(pos_ref, l_ref, t_ref, ids_ref, scale_ref, stats_ref, w_ref, g_ref, far_ref):
     rows, cols = l_ref.shape
-    parts = (s0, s1, s2, s3)
-    first, second = (
-        jnp.concatenate([part[at : at + 1, :] for part in parts], axis=0) for at in (0, 1)
-    )
-    norm_s, norm_t, cross, picked = merge(first, second)
+    norm_s, norm_t, cross, picked = merge(stats_ref[:, 0, :], stats_ref[:, 1, :])
     terms = cross - norm_t + (1.0 + CE_WEIGHT) * norm_s
     terms = jnp.sum(terms, axis=1, keepdims=True) - CE_WEIGHT * picked
     high = terms.astype(BF16).astype(F32)
@@ -271,7 +265,7 @@
     hidden_product((chunk(2),), pos_ref, w_ref, g, (far_ref,))
 
 
-def grad_logits(pos, logits, teacher, ids, scale, parts, head5):
+def grad_logits(pos, logits, teacher, ids, scale, stats, head5):
     rows, cols = logits.shape
     _, nz, _, sub, _ = head5.shape
     return pl.pallas_call(
@@ -280,7 +274,7 @@
             jax.ShapeDtypeStruct((rows + LOSS_ROWS, cols), BF16),
             jax.ShapeDtypeStruct((4, nz, sub, rows), F32),
         ),
-        in_specs=[pl.BlockSpec(memory_space=pltpu.SMEM)] + [WHOLE] * 9,
+        in_specs=[pl.BlockSpec(memory_space=pltpu.SMEM)] + [WHOLE] * 6,
         out_specs=(WHOLE, WHOLE),
         compiler_params=params(16),
         cost_estimate=pl.CostEstimate(
@@ -289,7 +283,7 @@
             transcendentals=2 * rows * cols,
         ),
         name="grad_logits",
-    )(pos, logits, teacher, ids, scale, *parts, head5)
+    )(pos, logits, teacher, ids, scale, stats, head5)
 
 
 def head_kernel(pos_ref, own_ref, oth_ref, g_own_ref, g_oth_ref, out_ref, loss_ref, buf, sem):
@@ -349,16 +343,18 @@
     scale = row_scale.reshape(-1, 128)
 
     teacher_oth = shift(teacher, "c", 1)
+    hidden_oth = shift(lax.optimization_barrier((hidden, pos))[0], "c", 1)
     logits = student_logits(hidden, head)
     stats, teacher_rows = local_stats(pos, logits, teacher, teacher_oth, assign, ids)
-    stats, scale = lax.optimization_barrier((stats, scale))
-    stats = jnp.broadcast_to(stats[None], (nz * nx,) + stats.shape)
-    stats = merge_stats(lax.all_to_all(stats, ("z", "x"), 0, 0, tiled=True))
-    parts = [stats] + [shift(stats, "y", d) for d in (2, 1, 3)]
-    hidden_oth = shift(lax.optimization_barrier((hidden, stats))[0], "c", 1)
+    stats, scale, hidden_oth = lax.optimization_barrier((stats, scale, hidden_oth))
+
+    def gathered(value, axes, n):
+        value = jnp.broadcast_to(value[None], (n,) + value.shape)
+        return lax.all_to_all(value, axes, 0, 0, tiled=True)
+
+    stats = gathered(merge_stats(gathered(stats, ("y", "x"), ny * nx)), "z", nz)
     head5 = head.reshape(ny, nz, nx, depth // (ny * nz * nx), cols)
-    g, far2 = grad_logits(pos, logits, teacher_rows, ids, scale, parts, head5)
-    g, far2, hidden_oth = lax.optimization_barrier((g, far2, hidden_oth))
+    g, far2 = grad_logits(pos, logits, teacher_rows, ids, scale, stats, head5)
 
     def coded(value):
         return (value * SEND_SCALE).astype(F16)

time: 87.9 us -> 88.3 us (level)
  blocking collectives: 33.6 us -> 41.8 us
  starting transfers between devices: 14.1 us -> 8.54 us
  waiting for transfers between devices: 17.3 us -> 15 us
    all_to_all x1 -> x2, blocking collectives: 21.9 us -> 29.6 us  [gathered(): return lax.all_to_all(value, axes, 0, 0, tiled=True)]
    ppermute x6 -> x3, starting transfers between devices: 5.44 us -> 0.59 us  [shift(): return lax.ppermute(a, axis, [(i, (i + by) % n) for i in range(n)])]
    ppermute x6 -> x3, waiting for transfers between devices: 3.43 us -> 0.56 us  [shift(): return lax.ppermute(a, axis, [(i, (i + by) % n) for i in range(n)])]
  transfers between devices with their start and end apart: 12 -> 9, of which waited for: 7 -> 6; matrix products, arithmetic and copies ran while one was open for 1% -> 0% of each run, Pallas kernels for 19% -> 20%
where the time goes in v10:
time: 88.3 us; the launch traced here: 87.7 us
  blocking collectives  41.8 us (47%)
  Pallas kernels  19.4 us (22%)
  waiting for transfers between devices  15 us (17%)
  starting transfers between devices  8.54 us (10%)
  other arithmetic  2.16 us (2%)
    all_to_all x2, blocking collectives, gathered(): return lax.all_to_all(value, axes, 0, 0, tiled=True)  29.6 us
    ppermute x6, waiting for transfers between devices, shift_by_core(): return lax.ppermute(a, axes, pairs)  14.4 us
    all_to_all x1, blocking collectives, body(): both = lax.all_to_all(both, 'z', 0, 0, tiled=True)  12.2 us
    ppermute x6, starting transfers between devices, shift_by_core(): return lax.ppermute(a, axes, pairs)  7.95 us
    pallas_call x1, Pallas kernels, student_logits(): pl.pallas_call(functools.partial(logits_kernel, steps), out_shape=jax.Sha...  6.13 us
    pallas_call x1, Pallas kernels, head_grad(): pl.pallas_call(head_kernel, out_shape=(jax.ShapeDtypeStruct((width, cols)...  4.92 us
    pallas_call x2, Pallas kernels, hidden_part(): pl.pallas_call(functools.partial(hidden_kernel, groups), out_shape=out_sh...  3.87 us
    pallas_call x1, Pallas kernels, local_stats(): pl.pallas_call(stats_kernel, out_shape=(jax.ShapeDtypeStruct((2, rows + S...  2.26 us
  transfers between devices with their start and end apart: 9, of which 6 were waited for; matrix products, arithmetic and copies ran while one was open for 0% of the time, Pallas kernels for 20%

profile of v10, /device:TPU:32, one launch (start us, length us, event | category | flops | bytes accessed | tf_op | source)
XLA Modules:
  0.0 87.7 jit_solution(2171099579580431931)
XLA Ops:
  0.6 0.0 slice-start
  0.7 0.1 pad_add_fusion.pos_ref
  0.7 0.0 copy-start.2
  0.7 0.0 copy-start.3
  0.7 0.0 slice-start.1
  0.7 0.1 collective-permute-start.1
  0.8 0.5 collective-permute-start
  1.3 6.1 %student_logits.1.l_ref = f32[384,768]{1,0:T(8,128)S(1)} custom-call(bf16[384,4096]{1,0:T(8,128)(2,1)} %own_ref.3, bf16[4096,768]{1,0:T(8,128)(2,1)} %w_ref.1), custom_call_target="tpu_custom_call" | custom-call | flops 2415919104 | bytes 10616832 | tf_op jit(solution)/shard_map/student_logits/pallas_call | solution.py:75
  7.5 0.0 copy-start.4
  7.5 0.1 collective-permute-done.oth_ref
  7.5 0.0 copy-done.1
  7.5 0.0 copy-done.2
  7.6 0.0 copy-done.3
  7.6 2.3 %local_stats.1 = (f32[2,640]{1,0:T(2,128)S(1)}, bf16[384,768]{1,0:T(8,128)(2,1)S(1)}) custom-call(s32[4]{0:T(128)S(1)} %pad_add_fusion.pos_ref, f32[384,768]{1,0:T(8,128)S(1)} %student_logits.1.l_ref, bf16[768,384]{1,0:T(8,128)(2,1)S(1)} %copy-done.1, bf16[768,384]{1,0:T(8,128)(2,1)S(1)} %collective-permute-done.oth_ref, s32[6,128]{1,0:T(8,128)S(1)} %bitcast.34, ...), custom_call_target="tpu_custom_call" | custom-call | flops 452984832 | bytes 2949120 | tf_op jit(solution)/shard_map/local_stats/pallas_call | solution.py:190
  9.8 0.0 collective-permute-done.1.oth_ref
  9.9 14.6 %all_to_all.15.in_ref = f32[16,2,640]{2,1,0:T(2,128)S(1)} all-to-all(f32[16,2,640]{2,1,0:T(2,128)S(1)} %broadcast_in_dim.4), channel_id=1, replica_groups=mesh['y'=4,'z'=8,'x'=4,'c'=2] {'y','x'}, dimensions={0} | all-to-all | bytes 163840 | tf_op jit(solution)/shard_map/all_to_all | solution.py:353
  24.4 0.1 merge_stats.1
  24.6 15.0 %all_to_all.16.stats_ref = f32[8,2,640]{2,1,0:T(2,128)S(1)} all-to-all(f32[8,2,640]{2,1,0:T(2,128)S(1)} %broadcast_in_dim.5), channel_id=1, replica_groups=mesh['y'=4,'z'=8,'x'=4,'c'=2] {'z'}, dimensions={0} | all-to-all | bytes 81920 | tf_op jit(solution)/shard_map/all_to_all | solution.py:353
  39.6 0.0 slice-done
  39.6 0.0 slice-done.1
  39.6 0.0 copy-done.4
  39.6 2.1 %grad_logits.1 = (bf16[400,768]{1,0:T(8,128)(2,1)S(1)}, f32[4,8,32,384]{3,2,1,0:T(8,128)S(1)}) custom-call(s32[4]{0:T(128)S(1)} %pad_add_fusion.pos_ref, f32[384,768]{1,0:T(8,128)S(1)} %student_logits.1.l_ref, bf16[384,768]{1,0:T(8,128)(2,1)S(1)} %get-tuple-element.25.t_ref, s32[3,128]{1,0:T(4,128)S(1)} %bitcast.33, f32[3,128]{1,0:T(4,128)S(1)} %bitcast.35, ...), custom_call_target="tpu_custom_call" | custom-call | flops 2359296 | bytes 2359296 | tf_op jit(solution)/shard_map/grad_logits/pallas_call | solution.py:271
  41.7 0.2 multiply_convert_fusion.2
  41.9 1.4 %collective-permute-start.2 = (f16[4,8,32,384]{3,2,1,0:T(8,128)(2,1)S(1)}, f16[4,8,32,384]{3,2,1,0:T(8,128)(2,1)S(1)}, u32[]{:S(2)}, u32[]{:S(2)}) collective-permute-start(f16[4,8,32,384]{3,2,1,0:T(8,128)(2,1)S(1)} %multiply_convert_fusion.2), channel_id=1, source_target_pairs={{0,4},{1,129},{2,6},{3,131},{4,0},{5,133},{6,2},{7,135},{8,12},{9,... | collective-permute-start | bytes 2359304 | tf_op jit(solution)/shard_map/ppermute | solution.py:44
  43.3 2.3 %hidden_part.2 = (f32[4,8,32,384]{3,2,1,0:T(8,128)S(1)}, f32[4,8,32,384]{3,2,1,0:T(8,128)S(1)}) custom-call(s32[4]{0:T(128)S(1)} %pad_add_fusion.pos_ref, bf16[4,8,4,32,768]{4,3,2,1,0:T(8,128)(2,1)S(1)} %bitcast.30, bf16[400,768]{1,0:T(8,128)(2,1)S(1)} %get-tuple-element.39.g_ref.g_own_ref), custom_call_target="tpu_custom_call" | custom-call | flops 1 | bytes 1 | tf_op jit(solution)/shard_map/hidden_part/pallas_call | solution.py:236
  45.6 0.4 multiply_convert_fusion
  46.0 0.8 collective-permute-start.3
  46.8 2.5 %collective-permute-start.4 = (f16[4,8,32,384]{3,2,1,0:T(8,128)(2,1)S(1)}, f16[4,8,32,384]{3,2,1,0:T(8,128)(2,1)S(1)}, u32[]{:S(2)}, u32[]{:S(2)}) collective-permute-start(f16[4,8,32,384]{3,2,1,0:T(8,128)(2,1)S(1)} %get-tuple-element.37), channel_id=1, source_target_pairs={{0,6},{1,193},{2,0},{3,195},{4,2},{5,197},{6,4},{7,199},{8,14},{9,... | collective-permute-start | bytes 2359304 | tf_op jit(solution)/shard_map/ppermute | solution.py:44
  49.4 0.0 collective-permute-start.5
  49.4 0.0 copy-start
  49.4 1.5 %hidden_part.3 = f32[4,8,32,384]{3,2,1,0:T(8,128)S(1)} custom-call(s32[4]{0:T(128)S(1)} %pad_add_fusion.pos_ref, bf16[4,8,4,32,768]{4,3,2,1,0:T(8,128)(2,1)S(1)} %bitcast.31, bf16[400,768]{1,0:T(8,128)(2,1)S(1)} %get-tuple-element.39.g_ref.g_own_ref), custom_call_target="tpu_custom_call" | custom-call | flops 1 | bytes 1 | tf_op jit(solution)/shard_map/hidden_part/pallas_call | solution.py:236
  50.9 0.5 collective-permute-done.5.g_oth_ref
  51.4 0.0 copy-done
  51.4 4.9 %head_grad.1 = (bf16[2048,768]{1,0:T(8,128)(2,1)}, f32[1,128]{1,0:T(1,128)}) custom-call(s32[4]{0:T(128)S(1)} %pad_add_fusion.pos_ref, bf16[384,4096]{1,0:T(8,128)(2,1)S(1)} %copy-done, bf16[384,4096]{1,0:T(8,128)(2,1)S(1)} %collective-permute-done.1.oth_ref, bf16[400,768]{1,0:T(8,128)(2,1)S(1)} %get-tuple-element.39.g_ref.g_own_ref, ...), custom_call_target="tpu_custom_call" | custom-call | flops 1 | bytes 1 | tf_op jit(solution)/shard_map/head_grad/pallas_call | solution.py:316
  56.3 0.0 collective-permute-done.2
  56.3 7.6 %collective-permute-done.3 = f16[4,8,32,384]{3,2,1,0:T(8,128)(2,1)S(1)} collective-permute-done((f16[4,8,32,384]{3,2,1,0:T(8,128)(2,1)S(1)}, f16[4,8,32,384]{3,2,1,0:T(8,128)(2,1)S(1)}, u32[]{:S(2)}, u32[]{:S(2)}) %collective-permute-start.3) | collective-permute-done | bytes 786464 | tf_op jit(solution)/shard_map/ppermute | solution.py:44
  63.9 0.0 collective-permute-done.4
  63.9 0.6 multiply_add_fusion
  64.5 0.1 fusion.6
  64.6 1.2 %collective-permute-start.6 = (f16[8,32,384]{2,1,0:T(8,128)(2,1)S(1)}, f16[8,32,384]{2,1,0:T(8,128)(2,1)S(1)}, u32[]{:S(2)}, u32[]{:S(2)}) collective-permute-start(f16[8,32,384]{2,1,0:T(8,128)(2,1)S(1)} %get-tuple-element.47), channel_id=1, source_target_pairs={{0,128},{1,5},{2,130},{3,7},{4,132},{5,1},{6,134},{7,3},{8,136},{9... | collective-permute-start | bytes 589832 | tf_op jit(solution)/shard_map/ppermute | solution.py:44
  65.8 2.0 %collective-permute-start.8 = (f16[8,32,384]{2,1,0:T(8,128)(2,1)S(1)}, f16[8,32,384]{2,1,0:T(8,128)(2,1)S(1)}, u32[]{:S(2)}, u32[]{:S(2)}) collective-permute-start(f16[8,32,384]{2,1,0:T(8,128)(2,1)S(1)} %get-tuple-element.48), channel_id=1, source_target_pairs={{0,192},{1,7},{2,194},{3,1},{4,196},{5,3},{6,198},{7,5},{8,200},{9... | collective-permute-start | bytes 589832 | tf_op jit(solution)/shard_map/ppermute | solution.py:44
  67.8 0.0 collective-permute-start.7
  67.8 4.0 %collective-permute-done.6 = f16[8,32,384]{2,1,0:T(8,128)(2,1)S(1)} collective-permute-done((f16[8,32,384]{2,1,0:T(8,128)(2,1)S(1)}, f16[8,32,384]{2,1,0:T(8,128)(2,1)S(1)}, u32[]{:S(2)}, u32[]{:S(2)}) %collective-permute-start.6) | collective-permute-done | bytes 196640 | tf_op jit(solution)/shard_map/ppermute | solution.py:44
  71.9 0.5 collective-permute-done.8
  72.4 2.3 %collective-permute-done.7 = f16[8,32,384]{2,1,0:T(8,128)(2,1)S(1)} collective-permute-done((f16[8,32,384]{2,1,0:T(8,128)(2,1)S(1)}, f16[8,32,384]{2,1,0:T(8,128)(2,1)S(1)}, u32[]{:S(2)}, u32[]{:S(2)}) %collective-permute-start.7) | collective-permute-done | bytes 196640 | tf_op jit(solution)/shard_map/ppermute | solution.py:44
  74.7 0.1 fusion.5
  74.9 12.2 %all_to_all.17 = f16[8,32,384]{2,1,0:T(8,128)(2,1)S(1)} all-to-all(f16[8,32,384]{2,1,0:T(8,128)(2,1)S(1)} %fusion.5), channel_id=1, replica_groups=mesh['y'=4,'z'=8,'x'=4,'c'=2] {'z'}, dimensions={0} | all-to-all | bytes 393216 | tf_op jit(solution)/shard_map/all_to_all | solution.py:378
  87.0 0.7 multiply_reduce_fusion
  (4 shorter events, 0.0 us)
Async XLA Ops:
  0.6 39.0 %slice-start = ((s8[6291456]{0:T(1024)(128)(4,1)}), s8[4194304]{0:T(1024)(128)(4,1)S(1)}, s32[]{:S(2)}) async-start(s8[6291456]{0:T(1024)(128)(4,1)} %bitcast.27), calls=%async_computation.3 | async-start | bytes 8388608
  0.7 6.8 %copy-start.1 = (bf16[768,384]{1,0:T(8,128)(2,1)S(1)}, bf16[768,384]{1,0:T(8,128)(2,1)}, u32[]{:S(2)}) copy-start(bf16[768,384]{1,0:T(8,128)(2,1)} %own_ref.2) | copy-start | bytes 1769476
  0.7 6.8 %copy-start.2 = (s32[384]{0:T(512)S(1)}, s32[384]{0:T(512)}, u32[]{:S(2)}) copy-start(s32[384]{0:T(512)} %param.9) | copy-start | bytes 4612
  0.7 6.8 %copy-start.3 = (s32[768]{0:T(1024)S(1)}, s32[768]{0:T(1024)}, u32[]{:S(2)}) copy-start(s32[768]{0:T(1024)} %param.10) | copy-start | bytes 9220
  0.7 38.9 %slice-start.1 = ((s8[6291456]{0:T(1024)(128)(4,1)}), s8[2097152]{0:T(1024)(128)(4,1)S(1)}, s32[]{:S(2)}) async-start(s8[6291456]{0:T(1024)(128)(4,1)} %bitcast.27), calls=%async_computation.4 | async-start | bytes 4194304
  0.7 9.1 %collective-permute-start.1 = (bf16[384,4096]{1,0:T(8,128)(2,1)}, bf16[384,4096]{1,0:T(8,128)(2,1)S(1)}, u32[]{:S(2)}, u32[]{:S(2)}) collective-permute-start(bf16[384,4096]{1,0:T(8,128)(2,1)} %own_ref.3), channel_id=1, source_target_pairs={{0,1},{1,0},{2,3},{3,2},{4,5},{5,4},{6,7},{7,6},{8,9},{9,8},{10,11... | collective-permute-start | bytes 9437192 | tf_op jit(solution)/shard_map/ppermute | solution.py:32
  0.8 6.7 %collective-permute-start = (bf16[768,384]{1,0:T(8,128)(2,1)}, bf16[768,384]{1,0:T(8,128)(2,1)S(1)}, u32[]{:S(2)}, u32[]{:S(2)}) collective-permute-start(bf16[768,384]{1,0:T(8,128)(2,1)} %own_ref.2), channel_id=1, source_target_pairs={{0,1},{1,0},{2,3},{3,2},{4,5},{5,4},{6,7},{7,6},{8,9},{9,8},{10,11... | collective-permute-start | bytes 1769480 | tf_op jit(solution)/shard_map/ppermute | solution.py:32
  7.5 32.1 %copy-start.4 = (f32[384]{0:T(512)S(1)}, f32[384]{0:T(512)}, u32[]{:S(2)}) copy-start(f32[384]{0:T(512)} %param.11) | copy-start | bytes 4612
  41.9 14.4 %collective-permute-start.2 = (f16[4,8,32,384]{3,2,1,0:T(8,128)(2,1)S(1)}, f16[4,8,32,384]{3,2,1,0:T(8,128)(2,1)S(1)}, u32[]{:S(2)}, u32[]{:S(2)}) collective-permute-start(f16[4,8,32,384]{3,2,1,0:T(8,128)(2,1)S(1)} %multiply_convert_fusion.2), channel_id=1, source_target_pairs={{0,4},{1,129},{2,6},{3,131},{4,0},{5,133},{6,2},{7,135},{8,12},{9,... | collective-permute-start | bytes 2359304 | tf_op jit(solution)/shard_map/ppermute | solution.py:44
  46.0 17.9 %collective-permute-start.3 = (f16[4,8,32,384]{3,2,1,0:T(8,128)(2,1)S(1)}, f16[4,8,32,384]{3,2,1,0:T(8,128)(2,1)S(1)}, u32[]{:S(2)}, u32[]{:S(2)}) collective-permute-start(f16[4,8,32,384]{3,2,1,0:T(8,128)(2,1)S(1)} %get-tuple-element.36), channel_id=1, source_target_pairs={{0,2},{1,65},{2,4},{3,67},{4,6},{5,69},{6,0},{7,71},{8,10},{9,73},... | collective-permute-start | bytes 2359304 | tf_op jit(solution)/shard_map/ppermute | solution.py:44
  46.8 17.1 %collective-permute-start.4 = (f16[4,8,32,384]{3,2,1,0:T(8,128)(2,1)S(1)}, f16[4,8,32,384]{3,2,1,0:T(8,128)(2,1)S(1)}, u32[]{:S(2)}, u32[]{:S(2)}) collective-permute-start(f16[4,8,32,384]{3,2,1,0:T(8,128)(2,1)S(1)} %get-tuple-element.37), channel_id=1, source_target_pairs={{0,6},{1,193},{2,0},{3,195},{4,2},{5,197},{6,4},{7,199},{8,14},{9,... | collective-permute-start | bytes 2359304 | tf_op jit(solution)/shard_map/ppermute | solution.py:44
  49.4 2.0 %collective-permute-start.5 = (bf16[400,768]{1,0:T(8,128)(2,1)S(1)}, bf16[400,768]{1,0:T(8,128)(2,1)S(1)}, u32[]{:S(2)}, u32[]{:S(2)}) collective-permute-start(bf16[400,768]{1,0:T(8,128)(2,1)S(1)} %get-tuple-element.39.g_ref.g_own_ref), channel_id=1, source_target_pairs={{0,1},{1,0},{2,3},{3,2},{4,5},{5,4},{6,7},{7,6},{8,9},{9,8},{10,11... | collective-permute-start | bytes 1843208 | tf_op jit(solution)/shard_map/ppermute | solution.py:32
  49.4 2.0 %copy-start = (bf16[384,4096]{1,0:T(8,128)(2,1)S(1)}, bf16[384,4096]{1,0:T(8,128)(2,1)}, u32[]{:S(2)}) copy-start(bf16[384,4096]{1,0:T(8,128)(2,1)} %own_ref.3) | copy-start | bytes 9437188
  64.6 7.3 %collective-permute-start.6 = (f16[8,32,384]{2,1,0:T(8,128)(2,1)S(1)}, f16[8,32,384]{2,1,0:T(8,128)(2,1)S(1)}, u32[]{:S(2)}, u32[]{:S(2)}) collective-permute-start(f16[8,32,384]{2,1,0:T(8,128)(2,1)S(1)} %get-tuple-element.47), channel_id=1, source_target_pairs={{0,128},{1,5},{2,130},{3,7},{4,132},{5,1},{6,134},{7,3},{8,136},{9... | collective-permute-start | bytes 589832 | tf_op jit(solution)/shard_map/ppermute | solution.py:44
  65.8 6.6 %collective-permute-start.8 = (f16[8,32,384]{2,1,0:T(8,128)(2,1)S(1)}, f16[8,32,384]{2,1,0:T(8,128)(2,1)S(1)}, u32[]{:S(2)}, u32[]{:S(2)}) collective-permute-start(f16[8,32,384]{2,1,0:T(8,128)(2,1)S(1)} %get-tuple-element.48), channel_id=1, source_target_pairs={{0,192},{1,7},{2,194},{3,1},{4,196},{5,3},{6,198},{7,5},{8,200},{9... | collective-permute-start | bytes 589832 | tf_op jit(solution)/shard_map/ppermute | solution.py:44
  67.8 6.9 %collective-permute-start.7 = (f16[8,32,384]{2,1,0:T(8,128)(2,1)S(1)}, f16[8,32,384]{2,1,0:T(8,128)(2,1)S(1)}, u32[]{:S(2)}, u32[]{:S(2)}) collective-permute-start(f16[8,32,384]{2,1,0:T(8,128)(2,1)S(1)} %get-tuple-element.49), channel_id=1, source_target_pairs={{0,64},{1,3},{2,66},{3,5},{4,68},{5,7},{6,70},{7,1},{8,72},{9,11},... | collective-permute-start | bytes 589832 | tf_op jit(solution)/shard_map/ppermute | solution.py:44

commit v11 on v10

--- a/solution.py
+++ b/solution.py
@@ -343,10 +343,10 @@
     scale = row_scale.reshape(-1, 128)
 
     teacher_oth = shift(teacher, "c", 1)
-    hidden_oth = shift(lax.optimization_barrier((hidden, pos))[0], "c", 1)
     logits = student_logits(hidden, head)
     stats, teacher_rows = local_stats(pos, logits, teacher, teacher_oth, assign, ids)
-    stats, scale, hidden_oth = lax.optimization_barrier((stats, scale, hidden_oth))
+    stats, scale, hidden_far = lax.optimization_barrier((stats, scale, hidden))
+    hidden_oth = shift(hidden_far, "c", 1)
 
     def gathered(value, axes, n):
         value = jnp.broadcast_to(value[None], (n,) + value.shape)
@@ -372,9 +372,12 @@
     head_out, loss = head_grad(pos, hidden, hidden_oth, g, g_oth)
     loss = loss[0, :1]
     *got, loss, head_out = lax.optimization_barrier((*got, loss, head_out))
-    total = own + sum(taken(v) for v in got)
-    got = [shift_by_core(coded(total[d]), d, False) for d in (2, 1, 3)]
-    both = coded(total[0] + sum(taken(v) for v in got))
+
+    def summed(near):
+        return own[near] + sum(taken(v[near]) for v in got)
+
+    far = [shift_by_core(coded(summed(d)), d, False) for d in (2, 1, 3)]
+    both = coded(summed(0) + sum(taken(v) for v in far))
     both = lax.all_to_all(both, "z", 0, 0, tiled=True)
     hidden_grad = jnp.sum(taken(both), axis=0).T.astype(BF16)
     return loss, hidden_grad, head_out

time: 88.3 us -> 88.6 us (level)
  transfers between devices with their start and end apart: 9 -> 9, of which waited for: 6 -> 4; matrix products, arithmetic and copies ran while one was open for 0% -> 1% of each run, Pallas kernels for 20% -> 19%
where the time goes in v11:
time: 88.6 us; the launch traced here: 87.3 us
  blocking collectives  41.8 us (47%)
  Pallas kernels  19.2 us (22%)
  waiting for transfers between devices  15 us (17%)
  starting transfers between devices  8.54 us (10%)
  other arithmetic  1.97 us (2%)
    all_to_all x2, blocking collectives, gathered(): return lax.all_to_all(value, axes, 0, 0, tiled=True)  29.6 us
    ppermute x6, waiting for transfers between devices, shift_by_core(): return lax.ppermute(a, axes, pairs)  14.5 us
    all_to_all x1, blocking collectives, body(): both = lax.all_to_all(both, 'z', 0, 0, tiled=True)  12.2 us
    ppermute x6, starting transfers between devices, shift_by_core(): return lax.ppermute(a, axes, pairs)  7.93 us
    pallas_call x1, Pallas kernels, student_logits(): pl.pallas_call(functools.partial(logits_kernel, steps), out_shape=jax.Sha...  5.91 us
    pallas_call x1, Pallas kernels, head_grad(): pl.pallas_call(head_kernel, out_shape=(jax.ShapeDtypeStruct((width, cols)...  4.94 us
    pallas_call x2, Pallas kernels, hidden_part(): pl.pallas_call(functools.partial(hidden_kernel, groups), out_shape=out_sh...  3.87 us
    pallas_call x1, Pallas kernels, local_stats(): pl.pallas_call(stats_kernel, out_shape=(jax.ShapeDtypeStruct((2, rows + S...  2.26 us
  transfers between devices with their start and end apart: 9, of which 4 were waited for; matrix products, arithmetic and copies ran while one was open for 1% of the time, Pallas kernels for 19%

profile of v11, /device:TPU:32, one launch (start us, length us, event | category | flops | bytes accessed | tf_op | source)
XLA Modules:
  0.0 87.3 jit_solution(6081167604853206624)
XLA Ops:
  0.6 0.1 collective-permute-start
  0.7 0.0 slice-start
  0.8 0.1 pad_add_fusion.pos_ref
  0.8 0.0 copy-start.1
  0.8 0.0 copy-start.2
  0.8 0.0 copy-start.3
  0.8 0.0 copy-start
  0.8 0.0 slice-start.1
  0.9 5.9 %student_logits.1.l_ref = f32[384,768]{1,0:T(8,128)S(1)} custom-call(bf16[384,4096]{1,0:T(8,128)(2,1)} %own_ref.3, bf16[4096,768]{1,0:T(8,128)(2,1)} %w_ref.1), custom_call_target="tpu_custom_call" | custom-call | flops 2415919104 | bytes 10616832 | tf_op jit(solution)/shard_map/student_logits/pallas_call | solution.py:75
  6.8 0.0 copy-start.4
  6.8 0.0 collective-permute-done.oth_ref
  6.8 0.0 copy-done.1
  6.8 0.0 copy-done.2
  6.8 0.0 copy-done.3
  6.8 2.3 %local_stats.1 = (f32[2,640]{1,0:T(2,128)S(1)}, bf16[384,768]{1,0:T(8,128)(2,1)S(1)}) custom-call(s32[4]{0:T(128)S(1)} %pad_add_fusion.pos_ref, f32[384,768]{1,0:T(8,128)S(1)} %student_logits.1.l_ref, bf16[768,384]{1,0:T(8,128)(2,1)S(1)} %copy-done.1, bf16[768,384]{1,0:T(8,128)(2,1)S(1)} %collective-permute-done.oth_ref, s32[6,128]{1,0:T(8,128)S(1)} %bitcast.34, ...), custom_call_target="tpu_custom_call" | custom-call | flops 452984832 | bytes 2949120 | tf_op jit(solution)/shard_map/local_stats/pallas_call | solution.py:190
  9.1 0.0 copy-done
  9.1 0.5 collective-permute-start.4
  9.6 14.6 %all_to_all.15.in_ref = f32[16,2,640]{2,1,0:T(2,128)S(1)} all-to-all(f32[16,2,640]{2,1,0:T(2,128)S(1)} %broadcast_in_dim.4), channel_id=1, replica_groups=mesh['y'=4,'z'=8,'x'=4,'c'=2] {'y','x'}, dimensions={0} | all-to-all | bytes 163840 | tf_op jit(solution)/shard_map/all_to_all | solution.py:353
  24.2 0.1 merge_stats.1
  24.3 15.0 %all_to_all.16.stats_ref = f32[8,2,640]{2,1,0:T(2,128)S(1)} all-to-all(f32[8,2,640]{2,1,0:T(2,128)S(1)} %broadcast_in_dim.5), channel_id=1, replica_groups=mesh['y'=4,'z'=8,'x'=4,'c'=2] {'z'}, dimensions={0} | all-to-all | bytes 81920 | tf_op jit(solution)/shard_map/all_to_all | solution.py:353
  39.4 0.0 slice-done
  39.4 0.0 slice-done.1
  39.4 0.0 copy-done.4
  39.4 2.1 %grad_logits.1 = (bf16[400,768]{1,0:T(8,128)(2,1)S(1)}, f32[4,8,32,384]{3,2,1,0:T(8,128)S(1)}) custom-call(s32[4]{0:T(128)S(1)} %pad_add_fusion.pos_ref, f32[384,768]{1,0:T(8,128)S(1)} %student_logits.1.l_ref, bf16[384,768]{1,0:T(8,128)(2,1)S(1)} %get-tuple-element.24.t_ref, s32[3,128]{1,0:T(4,128)S(1)} %bitcast.33, f32[3,128]{1,0:T(4,128)S(1)} %bitcast.35, ...), custom_call_target="tpu_custom_call" | custom-call | flops 2359296 | bytes 2359296 | tf_op jit(solution)/shard_map/grad_logits/pallas_call | solution.py:271
  41.5 0.2 multiply_convert_fusion.2
  41.7 1.4 %collective-permute-start.1 = (f16[4,8,32,384]{3,2,1,0:T(8,128)(2,1)S(1)}, f16[4,8,32,384]{3,2,1,0:T(8,128)(2,1)S(1)}, u32[]{:S(2)}, u32[]{:S(2)}) collective-permute-start(f16[4,8,32,384]{3,2,1,0:T(8,128)(2,1)S(1)} %multiply_convert_fusion.2), channel_id=1, source_target_pairs={{0,4},{1,129},{2,6},{3,131},{4,0},{5,133},{6,2},{7,135},{8,12},{9,... | collective-permute-start | bytes 2359304 | tf_op jit(solution)/shard_map/ppermute | solution.py:44
  43.0 2.3 %hidden_part.2 = (f32[4,8,32,384]{3,2,1,0:T(8,128)S(1)}, f32[4,8,32,384]{3,2,1,0:T(8,128)S(1)}) custom-call(s32[4]{0:T(128)S(1)} %pad_add_fusion.pos_ref, bf16[4,8,4,32,768]{4,3,2,1,0:T(8,128)(2,1)S(1)} %bitcast.30, bf16[400,768]{1,0:T(8,128)(2,1)S(1)} %get-tuple-element.37.g_ref.g_own_ref), custom_call_target="tpu_custom_call" | custom-call | flops 1 | bytes 1 | tf_op jit(solution)/shard_map/hidden_part/pallas_call | solution.py:236
  45.4 0.4 multiply_convert_fusion
  45.8 0.8 collective-permute-start.2
  46.6 2.5 %collective-permute-start.3 = (f16[4,8,32,384]{3,2,1,0:T(8,128)(2,1)S(1)}, f16[4,8,32,384]{3,2,1,0:T(8,128)(2,1)S(1)}, u32[]{:S(2)}, u32[]{:S(2)}) collective-permute-start(f16[4,8,32,384]{3,2,1,0:T(8,128)(2,1)S(1)} %get-tuple-element.35), channel_id=1, source_target_pairs={{0,6},{1,193},{2,0},{3,195},{4,2},{5,197},{6,4},{7,199},{8,14},{9,... | collective-permute-start | bytes 2359304 | tf_op jit(solution)/shard_map/ppermute | solution.py:44
  49.1 0.0 collective-permute-start.5
  49.1 1.5 %hidden_part.3 = f32[4,8,32,384]{3,2,1,0:T(8,128)S(1)} custom-call(s32[4]{0:T(128)S(1)} %pad_add_fusion.pos_ref, bf16[4,8,4,32,768]{4,3,2,1,0:T(8,128)(2,1)S(1)} %bitcast.31, bf16[400,768]{1,0:T(8,128)(2,1)S(1)} %get-tuple-element.37.g_ref.g_own_ref), custom_call_target="tpu_custom_call" | custom-call | flops 1 | bytes 1 | tf_op jit(solution)/shard_map/hidden_part/pallas_call | solution.py:236
  50.7 0.5 collective-permute-done.5.g_oth_ref
  51.2 0.0 collective-permute-done.4.oth_ref
  51.2 4.9 %head_grad.1 = (bf16[2048,768]{1,0:T(8,128)(2,1)}, f32[1,128]{1,0:T(1,128)}) custom-call(s32[4]{0:T(128)S(1)} %pad_add_fusion.pos_ref, bf16[384,4096]{1,0:T(8,128)(2,1)S(1)} %copy-done, bf16[384,4096]{1,0:T(8,128)(2,1)S(1)} %collective-permute-done.4.oth_ref, bf16[400,768]{1,0:T(8,128)(2,1)S(1)} %get-tuple-element.37.g_ref.g_own_ref, ...), custom_call_target="tpu_custom_call" | custom-call | flops 1 | bytes 1 | tf_op jit(solution)/shard_map/head_grad/pallas_call | solution.py:316
  56.1 0.0 collective-permute-done.1
  56.1 7.6 %collective-permute-done.2 = f16[4,8,32,384]{3,2,1,0:T(8,128)(2,1)S(1)} collective-permute-done((f16[4,8,32,384]{3,2,1,0:T(8,128)(2,1)S(1)}, f16[4,8,32,384]{3,2,1,0:T(8,128)(2,1)S(1)}, u32[]{:S(2)}, u32[]{:S(2)}) %collective-permute-start.2) | collective-permute-done | bytes 786464 | tf_op jit(solution)/shard_map/ppermute | solution.py:44
  63.7 0.0 collective-permute-done.3
  63.7 0.4 fusion.10
  64.1 1.1 %collective-permute-start.8 = (f16[8,32,384]{2,1,0:T(8,128)(2,1)S(1)}, f16[8,32,384]{2,1,0:T(8,128)(2,1)S(1)}, u32[]{:S(2)}, u32[]{:S(2)}) collective-permute-start(f16[8,32,384]{2,1,0:T(8,128)(2,1)S(1)} %get-tuple-element.46), channel_id=1, source_target_pairs={{0,192},{1,7},{2,194},{3,1},{4,196},{5,3},{6,198},{7,5},{8,200},{9... | collective-permute-start | bytes 589832 | tf_op jit(solution)/shard_map/ppermute | solution.py:44
  65.2 1.0 %collective-permute-start.7 = (f16[8,32,384]{2,1,0:T(8,128)(2,1)S(1)}, f16[8,32,384]{2,1,0:T(8,128)(2,1)S(1)}, u32[]{:S(2)}, u32[]{:S(2)}) collective-permute-start(f16[8,32,384]{2,1,0:T(8,128)(2,1)S(1)} %get-tuple-element.47), channel_id=1, source_target_pairs={{0,64},{1,3},{2,66},{3,5},{4,68},{5,7},{6,70},{7,1},{8,72},{9,11},... | collective-permute-start | bytes 589832 | tf_op jit(solution)/shard_map/ppermute | solution.py:44
  66.2 1.1 %collective-permute-start.6 = (f16[8,32,384]{2,1,0:T(8,128)(2,1)S(1)}, f16[8,32,384]{2,1,0:T(8,128)(2,1)S(1)}, u32[]{:S(2)}, u32[]{:S(2)}) collective-permute-start(f16[8,32,384]{2,1,0:T(8,128)(2,1)S(1)} %get-tuple-element.45), channel_id=1, source_target_pairs={{0,128},{1,5},{2,130},{3,7},{4,132},{5,1},{6,134},{7,3},{8,136},{9... | collective-permute-start | bytes 589832 | tf_op jit(solution)/shard_map/ppermute | solution.py:44
  67.3 2.5 %collective-permute-done.8 = f16[8,32,384]{2,1,0:T(8,128)(2,1)S(1)} collective-permute-done((f16[8,32,384]{2,1,0:T(8,128)(2,1)S(1)}, f16[8,32,384]{2,1,0:T(8,128)(2,1)S(1)}, u32[]{:S(2)}, u32[]{:S(2)}) %collective-permute-start.8) | collective-permute-done | bytes 196640 | tf_op jit(solution)/shard_map/ppermute | solution.py:44
  69.9 4.4 %collective-permute-done.7 = f16[8,32,384]{2,1,0:T(8,128)(2,1)S(1)} collective-permute-done((f16[8,32,384]{2,1,0:T(8,128)(2,1)S(1)}, f16[8,32,384]{2,1,0:T(8,128)(2,1)S(1)}, u32[]{:S(2)}, u32[]{:S(2)}) %collective-permute-start.7) | collective-permute-done | bytes 196640 | tf_op jit(solution)/shard_map/ppermute | solution.py:44
  74.2 0.0 collective-permute-done.6
  74.2 0.2 fusion.9
  74.5 12.2 %all_to_all.17 = f16[8,32,384]{2,1,0:T(8,128)(2,1)S(1)} all-to-all(f16[8,32,384]{2,1,0:T(8,128)(2,1)S(1)} %fusion.9), channel_id=1, replica_groups=mesh['y'=4,'z'=8,'x'=4,'c'=2] {'z'}, dimensions={0} | all-to-all | bytes 393216 | tf_op jit(solution)/shard_map/all_to_all | solution.py:381
  86.7 0.7 multiply_reduce_fusion
  (3 shorter events, 0.0 us)
Async XLA Ops:
  0.6 6.2 %collective-permute-start = (bf16[768,384]{1,0:T(8,128)(2,1)}, bf16[768,384]{1,0:T(8,128)(2,1)S(1)}, u32[]{:S(2)}, u32[]{:S(2)}) collective-permute-start(bf16[768,384]{1,0:T(8,128)(2,1)} %own_ref.2), channel_id=1, source_target_pairs={{0,1},{1,0},{2,3},{3,2},{4,5},{5,4},{6,7},{7,6},{8,9},{9,8},{10,11... | collective-permute-start | bytes 1769480 | tf_op jit(solution)/shard_map/ppermute | solution.py:32
  0.7 38.6 %slice-start = ((s8[6291456]{0:T(1024)(128)(4,1)}), s8[4194304]{0:T(1024)(128)(4,1)S(1)}, s32[]{:S(2)}) async-start(s8[6291456]{0:T(1024)(128)(4,1)} %bitcast.27), calls=%async_computation.3 | async-start | bytes 8388608
  0.8 6.0 %copy-start.1 = (bf16[768,384]{1,0:T(8,128)(2,1)S(1)}, bf16[768,384]{1,0:T(8,128)(2,1)}, u32[]{:S(2)}) copy-start(bf16[768,384]{1,0:T(8,128)(2,1)} %own_ref.2) | copy-start | bytes 1769476
  0.8 6.0 %copy-start.2 = (s32[384]{0:T(512)S(1)}, s32[384]{0:T(512)}, u32[]{:S(2)}) copy-start(s32[384]{0:T(512)} %param.9) | copy-start | bytes 4612
  0.8 6.0 %copy-start.3 = (s32[768]{0:T(1024)S(1)}, s32[768]{0:T(1024)}, u32[]{:S(2)}) copy-start(s32[768]{0:T(1024)} %param.10) | copy-start | bytes 9220
  0.8 8.3 %copy-start = (bf16[384,4096]{1,0:T(8,128)(2,1)S(1)}, bf16[384,4096]{1,0:T(8,128)(2,1)}, u32[]{:S(2)}) copy-start(bf16[384,4096]{1,0:T(8,128)(2,1)} %own_ref.3) | copy-start | bytes 9437188
  0.8 38.5 %slice-start.1 = ((s8[6291456]{0:T(1024)(128)(4,1)}), s8[2097152]{0:T(1024)(128)(4,1)S(1)}, s32[]{:S(2)}) async-start(s8[6291456]{0:T(1024)(128)(4,1)} %bitcast.27), calls=%async_computation.4 | async-start | bytes 4194304
  6.8 32.6 %copy-start.4 = (f32[384]{0:T(512)S(1)}, f32[384]{0:T(512)}, u32[]{:S(2)}) copy-start(f32[384]{0:T(512)} %param.11) | copy-start | bytes 4612
  9.1 42.1 %collective-permute-start.4 = (bf16[384,4096]{1,0:T(8,128)(2,1)S(1)}, bf16[384,4096]{1,0:T(8,128)(2,1)S(1)}, u32[]{:S(2)}, u32[]{:S(2)}) collective-permute-start(bf16[384,4096]{1,0:T(8,128)(2,1)S(1)} %copy-done), channel_id=1, source_target_pairs={{0,1},{1,0},{2,3},{3,2},{4,5},{5,4},{6,7},{7,6},{8,9},{9,8},{10,11... | collective-permute-start | bytes 9437192 | tf_op jit(solution)/shard_map/ppermute | solution.py:32
  41.7 14.4 %collective-permute-start.1 = (f16[4,8,32,384]{3,2,1,0:T(8,128)(2,1)S(1)}, f16[4,8,32,384]{3,2,1,0:T(8,128)(2,1)S(1)}, u32[]{:S(2)}, u32[]{:S(2)}) collective-permute-start(f16[4,8,32,384]{3,2,1,0:T(8,128)(2,1)S(1)} %multiply_convert_fusion.2), channel_id=1, source_target_pairs={{0,4},{1,129},{2,6},{3,131},{4,0},{5,133},{6,2},{7,135},{8,12},{9,... | collective-permute-start | bytes 2359304 | tf_op jit(solution)/shard_map/ppermute | solution.py:44
  45.8 17.9 %collective-permute-start.2 = (f16[4,8,32,384]{3,2,1,0:T(8,128)(2,1)S(1)}, f16[4,8,32,384]{3,2,1,0:T(8,128)(2,1)S(1)}, u32[]{:S(2)}, u32[]{:S(2)}) collective-permute-start(f16[4,8,32,384]{3,2,1,0:T(8,128)(2,1)S(1)} %get-tuple-element.34), channel_id=1, source_target_pairs={{0,2},{1,65},{2,4},{3,67},{4,6},{5,69},{6,0},{7,71},{8,10},{9,73},... | collective-permute-start | bytes 2359304 | tf_op jit(solution)/shard_map/ppermute | solution.py:44
  46.6 17.1 %collective-permute-start.3 = (f16[4,8,32,384]{3,2,1,0:T(8,128)(2,1)S(1)}, f16[4,8,32,384]{3,2,1,0:T(8,128)(2,1)S(1)}, u32[]{:S(2)}, u32[]{:S(2)}) collective-permute-start(f16[4,8,32,384]{3,2,1,0:T(8,128)(2,1)S(1)} %get-tuple-element.35), channel_id=1, source_target_pairs={{0,6},{1,193},{2,0},{3,195},{4,2},{5,197},{6,4},{7,199},{8,14},{9,... | collective-permute-start | bytes 2359304 | tf_op jit(solution)/shard_map/ppermute | solution.py:44
  49.1 2.0 %collective-permute-start.5 = (bf16[400,768]{1,0:T(8,128)(2,1)S(1)}, bf16[400,768]{1,0:T(8,128)(2,1)S(1)}, u32[]{:S(2)}, u32[]{:S(2)}) collective-permute-start(bf16[400,768]{1,0:T(8,128)(2,1)S(1)} %get-tuple-element.37.g_ref.g_own_ref), channel_id=1, source_target_pairs={{0,1},{1,0},{2,3},{3,2},{4,5},{5,4},{6,7},{7,6},{8,9},{9,8},{10,11... | collective-permute-start | bytes 1843208 | tf_op jit(solution)/shard_map/ppermute | solution.py:32
  64.1 5.7 %collective-permute-start.8 = (f16[8,32,384]{2,1,0:T(8,128)(2,1)S(1)}, f16[8,32,384]{2,1,0:T(8,128)(2,1)S(1)}, u32[]{:S(2)}, u32[]{:S(2)}) collective-permute-start(f16[8,32,384]{2,1,0:T(8,128)(2,1)S(1)} %get-tuple-element.46), channel_id=1, source_target_pairs={{0,192},{1,7},{2,194},{3,1},{4,196},{5,3},{6,198},{7,5},{8,200},{9... | collective-permute-start | bytes 589832 | tf_op jit(solution)/shard_map/ppermute | solution.py:44
  65.2 9.0 %collective-permute-start.7 = (f16[8,32,384]{2,1,0:T(8,128)(2,1)S(1)}, f16[8,32,384]{2,1,0:T(8,128)(2,1)S(1)}, u32[]{:S(2)}, u32[]{:S(2)}) collective-permute-start(f16[8,32,384]{2,1,0:T(8,128)(2,1)S(1)} %get-tuple-element.47), channel_id=1, source_target_pairs={{0,64},{1,3},{2,66},{3,5},{4,68},{5,7},{6,70},{7,1},{8,72},{9,11},... | collective-permute-start | bytes 589832 | tf_op jit(solution)/shard_map/ppermute | solution.py:44
  66.2 8.0 %collective-permute-start.6 = (f16[8,32,384]{2,1,0:T(8,128)(2,1)S(1)}, f16[8,32,384]{2,1,0:T(8,128)(2,1)S(1)}, u32[]{:S(2)}, u32[]{:S(2)}) collective-permute-start(f16[8,32,384]{2,1,0:T(8,128)(2,1)S(1)} %get-tuple-element.45), channel_id=1, source_target_pairs={{0,128},{1,5},{2,130},{3,7},{4,132},{5,1},{6,134},{7,3},{8,136},{9... | collective-permute-start | bytes 589832 | tf_op jit(solution)/shard_map/ppermute | solution.py:44

commit v12 on v11

--- a/solution.py
+++ b/solution.py
@@ -345,14 +345,16 @@
     teacher_oth = shift(teacher, "c", 1)
     logits = student_logits(hidden, head)
     stats, teacher_rows = local_stats(pos, logits, teacher, teacher_oth, assign, ids)
-    stats, scale, hidden_far = lax.optimization_barrier((stats, scale, hidden))
-    hidden_oth = shift(hidden_far, "c", 1)
+    stats, scale = lax.optimization_barrier((stats, scale))
 
     def gathered(value, axes, n):
         value = jnp.broadcast_to(value[None], (n,) + value.shape)
         return lax.all_to_all(value, axes, 0, 0, tiled=True)
 
-    stats = gathered(merge_stats(gathered(stats, ("y", "x"), ny * nx)), "z", nz)
+    stats = merge_stats(gathered(stats, ("y", "x"), ny * nx))
+    stats, hidden_far = lax.optimization_barrier((stats, hidden))
+    hidden_oth = shift(hidden_far, "c", 1)
+    stats = gathered(stats, "z", nz)
     head5 = head.reshape(ny, nz, nx, depth // (ny * nz * nx), cols)
     g, far2 = grad_logits(pos, logits, teacher_rows, ids, scale, stats, head5)
 
@@ -376,7 +378,10 @@
     def summed(near):
         return own[near] + sum(taken(v[near]) for v in got)
 
-    far = [shift_by_core(coded(summed(d)), d, False) for d in (2, 1, 3)]
+    far2 = coded(summed(2))
+    far2, own, *got = lax.optimization_barrier((far2, own, *got))
+    far = [shift_by_core(coded(summed(d)), d, False) for d in (3, 1)]
+    far += [shift_by_core(far2, 2, False)]
     both = coded(summed(0) + sum(taken(v) for v in far))
     both = lax.all_to_all(both, "z", 0, 0, tiled=True)
     hidden_grad = jnp.sum(taken(both), axis=0).T.astype(BF16)

time: 88.6 us -> 86.7 us (0.979)
  waiting for transfers between devices: 15 us -> 12.6 us
    ppermute x6, waiting for transfers between devices: 14.5 us -> 12.1 us  [shift_by_core(): return lax.ppermute(a, axes, pairs)]
    ppermute x6, starting transfers between devices: 7.93 us -> 9.23 us  [shift_by_core(): return lax.ppermute(a, axes, pairs)]
  transfers between devices with their start and end apart: 9 -> 9, of which waited for: 4 -> 4; matrix products, arithmetic and copies ran while one was open for 1% -> 1% of each run, Pallas kernels for 19% -> 20%
where the time goes in v12:
time: 86.7 us; the launch traced here: 85.7 us
  blocking collectives  41.6 us (48%)
  Pallas kernels  19.2 us (22%)
  waiting for transfers between devices  12.6 us (15%)
  starting transfers between devices  9.38 us (11%)
  other arithmetic  1.97 us (2%)
    all_to_all x2, blocking collectives, gathered(): return lax.all_to_all(value, axes, 0, 0, tiled=True)  29.6 us
    ppermute x6, waiting for transfers between devices, shift_by_core(): return lax.ppermute(a, axes, pairs)  12.1 us
    all_to_all x1, blocking collectives, body(): both = lax.all_to_all(both, 'z', 0, 0, tiled=True)  12 us
    ppermute x6, starting transfers between devices, shift_by_core(): return lax.ppermute(a, axes, pairs)  9.23 us
    pallas_call x1, Pallas kernels, student_logits(): pl.pallas_call(functools.partial(logits_kernel, steps), out_shape=jax.Sha...  5.91 us
    pallas_call x1, Pallas kernels, head_grad(): pl.pallas_call(head_kernel, out_shape=(jax.ShapeDtypeStruct((width, cols)...  4.93 us
    pallas_call x2, Pallas kernels, hidden_part(): pl.pallas_call(functools.partial(hidden_kernel, groups), out_shape=out_sh...  3.87 us
    pallas_call x1, Pallas kernels, local_stats(): pl.pallas_call(stats_kernel, out_shape=(jax.ShapeDtypeStruct((2, rows + S...  2.26 us
  transfers between devices with their start and end apart: 9, of which 4 were waited for; matrix products, arithmetic and copies ran while one was open for 1% of the time, Pallas kernels for 20%

profile of v12, /device:TPU:32, one launch (start us, length us, event | category | flops | bytes accessed | tf_op | source)
XLA Modules:
  0.0 85.7 jit_solution(16845286841642487750)
XLA Ops:
  0.6 0.1 collective-permute-start
  0.7 0.0 slice-start
  0.8 0.1 pad_add_fusion.pos_ref
  0.8 0.0 copy-start.1
  0.8 0.0 copy-start.2
  0.8 0.0 copy-start.3
  0.8 0.0 slice-start.1
  0.9 5.9 %student_logits.1.l_ref = f32[384,768]{1,0:T(8,128)S(1)} custom-call(bf16[384,4096]{1,0:T(8,128)(2,1)} %own_ref.3, bf16[4096,768]{1,0:T(8,128)(2,1)} %w_ref.1), custom_call_target="tpu_custom_call" | custom-call | flops 2415919104 | bytes 10616832 | tf_op jit(solution)/shard_map/student_logits/pallas_call | solution.py:75
  6.8 0.0 copy-start.4
  6.8 0.0 collective-permute-done.oth_ref
  6.8 0.0 copy-done.1
  6.8 0.0 copy-done.2
  6.8 0.0 copy-done.3
  6.8 2.3 %local_stats.1 = (f32[2,640]{1,0:T(2,128)S(1)}, bf16[384,768]{1,0:T(8,128)(2,1)S(1)}) custom-call(s32[4]{0:T(128)S(1)} %pad_add_fusion.pos_ref, f32[384,768]{1,0:T(8,128)S(1)} %student_logits.1.l_ref, bf16[768,384]{1,0:T(8,128)(2,1)S(1)} %copy-done.1, bf16[768,384]{1,0:T(8,128)(2,1)S(1)} %collective-permute-done.oth_ref, s32[6,128]{1,0:T(8,128)S(1)} %bitcast.32, ...), custom_call_target="tpu_custom_call" | custom-call | flops 452984832 | bytes 2949120 | tf_op jit(solution)/shard_map/local_stats/pallas_call | solution.py:190
  9.1 14.6 %all_to_all.15.in_ref = f32[16,2,640]{2,1,0:T(2,128)S(1)} all-to-all(f32[16,2,640]{2,1,0:T(2,128)S(1)} %broadcast_in_dim.4), channel_id=1, replica_groups=mesh['y'=4,'z'=8,'x'=4,'c'=2] {'y','x'}, dimensions={0} | all-to-all | bytes 163840 | tf_op jit(solution)/shard_map/all_to_all | solution.py:352
  23.7 0.1 merge_stats.1
  23.8 0.0 copy-done
  23.8 0.1 collective-permute-start.4
  23.9 15.0 %all_to_all.16.stats_ref = f32[8,2,640]{2,1,0:T(2,128)S(1)} all-to-all(f32[8,2,640]{2,1,0:T(2,128)S(1)} %broadcast_in_dim.5), channel_id=1, replica_groups=mesh['y'=4,'z'=8,'x'=4,'c'=2] {'z'}, dimensions={0} | all-to-all | bytes 81920 | tf_op jit(solution)/shard_map/all_to_all | solution.py:352
  38.9 0.0 slice-done
  38.9 0.0 slice-done.1
  38.9 0.0 copy-done.4
  39.0 2.1 %grad_logits.1 = (bf16[400,768]{1,0:T(8,128)(2,1)S(1)}, f32[4,8,32,384]{3,2,1,0:T(8,128)S(1)}) custom-call(s32[4]{0:T(128)S(1)} %pad_add_fusion.pos_ref, f32[384,768]{1,0:T(8,128)S(1)} %student_logits.1.l_ref, bf16[384,768]{1,0:T(8,128)(2,1)S(1)} %get-tuple-element.30.t_ref, s32[3,128]{1,0:T(4,128)S(1)} %bitcast.31, f32[3,128]{1,0:T(4,128)S(1)} %bitcast.33, ...), custom_call_target="tpu_custom_call" | custom-call | flops 2359296 | bytes 2359296 | tf_op jit(solution)/shard_map/grad_logits/pallas_call | solution.py:271
  41.1 0.2 multiply_convert_fusion.2
  41.2 1.4 %collective-permute-start.1 = (f16[4,8,32,384]{3,2,1,0:T(8,128)(2,1)S(1)}, f16[4,8,32,384]{3,2,1,0:T(8,128)(2,1)S(1)}, u32[]{:S(2)}, u32[]{:S(2)}) collective-permute-start(f16[4,8,32,384]{3,2,1,0:T(8,128)(2,1)S(1)} %multiply_convert_fusion.2), channel_id=1, source_target_pairs={{0,4},{1,129},{2,6},{3,131},{4,0},{5,133},{6,2},{7,135},{8,12},{9,... | collective-permute-start | bytes 2359304 | tf_op jit(solution)/shard_map/ppermute | solution.py:44
  42.6 2.3 %hidden_part.2 = (f32[4,8,32,384]{3,2,1,0:T(8,128)S(1)}, f32[4,8,32,384]{3,2,1,0:T(8,128)S(1)}) custom-call(s32[4]{0:T(128)S(1)} %pad_add_fusion.pos_ref, bf16[4,8,4,32,768]{4,3,2,1,0:T(8,128)(2,1)S(1)} %bitcast.28, bf16[400,768]{1,0:T(8,128)(2,1)S(1)} %get-tuple-element.44.g_ref.g_own_ref), custom_call_target="tpu_custom_call" | custom-call | flops 1 | bytes 1 | tf_op jit(solution)/shard_map/hidden_part/pallas_call | solution.py:236
  45.0 0.4 multiply_convert_fusion
  45.4 0.8 collective-permute-start.2
  46.2 2.5 %collective-permute-start.3 = (f16[4,8,32,384]{3,2,1,0:T(8,128)(2,1)S(1)}, f16[4,8,32,384]{3,2,1,0:T(8,128)(2,1)S(1)}, u32[]{:S(2)}, u32[]{:S(2)}) collective-permute-start(f16[4,8,32,384]{3,2,1,0:T(8,128)(2,1)S(1)} %get-tuple-element.42), channel_id=1, source_target_pairs={{0,6},{1,193},{2,0},{3,195},{4,2},{5,197},{6,4},{7,199},{8,14},{9,... | collective-permute-start | bytes 2359304 | tf_op jit(solution)/shard_map/ppermute | solution.py:44
  48.7 0.0 collective-permute-start.5
  48.7 1.5 %hidden_part.3 = f32[4,8,32,384]{3,2,1,0:T(8,128)S(1)} custom-call(s32[4]{0:T(128)S(1)} %pad_add_fusion.pos_ref, bf16[4,8,4,32,768]{4,3,2,1,0:T(8,128)(2,1)S(1)} %bitcast.29, bf16[400,768]{1,0:T(8,128)(2,1)S(1)} %get-tuple-element.44.g_ref.g_own_ref), custom_call_target="tpu_custom_call" | custom-call | flops 1 | bytes 1 | tf_op jit(solution)/shard_map/hidden_part/pallas_call | solution.py:236
  50.2 0.5 collective-permute-done.5.g_oth_ref
  50.7 0.0 collective-permute-done.4.oth_ref
  50.7 4.9 %head_grad.1 = (bf16[2048,768]{1,0:T(8,128)(2,1)}, f32[1,128]{1,0:T(1,128)}) custom-call(s32[4]{0:T(128)S(1)} %pad_add_fusion.pos_ref, bf16[384,4096]{1,0:T(8,128)(2,1)S(1)} %copy-done, bf16[384,4096]{1,0:T(8,128)(2,1)S(1)} %collective-permute-done.4.oth_ref, bf16[400,768]{1,0:T(8,128)(2,1)S(1)} %get-tuple-element.44.g_ref.g_own_ref, ...), custom_call_target="tpu_custom_call" | custom-call | flops 1 | bytes 1 | tf_op jit(solution)/shard_map/head_grad/pallas_call | solution.py:316
  55.7 0.0 collective-permute-done.1
  55.7 7.6 %collective-permute-done.2 = f16[4,8,32,384]{3,2,1,0:T(8,128)(2,1)S(1)} collective-permute-done((f16[4,8,32,384]{3,2,1,0:T(8,128)(2,1)S(1)}, f16[4,8,32,384]{3,2,1,0:T(8,128)(2,1)S(1)}, u32[]{:S(2)}, u32[]{:S(2)}) %collective-permute-start.2) | collective-permute-done | bytes 786464 | tf_op jit(solution)/shard_map/ppermute | solution.py:44
  63.2 0.0 collective-permute-done.3
  63.3 0.1 fusion.6
  63.4 1.2 %collective-permute-start.8 = (f16[8,32,384]{2,1,0:T(8,128)(2,1)S(1)}, f16[8,32,384]{2,1,0:T(8,128)(2,1)S(1)}, u32[]{:S(2)}, u32[]{:S(2)}) collective-permute-start(f16[8,32,384]{2,1,0:T(8,128)(2,1)S(1)} %fusion.6), channel_id=1, source_target_pairs={{0,128},{1,5},{2,130},{3,7},{4,132},{5,1},{6,134},{7,3},{8,136},{9... | collective-permute-start | bytes 589832 | tf_op jit(solution)/shard_map/ppermute | solution.py:44
  64.6 0.3 fusion.4
  64.9 0.9 %collective-permute-start.7 = (f16[8,32,384]{2,1,0:T(8,128)(2,1)S(1)}, f16[8,32,384]{2,1,0:T(8,128)(2,1)S(1)}, u32[]{:S(2)}, u32[]{:S(2)}) collective-permute-start(f16[8,32,384]{2,1,0:T(8,128)(2,1)S(1)} %get-tuple-element.58), channel_id=1, source_target_pairs={{0,64},{1,3},{2,66},{3,5},{4,68},{5,7},{6,70},{7,1},{8,72},{9,11},... | collective-permute-start | bytes 589832 | tf_op jit(solution)/shard_map/ppermute | solution.py:44
  65.8 2.4 %collective-permute-start.6 = (f16[8,32,384]{2,1,0:T(8,128)(2,1)S(1)}, f16[8,32,384]{2,1,0:T(8,128)(2,1)S(1)}, u32[]{:S(2)}, u32[]{:S(2)}) collective-permute-start(f16[8,32,384]{2,1,0:T(8,128)(2,1)S(1)} %get-tuple-element.57), channel_id=1, source_target_pairs={{0,192},{1,7},{2,194},{3,1},{4,196},{5,3},{6,198},{7,5},{8,200},{9... | collective-permute-start | bytes 589832 | tf_op jit(solution)/shard_map/ppermute | solution.py:44
  68.2 2.5 %collective-permute-done.8 = f16[8,32,384]{2,1,0:T(8,128)(2,1)S(1)} collective-permute-done((f16[8,32,384]{2,1,0:T(8,128)(2,1)S(1)}, f16[8,32,384]{2,1,0:T(8,128)(2,1)S(1)}, u32[]{:S(2)}, u32[]{:S(2)}) %collective-permute-start.8) | collective-permute-done | bytes 196640 | tf_op jit(solution)/shard_map/ppermute | solution.py:44
  70.8 2.0 %collective-permute-done.7 = f16[8,32,384]{2,1,0:T(8,128)(2,1)S(1)} collective-permute-done((f16[8,32,384]{2,1,0:T(8,128)(2,1)S(1)}, f16[8,32,384]{2,1,0:T(8,128)(2,1)S(1)}, u32[]{:S(2)}, u32[]{:S(2)}) %collective-permute-start.7) | collective-permute-done | bytes 196640 | tf_op jit(solution)/shard_map/ppermute | solution.py:44
  72.8 0.0 collective-permute-done.6
  72.8 0.2 fusion.3
  73.0 12.0 %all_to_all.17 = f16[8,32,384]{2,1,0:T(8,128)(2,1)S(1)} all-to-all(f16[8,32,384]{2,1,0:T(8,128)(2,1)S(1)} %fusion.3), channel_id=1, replica_groups=mesh['y'=4,'z'=8,'x'=4,'c'=2] {'z'}, dimensions={0} | all-to-all | bytes 393216 | tf_op jit(solution)/shard_map/all_to_all | solution.py:386
  85.0 0.7 multiply_reduce_fusion
  (4 shorter events, 0.0 us)
Async XLA Ops:
  0.6 6.2 %collective-permute-start = (bf16[768,384]{1,0:T(8,128)(2,1)}, bf16[768,384]{1,0:T(8,128)(2,1)S(1)}, u32[]{:S(2)}, u32[]{:S(2)}) collective-permute-start(bf16[768,384]{1,0:T(8,128)(2,1)} %own_ref.2), channel_id=1, source_target_pairs={{0,1},{1,0},{2,3},{3,2},{4,5},{5,4},{6,7},{7,6},{8,9},{9,8},{10,11... | collective-permute-start | bytes 1769480 | tf_op jit(solution)/shard_map/ppermute | solution.py:32
  0.7 38.2 %slice-start = ((s8[6291456]{0:T(1024)(128)(4,1)}), s8[4194304]{0:T(1024)(128)(4,1)S(1)}, s32[]{:S(2)}) async-start(s8[6291456]{0:T(1024)(128)(4,1)} %bitcast.25), calls=%async_computation.3 | async-start | bytes 8388608
  0.8 6.0 %copy-start.1 = (bf16[768,384]{1,0:T(8,128)(2,1)S(1)}, bf16[768,384]{1,0:T(8,128)(2,1)}, u32[]{:S(2)}) copy-start(bf16[768,384]{1,0:T(8,128)(2,1)} %own_ref.2) | copy-start | bytes 1769476
  0.8 6.0 %copy-start.2 = (s32[384]{0:T(512)S(1)}, s32[384]{0:T(512)}, u32[]{:S(2)}) copy-start(s32[384]{0:T(512)} %param.9) | copy-start | bytes 4612
  0.8 6.0 %copy-start.3 = (s32[768]{0:T(1024)S(1)}, s32[768]{0:T(1024)}, u32[]{:S(2)}) copy-start(s32[768]{0:T(1024)} %param.10) | copy-start | bytes 9220
  0.8 23.0 %copy-start = (bf16[384,4096]{1,0:T(8,128)(2,1)S(1)}, bf16[384,4096]{1,0:T(8,128)(2,1)}, u32[]{:S(2)}) copy-start(bf16[384,4096]{1,0:T(8,128)(2,1)} %own_ref.3) | copy-start | bytes 9437188
  0.8 38.1 %slice-start.1 = ((s8[6291456]{0:T(1024)(128)(4,1)}), s8[2097152]{0:T(1024)(128)(4,1)S(1)}, s32[]{:S(2)}) async-start(s8[6291456]{0:T(1024)(128)(4,1)} %bitcast.25), calls=%async_computation.4 | async-start | bytes 4194304
  6.8 32.2 %copy-start.4 = (f32[384]{0:T(512)S(1)}, f32[384]{0:T(512)}, u32[]{:S(2)}) copy-start(f32[384]{0:T(512)} %param.11) | copy-start | bytes 4612
  23.8 26.9 %collective-permute-start.4 = (bf16[384,4096]{1,0:T(8,128)(2,1)S(1)}, bf16[384,4096]{1,0:T(8,128)(2,1)S(1)}, u32[]{:S(2)}, u32[]{:S(2)}) collective-permute-start(bf16[384,4096]{1,0:T(8,128)(2,1)S(1)} %copy-done), channel_id=1, source_target_pairs={{0,1},{1,0},{2,3},{3,2},{4,5},{5,4},{6,7},{7,6},{8,9},{9,8},{10,11... | collective-permute-start | bytes 9437192 | tf_op jit(solution)/shard_map/ppermute | solution.py:32
  41.2 14.4 %collective-permute-start.1 = (f16[4,8,32,384]{3,2,1,0:T(8,128)(2,1)S(1)}, f16[4,8,32,384]{3,2,1,0:T(8,128)(2,1)S(1)}, u32[]{:S(2)}, u32[]{:S(2)}) collective-permute-start(f16[4,8,32,384]{3,2,1,0:T(8,128)(2,1)S(1)} %multiply_convert_fusion.2), channel_id=1, source_target_pairs={{0,4},{1,129},{2,6},{3,131},{4,0},{5,133},{6,2},{7,135},{8,12},{9,... | collective-permute-start | bytes 2359304 | tf_op jit(solution)/shard_map/ppermute | solution.py:44
  45.4 17.9 %collective-permute-start.2 = (f16[4,8,32,384]{3,2,1,0:T(8,128)(2,1)S(1)}, f16[4,8,32,384]{3,2,1,0:T(8,128)(2,1)S(1)}, u32[]{:S(2)}, u32[]{:S(2)}) collective-permute-start(f16[4,8,32,384]{3,2,1,0:T(8,128)(2,1)S(1)} %get-tuple-element.41), channel_id=1, source_target_pairs={{0,2},{1,65},{2,4},{3,67},{4,6},{5,69},{6,0},{7,71},{8,10},{9,73},... | collective-permute-start | bytes 2359304 | tf_op jit(solution)/shard_map/ppermute | solution.py:44
  46.2 17.1 %collective-permute-start.3 = (f16[4,8,32,384]{3,2,1,0:T(8,128)(2,1)S(1)}, f16[4,8,32,384]{3,2,1,0:T(8,128)(2,1)S(1)}, u32[]{:S(2)}, u32[]{:S(2)}) collective-permute-start(f16[4,8,32,384]{3,2,1,0:T(8,128)(2,1)S(1)} %get-tuple-element.42), channel_id=1, source_target_pairs={{0,6},{1,193},{2,0},{3,195},{4,2},{5,197},{6,4},{7,199},{8,14},{9,... | collective-permute-start | bytes 2359304 | tf_op jit(solution)/shard_map/ppermute | solution.py:44
  48.7 2.0 %collective-permute-start.5 = (bf16[400,768]{1,0:T(8,128)(2,1)S(1)}, bf16[400,768]{1,0:T(8,128)(2,1)S(1)}, u32[]{:S(2)}, u32[]{:S(2)}) collective-permute-start(bf16[400,768]{1,0:T(8,128)(2,1)S(1)} %get-tuple-element.44.g_ref.g_own_ref), channel_id=1, source_target_pairs={{0,1},{1,0},{2,3},{3,2},{4,5},{5,4},{6,7},{7,6},{8,9},{9,8},{10,11... | collective-permute-start | bytes 1843208 | tf_op jit(solution)/shard_map/ppermute | solution.py:32
  63.4 7.4 %collective-permute-start.8 = (f16[8,32,384]{2,1,0:T(8,128)(2,1)S(1)}, f16[8,32,384]{2,1,0:T(8,128)(2,1)S(1)}, u32[]{:S(2)}, u32[]{:S(2)}) collective-permute-start(f16[8,32,384]{2,1,0:T(8,128)(2,1)S(1)} %fusion.6), channel_id=1, source_target_pairs={{0,128},{1,5},{2,130},{3,7},{4,132},{5,1},{6,134},{7,3},{8,136},{9... | collective-permute-start | bytes 589832 | tf_op jit(solution)/shard_map/ppermute | solution.py:44
  64.9 7.9 %collective-permute-start.7 = (f16[8,32,384]{2,1,0:T(8,128)(2,1)S(1)}, f16[8,32,384]{2,1,0:T(8,128)(2,1)S(1)}, u32[]{:S(2)}, u32[]{:S(2)}) collective-permute-start(f16[8,32,384]{2,1,0:T(8,128)(2,1)S(1)} %get-tuple-element.58), channel_id=1, source_target_pairs={{0,64},{1,3},{2,66},{3,5},{4,68},{5,7},{6,70},{7,1},{8,72},{9,11},... | collective-permute-start | bytes 589832 | tf_op jit(solution)/shard_map/ppermute | solution.py:44
  65.8 7.0 %collective-permute-start.6 = (f16[8,32,384]{2,1,0:T(8,128)(2,1)S(1)}, f16[8,32,384]{2,1,0:T(8,128)(2,1)S(1)}, u32[]{:S(2)}, u32[]{:S(2)}) collective-permute-start(f16[8,32,384]{2,1,0:T(8,128)(2,1)S(1)} %get-tuple-element.57), channel_id=1, source_target_pairs={{0,192},{1,7},{2,194},{3,1},{4,196},{5,3},{6,198},{7,5},{8,200},{9... | collective-permute-start | bytes 589832 | tf_op jit(solution)/shard_map/ppermute | solution.py:44

commit v13 on v12

--- a/solution.py
+++ b/solution.py
@@ -366,23 +366,26 @@
 
     far2, g = lax.optimization_barrier((coded(far2), g))
     got2 = shift_by_core(far2, 2, True)
-    far1, far3 = hidden_part(pos, head5, g, (chunk(1), chunk(3)))
-    far1, far3, g = lax.optimization_barrier((coded(far1), coded(far3), g))
-    got = [got2, shift_by_core(far1, 1, True), shift_by_core(far3, 3, True)]
+    groups = (chunk(1)[1:], chunk(3)[1:], chunk(1)[:1], chunk(3)[:1])
+    far1, far3, late1, late3 = (coded(v) for v in hidden_part(pos, head5, g, groups))
+    far1, far3, g = lax.optimization_barrier((far1, far3, g))
+    got = [shift_by_core(far1, 1, True), shift_by_core(far3, 3, True)]
     g_oth = shift(g, "c", 1)
     (own,) = hidden_part(pos, head5, g, (chunk(0),))
     head_out, loss = head_grad(pos, hidden, hidden_oth, g, g_oth)
     loss = loss[0, :1]
-    *got, loss, head_out = lax.optimization_barrier((*got, loss, head_out))
+    got2, *got, loss, head_out = lax.optimization_barrier((got2, *got, loss, head_out))
 
     def summed(near):
-        return own[near] + sum(taken(v[near]) for v in got)
+        return own[near] + taken(got2[near]) + sum(taken(v[near - 1]) for v in got)
 
     far2 = coded(summed(2))
-    far2, own, *got = lax.optimization_barrier((far2, own, *got))
-    far = [shift_by_core(coded(summed(d)), d, False) for d in (3, 1)]
-    far += [shift_by_core(far2, 2, False)]
-    both = coded(summed(0) + sum(taken(v) for v in far))
+    far2, own, got2, *got = lax.optimization_barrier((far2, own, got2, *got))
+    far1, far3 = coded(summed(1)), coded(summed(3))
+    far1, far3, late1, late3 = lax.optimization_barrier((far1, far3, late1, late3))
+    last = [shift_by_core(late1, 1, True)[0], shift_by_core(late3, 3, True)[0]]
+    last += [shift_by_core(v, d, False) for v, d in ((far3, 3), (far1, 1), (far2, 2))]
+    both = coded(own[0] + taken(got2[0]) + sum(taken(v) for v in last))
     both = lax.all_to_all(both, "z", 0, 0, tiled=True)
     hidden_grad = jnp.sum(taken(both), axis=0).T.astype(BF16)
     return loss, hidden_grad, head_out

time: 86.7 us -> 87.9 us (1.014)
  starting transfers between devices: 9.38 us -> 11.5 us
    ppermute x6 -> x8, starting transfers between devices: 9.23 us -> 11.3 us  [shift_by_core(): return lax.ppermute(a, axes, pairs)]
    ppermute x6 -> x8, waiting for transfers between devices: 12.1 us -> 11.9 us  [shift_by_core(): return lax.ppermute(a, axes, pairs)]
  transfers between devices with their start and end apart: 9 -> 11, of which waited for: 4 -> 4; matrix products, arithmetic and copies ran while one was open for 1% -> 1% of each run, Pallas kernels for 20% -> 19%
where the time goes in v13:
time: 87.9 us; the launch traced here: 87.3 us
  blocking collectives  41.8 us (48%)
  Pallas kernels  19.2 us (22%)
  waiting for transfers between devices  11.9 us (14%)
  starting transfers between devices  11.5 us (13%)
  other arithmetic  1.97 us (2%)
    all_to_all x2, blocking collectives, gathered(): return lax.all_to_all(value, axes, 0, 0, tiled=True)  29.6 us
    all_to_all x1, blocking collectives, body(): both = lax.all_to_all(both, 'z', 0, 0, tiled=True)  12.2 us
    ppermute x8, waiting for transfers between devices, shift_by_core(): return lax.ppermute(a, axes, pairs)  11.9 us
    ppermute x8, starting transfers between devices, shift_by_core(): return lax.ppermute(a, axes, pairs)  11.3 us
    pallas_call x1, Pallas kernels, student_logits(): pl.pallas_call(functools.partial(logits_kernel, steps), out_shape=jax.Sha...  5.91 us
    pallas_call x1, Pallas kernels, head_grad(): pl.pallas_call(head_kernel, out_shape=(jax.ShapeDtypeStruct((width, cols)...  4.94 us
    pallas_call x2, Pallas kernels, hidden_part(): pl.pallas_call(functools.partial(hidden_kernel, groups), out_shape=out_sh...  3.86 us
    pallas_call x1, Pallas kernels, local_stats(): pl.pallas_call(stats_kernel, out_shape=(jax.ShapeDtypeStruct((2, rows + S...  2.26 us
  transfers between devices with their start and end apart: 11, of which 4 were waited for; matrix products, arithmetic and copies ran while one was open for 1% of the time, Pallas kernels for 19%

profile of v13, /device:TPU:32, one launch (start us, length us, event | category | flops | bytes accessed | tf_op | source)
XLA Modules:
  0.0 87.3 jit_solution(4645896293114235311)
XLA Ops:
  0.6 0.1 collective-permute-start
  0.7 0.0 slice-start
  0.8 0.1 pad_add_fusion.pos_ref
  0.8 0.0 slice-start.1
  0.9 5.9 %student_logits.1.l_ref = f32[384,768]{1,0:T(8,128)S(1)} custom-call(bf16[384,4096]{1,0:T(8,128)(2,1)} %own_ref.3, bf16[4096,768]{1,0:T(8,128)(2,1)} %w_ref.1), custom_call_target="tpu_custom_call" | custom-call | flops 2415919104 | bytes 10616832 | tf_op jit(solution)/shard_map/student_logits/pallas_call | solution.py:75
  6.8 0.0 copy-start.4
  6.8 0.0 collective-permute-done.oth_ref
  6.8 0.0 copy-done.1
  6.8 0.0 copy-done.2
  6.8 0.0 copy-done.3
  6.8 2.3 %local_stats.1 = (f32[2,640]{1,0:T(2,128)S(1)}, bf16[384,768]{1,0:T(8,128)(2,1)S(1)}) custom-call(s32[4]{0:T(128)S(1)} %pad_add_fusion.pos_ref, f32[384,768]{1,0:T(8,128)S(1)} %student_logits.1.l_ref, bf16[768,384]{1,0:T(8,128)(2,1)S(1)} %copy-done.1, bf16[768,384]{1,0:T(8,128)(2,1)S(1)} %collective-permute-done.oth_ref, s32[6,128]{1,0:T(8,128)S(1)} %bitcast.42, ...), custom_call_target="tpu_custom_call" | custom-call | flops 452984832 | bytes 2949120 | tf_op jit(solution)/shard_map/local_stats/pallas_call | solution.py:190
  9.1 14.6 %all_to_all.15.in_ref = f32[16,2,640]{2,1,0:T(2,128)S(1)} all-to-all(f32[16,2,640]{2,1,0:T(2,128)S(1)} %broadcast_in_dim.4), channel_id=1, replica_groups=mesh['y'=4,'z'=8,'x'=4,'c'=2] {'y','x'}, dimensions={0} | all-to-all | bytes 163840 | tf_op jit(solution)/shard_map/all_to_all | solution.py:352
  23.7 0.1 merge_stats.1
  23.8 0.0 copy-done
  23.8 0.1 collective-permute-start.4
  23.9 15.0 %all_to_all.16.stats_ref = f32[8,2,640]{2,1,0:T(2,128)S(1)} all-to-all(f32[8,2,640]{2,1,0:T(2,128)S(1)} %broadcast_in_dim.5), channel_id=1, replica_groups=mesh['y'=4,'z'=8,'x'=4,'c'=2] {'z'}, dimensions={0} | all-to-all | bytes 81920 | tf_op jit(solution)/shard_map/all_to_all | solution.py:352
  38.9 0.0 slice-done
  39.0 2.1 %grad_logits.1 = (bf16[400,768]{1,0:T(8,128)(2,1)S(1)}, f32[4,8,32,384]{3,2,1,0:T(8,128)S(1)}) custom-call(s32[4]{0:T(128)S(1)} %pad_add_fusion.pos_ref, f32[384,768]{1,0:T(8,128)S(1)} %student_logits.1.l_ref, bf16[384,768]{1,0:T(8,128)(2,1)S(1)} %get-tuple-element.36.t_ref, s32[3,128]{1,0:T(4,128)S(1)} %bitcast.41, f32[3,128]{1,0:T(4,128)S(1)} %bitcast.43, ...), custom_call_target="tpu_custom_call" | custom-call | flops 2359296 | bytes 2359296 | tf_op jit(solution)/shard_map/grad_logits/pallas_call | solution.py:271
  41.1 0.2 multiply_convert_fusion
  41.2 1.4 %collective-permute-start.1 = (f16[4,8,32,384]{3,2,1,0:T(8,128)(2,1)S(1)}, f16[4,8,32,384]{3,2,1,0:T(8,128)(2,1)S(1)}, u32[]{:S(2)}, u32[]{:S(2)}) collective-permute-start(f16[4,8,32,384]{3,2,1,0:T(8,128)(2,1)S(1)} %multiply_convert_fusion), channel_id=1, source_target_pairs={{0,4},{1,129},{2,6},{3,131},{4,0},{5,133},{6,2},{7,135},{8,12},{9,... | collective-permute-start | bytes 2359304 | tf_op jit(solution)/shard_map/ppermute | solution.py:44
  42.6 2.3 %hidden_part.2 = (f32[3,8,32,384]{3,2,1,0:T(8,128)S(1)}, f32[3,8,32,384]{3,2,1,0:T(8,128)S(1)}, f32[1,8,32,384]{3,2,1,0:T(8,128)S(1)}, f32[1,8,32,384]{3,2,1,0:T(8,128)S(1)}) custom-call(s32[4]{0:T(128)S(1)} %pad_add_fusion.pos_ref, bf16[4,8,4,32,768]{4,3,2,1,0:T(8,128)(2,1)S(1)} %bitcast.38, bf16[400,768]{1,0:T(8,128)(2,1)S(1)} %get-tuple-element.50.g_ref.g_own_ref), custom_call_target="tpu_custom_call" | custom-call | flops 1 | bytes 1 | tf_op jit(solution)/shard_map/hidden_part/pallas_call | solution.py:236
  45.0 0.3 multiply_convert_fusion.1
  45.3 0.1 collective-permute-start.5
  45.4 0.8 collective-permute-start.2
  46.1 2.5 %collective-permute-start.3 = (f16[3,8,32,384]{3,2,1,0:T(8,128)(2,1)S(1)}, f16[3,8,32,384]{3,2,1,0:T(8,128)(2,1)S(1)}, u32[]{:S(2)}, u32[]{:S(2)}) collective-permute-start(f16[3,8,32,384]{3,2,1,0:T(8,128)(2,1)S(1)} %get-tuple-element.48), channel_id=1, source_target_pairs={{0,6},{1,193},{2,0},{3,195},{4,2},{5,197},{6,4},{7,199},{8,14},{9,... | collective-permute-start | bytes 1769480 | tf_op jit(solution)/shard_map/ppermute | solution.py:44
  48.7 1.5 %hidden_part.3 = f32[4,8,32,384]{3,2,1,0:T(8,128)S(1)} custom-call(s32[4]{0:T(128)S(1)} %pad_add_fusion.pos_ref, bf16[4,8,4,32,768]{4,3,2,1,0:T(8,128)(2,1)S(1)} %bitcast.39, bf16[400,768]{1,0:T(8,128)(2,1)S(1)} %get-tuple-element.50.g_ref.g_own_ref), custom_call_target="tpu_custom_call" | custom-call | flops 1 | bytes 1 | tf_op jit(solution)/shard_map/hidden_part/pallas_call | solution.py:236
  50.2 0.1 multiply_convert_fusion.5
  50.3 0.0 collective-permute-done.5.g_oth_ref
  50.3 0.0 collective-permute-done.4.oth_ref
  50.3 4.9 %head_grad.1 = (bf16[2048,768]{1,0:T(8,128)(2,1)}, f32[1,128]{1,0:T(1,128)}) custom-call(s32[4]{0:T(128)S(1)} %pad_add_fusion.pos_ref, bf16[384,4096]{1,0:T(8,128)(2,1)S(1)} %copy-done, bf16[384,4096]{1,0:T(8,128)(2,1)S(1)} %collective-permute-done.4.oth_ref, bf16[400,768]{1,0:T(8,128)(2,1)S(1)} %get-tuple-element.50.g_ref.g_own_ref, ...), custom_call_target="tpu_custom_call" | custom-call | flops 1 | bytes 1 | tf_op jit(solution)/shard_map/head_grad/pallas_call | solution.py:316
  55.3 5.9 %collective-permute-done.2 = f16[3,8,32,384]{3,2,1,0:T(8,128)(2,1)S(1)} collective-permute-done((f16[3,8,32,384]{3,2,1,0:T(8,128)(2,1)S(1)}, f16[3,8,32,384]{3,2,1,0:T(8,128)(2,1)S(1)}, u32[]{:S(2)}, u32[]{:S(2)}) %collective-permute-start.2) | collective-permute-done | bytes 589856 | tf_op jit(solution)/shard_map/ppermute | solution.py:44
  61.1 0.0 collective-permute-done.3
  61.1 0.0 collective-permute-done.1
  61.1 0.2 fusion.11
  61.3 1.2 %collective-permute-start.10 = (f16[8,32,384]{2,1,0:T(8,128)(2,1)S(1)}, f16[8,32,384]{2,1,0:T(8,128)(2,1)S(1)}, u32[]{:S(2)}, u32[]{:S(2)}) collective-permute-start(f16[8,32,384]{2,1,0:T(8,128)(2,1)S(1)} %fusion.11), channel_id=1, source_target_pairs={{0,128},{1,5},{2,130},{3,7},{4,132},{5,1},{6,134},{7,3},{8,136},{9... | collective-permute-start | bytes 589832 | tf_op jit(solution)/shard_map/ppermute | solution.py:44
  62.5 0.3 fusion.10
  62.8 0.9 collective-permute-start.9
  63.7 2.4 %collective-permute-start.8 = (f16[8,32,384]{2,1,0:T(8,128)(2,1)S(1)}, f16[8,32,384]{2,1,0:T(8,128)(2,1)S(1)}, u32[]{:S(2)}, u32[]{:S(2)}) collective-permute-start(f16[8,32,384]{2,1,0:T(8,128)(2,1)S(1)} %get-tuple-element.65), channel_id=1, source_target_pairs={{0,192},{1,7},{2,194},{3,1},{4,196},{5,3},{6,198},{7,5},{8,200},{9... | collective-permute-start | bytes 589832 | tf_op jit(solution)/shard_map/ppermute | solution.py:44
  66.1 1.2 %collective-permute-start.7 = (f16[1,8,32,384]{3,2,1,0:T(8,128)(2,1)S(1)}, f16[1,8,32,384]{3,2,1,0:T(8,128)(2,1)S(1)}, u32[]{:S(2)}, u32[]{:S(2)}) collective-permute-start(f16[1,8,32,384]{3,2,1,0:T(8,128)(2,1)S(1)} %get-tuple-element.64), channel_id=1, source_target_pairs={{0,6},{1,193},{2,0},{3,195},{4,2},{5,197},{6,4},{7,199},{8,14},{9,... | collective-permute-start | bytes 589832 | tf_op jit(solution)/shard_map/ppermute | solution.py:44
  67.4 0.8 collective-permute-start.6
  68.2 1.8 %collective-permute-done.10 = f16[8,32,384]{2,1,0:T(8,128)(2,1)S(1)} collective-permute-done((f16[8,32,384]{2,1,0:T(8,128)(2,1)S(1)}, f16[8,32,384]{2,1,0:T(8,128)(2,1)S(1)}, u32[]{:S(2)}, u32[]{:S(2)}) %collective-permute-start.10) | collective-permute-done | bytes 196640 | tf_op jit(solution)/shard_map/ppermute | solution.py:44
  70.0 2.9 %collective-permute-done.9 = f16[8,32,384]{2,1,0:T(8,128)(2,1)S(1)} collective-permute-done((f16[8,32,384]{2,1,0:T(8,128)(2,1)S(1)}, f16[8,32,384]{2,1,0:T(8,128)(2,1)S(1)}, u32[]{:S(2)}, u32[]{:S(2)}) %collective-permute-start.9) | collective-permute-done | bytes 196640 | tf_op jit(solution)/shard_map/ppermute | solution.py:44
  72.8 0.0 collective-permute-done.8
  72.8 0.0 collective-permute-done.7
  72.9 1.4 %collective-permute-done.6 = f16[1,8,32,384]{3,2,1,0:T(8,128)(2,1)S(1)} collective-permute-done((f16[1,8,32,384]{3,2,1,0:T(8,128)(2,1)S(1)}, f16[1,8,32,384]{3,2,1,0:T(8,128)(2,1)S(1)}, u32[]{:S(2)}, u32[]{:S(2)}) %collective-permute-start.6) | collective-permute-done | bytes 196640 | tf_op jit(solution)/shard_map/ppermute | solution.py:44
  74.2 0.2 fusion.8
  74.5 12.2 %all_to_all.17 = f16[8,32,384]{2,1,0:T(8,128)(2,1)S(1)} all-to-all(f16[8,32,384]{2,1,0:T(8,128)(2,1)S(1)} %fusion.8), channel_id=1, replica_groups=mesh['y'=4,'z'=8,'x'=4,'c'=2] {'z'}, dimensions={0} | all-to-all | bytes 393216 | tf_op jit(solution)/shard_map/all_to_all | solution.py:389
  86.7 0.7 multiply_reduce_fusion
  (9 shorter events, 0.1 us)
Async XLA Ops:
  0.6 6.2 %collective-permute-start = (bf16[768,384]{1,0:T(8,128)(2,1)}, bf16[768,384]{1,0:T(8,128)(2,1)S(1)}, u32[]{:S(2)}, u32[]{:S(2)}) collective-permute-start(bf16[768,384]{1,0:T(8,128)(2,1)} %own_ref.2), channel_id=1, source_target_pairs={{0,1},{1,0},{2,3},{3,2},{4,5},{5,4},{6,7},{7,6},{8,9},{9,8},{10,11... | collective-permute-start | bytes 1769480 | tf_op jit(solution)/shard_map/ppermute | solution.py:32
  0.7 38.2 %slice-start = ((s8[6291456]{0:T(1024)(128)(4,1)}), s8[4194304]{0:T(1024)(128)(4,1)S(1)}, s32[]{:S(2)}) async-start(s8[6291456]{0:T(1024)(128)(4,1)} %bitcast.35), calls=%async_computation.3 | async-start | bytes 8388608
  0.8 6.0 %copy-start.1 = (bf16[768,384]{1,0:T(8,128)(2,1)S(1)}, bf16[768,384]{1,0:T(8,128)(2,1)}, u32[]{:S(2)}) copy-start(bf16[768,384]{1,0:T(8,128)(2,1)} %own_ref.2) | copy-start | bytes 1769476
  0.8 6.0 %copy-start.2 = (s32[384]{0:T(512)S(1)}, s32[384]{0:T(512)}, u32[]{:S(2)}) copy-start(s32[384]{0:T(512)} %param.9) | copy-start | bytes 4612
  0.8 6.0 %copy-start.3 = (s32[768]{0:T(1024)S(1)}, s32[768]{0:T(1024)}, u32[]{:S(2)}) copy-start(s32[768]{0:T(1024)} %param.10) | copy-start | bytes 9220
  0.8 23.0 %copy-start = (bf16[384,4096]{1,0:T(8,128)(2,1)S(1)}, bf16[384,4096]{1,0:T(8,128)(2,1)}, u32[]{:S(2)}) copy-start(bf16[384,4096]{1,0:T(8,128)(2,1)} %own_ref.3) | copy-start | bytes 9437188
  0.8 38.1 %slice-start.1 = ((s8[6291456]{0:T(1024)(128)(4,1)}), s8[2097152]{0:T(1024)(128)(4,1)S(1)}, s32[]{:S(2)}) async-start(s8[6291456]{0:T(1024)(128)(4,1)} %bitcast.35), calls=%async_computation.4 | async-start | bytes 4194304
  6.8 32.2 %copy-start.4 = (f32[384]{0:T(512)S(1)}, f32[384]{0:T(512)}, u32[]{:S(2)}) copy-start(f32[384]{0:T(512)} %param.11) | copy-start | bytes 4612
  23.8 26.5 %collective-permute-start.4 = (bf16[384,4096]{1,0:T(8,128)(2,1)S(1)}, bf16[384,4096]{1,0:T(8,128)(2,1)S(1)}, u32[]{:S(2)}, u32[]{:S(2)}) collective-permute-start(bf16[384,4096]{1,0:T(8,128)(2,1)S(1)} %copy-done), channel_id=1, source_target_pairs={{0,1},{1,0},{2,3},{3,2},{4,5},{5,4},{6,7},{7,6},{8,9},{9,8},{10,11... | collective-permute-start | bytes 9437192 | tf_op jit(solution)/shard_map/ppermute | solution.py:32
  41.2 19.9 %collective-permute-start.1 = (f16[4,8,32,384]{3,2,1,0:T(8,128)(2,1)S(1)}, f16[4,8,32,384]{3,2,1,0:T(8,128)(2,1)S(1)}, u32[]{:S(2)}, u32[]{:S(2)}) collective-permute-start(f16[4,8,32,384]{3,2,1,0:T(8,128)(2,1)S(1)} %multiply_convert_fusion), channel_id=1, source_target_pairs={{0,4},{1,129},{2,6},{3,131},{4,0},{5,133},{6,2},{7,135},{8,12},{9,... | collective-permute-start | bytes 2359304 | tf_op jit(solution)/shard_map/ppermute | solution.py:44
  45.3 5.0 %collective-permute-start.5 = (bf16[400,768]{1,0:T(8,128)(2,1)S(1)}, bf16[400,768]{1,0:T(8,128)(2,1)S(1)}, u32[]{:S(2)}, u32[]{:S(2)}) collective-permute-start(bf16[400,768]{1,0:T(8,128)(2,1)S(1)} %get-tuple-element.50.g_ref.g_own_ref), channel_id=1, source_target_pairs={{0,1},{1,0},{2,3},{3,2},{4,5},{5,4},{6,7},{7,6},{8,9},{9,8},{10,11... | collective-permute-start | bytes 1843208 | tf_op jit(solution)/shard_map/ppermute | solution.py:32
  45.4 15.8 %collective-permute-start.2 = (f16[3,8,32,384]{3,2,1,0:T(8,128)(2,1)S(1)}, f16[3,8,32,384]{3,2,1,0:T(8,128)(2,1)S(1)}, u32[]{:S(2)}, u32[]{:S(2)}) collective-permute-start(f16[3,8,32,384]{3,2,1,0:T(8,128)(2,1)S(1)} %get-tuple-element.47), channel_id=1, source_target_pairs={{0,2},{1,65},{2,4},{3,67},{4,6},{5,69},{6,0},{7,71},{8,10},{9,73},... | collective-permute-start | bytes 1769480 | tf_op jit(solution)/shard_map/ppermute | solution.py:44
  46.1 15.0 %collective-permute-start.3 = (f16[3,8,32,384]{3,2,1,0:T(8,128)(2,1)S(1)}, f16[3,8,32,384]{3,2,1,0:T(8,128)(2,1)S(1)}, u32[]{:S(2)}, u32[]{:S(2)}) collective-permute-start(f16[3,8,32,384]{3,2,1,0:T(8,128)(2,1)S(1)} %get-tuple-element.48), channel_id=1, source_target_pairs={{0,6},{1,193},{2,0},{3,195},{4,2},{5,197},{6,4},{7,199},{8,14},{9,... | collective-permute-start | bytes 1769480 | tf_op jit(solution)/shard_map/ppermute | solution.py:44
  61.3 8.7 %collective-permute-start.10 = (f16[8,32,384]{2,1,0:T(8,128)(2,1)S(1)}, f16[8,32,384]{2,1,0:T(8,128)(2,1)S(1)}, u32[]{:S(2)}, u32[]{:S(2)}) collective-permute-start(f16[8,32,384]{2,1,0:T(8,128)(2,1)S(1)} %fusion.11), channel_id=1, source_target_pairs={{0,128},{1,5},{2,130},{3,7},{4,132},{5,1},{6,134},{7,3},{8,136},{9... | collective-permute-start | bytes 589832 | tf_op jit(solution)/shard_map/ppermute | solution.py:44
  62.8 10.0 %collective-permute-start.9 = (f16[8,32,384]{2,1,0:T(8,128)(2,1)S(1)}, f16[8,32,384]{2,1,0:T(8,128)(2,1)S(1)}, u32[]{:S(2)}, u32[]{:S(2)}) collective-permute-start(f16[8,32,384]{2,1,0:T(8,128)(2,1)S(1)} %get-tuple-element.66), channel_id=1, source_target_pairs={{0,64},{1,3},{2,66},{3,5},{4,68},{5,7},{6,70},{7,1},{8,72},{9,11},... | collective-permute-start | bytes 589832 | tf_op jit(solution)/shard_map/ppermute | solution.py:44
  63.7 9.2 %collective-permute-start.8 = (f16[8,32,384]{2,1,0:T(8,128)(2,1)S(1)}, f16[8,32,384]{2,1,0:T(8,128)(2,1)S(1)}, u32[]{:S(2)}, u32[]{:S(2)}) collective-permute-start(f16[8,32,384]{2,1,0:T(8,128)(2,1)S(1)} %get-tuple-element.65), channel_id=1, source_target_pairs={{0,192},{1,7},{2,194},{3,1},{4,196},{5,3},{6,198},{7,5},{8,200},{9... | collective-permute-start | bytes 589832 | tf_op jit(solution)/shard_map/ppermute | solution.py:44
  66.1 6.7 %collective-permute-start.7 = (f16[1,8,32,384]{3,2,1,0:T(8,128)(2,1)S(1)}, f16[1,8,32,384]{3,2,1,0:T(8,128)(2,1)S(1)}, u32[]{:S(2)}, u32[]{:S(2)}) collective-permute-start(f16[1,8,32,384]{3,2,1,0:T(8,128)(2,1)S(1)} %get-tuple-element.64), channel_id=1, source_target_pairs={{0,6},{1,193},{2,0},{3,195},{4,2},{5,197},{6,4},{7,199},{8,14},{9,... | collective-permute-start | bytes 589832 | tf_op jit(solution)/shard_map/ppermute | solution.py:44
  67.4 6.9 %collective-permute-start.6 = (f16[1,8,32,384]{3,2,1,0:T(8,128)(2,1)S(1)}, f16[1,8,32,384]{3,2,1,0:T(8,128)(2,1)S(1)}, u32[]{:S(2)}, u32[]{:S(2)}) collective-permute-start(f16[1,8,32,384]{3,2,1,0:T(8,128)(2,1)S(1)} %get-tuple-element.63), channel_id=1, source_target_pairs={{0,2},{1,65},{2,4},{3,67},{4,6},{5,69},{6,0},{7,71},{8,10},{9,73},... | collective-permute-start | bytes 589832 | tf_op jit(solution)/shard_map/ppermute | solution.py:44

commit v14 on v12

--- a/solution.py
+++ b/solution.py
@@ -351,10 +351,10 @@
         value = jnp.broadcast_to(value[None], (n,) + value.shape)
         return lax.all_to_all(value, axes, 0, 0, tiled=True)
 
-    stats = merge_stats(gathered(stats, ("y", "x"), ny * nx))
+    stats = merge_stats(gathered(stats, "z", nz))
     stats, hidden_far = lax.optimization_barrier((stats, hidden))
     hidden_oth = shift(hidden_far, "c", 1)
-    stats = gathered(stats, "z", nz)
+    stats = gathered(stats, ("y", "x"), ny * nx)
     head5 = head.reshape(ny, nz, nx, depth // (ny * nz * nx), cols)
     g, far2 = grad_logits(pos, logits, teacher_rows, ids, scale, stats, head5)
 

time: 86.7 us -> 86.7 us (level)
  no operation moved by 1% of the time
where the time goes in v14:
time: 86.7 us; the launch traced here: 85.7 us
  blocking collectives  41.6 us (48%)
  Pallas kernels  19.2 us (22%)
  waiting for transfers between devices  12.6 us (15%)
  starting transfers between devices  9.38 us (11%)
  other arithmetic  1.97 us (2%)
    all_to_all x2, blocking collectives, gathered(): return lax.all_to_all(value, axes, 0, 0, tiled=True)  29.6 us
    ppermute x6, waiting for transfers between devices, shift_by_core(): return lax.ppermute(a, axes, pairs)  12.1 us
    all_to_all x1, blocking collectives, body(): both = lax.all_to_all(both, 'z', 0, 0, tiled=True)  12 us
    ppermute x6, starting transfers between devices, shift_by_core(): return lax.ppermute(a, axes, pairs)  9.22 us
    pallas_call x1, Pallas kernels, student_logits(): pl.pallas_call(functools.partial(logits_kernel, steps), out_shape=jax.Sha...  5.91 us
    pallas_call x1, Pallas kernels, head_grad(): pl.pallas_call(head_kernel, out_shape=(jax.ShapeDtypeStruct((width, cols)...  4.93 us
    pallas_call x2, Pallas kernels, hidden_part(): pl.pallas_call(functools.partial(hidden_kernel, groups), out_shape=out_sh...  3.87 us
    pallas_call x1, Pallas kernels, local_stats(): pl.pallas_call(stats_kernel, out_shape=(jax.ShapeDtypeStruct((2, rows + S...  2.26 us
  transfers between devices with their start and end apart: 9, of which 4 were waited for; matrix products, arithmetic and copies ran while one was open for 1% of the time, Pallas kernels for 20%

profile of v14, /device:TPU:32, one launch (start us, length us, event | category | flops | bytes accessed | tf_op | source)
XLA Modules:
  0.0 85.7 jit_solution(13818489222549529532)
XLA Ops:
  0.6 0.1 collective-permute-start
  0.7 0.0 slice-start
  0.8 0.1 pad_add_fusion.pos_ref
  0.8 0.0 copy-start.1
  0.8 0.0 copy-start.2
  0.8 0.0 copy-start.3
  0.8 0.0 slice-start.1
  0.9 5.9 %student_logits.1.l_ref = f32[384,768]{1,0:T(8,128)S(1)} custom-call(bf16[384,4096]{1,0:T(8,128)(2,1)} %own_ref.3, bf16[4096,768]{1,0:T(8,128)(2,1)} %w_ref.1), custom_call_target="tpu_custom_call" | custom-call | flops 2415919104 | bytes 10616832 | tf_op jit(solution)/shard_map/student_logits/pallas_call | solution.py:75
  6.8 0.0 copy-start.4
  6.8 0.0 collective-permute-done.oth_ref
  6.8 0.0 copy-done.1
  6.8 0.0 copy-done.2
  6.8 0.0 copy-done.3
  6.8 2.3 %local_stats.1 = (f32[2,640]{1,0:T(2,128)S(1)}, bf16[384,768]{1,0:T(8,128)(2,1)S(1)}) custom-call(s32[4]{0:T(128)S(1)} %pad_add_fusion.pos_ref, f32[384,768]{1,0:T(8,128)S(1)} %student_logits.1.l_ref, bf16[768,384]{1,0:T(8,128)(2,1)S(1)} %copy-done.1, bf16[768,384]{1,0:T(8,128)(2,1)S(1)} %collective-permute-done.oth_ref, s32[6,128]{1,0:T(8,128)S(1)} %bitcast.32, ...), custom_call_target="tpu_custom_call" | custom-call | flops 452984832 | bytes 2949120 | tf_op jit(solution)/shard_map/local_stats/pallas_call | solution.py:190
  9.1 15.0 %all_to_all.15.in_ref = f32[8,2,640]{2,1,0:T(2,128)S(1)} all-to-all(f32[8,2,640]{2,1,0:T(2,128)S(1)} %broadcast_in_dim.4), channel_id=1, replica_groups=mesh['y'=4,'z'=8,'x'=4,'c'=2] {'z'}, dimensions={0} | all-to-all | bytes 81920 | tf_op jit(solution)/shard_map/all_to_all | solution.py:352
  24.1 0.1 merge_stats.1
  24.2 0.0 copy-done
  24.3 0.1 collective-permute-start.4
  24.4 14.6 %all_to_all.16.stats_ref = f32[16,2,640]{2,1,0:T(2,128)S(1)} all-to-all(f32[16,2,640]{2,1,0:T(2,128)S(1)} %broadcast_in_dim.5), channel_id=1, replica_groups=mesh['y'=4,'z'=8,'x'=4,'c'=2] {'y','x'}, dimensions={0} | all-to-all | bytes 163840 | tf_op jit(solution)/shard_map/all_to_all | solution.py:352
  38.9 0.0 slice-done
  38.9 0.0 slice-done.1
  38.9 0.0 copy-done.4
  38.9 2.1 %grad_logits.1 = (bf16[400,768]{1,0:T(8,128)(2,1)S(1)}, f32[4,8,32,384]{3,2,1,0:T(8,128)S(1)}) custom-call(s32[4]{0:T(128)S(1)} %pad_add_fusion.pos_ref, f32[384,768]{1,0:T(8,128)S(1)} %student_logits.1.l_ref, bf16[384,768]{1,0:T(8,128)(2,1)S(1)} %get-tuple-element.30.t_ref, s32[3,128]{1,0:T(4,128)S(1)} %bitcast.31, f32[3,128]{1,0:T(4,128)S(1)} %bitcast.33, ...), custom_call_target="tpu_custom_call" | custom-call | flops 2359296 | bytes 2359296 | tf_op jit(solution)/shard_map/grad_logits/pallas_call | solution.py:271
  41.0 0.2 multiply_convert_fusion.2
  41.2 1.4 %collective-permute-start.1 = (f16[4,8,32,384]{3,2,1,0:T(8,128)(2,1)S(1)}, f16[4,8,32,384]{3,2,1,0:T(8,128)(2,1)S(1)}, u32[]{:S(2)}, u32[]{:S(2)}) collective-permute-start(f16[4,8,32,384]{3,2,1,0:T(8,128)(2,1)S(1)} %multiply_convert_fusion.2), channel_id=1, source_target_pairs={{0,4},{1,129},{2,6},{3,131},{4,0},{5,133},{6,2},{7,135},{8,12},{9,... | collective-permute-start | bytes 2359304 | tf_op jit(solution)/shard_map/ppermute | solution.py:44
  42.6 2.3 %hidden_part.2 = (f32[4,8,32,384]{3,2,1,0:T(8,128)S(1)}, f32[4,8,32,384]{3,2,1,0:T(8,128)S(1)}) custom-call(s32[4]{0:T(128)S(1)} %pad_add_fusion.pos_ref, bf16[4,8,4,32,768]{4,3,2,1,0:T(8,128)(2,1)S(1)} %bitcast.28, bf16[400,768]{1,0:T(8,128)(2,1)S(1)} %get-tuple-element.44.g_ref.g_own_ref), custom_call_target="tpu_custom_call" | custom-call | flops 1 | bytes 1 | tf_op jit(solution)/shard_map/hidden_part/pallas_call | solution.py:236
  45.0 0.4 multiply_convert_fusion
  45.4 0.8 collective-permute-start.2
  46.2 2.5 %collective-permute-start.3 = (f16[4,8,32,384]{3,2,1,0:T(8,128)(2,1)S(1)}, f16[4,8,32,384]{3,2,1,0:T(8,128)(2,1)S(1)}, u32[]{:S(2)}, u32[]{:S(2)}) collective-permute-start(f16[4,8,32,384]{3,2,1,0:T(8,128)(2,1)S(1)} %get-tuple-element.42), channel_id=1, source_target_pairs={{0,6},{1,193},{2,0},{3,195},{4,2},{5,197},{6,4},{7,199},{8,14},{9,... | collective-permute-start | bytes 2359304 | tf_op jit(solution)/shard_map/ppermute | solution.py:44
  48.7 0.0 collective-permute-start.5
  48.7 1.5 %hidden_part.3 = f32[4,8,32,384]{3,2,1,0:T(8,128)S(1)} custom-call(s32[4]{0:T(128)S(1)} %pad_add_fusion.pos_ref, bf16[4,8,4,32,768]{4,3,2,1,0:T(8,128)(2,1)S(1)} %bitcast.29, bf16[400,768]{1,0:T(8,128)(2,1)S(1)} %get-tuple-element.44.g_ref.g_own_ref), custom_call_target="tpu_custom_call" | custom-call | flops 1 | bytes 1 | tf_op jit(solution)/shard_map/hidden_part/pallas_call | solution.py:236
  50.2 0.5 collective-permute-done.5.g_oth_ref
  50.7 0.0 collective-permute-done.4.oth_ref
  50.7 4.9 %head_grad.1 = (bf16[2048,768]{1,0:T(8,128)(2,1)}, f32[1,128]{1,0:T(1,128)}) custom-call(s32[4]{0:T(128)S(1)} %pad_add_fusion.pos_ref, bf16[384,4096]{1,0:T(8,128)(2,1)S(1)} %copy-done, bf16[384,4096]{1,0:T(8,128)(2,1)S(1)} %collective-permute-done.4.oth_ref, bf16[400,768]{1,0:T(8,128)(2,1)S(1)} %get-tuple-element.44.g_ref.g_own_ref, ...), custom_call_target="tpu_custom_call" | custom-call | flops 1 | bytes 1 | tf_op jit(solution)/shard_map/head_grad/pallas_call | solution.py:316
  55.7 0.0 collective-permute-done.1
  55.7 7.6 %collective-permute-done.2 = f16[4,8,32,384]{3,2,1,0:T(8,128)(2,1)S(1)} collective-permute-done((f16[4,8,32,384]{3,2,1,0:T(8,128)(2,1)S(1)}, f16[4,8,32,384]{3,2,1,0:T(8,128)(2,1)S(1)}, u32[]{:S(2)}, u32[]{:S(2)}) %collective-permute-start.2) | collective-permute-done | bytes 786464 | tf_op jit(solution)/shard_map/ppermute | solution.py:44
  63.3 0.0 collective-permute-done.3
  63.3 0.1 fusion.6
  63.4 1.2 %collective-permute-start.8 = (f16[8,32,384]{2,1,0:T(8,128)(2,1)S(1)}, f16[8,32,384]{2,1,0:T(8,128)(2,1)S(1)}, u32[]{:S(2)}, u32[]{:S(2)}) collective-permute-start(f16[8,32,384]{2,1,0:T(8,128)(2,1)S(1)} %fusion.6), channel_id=1, source_target_pairs={{0,128},{1,5},{2,130},{3,7},{4,132},{5,1},{6,134},{7,3},{8,136},{9... | collective-permute-start | bytes 589832 | tf_op jit(solution)/shard_map/ppermute | solution.py:44
  64.6 0.3 fusion.4
  64.9 0.9 %collective-permute-start.7 = (f16[8,32,384]{2,1,0:T(8,128)(2,1)S(1)}, f16[8,32,384]{2,1,0:T(8,128)(2,1)S(1)}, u32[]{:S(2)}, u32[]{:S(2)}) collective-permute-start(f16[8,32,384]{2,1,0:T(8,128)(2,1)S(1)} %get-tuple-element.58), channel_id=1, source_target_pairs={{0,64},{1,3},{2,66},{3,5},{4,68},{5,7},{6,70},{7,1},{8,72},{9,11},... | collective-permute-start | bytes 589832 | tf_op jit(solution)/shard_map/ppermute | solution.py:44
  65.8 2.4 %collective-permute-start.6 = (f16[8,32,384]{2,1,0:T(8,128)(2,1)S(1)}, f16[8,32,384]{2,1,0:T(8,128)(2,1)S(1)}, u32[]{:S(2)}, u32[]{:S(2)}) collective-permute-start(f16[8,32,384]{2,1,0:T(8,128)(2,1)S(1)} %get-tuple-element.57), channel_id=1, source_target_pairs={{0,192},{1,7},{2,194},{3,1},{4,196},{5,3},{6,198},{7,5},{8,200},{9... | collective-permute-start | bytes 589832 | tf_op jit(solution)/shard_map/ppermute | solution.py:44
  68.2 2.5 %collective-permute-done.8 = f16[8,32,384]{2,1,0:T(8,128)(2,1)S(1)} collective-permute-done((f16[8,32,384]{2,1,0:T(8,128)(2,1)S(1)}, f16[8,32,384]{2,1,0:T(8,128)(2,1)S(1)}, u32[]{:S(2)}, u32[]{:S(2)}) %collective-permute-start.8) | collective-permute-done | bytes 196640 | tf_op jit(solution)/shard_map/ppermute | solution.py:44
  70.8 2.0 %collective-permute-done.7 = f16[8,32,384]{2,1,0:T(8,128)(2,1)S(1)} collective-permute-done((f16[8,32,384]{2,1,0:T(8,128)(2,1)S(1)}, f16[8,32,384]{2,1,0:T(8,128)(2,1)S(1)}, u32[]{:S(2)}, u32[]{:S(2)}) %collective-permute-start.7) | collective-permute-done | bytes 196640 | tf_op jit(solution)/shard_map/ppermute | solution.py:44
  72.8 0.0 collective-permute-done.6
  72.8 0.2 fusion.3
  73.0 12.0 %all_to_all.17 = f16[8,32,384]{2,1,0:T(8,128)(2,1)S(1)} all-to-all(f16[8,32,384]{2,1,0:T(8,128)(2,1)S(1)} %fusion.3), channel_id=1, replica_groups=mesh['y'=4,'z'=8,'x'=4,'c'=2] {'z'}, dimensions={0} | all-to-all | bytes 393216 | tf_op jit(solution)/shard_map/all_to_all | solution.py:386
  85.0 0.7 multiply_reduce_fusion
  (4 shorter events, 0.0 us)
Async XLA Ops:
  0.6 6.2 %collective-permute-start = (bf16[768,384]{1,0:T(8,128)(2,1)}, bf16[768,384]{1,0:T(8,128)(2,1)S(1)}, u32[]{:S(2)}, u32[]{:S(2)}) collective-permute-start(bf16[768,384]{1,0:T(8,128)(2,1)} %own_ref.2), channel_id=1, source_target_pairs={{0,1},{1,0},{2,3},{3,2},{4,5},{5,4},{6,7},{7,6},{8,9},{9,8},{10,11... | collective-permute-start | bytes 1769480 | tf_op jit(solution)/shard_map/ppermute | solution.py:32
  0.7 38.2 %slice-start = ((s8[6291456]{0:T(1024)(128)(4,1)}), s8[4194304]{0:T(1024)(128)(4,1)S(1)}, s32[]{:S(2)}) async-start(s8[6291456]{0:T(1024)(128)(4,1)} %bitcast.25), calls=%async_computation.3 | async-start | bytes 8388608
  0.8 6.0 %copy-start.1 = (bf16[768,384]{1,0:T(8,128)(2,1)S(1)}, bf16[768,384]{1,0:T(8,128)(2,1)}, u32[]{:S(2)}) copy-start(bf16[768,384]{1,0:T(8,128)(2,1)} %own_ref.2) | copy-start | bytes 1769476
  0.8 6.0 %copy-start.2 = (s32[384]{0:T(512)S(1)}, s32[384]{0:T(512)}, u32[]{:S(2)}) copy-start(s32[384]{0:T(512)} %param.9) | copy-start | bytes 4612
  0.8 6.0 %copy-start.3 = (s32[768]{0:T(1024)S(1)}, s32[768]{0:T(1024)}, u32[]{:S(2)}) copy-start(s32[768]{0:T(1024)} %param.10) | copy-start | bytes 9220
  0.8 23.4 %copy-start = (bf16[384,4096]{1,0:T(8,128)(2,1)S(1)}, bf16[384,4096]{1,0:T(8,128)(2,1)}, u32[]{:S(2)}) copy-start(bf16[384,4096]{1,0:T(8,128)(2,1)} %own_ref.3) | copy-start | bytes 9437188
  0.8 38.1 %slice-start.1 = ((s8[6291456]{0:T(1024)(128)(4,1)}), s8[2097152]{0:T(1024)(128)(4,1)S(1)}, s32[]{:S(2)}) async-start(s8[6291456]{0:T(1024)(128)(4,1)} %bitcast.25), calls=%async_computation.4 | async-start | bytes 4194304
  6.8 32.2 %copy-start.4 = (f32[384]{0:T(512)S(1)}, f32[384]{0:T(512)}, u32[]{:S(2)}) copy-start(f32[384]{0:T(512)} %param.11) | copy-start | bytes 4612
  24.3 26.5 %collective-permute-start.4 = (bf16[384,4096]{1,0:T(8,128)(2,1)S(1)}, bf16[384,4096]{1,0:T(8,128)(2,1)S(1)}, u32[]{:S(2)}, u32[]{:S(2)}) collective-permute-start(bf16[384,4096]{1,0:T(8,128)(2,1)S(1)} %copy-done), channel_id=1, source_target_pairs={{0,1},{1,0},{2,3},{3,2},{4,5},{5,4},{6,7},{7,6},{8,9},{9,8},{10,11... | collective-permute-start | bytes 9437192 | tf_op jit(solution)/shard_map/ppermute | solution.py:32
  41.2 14.4 %collective-permute-start.1 = (f16[4,8,32,384]{3,2,1,0:T(8,128)(2,1)S(1)}, f16[4,8,32,384]{3,2,1,0:T(8,128)(2,1)S(1)}, u32[]{:S(2)}, u32[]{:S(2)}) collective-permute-start(f16[4,8,32,384]{3,2,1,0:T(8,128)(2,1)S(1)} %multiply_convert_fusion.2), channel_id=1, source_target_pairs={{0,4},{1,129},{2,6},{3,131},{4,0},{5,133},{6,2},{7,135},{8,12},{9,... | collective-permute-start | bytes 2359304 | tf_op jit(solution)/shard_map/ppermute | solution.py:44
  45.4 17.9 %collective-permute-start.2 = (f16[4,8,32,384]{3,2,1,0:T(8,128)(2,1)S(1)}, f16[4,8,32,384]{3,2,1,0:T(8,128)(2,1)S(1)}, u32[]{:S(2)}, u32[]{:S(2)}) collective-permute-start(f16[4,8,32,384]{3,2,1,0:T(8,128)(2,1)S(1)} %get-tuple-element.41), channel_id=1, source_target_pairs={{0,2},{1,65},{2,4},{3,67},{4,6},{5,69},{6,0},{7,71},{8,10},{9,73},... | collective-permute-start | bytes 2359304 | tf_op jit(solution)/shard_map/ppermute | solution.py:44
  46.2 17.1 %collective-permute-start.3 = (f16[4,8,32,384]{3,2,1,0:T(8,128)(2,1)S(1)}, f16[4,8,32,384]{3,2,1,0:T(8,128)(2,1)S(1)}, u32[]{:S(2)}, u32[]{:S(2)}) collective-permute-start(f16[4,8,32,384]{3,2,1,0:T(8,128)(2,1)S(1)} %get-tuple-element.42), channel_id=1, source_target_pairs={{0,6},{1,193},{2,0},{3,195},{4,2},{5,197},{6,4},{7,199},{8,14},{9,... | collective-permute-start | bytes 2359304 | tf_op jit(solution)/shard_map/ppermute | solution.py:44
  48.7 2.0 %collective-permute-start.5 = (bf16[400,768]{1,0:T(8,128)(2,1)S(1)}, bf16[400,768]{1,0:T(8,128)(2,1)S(1)}, u32[]{:S(2)}, u32[]{:S(2)}) collective-permute-start(bf16[400,768]{1,0:T(8,128)(2,1)S(1)} %get-tuple-element.44.g_ref.g_own_ref), channel_id=1, source_target_pairs={{0,1},{1,0},{2,3},{3,2},{4,5},{5,4},{6,7},{7,6},{8,9},{9,8},{10,11... | collective-permute-start | bytes 1843208 | tf_op jit(solution)/shard_map/ppermute | solution.py:32
  63.4 7.4 %collective-permute-start.8 = (f16[8,32,384]{2,1,0:T(8,128)(2,1)S(1)}, f16[8,32,384]{2,1,0:T(8,128)(2,1)S(1)}, u32[]{:S(2)}, u32[]{:S(2)}) collective-permute-start(f16[8,32,384]{2,1,0:T(8,128)(2,1)S(1)} %fusion.6), channel_id=1, source_target_pairs={{0,128},{1,5},{2,130},{3,7},{4,132},{5,1},{6,134},{7,3},{8,136},{9... | collective-permute-start | bytes 589832 | tf_op jit(solution)/shard_map/ppermute | solution.py:44
  64.9 7.9 %collective-permute-start.7 = (f16[8,32,384]{2,1,0:T(8,128)(2,1)S(1)}, f16[8,32,384]{2,1,0:T(8,128)(2,1)S(1)}, u32[]{:S(2)}, u32[]{:S(2)}) collective-permute-start(f16[8,32,384]{2,1,0:T(8,128)(2,1)S(1)} %get-tuple-element.58), channel_id=1, source_target_pairs={{0,64},{1,3},{2,66},{3,5},{4,68},{5,7},{6,70},{7,1},{8,72},{9,11},... | collective-permute-start | bytes 589832 | tf_op jit(solution)/shard_map/ppermute | solution.py:44
  65.8 7.0 %collective-permute-start.6 = (f16[8,32,384]{2,1,0:T(8,128)(2,1)S(1)}, f16[8,32,384]{2,1,0:T(8,128)(2,1)S(1)}, u32[]{:S(2)}, u32[]{:S(2)}) collective-permute-start(f16[8,32,384]{2,1,0:T(8,128)(2,1)S(1)} %get-tuple-element.57), channel_id=1, source_target_pairs={{0,192},{1,7},{2,194},{3,1},{4,196},{5,3},{6,198},{7,5},{8,200},{9... | collective-permute-start | bytes 589832 | tf_op jit(solution)/shard_map/ppermute | solution.py:44

commit v15 on v14

--- a/solution.py
+++ b/solution.py
@@ -38,7 +38,7 @@
     pairs = []
     for source in np.ndindex(shape):
         target = list(source)
-        axis = 2 if (source[3] == 0) == first else 0
+        axis = 0 if (source[3] == 0) == first else 2
         target[axis] = (target[axis] + by) % shape[axis]
         pairs.append(tuple(int(np.ravel_multi_index(at, shape)) for at in (source, target)))
     return lax.ppermute(a, axes, pairs)
@@ -151,8 +151,11 @@
     )(stats)
 
 
-def stats_kernel(pos_ref, l_ref, own_ref, oth_ref, assign_ref, ids_ref, stats_ref, t_ref):
+def stats_kernel(
+    pos_ref, l_ref, own_ref, oth_ref, assign_ref, ids_ref, stats_ref, t_ref, both_ref
+):
     rows, cols = l_ref.shape
+    half = cols // 2
     total = own_ref.shape[0]
     first = pos_ref[0] == 0
     assign = in_row(assign_ref)
@@ -160,9 +163,9 @@
     assign, ids = columns_of(assign, in_row(ids_ref))
     lanes = lax.broadcasted_iota(jnp.int32, (rows, total), 1).astype(F32)
     pick = (lanes == assign).astype(BF16)
-    own = jnp.dot(pick, own_ref[...], preferred_element_type=F32)
-    oth = jnp.dot(pick, oth_ref[...], preferred_element_type=F32)
-    teacher = jnp.concatenate([jnp.where(first, own, oth), jnp.where(first, oth, own)], axis=1)
+    both_ref[:, pl.ds(pl.multiple_of(pos_ref[0] * half, half), half)] = own_ref[...]
+    both_ref[:, pl.ds(pl.multiple_of((1 - pos_ref[0]) * half, half), half)] = oth_ref[...]
+    teacher = jnp.dot(pick, both_ref[...], preferred_element_type=F32)
     t_ref[...] = teacher.astype(BF16)
     logits = l_ref[...]
     top_s = jnp.max(logits, axis=1, keepdims=True)
@@ -195,6 +198,7 @@
         ),
         in_specs=[pl.BlockSpec(memory_space=pltpu.SMEM)] + [WHOLE] * 5,
         out_specs=(WHOLE, WHOLE),
+        scratch_shapes=[pltpu.VMEM((own.shape[0], cols), BF16)],
         compiler_params=params(16),
         cost_estimate=pl.CostEstimate(
             flops=2 * rows * cols * own.shape[0],
@@ -211,7 +215,7 @@
 
 def hidden_product(groups, pos_ref, w_ref, g, outs):
     ny, nz, nx, sub, cols = w_ref.shape
-    x_first, y, x = pos_ref[0] == 0, pos_ref[2], pos_ref[3]
+    x_first, y, x = pos_ref[0] == 1, pos_ref[2], pos_ref[3]
 
     def block(far, near):
         dx = jnp.where(x_first, far, near)

time: 86.7 us -> 86.9 us (level)
  no operation moved by 1% of the time
where the time goes in v15:
time: 86.9 us; the launch traced here: 85.5 us
  blocking collectives  41.6 us (48%)
  Pallas kernels  19 us (22%)
  waiting for transfers between devices  12.6 us (14%)
  starting transfers between devices  9.4 us (11%)
  other arithmetic  1.97 us (2%)
    all_to_all x2, blocking collectives, gathered(): return lax.all_to_all(value, axes, 0, 0, tiled=True)  29.6 us
    ppermute x6, waiting for transfers between devices, shift_by_core(): return lax.ppermute(a, axes, pairs)  12.1 us
    all_to_all x1, blocking collectives, body(): both = lax.all_to_all(both, 'z', 0, 0, tiled=True)  12 us
    ppermute x6, starting transfers between devices, shift_by_core(): return lax.ppermute(a, axes, pairs)  9.24 us
    pallas_call x1, Pallas kernels, student_logits(): pl.pallas_call(functools.partial(logits_kernel, steps), out_shape=jax.Sha...  5.91 us
    pallas_call x1, Pallas kernels, head_grad(): pl.pallas_call(head_kernel, out_shape=(jax.ShapeDtypeStruct((width, cols)...  4.94 us
    pallas_call x2, Pallas kernels, hidden_part(): pl.pallas_call(functools.partial(hidden_kernel, groups), out_shape=out_sh...  3.87 us
    pallas_call x1, Pallas kernels, grad_logits(): pl.pallas_call(grad_kernel, out_shape=(jax.ShapeDtypeStruct((rows + LOSS_...  2.1 us
  transfers between devices with their start and end apart: 9, of which 4 were waited for; matrix products, arithmetic and copies ran while one was open for 1% of the time, Pallas kernels for 20%

profile of v15, /device:TPU:32, one launch (start us, length us, event | category | flops | bytes accessed | tf_op | source)
XLA Modules:
  0.0 85.5 jit_solution(17816550117531971305)
XLA Ops:
  0.6 0.1 collective-permute-start
  0.7 0.0 slice-start
  0.8 0.1 pad_add_fusion.pos_ref
  0.8 0.0 copy-start.1
  0.8 0.0 copy-start.2
  0.8 0.0 copy-start.3
  0.8 0.0 slice-start.1
  0.9 5.9 %student_logits.1.l_ref = f32[384,768]{1,0:T(8,128)S(1)} custom-call(bf16[384,4096]{1,0:T(8,128)(2,1)} %own_ref.3, bf16[4096,768]{1,0:T(8,128)(2,1)} %w_ref.1), custom_call_target="tpu_custom_call" | custom-call | flops 2415919104 | bytes 10616832 | tf_op jit(solution)/shard_map/student_logits/pallas_call | solution.py:75
  6.8 0.0 copy-start.4
  6.8 0.0 collective-permute-done.oth_ref
  6.8 0.0 copy-done.1
  6.8 0.0 copy-done.2
  6.8 0.0 copy-done.3
  6.8 2.1 %local_stats.1 = (f32[2,640]{1,0:T(2,128)S(1)}, bf16[384,768]{1,0:T(8,128)(2,1)S(1)}) custom-call(s32[4]{0:T(128)S(1)} %pad_add_fusion.pos_ref, f32[384,768]{1,0:T(8,128)S(1)} %student_logits.1.l_ref, bf16[768,384]{1,0:T(8,128)(2,1)S(1)} %copy-done.1, bf16[768,384]{1,0:T(8,128)(2,1)S(1)} %collective-permute-done.oth_ref, s32[6,128]{1,0:T(8,128)S(1)} %bitcast.32, ...), custom_call_target="tpu_custom_call" | custom-call | flops 452984832 | bytes 2949120 | tf_op jit(solution)/shard_map/local_stats/pallas_call | solution.py:193
  8.9 15.0 %all_to_all.15.in_ref = f32[8,2,640]{2,1,0:T(2,128)S(1)} all-to-all(f32[8,2,640]{2,1,0:T(2,128)S(1)} %broadcast_in_dim.4), channel_id=1, replica_groups=mesh['y'=4,'z'=8,'x'=4,'c'=2] {'z'}, dimensions={0} | all-to-all | bytes 81920 | tf_op jit(solution)/shard_map/all_to_all | solution.py:356
  24.0 0.1 merge_stats.1
  24.1 0.0 copy-done
  24.1 0.1 collective-permute-start.4
  24.2 14.6 %all_to_all.16.stats_ref = f32[16,2,640]{2,1,0:T(2,128)S(1)} all-to-all(f32[16,2,640]{2,1,0:T(2,128)S(1)} %broadcast_in_dim.5), channel_id=1, replica_groups=mesh['y'=4,'z'=8,'x'=4,'c'=2] {'y','x'}, dimensions={0} | all-to-all | bytes 163840 | tf_op jit(solution)/shard_map/all_to_all | solution.py:356
  38.7 0.0 slice-done
  38.7 0.0 slice-done.1
  38.7 0.0 copy-done.4
  38.7 2.1 %grad_logits.1 = (bf16[400,768]{1,0:T(8,128)(2,1)S(1)}, f32[4,8,32,384]{3,2,1,0:T(8,128)S(1)}) custom-call(s32[4]{0:T(128)S(1)} %pad_add_fusion.pos_ref, f32[384,768]{1,0:T(8,128)S(1)} %student_logits.1.l_ref, bf16[384,768]{1,0:T(8,128)(2,1)S(1)} %get-tuple-element.30.t_ref, s32[3,128]{1,0:T(4,128)S(1)} %bitcast.31, f32[3,128]{1,0:T(4,128)S(1)} %bitcast.33, ...), custom_call_target="tpu_custom_call" | custom-call | flops 2359296 | bytes 2359296 | tf_op jit(solution)/shard_map/grad_logits/pallas_call | solution.py:275
  40.9 0.2 multiply_convert_fusion.2
  41.0 1.2 %collective-permute-start.1 = (f16[4,8,32,384]{3,2,1,0:T(8,128)(2,1)S(1)}, f16[4,8,32,384]{3,2,1,0:T(8,128)(2,1)S(1)}, u32[]{:S(2)}, u32[]{:S(2)}) collective-permute-start(f16[4,8,32,384]{3,2,1,0:T(8,128)(2,1)S(1)} %multiply_convert_fusion.2), channel_id=1, source_target_pairs={{0,128},{1,5},{2,130},{3,7},{4,132},{5,1},{6,134},{7,3},{8,136},{9... | collective-permute-start | bytes 2359304 | tf_op jit(solution)/shard_map/ppermute | solution.py:44
  42.3 2.3 %hidden_part.2 = (f32[4,8,32,384]{3,2,1,0:T(8,128)S(1)}, f32[4,8,32,384]{3,2,1,0:T(8,128)S(1)}) custom-call(s32[4]{0:T(128)S(1)} %pad_add_fusion.pos_ref, bf16[4,8,4,32,768]{4,3,2,1,0:T(8,128)(2,1)S(1)} %bitcast.28, bf16[400,768]{1,0:T(8,128)(2,1)S(1)} %get-tuple-element.44.g_ref.g_own_ref), custom_call_target="tpu_custom_call" | custom-call | flops 1 | bytes 1 | tf_op jit(solution)/shard_map/hidden_part/pallas_call | solution.py:240
  44.6 0.4 multiply_convert_fusion
  45.0 0.9 %collective-permute-start.2 = (f16[4,8,32,384]{3,2,1,0:T(8,128)(2,1)S(1)}, f16[4,8,32,384]{3,2,1,0:T(8,128)(2,1)S(1)}, u32[]{:S(2)}, u32[]{:S(2)}) collective-permute-start(f16[4,8,32,384]{3,2,1,0:T(8,128)(2,1)S(1)} %get-tuple-element.41), channel_id=1, source_target_pairs={{0,64},{1,3},{2,66},{3,5},{4,68},{5,7},{6,70},{7,1},{8,72},{9,11},... | collective-permute-start | bytes 2359304 | tf_op jit(solution)/shard_map/ppermute | solution.py:44
  45.9 2.4 %collective-permute-start.3 = (f16[4,8,32,384]{3,2,1,0:T(8,128)(2,1)S(1)}, f16[4,8,32,384]{3,2,1,0:T(8,128)(2,1)S(1)}, u32[]{:S(2)}, u32[]{:S(2)}) collective-permute-start(f16[4,8,32,384]{3,2,1,0:T(8,128)(2,1)S(1)} %get-tuple-element.42), channel_id=1, source_target_pairs={{0,192},{1,7},{2,194},{3,1},{4,196},{5,3},{6,198},{7,5},{8,200},{9... | collective-permute-start | bytes 2359304 | tf_op jit(solution)/shard_map/ppermute | solution.py:44
  48.3 0.0 collective-permute-start.5
  48.3 1.5 %hidden_part.3 = f32[4,8,32,384]{3,2,1,0:T(8,128)S(1)} custom-call(s32[4]{0:T(128)S(1)} %pad_add_fusion.pos_ref, bf16[4,8,4,32,768]{4,3,2,1,0:T(8,128)(2,1)S(1)} %bitcast.29, bf16[400,768]{1,0:T(8,128)(2,1)S(1)} %get-tuple-element.44.g_ref.g_own_ref), custom_call_target="tpu_custom_call" | custom-call | flops 1 | bytes 1 | tf_op jit(solution)/shard_map/hidden_part/pallas_call | solution.py:240
  49.9 0.5 collective-permute-done.5.g_oth_ref
  50.4 0.0 collective-permute-done.4.oth_ref
  50.4 4.9 %head_grad.1 = (bf16[2048,768]{1,0:T(8,128)(2,1)}, f32[1,128]{1,0:T(1,128)}) custom-call(s32[4]{0:T(128)S(1)} %pad_add_fusion.pos_ref, bf16[384,4096]{1,0:T(8,128)(2,1)S(1)} %copy-done, bf16[384,4096]{1,0:T(8,128)(2,1)S(1)} %collective-permute-done.4.oth_ref, bf16[400,768]{1,0:T(8,128)(2,1)S(1)} %get-tuple-element.44.g_ref.g_own_ref, ...), custom_call_target="tpu_custom_call" | custom-call | flops 1 | bytes 1 | tf_op jit(solution)/shard_map/head_grad/pallas_call | solution.py:320
  55.3 0.0 collective-permute-done.1
  55.3 7.7 %collective-permute-done.2 = f16[4,8,32,384]{3,2,1,0:T(8,128)(2,1)S(1)} collective-permute-done((f16[4,8,32,384]{3,2,1,0:T(8,128)(2,1)S(1)}, f16[4,8,32,384]{3,2,1,0:T(8,128)(2,1)S(1)}, u32[]{:S(2)}, u32[]{:S(2)}) %collective-permute-start.2) | collective-permute-done | bytes 786464 | tf_op jit(solution)/shard_map/ppermute | solution.py:44
  63.1 0.0 collective-permute-done.3
  63.1 0.1 fusion.6
  63.2 1.4 %collective-permute-start.8 = (f16[8,32,384]{2,1,0:T(8,128)(2,1)S(1)}, f16[8,32,384]{2,1,0:T(8,128)(2,1)S(1)}, u32[]{:S(2)}, u32[]{:S(2)}) collective-permute-start(f16[8,32,384]{2,1,0:T(8,128)(2,1)S(1)} %fusion.6), channel_id=1, source_target_pairs={{0,4},{1,129},{2,6},{3,131},{4,0},{5,133},{6,2},{7,135},{8,12},{9,... | collective-permute-start | bytes 589832 | tf_op jit(solution)/shard_map/ppermute | solution.py:44
  64.6 0.3 fusion.4
  64.9 0.8 collective-permute-start.7
  65.6 2.5 %collective-permute-start.6 = (f16[8,32,384]{2,1,0:T(8,128)(2,1)S(1)}, f16[8,32,384]{2,1,0:T(8,128)(2,1)S(1)}, u32[]{:S(2)}, u32[]{:S(2)}) collective-permute-start(f16[8,32,384]{2,1,0:T(8,128)(2,1)S(1)} %get-tuple-element.57), channel_id=1, source_target_pairs={{0,6},{1,193},{2,0},{3,195},{4,2},{5,197},{6,4},{7,199},{8,14},{9,... | collective-permute-start | bytes 589832 | tf_op jit(solution)/shard_map/ppermute | solution.py:44
  68.2 2.4 %collective-permute-done.8 = f16[8,32,384]{2,1,0:T(8,128)(2,1)S(1)} collective-permute-done((f16[8,32,384]{2,1,0:T(8,128)(2,1)S(1)}, f16[8,32,384]{2,1,0:T(8,128)(2,1)S(1)}, u32[]{:S(2)}, u32[]{:S(2)}) %collective-permute-start.8) | collective-permute-done | bytes 196640 | tf_op jit(solution)/shard_map/ppermute | solution.py:44
  70.5 2.0 %collective-permute-done.7 = f16[8,32,384]{2,1,0:T(8,128)(2,1)S(1)} collective-permute-done((f16[8,32,384]{2,1,0:T(8,128)(2,1)S(1)}, f16[8,32,384]{2,1,0:T(8,128)(2,1)S(1)}, u32[]{:S(2)}, u32[]{:S(2)}) %collective-permute-start.7) | collective-permute-done | bytes 196640 | tf_op jit(solution)/shard_map/ppermute | solution.py:44
  72.6 0.0 collective-permute-done.6
  72.6 0.2 fusion.3
  72.8 12.0 %all_to_all.17 = f16[8,32,384]{2,1,0:T(8,128)(2,1)S(1)} all-to-all(f16[8,32,384]{2,1,0:T(8,128)(2,1)S(1)} %fusion.3), channel_id=1, replica_groups=mesh['y'=4,'z'=8,'x'=4,'c'=2] {'z'}, dimensions={0} | all-to-all | bytes 393216 | tf_op jit(solution)/shard_map/all_to_all | solution.py:390
  84.8 0.7 multiply_reduce_fusion
  (4 shorter events, 0.1 us)
Async XLA Ops:
  0.6 6.2 %collective-permute-start = (bf16[768,384]{1,0:T(8,128)(2,1)}, bf16[768,384]{1,0:T(8,128)(2,1)S(1)}, u32[]{:S(2)}, u32[]{:S(2)}) collective-permute-start(bf16[768,384]{1,0:T(8,128)(2,1)} %own_ref.2), channel_id=1, source_target_pairs={{0,1},{1,0},{2,3},{3,2},{4,5},{5,4},{6,7},{7,6},{8,9},{9,8},{10,11... | collective-permute-start | bytes 1769480 | tf_op jit(solution)/shard_map/ppermute | solution.py:32
  0.7 38.0 %slice-start = ((s8[6291456]{0:T(1024)(128)(4,1)}), s8[4194304]{0:T(1024)(128)(4,1)S(1)}, s32[]{:S(2)}) async-start(s8[6291456]{0:T(1024)(128)(4,1)} %bitcast.25), calls=%async_computation.3 | async-start | bytes 8388608
  0.8 6.0 %copy-start.1 = (bf16[768,384]{1,0:T(8,128)(2,1)S(1)}, bf16[768,384]{1,0:T(8,128)(2,1)}, u32[]{:S(2)}) copy-start(bf16[768,384]{1,0:T(8,128)(2,1)} %own_ref.2) | copy-start | bytes 1769476
  0.8 6.0 %copy-start.2 = (s32[384]{0:T(512)S(1)}, s32[384]{0:T(512)}, u32[]{:S(2)}) copy-start(s32[384]{0:T(512)} %param.9) | copy-start | bytes 4612
  0.8 6.0 %copy-start.3 = (s32[768]{0:T(1024)S(1)}, s32[768]{0:T(1024)}, u32[]{:S(2)}) copy-start(s32[768]{0:T(1024)} %param.10) | copy-start | bytes 9220
  0.8 23.2 %copy-start = (bf16[384,4096]{1,0:T(8,128)(2,1)S(1)}, bf16[384,4096]{1,0:T(8,128)(2,1)}, u32[]{:S(2)}) copy-start(bf16[384,4096]{1,0:T(8,128)(2,1)} %own_ref.3) | copy-start | bytes 9437188
  0.8 37.9 %slice-start.1 = ((s8[6291456]{0:T(1024)(128)(4,1)}), s8[2097152]{0:T(1024)(128)(4,1)S(1)}, s32[]{:S(2)}) async-start(s8[6291456]{0:T(1024)(128)(4,1)} %bitcast.25), calls=%async_computation.4 | async-start | bytes 4194304
  6.8 32.0 %copy-start.4 = (f32[384]{0:T(512)S(1)}, f32[384]{0:T(512)}, u32[]{:S(2)}) copy-start(f32[384]{0:T(512)} %param.11) | copy-start | bytes 4612
  24.1 26.3 %collective-permute-start.4 = (bf16[384,4096]{1,0:T(8,128)(2,1)S(1)}, bf16[384,4096]{1,0:T(8,128)(2,1)S(1)}, u32[]{:S(2)}, u32[]{:S(2)}) collective-permute-start(bf16[384,4096]{1,0:T(8,128)(2,1)S(1)} %copy-done), channel_id=1, source_target_pairs={{0,1},{1,0},{2,3},{3,2},{4,5},{5,4},{6,7},{7,6},{8,9},{9,8},{10,11... | collective-permute-start | bytes 9437192 | tf_op jit(solution)/shard_map/ppermute | solution.py:32
  41.0 14.3 %collective-permute-start.1 = (f16[4,8,32,384]{3,2,1,0:T(8,128)(2,1)S(1)}, f16[4,8,32,384]{3,2,1,0:T(8,128)(2,1)S(1)}, u32[]{:S(2)}, u32[]{:S(2)}) collective-permute-start(f16[4,8,32,384]{3,2,1,0:T(8,128)(2,1)S(1)} %multiply_convert_fusion.2), channel_id=1, source_target_pairs={{0,128},{1,5},{2,130},{3,7},{4,132},{5,1},{6,134},{7,3},{8,136},{9... | collective-permute-start | bytes 2359304 | tf_op jit(solution)/shard_map/ppermute | solution.py:44
  45.0 18.0 %collective-permute-start.2 = (f16[4,8,32,384]{3,2,1,0:T(8,128)(2,1)S(1)}, f16[4,8,32,384]{3,2,1,0:T(8,128)(2,1)S(1)}, u32[]{:S(2)}, u32[]{:S(2)}) collective-permute-start(f16[4,8,32,384]{3,2,1,0:T(8,128)(2,1)S(1)} %get-tuple-element.41), channel_id=1, source_target_pairs={{0,64},{1,3},{2,66},{3,5},{4,68},{5,7},{6,70},{7,1},{8,72},{9,11},... | collective-permute-start | bytes 2359304 | tf_op jit(solution)/shard_map/ppermute | solution.py:44
  45.9 17.1 %collective-permute-start.3 = (f16[4,8,32,384]{3,2,1,0:T(8,128)(2,1)S(1)}, f16[4,8,32,384]{3,2,1,0:T(8,128)(2,1)S(1)}, u32[]{:S(2)}, u32[]{:S(2)}) collective-permute-start(f16[4,8,32,384]{3,2,1,0:T(8,128)(2,1)S(1)} %get-tuple-element.42), channel_id=1, source_target_pairs={{0,192},{1,7},{2,194},{3,1},{4,196},{5,3},{6,198},{7,5},{8,200},{9... | collective-permute-start | bytes 2359304 | tf_op jit(solution)/shard_map/ppermute | solution.py:44
  48.3 2.0 %collective-permute-start.5 = (bf16[400,768]{1,0:T(8,128)(2,1)S(1)}, bf16[400,768]{1,0:T(8,128)(2,1)S(1)}, u32[]{:S(2)}, u32[]{:S(2)}) collective-permute-start(bf16[400,768]{1,0:T(8,128)(2,1)S(1)} %get-tuple-element.44.g_ref.g_own_ref), channel_id=1, source_target_pairs={{0,1},{1,0},{2,3},{3,2},{4,5},{5,4},{6,7},{7,6},{8,9},{9,8},{10,11... | collective-permute-start | bytes 1843208 | tf_op jit(solution)/shard_map/ppermute | solution.py:32
  63.2 7.3 %collective-permute-start.8 = (f16[8,32,384]{2,1,0:T(8,128)(2,1)S(1)}, f16[8,32,384]{2,1,0:T(8,128)(2,1)S(1)}, u32[]{:S(2)}, u32[]{:S(2)}) collective-permute-start(f16[8,32,384]{2,1,0:T(8,128)(2,1)S(1)} %fusion.6), channel_id=1, source_target_pairs={{0,4},{1,129},{2,6},{3,131},{4,0},{5,133},{6,2},{7,135},{8,12},{9,... | collective-permute-start | bytes 589832 | tf_op jit(solution)/shard_map/ppermute | solution.py:44
  64.9 7.7 %collective-permute-start.7 = (f16[8,32,384]{2,1,0:T(8,128)(2,1)S(1)}, f16[8,32,384]{2,1,0:T(8,128)(2,1)S(1)}, u32[]{:S(2)}, u32[]{:S(2)}) collective-permute-start(f16[8,32,384]{2,1,0:T(8,128)(2,1)S(1)} %get-tuple-element.58), channel_id=1, source_target_pairs={{0,2},{1,65},{2,4},{3,67},{4,6},{5,69},{6,0},{7,71},{8,10},{9,73},... | collective-permute-start | bytes 589832 | tf_op jit(solution)/shard_map/ppermute | solution.py:44
  65.6 6.9 %collective-permute-start.6 = (f16[8,32,384]{2,1,0:T(8,128)(2,1)S(1)}, f16[8,32,384]{2,1,0:T(8,128)(2,1)S(1)}, u32[]{:S(2)}, u32[]{:S(2)}) collective-permute-start(f16[8,32,384]{2,1,0:T(8,128)(2,1)S(1)} %get-tuple-element.57), channel_id=1, source_target_pairs={{0,6},{1,193},{2,0},{3,195},{4,2},{5,197},{6,4},{7,199},{8,14},{9,... | collective-permute-start | bytes 589832 | tf_op jit(solution)/shard_map/ppermute | solution.py:44

commit v16 on v15

--- a/solution.py
+++ b/solution.py
@@ -38,7 +38,7 @@
     pairs = []
     for source in np.ndindex(shape):
         target = list(source)
-        axis = 0 if (source[3] == 0) == first else 2
+        axis = 2 if (source[3] == 0) == first else 0
         target[axis] = (target[axis] + by) % shape[axis]
         pairs.append(tuple(int(np.ravel_multi_index(at, shape)) for at in (source, target)))
     return lax.ppermute(a, axes, pairs)
@@ -215,7 +215,7 @@
 
 def hidden_product(groups, pos_ref, w_ref, g, outs):
     ny, nz, nx, sub, cols = w_ref.shape
-    x_first, y, x = pos_ref[0] == 1, pos_ref[2], pos_ref[3]
+    x_first, y, x = pos_ref[0] == 0, pos_ref[2], pos_ref[3]
 
     def block(far, near):
         dx = jnp.where(x_first, far, near)

time: 86.9 us -> 86.5 us (level)
  no operation moved by 1% of the time
where the time goes in v16:
time: 86.5 us; the launch traced here: 85.5 us
  blocking collectives  41.6 us (48%)
  Pallas kernels  19 us (22%)
  waiting for transfers between devices  12.6 us (15%)
  starting transfers between devices  9.4 us (11%)
  other arithmetic  1.97 us (2%)
    all_to_all x2, blocking collectives, gathered(): return lax.all_to_all(value, axes, 0, 0, tiled=True)  29.6 us
    ppermute x6, waiting for transfers between devices, shift_by_core(): return lax.ppermute(a, axes, pairs)  12.1 us
    all_to_all x1, blocking collectives, body(): both = lax.all_to_all(both, 'z', 0, 0, tiled=True)  12 us
    ppermute x6, starting transfers between devices, shift_by_core(): return lax.ppermute(a, axes, pairs)  9.24 us
    pallas_call x1, Pallas kernels, student_logits(): pl.pallas_call(functools.partial(logits_kernel, steps), out_shape=jax.Sha...  5.91 us
    pallas_call x1, Pallas kernels, head_grad(): pl.pallas_call(head_kernel, out_shape=(jax.ShapeDtypeStruct((width, cols)...  4.94 us
    pallas_call x2, Pallas kernels, hidden_part(): pl.pallas_call(functools.partial(hidden_kernel, groups), out_shape=out_sh...  3.86 us
    pallas_call x1, Pallas kernels, grad_logits(): pl.pallas_call(grad_kernel, out_shape=(jax.ShapeDtypeStruct((rows + LOSS_...  2.1 us
  transfers between devices with their start and end apart: 9, of which 4 were waited for; matrix products, arithmetic and copies ran while one was open for 1% of the time, Pallas kernels for 20%

profile of v16, /device:TPU:32, one launch (start us, length us, event | category | flops | bytes accessed | tf_op | source)
XLA Modules:
  0.0 85.5 jit_solution(8951556106810209788)
XLA Ops:
  0.6 0.1 collective-permute-start
  0.7 0.0 slice-start
  0.8 0.1 pad_add_fusion.pos_ref
  0.8 0.0 copy-start.1
  0.8 0.0 copy-start.2
  0.8 0.0 copy-start.3
  0.8 0.0 slice-start.1
  0.9 5.9 %student_logits.1.l_ref = f32[384,768]{1,0:T(8,128)S(1)} custom-call(bf16[384,4096]{1,0:T(8,128)(2,1)} %own_ref.3, bf16[4096,768]{1,0:T(8,128)(2,1)} %w_ref.1), custom_call_target="tpu_custom_call" | custom-call | flops 2415919104 | bytes 10616832 | tf_op jit(solution)/shard_map/student_logits/pallas_call | solution.py:75
  6.8 0.0 copy-start.4
  6.8 0.0 collective-permute-done.oth_ref
  6.8 0.0 copy-done.1
  6.8 0.0 copy-done.2
  6.8 0.0 copy-done.3
  6.8 2.1 %local_stats.1 = (f32[2,640]{1,0:T(2,128)S(1)}, bf16[384,768]{1,0:T(8,128)(2,1)S(1)}) custom-call(s32[4]{0:T(128)S(1)} %pad_add_fusion.pos_ref, f32[384,768]{1,0:T(8,128)S(1)} %student_logits.1.l_ref, bf16[768,384]{1,0:T(8,128)(2,1)S(1)} %copy-done.1, bf16[768,384]{1,0:T(8,128)(2,1)S(1)} %collective-permute-done.oth_ref, s32[6,128]{1,0:T(8,128)S(1)} %bitcast.32, ...), custom_call_target="tpu_custom_call" | custom-call | flops 452984832 | bytes 2949120 | tf_op jit(solution)/shard_map/local_stats/pallas_call | solution.py:193
  8.9 15.0 %all_to_all.15.in_ref = f32[8,2,640]{2,1,0:T(2,128)S(1)} all-to-all(f32[8,2,640]{2,1,0:T(2,128)S(1)} %broadcast_in_dim.4), channel_id=1, replica_groups=mesh['y'=4,'z'=8,'x'=4,'c'=2] {'z'}, dimensions={0} | all-to-all | bytes 81920 | tf_op jit(solution)/shard_map/all_to_all | solution.py:356
  24.0 0.1 merge_stats.1
  24.1 0.0 copy-done
  24.1 0.1 collective-permute-start.4
  24.2 14.6 %all_to_all.16.stats_ref = f32[16,2,640]{2,1,0:T(2,128)S(1)} all-to-all(f32[16,2,640]{2,1,0:T(2,128)S(1)} %broadcast_in_dim.5), channel_id=1, replica_groups=mesh['y'=4,'z'=8,'x'=4,'c'=2] {'y','x'}, dimensions={0} | all-to-all | bytes 163840 | tf_op jit(solution)/shard_map/all_to_all | solution.py:356
  38.7 0.0 slice-done
  38.7 0.0 slice-done.1
  38.7 0.0 copy-done.4
  38.7 2.1 %grad_logits.1 = (bf16[400,768]{1,0:T(8,128)(2,1)S(1)}, f32[4,8,32,384]{3,2,1,0:T(8,128)S(1)}) custom-call(s32[4]{0:T(128)S(1)} %pad_add_fusion.pos_ref, f32[384,768]{1,0:T(8,128)S(1)} %student_logits.1.l_ref, bf16[384,768]{1,0:T(8,128)(2,1)S(1)} %get-tuple-element.30.t_ref, s32[3,128]{1,0:T(4,128)S(1)} %bitcast.31, f32[3,128]{1,0:T(4,128)S(1)} %bitcast.33, ...), custom_call_target="tpu_custom_call" | custom-call | flops 2359296 | bytes 2359296 | tf_op jit(solution)/shard_map/grad_logits/pallas_call | solution.py:275
  40.9 0.2 multiply_convert_fusion.2
  41.0 1.4 %collective-permute-start.1 = (f16[4,8,32,384]{3,2,1,0:T(8,128)(2,1)S(1)}, f16[4,8,32,384]{3,2,1,0:T(8,128)(2,1)S(1)}, u32[]{:S(2)}, u32[]{:S(2)}) collective-permute-start(f16[4,8,32,384]{3,2,1,0:T(8,128)(2,1)S(1)} %multiply_convert_fusion.2), channel_id=1, source_target_pairs={{0,4},{1,129},{2,6},{3,131},{4,0},{5,133},{6,2},{7,135},{8,12},{9,... | collective-permute-start | bytes 2359304 | tf_op jit(solution)/shard_map/ppermute | solution.py:44
  42.4 2.3 %hidden_part.2 = (f32[4,8,32,384]{3,2,1,0:T(8,128)S(1)}, f32[4,8,32,384]{3,2,1,0:T(8,128)S(1)}) custom-call(s32[4]{0:T(128)S(1)} %pad_add_fusion.pos_ref, bf16[4,8,4,32,768]{4,3,2,1,0:T(8,128)(2,1)S(1)} %bitcast.28, bf16[400,768]{1,0:T(8,128)(2,1)S(1)} %get-tuple-element.44.g_ref.g_own_ref), custom_call_target="tpu_custom_call" | custom-call | flops 1 | bytes 1 | tf_op jit(solution)/shard_map/hidden_part/pallas_call | solution.py:240
  44.8 0.4 multiply_convert_fusion
  45.2 0.8 collective-permute-start.2
  46.0 2.5 %collective-permute-start.3 = (f16[4,8,32,384]{3,2,1,0:T(8,128)(2,1)S(1)}, f16[4,8,32,384]{3,2,1,0:T(8,128)(2,1)S(1)}, u32[]{:S(2)}, u32[]{:S(2)}) collective-permute-start(f16[4,8,32,384]{3,2,1,0:T(8,128)(2,1)S(1)} %get-tuple-element.42), channel_id=1, source_target_pairs={{0,6},{1,193},{2,0},{3,195},{4,2},{5,197},{6,4},{7,199},{8,14},{9,... | collective-permute-start | bytes 2359304 | tf_op jit(solution)/shard_map/ppermute | solution.py:44
  48.5 0.0 collective-permute-start.5
  48.5 1.5 %hidden_part.3 = f32[4,8,32,384]{3,2,1,0:T(8,128)S(1)} custom-call(s32[4]{0:T(128)S(1)} %pad_add_fusion.pos_ref, bf16[4,8,4,32,768]{4,3,2,1,0:T(8,128)(2,1)S(1)} %bitcast.29, bf16[400,768]{1,0:T(8,128)(2,1)S(1)} %get-tuple-element.44.g_ref.g_own_ref), custom_call_target="tpu_custom_call" | custom-call | flops 1 | bytes 1 | tf_op jit(solution)/shard_map/hidden_part/pallas_call | solution.py:240
  50.1 0.5 collective-permute-done.5.g_oth_ref
  50.6 0.0 collective-permute-done.4.oth_ref
  50.6 4.9 %head_grad.1 = (bf16[2048,768]{1,0:T(8,128)(2,1)}, f32[1,128]{1,0:T(1,128)}) custom-call(s32[4]{0:T(128)S(1)} %pad_add_fusion.pos_ref, bf16[384,4096]{1,0:T(8,128)(2,1)S(1)} %copy-done, bf16[384,4096]{1,0:T(8,128)(2,1)S(1)} %collective-permute-done.4.oth_ref, bf16[400,768]{1,0:T(8,128)(2,1)S(1)} %get-tuple-element.44.g_ref.g_own_ref, ...), custom_call_target="tpu_custom_call" | custom-call | flops 1 | bytes 1 | tf_op jit(solution)/shard_map/head_grad/pallas_call | solution.py:320
  55.5 0.0 collective-permute-done.1
  55.5 7.5 %collective-permute-done.2 = f16[4,8,32,384]{3,2,1,0:T(8,128)(2,1)S(1)} collective-permute-done((f16[4,8,32,384]{3,2,1,0:T(8,128)(2,1)S(1)}, f16[4,8,32,384]{3,2,1,0:T(8,128)(2,1)S(1)}, u32[]{:S(2)}, u32[]{:S(2)}) %collective-permute-start.2) | collective-permute-done | bytes 786464 | tf_op jit(solution)/shard_map/ppermute | solution.py:44
  63.1 0.0 collective-permute-done.3
  63.1 0.1 fusion.6
  63.2 1.2 %collective-permute-start.8 = (f16[8,32,384]{2,1,0:T(8,128)(2,1)S(1)}, f16[8,32,384]{2,1,0:T(8,128)(2,1)S(1)}, u32[]{:S(2)}, u32[]{:S(2)}) collective-permute-start(f16[8,32,384]{2,1,0:T(8,128)(2,1)S(1)} %fusion.6), channel_id=1, source_target_pairs={{0,128},{1,5},{2,130},{3,7},{4,132},{5,1},{6,134},{7,3},{8,136},{9... | collective-permute-start | bytes 589832 | tf_op jit(solution)/shard_map/ppermute | solution.py:44
  64.4 0.3 fusion.4
  64.7 0.9 %collective-permute-start.7 = (f16[8,32,384]{2,1,0:T(8,128)(2,1)S(1)}, f16[8,32,384]{2,1,0:T(8,128)(2,1)S(1)}, u32[]{:S(2)}, u32[]{:S(2)}) collective-permute-start(f16[8,32,384]{2,1,0:T(8,128)(2,1)S(1)} %get-tuple-element.58), channel_id=1, source_target_pairs={{0,64},{1,3},{2,66},{3,5},{4,68},{5,7},{6,70},{7,1},{8,72},{9,11},... | collective-permute-start | bytes 589832 | tf_op jit(solution)/shard_map/ppermute | solution.py:44
  65.6 2.4 %collective-permute-start.6 = (f16[8,32,384]{2,1,0:T(8,128)(2,1)S(1)}, f16[8,32,384]{2,1,0:T(8,128)(2,1)S(1)}, u32[]{:S(2)}, u32[]{:S(2)}) collective-permute-start(f16[8,32,384]{2,1,0:T(8,128)(2,1)S(1)} %get-tuple-element.57), channel_id=1, source_target_pairs={{0,192},{1,7},{2,194},{3,1},{4,196},{5,3},{6,198},{7,5},{8,200},{9... | collective-permute-start | bytes 589832 | tf_op jit(solution)/shard_map/ppermute | solution.py:44
  68.0 2.5 %collective-permute-done.8 = f16[8,32,384]{2,1,0:T(8,128)(2,1)S(1)} collective-permute-done((f16[8,32,384]{2,1,0:T(8,128)(2,1)S(1)}, f16[8,32,384]{2,1,0:T(8,128)(2,1)S(1)}, u32[]{:S(2)}, u32[]{:S(2)}) %collective-permute-start.8) | collective-permute-done | bytes 196640 | tf_op jit(solution)/shard_map/ppermute | solution.py:44
  70.6 2.0 %collective-permute-done.7 = f16[8,32,384]{2,1,0:T(8,128)(2,1)S(1)} collective-permute-done((f16[8,32,384]{2,1,0:T(8,128)(2,1)S(1)}, f16[8,32,384]{2,1,0:T(8,128)(2,1)S(1)}, u32[]{:S(2)}, u32[]{:S(2)}) %collective-permute-start.7) | collective-permute-done | bytes 196640 | tf_op jit(solution)/shard_map/ppermute | solution.py:44
  72.6 0.0 collective-permute-done.6
  72.6 0.2 fusion.3
  72.8 12.0 %all_to_all.17 = f16[8,32,384]{2,1,0:T(8,128)(2,1)S(1)} all-to-all(f16[8,32,384]{2,1,0:T(8,128)(2,1)S(1)} %fusion.3), channel_id=1, replica_groups=mesh['y'=4,'z'=8,'x'=4,'c'=2] {'z'}, dimensions={0} | all-to-all | bytes 393216 | tf_op jit(solution)/shard_map/all_to_all | solution.py:390
  84.8 0.7 multiply_reduce_fusion
  (4 shorter events, 0.1 us)
Async XLA Ops:
  0.6 6.2 %collective-permute-start = (bf16[768,384]{1,0:T(8,128)(2,1)}, bf16[768,384]{1,0:T(8,128)(2,1)S(1)}, u32[]{:S(2)}, u32[]{:S(2)}) collective-permute-start(bf16[768,384]{1,0:T(8,128)(2,1)} %own_ref.2), channel_id=1, source_target_pairs={{0,1},{1,0},{2,3},{3,2},{4,5},{5,4},{6,7},{7,6},{8,9},{9,8},{10,11... | collective-permute-start | bytes 1769480 | tf_op jit(solution)/shard_map/ppermute | solution.py:32
  0.7 38.0 %slice-start = ((s8[6291456]{0:T(1024)(128)(4,1)}), s8[4194304]{0:T(1024)(128)(4,1)S(1)}, s32[]{:S(2)}) async-start(s8[6291456]{0:T(1024)(128)(4,1)} %bitcast.25), calls=%async_computation.3 | async-start | bytes 8388608
  0.8 6.0 %copy-start.1 = (bf16[768,384]{1,0:T(8,128)(2,1)S(1)}, bf16[768,384]{1,0:T(8,128)(2,1)}, u32[]{:S(2)}) copy-start(bf16[768,384]{1,0:T(8,128)(2,1)} %own_ref.2) | copy-start | bytes 1769476
  0.8 6.0 %copy-start.2 = (s32[384]{0:T(512)S(1)}, s32[384]{0:T(512)}, u32[]{:S(2)}) copy-start(s32[384]{0:T(512)} %param.9) | copy-start | bytes 4612
  0.8 6.0 %copy-start.3 = (s32[768]{0:T(1024)S(1)}, s32[768]{0:T(1024)}, u32[]{:S(2)}) copy-start(s32[768]{0:T(1024)} %param.10) | copy-start | bytes 9220
  0.8 23.2 %copy-start = (bf16[384,4096]{1,0:T(8,128)(2,1)S(1)}, bf16[384,4096]{1,0:T(8,128)(2,1)}, u32[]{:S(2)}) copy-start(bf16[384,4096]{1,0:T(8,128)(2,1)} %own_ref.3) | copy-start | bytes 9437188
  0.8 37.9 %slice-start.1 = ((s8[6291456]{0:T(1024)(128)(4,1)}), s8[2097152]{0:T(1024)(128)(4,1)S(1)}, s32[]{:S(2)}) async-start(s8[6291456]{0:T(1024)(128)(4,1)} %bitcast.25), calls=%async_computation.4 | async-start | bytes 4194304
  6.8 32.0 %copy-start.4 = (f32[384]{0:T(512)S(1)}, f32[384]{0:T(512)}, u32[]{:S(2)}) copy-start(f32[384]{0:T(512)} %param.11) | copy-start | bytes 4612
  24.1 26.5 %collective-permute-start.4 = (bf16[384,4096]{1,0:T(8,128)(2,1)S(1)}, bf16[384,4096]{1,0:T(8,128)(2,1)S(1)}, u32[]{:S(2)}, u32[]{:S(2)}) collective-permute-start(bf16[384,4096]{1,0:T(8,128)(2,1)S(1)} %copy-done), channel_id=1, source_target_pairs={{0,1},{1,0},{2,3},{3,2},{4,5},{5,4},{6,7},{7,6},{8,9},{9,8},{10,11... | collective-permute-start | bytes 9437192 | tf_op jit(solution)/shard_map/ppermute | solution.py:32
  41.0 14.5 %collective-permute-start.1 = (f16[4,8,32,384]{3,2,1,0:T(8,128)(2,1)S(1)}, f16[4,8,32,384]{3,2,1,0:T(8,128)(2,1)S(1)}, u32[]{:S(2)}, u32[]{:S(2)}) collective-permute-start(f16[4,8,32,384]{3,2,1,0:T(8,128)(2,1)S(1)} %multiply_convert_fusion.2), channel_id=1, source_target_pairs={{0,4},{1,129},{2,6},{3,131},{4,0},{5,133},{6,2},{7,135},{8,12},{9,... | collective-permute-start | bytes 2359304 | tf_op jit(solution)/shard_map/ppermute | solution.py:44
  45.2 17.9 %collective-permute-start.2 = (f16[4,8,32,384]{3,2,1,0:T(8,128)(2,1)S(1)}, f16[4,8,32,384]{3,2,1,0:T(8,128)(2,1)S(1)}, u32[]{:S(2)}, u32[]{:S(2)}) collective-permute-start(f16[4,8,32,384]{3,2,1,0:T(8,128)(2,1)S(1)} %get-tuple-element.41), channel_id=1, source_target_pairs={{0,2},{1,65},{2,4},{3,67},{4,6},{5,69},{6,0},{7,71},{8,10},{9,73},... | collective-permute-start | bytes 2359304 | tf_op jit(solution)/shard_map/ppermute | solution.py:44
  46.0 17.1 %collective-permute-start.3 = (f16[4,8,32,384]{3,2,1,0:T(8,128)(2,1)S(1)}, f16[4,8,32,384]{3,2,1,0:T(8,128)(2,1)S(1)}, u32[]{:S(2)}, u32[]{:S(2)}) collective-permute-start(f16[4,8,32,384]{3,2,1,0:T(8,128)(2,1)S(1)} %get-tuple-element.42), channel_id=1, source_target_pairs={{0,6},{1,193},{2,0},{3,195},{4,2},{5,197},{6,4},{7,199},{8,14},{9,... | collective-permute-start | bytes 2359304 | tf_op jit(solution)/shard_map/ppermute | solution.py:44
  48.5 2.0 %collective-permute-start.5 = (bf16[400,768]{1,0:T(8,128)(2,1)S(1)}, bf16[400,768]{1,0:T(8,128)(2,1)S(1)}, u32[]{:S(2)}, u32[]{:S(2)}) collective-permute-start(bf16[400,768]{1,0:T(8,128)(2,1)S(1)} %get-tuple-element.44.g_ref.g_own_ref), channel_id=1, source_target_pairs={{0,1},{1,0},{2,3},{3,2},{4,5},{5,4},{6,7},{7,6},{8,9},{9,8},{10,11... | collective-permute-start | bytes 1843208 | tf_op jit(solution)/shard_map/ppermute | solution.py:32
  63.2 7.4 %collective-permute-start.8 = (f16[8,32,384]{2,1,0:T(8,128)(2,1)S(1)}, f16[8,32,384]{2,1,0:T(8,128)(2,1)S(1)}, u32[]{:S(2)}, u32[]{:S(2)}) collective-permute-start(f16[8,32,384]{2,1,0:T(8,128)(2,1)S(1)} %fusion.6), channel_id=1, source_target_pairs={{0,128},{1,5},{2,130},{3,7},{4,132},{5,1},{6,134},{7,3},{8,136},{9... | collective-permute-start | bytes 589832 | tf_op jit(solution)/shard_map/ppermute | solution.py:44
  64.7 7.9 %collective-permute-start.7 = (f16[8,32,384]{2,1,0:T(8,128)(2,1)S(1)}, f16[8,32,384]{2,1,0:T(8,128)(2,1)S(1)}, u32[]{:S(2)}, u32[]{:S(2)}) collective-permute-start(f16[8,32,384]{2,1,0:T(8,128)(2,1)S(1)} %get-tuple-element.58), channel_id=1, source_target_pairs={{0,64},{1,3},{2,66},{3,5},{4,68},{5,7},{6,70},{7,1},{8,72},{9,11},... | collective-permute-start | bytes 589832 | tf_op jit(solution)/shard_map/ppermute | solution.py:44
  65.6 7.0 %collective-permute-start.6 = (f16[8,32,384]{2,1,0:T(8,128)(2,1)S(1)}, f16[8,32,384]{2,1,0:T(8,128)(2,1)S(1)}, u32[]{:S(2)}, u32[]{:S(2)}) collective-permute-start(f16[8,32,384]{2,1,0:T(8,128)(2,1)S(1)} %get-tuple-element.57), channel_id=1, source_target_pairs={{0,192},{1,7},{2,194},{3,1},{4,196},{5,3},{6,198},{7,5},{8,200},{9... | collective-permute-start | bytes 589832 | tf_op jit(solution)/shard_map/ppermute | solution.py:44
